TPU v7x, 32 devices: a whole 2x2x4 slice. The times are simulated.
32 devices in a mesh: expert: 8 (over z, x), tensor: 4 (over y, core).
Axes of the slice: x: 2, y: 2, z: 4, core: 2. Of those that a mesh axis runs over, the one named last changes fastest.
Arguments:
- hidden_in: bfloat16 [2048, 2048], P('expert'), may hold values from -6 to 6
- attn_gain: float32 [2048], replicated, may hold values from 0.5 to 1.5
- query_weight: bfloat16 [2048, 3072], P(None, 'tensor'), may hold values from -0.125 to 0.125
- latent_weight: bfloat16 [2048, 576], replicated, may hold values from -0.125 to 0.125
- latent_gain: float32 [512], replicated, may hold values from 0.5 to 1.5
- expand_weight: bfloat16 [512, 4096], P(None, 'tensor'), may hold values from -0.25 to 0.25
- output_weight: bfloat16 [2048, 2048], P('tensor'), may hold values from -2 to 2
- moe_gain: float32 [2048], replicated, may hold values from 0.5 to 1.5
- shared_gate: bfloat16 [2048, 2816], P(None, 'tensor'), may hold values from -0.125 to 0.125
- shared_up: bfloat16 [2048, 2816], P(None, 'tensor'), may hold values from -0.125 to 0.125
- shared_down: bfloat16 [2816, 2048], P('tensor'), may hold values from -0.109375 to 0.109375
- expert_gate: bfloat16 [16, 2048, 1408], P('expert', None, 'tensor'), may hold values from -0.125 to 0.125
- expert_up: bfloat16 [16, 2048, 1408], P('expert', None, 'tensor'), may hold values from -0.125 to 0.125
- expert_down: bfloat16 [16, 1408, 2048], P('expert', 'tensor'), may hold values from -0.625 to 0.625
- gate_values: float32 [2048, 6], P('expert'), may hold values from 0.15 to 0.45
- expert_routes: int32 [2048, 6], P('expert'), may hold values from 0 to 15, all different within a row; in each aligned block of 256 rows (0 to 255, 256 to 511, ...) at most 192 rows name the same one
- segments: int32 [2048], replicated, may hold values from 0 to 4, as said below
- cotangent: bfloat16 [2048, 2048], P('expert'), may hold values from -6 to 6
Outputs:
- layer_out: bfloat16 [2048, 2048], P('expert')
- grad_hidden: float32 [2048, 2048], P('expert')
- grad_attn_gain: float32 [2048], replicated
- grad_query_weight: float32 [2048, 3072], P(None, 'tensor')
- grad_latent_weight: float32 [2048, 576], replicated
- grad_latent_gain: float32 [512], replicated
- grad_expand_weight: float32 [512, 4096], P(None, 'tensor')
- grad_output_weight: float32 [2048, 2048], P('tensor')
- grad_moe_gain: float32 [2048], replicated
- grad_shared_gate: float32 [2048, 2816], P(None, 'tensor')
- grad_shared_up: float32 [2048, 2816], P(None, 'tensor')
- grad_shared_down: float32 [2816, 2048], P('tensor')
- grad_expert_gate: float32 [16, 2048, 1408], P('expert', None, 'tensor')
- grad_expert_up: float32 [16, 2048, 1408], P('expert', None, 'tensor')
- grad_expert_down: float32 [16, 1408, 2048], P('expert', 'tensor')
Inputs may be any that keep to these rules, and one draw needn't show every extreme that they name: `expert_routes`: each row names 6 different experts; among the 256 rows of one device no expert is named by more than 192 rows, and in every draw some expert reaches 192. `segments`: the first 1024 entries are 0; the rest never fall and take each of 1 to 4 at least once.
All inputs are finite; a program needn't handle non-finite values.
Results may differ from a plain program's by a relative error of at most 0.024.
Values may be sent and summed in bfloat16 or wider, within the bound.
A program may use at most 384 MiB of HBM per device.

v0:
```python
from functools import partial

import jax
import jax.numpy as jnp
from jax import lax
from jax.sharding import PartitionSpec as P

NOPE = 128
ROPE = 64
VDIM = 128
LATENT = 512
TOP = 6
EXP_DEV = 2


epsilon = 1e-06
masked_out = -1e30


def rms_scale(values, gain_vec):
    return (
        values * lax.rsqrt(jnp.mean(values * values, axis=-1, keepdims=True) + epsilon) * gain_vec
    )


def rotate(values, places):
    halfway = values.shape[-1] // 2
    frequency = 10000.0 ** (-jnp.arange(halfway, dtype=jnp.float32) / halfway)
    angles = places.astype(jnp.float32)[:, None] * frequency[None, :]
    cosine = jnp.cos(angles)
    sine_part = jnp.sin(angles)
    if values.ndim == 3:
        cosine = cosine[:, None, :]
        sine_part = sine_part[:, None, :]
    first_half = values[..., :halfway]
    second = values[..., halfway:]
    return jnp.concatenate(
        [first_half * cosine - second * sine_part, second * cosine + first_half * sine_part],
        axis=-1,
    )


def seq_places(segments):
    total_rows = segments.shape[0]
    ordinal = jnp.arange(total_rows, dtype=jnp.int32)
    starts = jnp.concatenate(
        [jnp.ones((1,), jnp.int32), (segments[1:] != segments[:-1]).astype(jnp.int32)]
    )
    seg_start = lax.cummax(jnp.where(starts > 0, ordinal, 0), axis=0)
    return jnp.where(segments == 0, ordinal, total_rows // 2 + ordinal - seg_start)


def silu_product(gate_pre, up_pre):
    return jax.nn.silu(gate_pre) * up_pre


def slot_rows(expert_routes, experts_all, capacity):
    onehot = (
        expert_routes[:, :, None] == jnp.arange(experts_all, dtype=jnp.int32)[None, None, :]
    ).astype(jnp.int32)
    per_token = jnp.sum(onehot, axis=1)
    earlier = jnp.cumsum(per_token, axis=0) - per_token
    member_rank = jnp.sum(onehot * earlier[:, None, :], axis=-1)
    return expert_routes * capacity + member_rank


def score_block(queries, key_plain, rope_all, visible):
    scale_factor = (NOPE + ROPE) ** (-0.5)
    raw_scores = jnp.einsum(
        "thc,shc->hts", queries[..., :NOPE], key_plain, preferred_element_type=jnp.float32
    )
    raw_scores = raw_scores + jnp.einsum(
        "thr,sr->hts", queries[..., NOPE:], rope_all, preferred_element_type=jnp.float32
    )
    return jnp.where(visible[None], scale_factor * raw_scores, masked_out)


def attention_pass(
    hidden_f,
    attn_gain,
    query_weight,
    latent_weight,
    latent_gain,
    expand_weight,
    output_weight,
    places,
    visible,
):
    tok_rows = hidden_f.shape[0]
    normed = rms_scale(hidden_f, attn_gain).astype(jnp.bfloat16)
    q_raw = jnp.dot(normed, query_weight, preferred_element_type=jnp.float32)
    heads_here = q_raw.shape[1] // (NOPE + ROPE)
    q_raw = q_raw.reshape(tok_rows, heads_here, NOPE + ROPE)
    queries = jnp.concatenate(
        [q_raw[..., :NOPE], rotate(q_raw[..., NOPE:], places)], axis=-1
    ).astype(jnp.bfloat16)
    compressed = jnp.dot(normed, latent_weight, preferred_element_type=jnp.float32)
    latents = rms_scale(compressed[:, :LATENT], latent_gain).astype(jnp.bfloat16)
    key_rope = rotate(compressed[:, LATENT:], places).astype(jnp.bfloat16)
    latents_all, rope_all = (
        lax.all_gather(latents, "expert", axis=0, tiled=True),
        lax.all_gather(key_rope, "expert", axis=0, tiled=True),
    )
    expanded = jnp.dot(latents_all, expand_weight, preferred_element_type=jnp.float32).astype(
        jnp.bfloat16
    )
    expanded = expanded.reshape(latents_all.shape[0], heads_here, NOPE + VDIM)
    scores = score_block(queries, expanded[..., :NOPE], rope_all, visible)
    peak = jnp.max(scores, axis=-1, keepdims=True)
    weights = jnp.exp(scores - peak)
    total_weight = jnp.sum(weights, axis=-1, keepdims=True)
    probs = (weights / total_weight).astype(jnp.bfloat16)
    context = jnp.einsum(
        "hts,shv->thv", probs, expanded[..., NOPE:], preferred_element_type=jnp.float32
    ).astype(jnp.bfloat16)
    merged = context.reshape(tok_rows, heads_here * VDIM)
    attn_out = lax.psum(
        jnp.dot(merged, output_weight, preferred_element_type=jnp.float32), "tensor"
    )
    residual = hidden_f + attn_out
    log_total = peak + jnp.log(total_weight)
    return (
        normed,
        q_raw,
        queries,
        compressed,
        latents,
        rope_all,
        expanded,
        merged,
        log_total,
        residual,
    )


def dispatch(moe_in, targets, experts_all, capacity, groups):
    tok_rows, model_width = moe_in.shape
    spread = jnp.broadcast_to(moe_in[:, None, :], (tok_rows, TOP, model_width))
    buffer = jnp.zeros((experts_all * capacity, model_width), jnp.bfloat16).at[targets].set(spread)
    buffer = buffer.reshape(groups, experts_all * capacity // groups, model_width)
    arrived = lax.all_to_all(buffer, "expert", split_axis=0, concat_axis=0, tiled=True)
    return arrived.reshape(groups, EXP_DEV, capacity, model_width)


def expert_front(arrived, expert_gate, expert_up):
    gate_pre = jnp.einsum(
        "skcd,kdf->skcf", arrived, expert_gate, preferred_element_type=jnp.float32
    )
    up_pre = jnp.einsum("skcd,kdf->skcf", arrived, expert_up, preferred_element_type=jnp.float32)
    return (gate_pre, up_pre)


def shards(
    hidden_in,
    attn_gain,
    query_weight,
    latent_weight,
    latent_gain,
    expand_weight,
    output_weight,
    moe_gain,
    shared_gate,
    shared_up,
    shared_down,
    expert_gate,
    expert_up,
    expert_down,
    gate_values,
    expert_routes,
    segments,
    cotangent,
):
    tok_rows, model_width = hidden_in.shape
    groups = lax.axis_size("expert")
    device = lax.axis_index("expert")
    total_rows = segments.shape[0]
    start_row = device * tok_rows
    places = lax.dynamic_slice_in_dim(seq_places(segments), start_row, tok_rows)
    own_seg = lax.dynamic_slice_in_dim(segments, start_row, tok_rows)
    own_ordinal = start_row + jnp.arange(tok_rows, dtype=jnp.int32)
    key_ordinal = jnp.arange(total_rows, dtype=jnp.int32)
    visible = (key_ordinal[None, :] <= own_ordinal[:, None]) & (
        (segments[None, :] == own_seg[:, None]) | (segments[None, :] == 0)
    )
    hidden_f = hidden_in.astype(jnp.float32)
    experts_all = EXP_DEV * groups
    capacity = 2 * tok_rows * TOP // experts_all
    targets = slot_rows(expert_routes, experts_all, capacity)
    scale_factor = (NOPE + ROPE) ** (-0.5)
    first_pass = attention_pass(
        hidden_f,
        attn_gain,
        query_weight,
        latent_weight,
        latent_gain,
        expand_weight,
        output_weight,
        places,
        visible,
    )
    residual = first_pass[9]
    moe_in = rms_scale(residual, moe_gain).astype(jnp.bfloat16)
    gate_pre = jnp.dot(moe_in, shared_gate, preferred_element_type=jnp.float32)
    up_pre = jnp.dot(moe_in, shared_up, preferred_element_type=jnp.float32)
    shared_act = silu_product(gate_pre, up_pre).astype(jnp.bfloat16)
    shared_part = jnp.dot(shared_act, shared_down, preferred_element_type=jnp.float32)
    arrived = dispatch(moe_in, targets, experts_all, capacity, groups)
    expert_g, expert_u = expert_front(arrived, expert_gate, expert_up)
    expert_act = silu_product(expert_g, expert_u).astype(jnp.bfloat16)
    expert_out = jnp.einsum(
        "skcf,kfd->skcd", expert_act, expert_down, preferred_element_type=jnp.float32
    ).astype(jnp.bfloat16)
    returned = lax.all_to_all(
        expert_out.reshape(groups, -1, model_width),
        "expert",
        split_axis=0,
        concat_axis=0,
        tiled=True,
    ).reshape(-1, model_width)
    routed = jnp.sum(gate_values[:, :, None] * returned[targets].astype(jnp.float32), axis=1)
    moe_out = lax.psum((shared_part + routed).astype(jnp.bfloat16), "tensor").astype(jnp.float32)
    layer_out = (residual + moe_out).astype(jnp.bfloat16)
    again = attention_pass(
        hidden_f,
        attn_gain,
        query_weight,
        latent_weight,
        latent_gain,
        expand_weight,
        output_weight,
        places,
        visible,
    )
    normed, q_raw, queries, compressed, latents, rope_all, expanded, merged, log_total, residual = (
        again
    )
    heads_here = queries.shape[1]
    moe_in = rms_scale(residual, moe_gain).astype(jnp.bfloat16)
    gate_pre = jnp.dot(moe_in, shared_gate, preferred_element_type=jnp.float32)
    up_pre = jnp.dot(moe_in, shared_up, preferred_element_type=jnp.float32)
    shared_act = silu_product(gate_pre, up_pre).astype(jnp.bfloat16)
    arrived_again = dispatch(moe_in, targets, experts_all, capacity, groups)
    expert_g, expert_u = expert_front(arrived_again, expert_gate, expert_up)
    expert_act = silu_product(expert_g, expert_u).astype(jnp.bfloat16)
    grad_out = cotangent.astype(jnp.float32)
    grad_shared_down = jnp.dot(shared_act.T, cotangent, preferred_element_type=jnp.float32)
    grad_shared_act = jnp.dot(cotangent, shared_down.T, preferred_element_type=jnp.float32)
    _, pull_shared = jax.vjp(silu_product, gate_pre, up_pre)
    grad_gate_pre, grad_up_pre = pull_shared(grad_shared_act)
    grad_gate_low = grad_gate_pre.astype(jnp.bfloat16)
    grad_up_low = grad_up_pre.astype(jnp.bfloat16)
    grad_shared_gate = jnp.dot(moe_in.T, grad_gate_low, preferred_element_type=jnp.float32)
    grad_shared_up = jnp.dot(moe_in.T, grad_up_low, preferred_element_type=jnp.float32)
    grad_moe_part = jnp.dot(
        grad_gate_low, shared_gate.T, preferred_element_type=jnp.float32
    ) + jnp.dot(grad_up_low, shared_up.T, preferred_element_type=jnp.float32)
    slot_grads = (gate_values[:, :, None] * grad_out[:, None, :]).astype(jnp.bfloat16)
    grad_buffer = (
        jnp.zeros((experts_all * capacity, model_width), jnp.bfloat16).at[targets].set(slot_grads)
    )
    grad_buffer = grad_buffer.reshape(groups, -1, model_width)
    grad_arrived = lax.all_to_all(grad_buffer, "expert", split_axis=0, concat_axis=0, tiled=True)
    grad_arrived = grad_arrived.reshape(groups, EXP_DEV, capacity, model_width)
    grad_expert_down = jnp.einsum(
        "skcf,skcd->kfd", expert_act, grad_arrived, preferred_element_type=jnp.float32
    )
    grad_active = jnp.einsum(
        "skcd,kfd->skcf", grad_arrived, expert_down, preferred_element_type=jnp.float32
    )
    _, pull_expert = jax.vjp(silu_product, expert_g, expert_u)
    grad_eg, grad_eu = pull_expert(grad_active)
    grad_eg_low = grad_eg.astype(jnp.bfloat16)
    grad_eu_low = grad_eu.astype(jnp.bfloat16)
    grad_expert_gate = jnp.einsum(
        "skcd,skcf->kdf", arrived_again, grad_eg_low, preferred_element_type=jnp.float32
    )
    grad_expert_up = jnp.einsum(
        "skcd,skcf->kdf", arrived_again, grad_eu_low, preferred_element_type=jnp.float32
    )
    grad_rows = jnp.einsum(
        "skcf,kdf->skcd", grad_eg_low, expert_gate, preferred_element_type=jnp.float32
    )
    grad_rows = (
        grad_rows
        + jnp.einsum("skcf,kdf->skcd", grad_eu_low, expert_up, preferred_element_type=jnp.float32)
    ).astype(jnp.bfloat16)
    grad_back = lax.all_to_all(
        grad_rows.reshape(groups, -1, model_width),
        "expert",
        split_axis=0,
        concat_axis=0,
        tiled=True,
    ).reshape(-1, model_width)
    routed_grad = jnp.sum(grad_back[targets].astype(jnp.float32), axis=1)
    grad_moe_in = lax.psum(grad_moe_part + routed_grad, "tensor")
    _, pull_moe = jax.vjp(rms_scale, residual, moe_gain)
    grad_residual, grad_moe_gain = pull_moe(grad_moe_in)
    grad_residual = grad_residual + grad_out
    grad_res_low = grad_residual.astype(jnp.bfloat16)
    grad_output_weight = jnp.dot(merged.T, grad_res_low, preferred_element_type=jnp.float32)
    grad_context = (
        jnp.dot(grad_res_low, output_weight.T, preferred_element_type=jnp.float32)
        .reshape(tok_rows, heads_here, VDIM)
        .astype(jnp.bfloat16)
    )
    key_plain = expanded[..., :NOPE]
    scores = score_block(queries, key_plain, rope_all, visible)
    probs = jnp.exp(scores - log_total)
    grad_probs = jnp.einsum(
        "thv,shv->hts", grad_context, expanded[..., NOPE:], preferred_element_type=jnp.float32
    )
    grad_values = jnp.einsum(
        "hts,thv->shv", probs.astype(jnp.bfloat16), grad_context, preferred_element_type=jnp.float32
    )
    grad_scores = (
        probs * (grad_probs - jnp.sum(probs * grad_probs, axis=-1, keepdims=True))
    ).astype(jnp.bfloat16)
    grad_q_plain = scale_factor * jnp.einsum(
        "hts,shc->thc", grad_scores, key_plain, preferred_element_type=jnp.float32
    )
    grad_q_rope = scale_factor * jnp.einsum(
        "hts,sr->thr", grad_scores, rope_all, preferred_element_type=jnp.float32
    )
    grad_k_plain = scale_factor * jnp.einsum(
        "hts,thc->shc", grad_scores, queries[..., :NOPE], preferred_element_type=jnp.float32
    )
    grad_k_rope = scale_factor * jnp.einsum(
        "hts,thr->sr", grad_scores, queries[..., NOPE:], preferred_element_type=jnp.float32
    )
    grad_expanded = jnp.concatenate([grad_k_plain, grad_values], axis=-1).reshape(
        total_rows, heads_here * (NOPE + VDIM)
    )
    grad_expanded, grad_k_rope = (
        lax.psum_scatter(grad_expanded, "expert", scatter_dimension=0, tiled=True),
        lax.psum_scatter(grad_k_rope, "expert", scatter_dimension=0, tiled=True),
    )
    grad_exp_low = grad_expanded.astype(jnp.bfloat16)
    grad_expand_weight = jnp.dot(latents.T, grad_exp_low, preferred_element_type=jnp.float32)
    grad_latents = jnp.dot(grad_exp_low, expand_weight.T, preferred_element_type=jnp.float32)
    _, pull_qrope = jax.vjp(partial(rotate, places=places), q_raw[..., NOPE:])
    (grad_q_turned,) = pull_qrope(grad_q_rope)
    grad_q_low = (
        jnp.concatenate([grad_q_plain, grad_q_turned], axis=-1)
        .reshape(tok_rows, -1)
        .astype(jnp.bfloat16)
    )
    grad_query_weight = jnp.dot(normed.T, grad_q_low, preferred_element_type=jnp.float32)
    grad_normed_q = jnp.dot(grad_q_low, query_weight.T, preferred_element_type=jnp.float32)
    grad_normed_q, grad_latents, grad_k_rope = (
        lax.psum(grad_normed_q.astype(jnp.bfloat16), "tensor").astype(jnp.float32),
        lax.psum(grad_latents.astype(jnp.bfloat16), "tensor").astype(jnp.float32),
        lax.psum(grad_k_rope.astype(jnp.bfloat16), "tensor").astype(jnp.float32),
    )
    _, pull_latent = jax.vjp(rms_scale, compressed[:, :LATENT], latent_gain)
    grad_plain_latent, grad_latent_gain = pull_latent(grad_latents)
    _, pull_krope = jax.vjp(partial(rotate, places=places), compressed[:, LATENT:])
    (grad_k_turned,) = pull_krope(grad_k_rope)
    grad_comp_low = jnp.concatenate([grad_plain_latent, grad_k_turned], axis=-1).astype(
        jnp.bfloat16
    )
    grad_latent_weight = jnp.dot(normed.T, grad_comp_low, preferred_element_type=jnp.float32)
    grad_normed = grad_normed_q + jnp.dot(
        grad_comp_low, latent_weight.T, preferred_element_type=jnp.float32
    )
    _, pull_input = jax.vjp(rms_scale, hidden_f, attn_gain)
    grad_input_norm, grad_attn_gain = pull_input(grad_normed)
    grad_hidden = grad_residual + grad_input_norm
    summed = (
        lax.psum(grad_attn_gain.astype(jnp.bfloat16), "expert").astype(jnp.float32),
        lax.psum(grad_query_weight.astype(jnp.bfloat16), "expert").astype(jnp.float32),
        lax.psum(grad_latent_weight.astype(jnp.bfloat16), "expert").astype(jnp.float32),
        lax.psum(grad_latent_gain.astype(jnp.bfloat16), "expert").astype(jnp.float32),
        lax.psum(grad_expand_weight.astype(jnp.bfloat16), "expert").astype(jnp.float32),
        lax.psum(grad_output_weight.astype(jnp.bfloat16), "expert").astype(jnp.float32),
        lax.psum(grad_moe_gain.astype(jnp.bfloat16), "expert").astype(jnp.float32),
        lax.psum(grad_shared_gate.astype(jnp.bfloat16), "expert").astype(jnp.float32),
        lax.psum(grad_shared_up.astype(jnp.bfloat16), "expert").astype(jnp.float32),
        lax.psum(grad_shared_down.astype(jnp.bfloat16), "expert").astype(jnp.float32),
    )
    return (
        layer_out,
        grad_hidden,
        summed[0],
        summed[1],
        summed[2],
        summed[3],
        summed[4],
        summed[5],
        summed[6],
        summed[7],
        summed[8],
        summed[9],
        grad_expert_gate,
        grad_expert_up,
        grad_expert_down,
    )


def solution(mesh):
    placed = (
        P("expert", None),
        P(),
        P(None, "tensor"),
        P(),
        P(),
        P(None, "tensor"),
        P("tensor", None),
        P(),
        P(None, "tensor"),
        P(None, "tensor"),
        P("tensor", None),
        P("expert", None, "tensor"),
        P("expert", None, "tensor"),
        P("expert", "tensor", None),
        P("expert", None),
        P("expert", None),
        P(),
        P("expert", None),
    )
    return jax.shard_map(
        shards,
        mesh=mesh,
        in_specs=placed,
        out_specs=(
            P("expert", None),
            P("expert", None),
            P(),
            P(None, "tensor"),
            P(),
            P(),
            P(None, "tensor"),
            P("tensor", None),
            P(),
            P(None, "tensor"),
            P(None, "tensor"),
            P("tensor", None),
            P("expert", None, "tensor"),
            P("expert", None, "tensor"),
            P("expert", "tensor", None),
        ),
        check_vma=False,
    )
```

profile of v0, /device:TPU:0, one launch (start us, length us, event | category | flops | bytes accessed | tf_op | source)
XLA Modules:
  0.0 2141.1 jit_solution(9977975420635886671)
XLA Ops:
  9.5 2.9 fusion.121
  16.2 33.2 %all_gather.9 = bf16[2048,64]{0,1:T(8,128)(2,1)S(1)} all-gather(bf16[256,64]{0,1:T(8,128)(2,1)S(1)} %pad_maximum_fusion.8), channel_id=1, replica_groups=mesh['expert'=8,'tensor'=4] {'expert'}, dimensions={0}, use_global_device_ids=true | all-gather | bytes 294912 | tf_op jit(solution)/shard_map/all_gather | solution.py:102
  49.4 2.7 fusion.119
  54.6 14.4 all-gather.2.cloned.1.call-done
  69.0 4.3 convolution_convert_fusion
  87.1 48.6 %all-reduce.12.cloned.1.call-done = f32[256,2048]{1,0:T(8,128)} async-done(((f32[256,2048]{1,0:T(8,128)}), f32[256,2048]{1,0:T(8,128)}) %all-reduce.12.cloned.1.call-update) | async-done | bytes 2097168 | tf_op jit(solution)/shard_map/psum | solution.py:117
  140.5 5.9 broadcast_in_dim.35
  146.4 11.0 reshape.333
  157.5 17.7 scatter_custom_fusion
  175.2 5.5 all-to-all-start
  182.4 3.9 multiply_convert_fusion
  186.3 11.0 reshape.341
  197.3 17.3 scatter_custom_fusion.1
  214.6 239.1 %all-to-all-done = bf16[8,384,2048]{2,1,0:T(8,128)(2,1)} async-done(((bf16[8,384,2048]{2,1,0:T(8,128)(2,1)}), bf16[8,384,2048]{2,1,0:T(8,128)(2,1)}, u32[]{:S(2)}, u32[]{:S(2)}) %all-to-all-start) | async-done | bytes 12582944 | tf_op jit(solution)/shard_map/all_to_all | solution.py:141
  453.7 5.5 all-to-all-start.2
  459.2 12.0 fusion.5
  471.3 11.2 fusion.7
  482.5 248.8 %all-to-all-done.2 = bf16[8,384,2048]{2,1,0:T(8,128)(2,1)} async-done(((bf16[8,384,2048]{2,1,0:T(8,128)(2,1)}), bf16[8,384,2048]{2,1,0:T(8,128)(2,1)}, u32[]{:S(2)}, u32[]{:S(2)}) %all-to-all-start.2) | async-done | bytes 12582944 | tf_op jit(solution)/shard_map/all_to_all | solution.py:262
  731.2 14.9 fusion.20
  746.2 11.8 fusion.37
  757.9 16.0 fusion
  773.9 10.8 copy.104
  784.7 5.4 all-to-all-start.3
  790.0 9.1 convert_bitcast_fusion
  799.1 5.1 copy.102
  804.2 257.3 %all-to-all-done.3 = bf16[8,384,2048]{2,1,0:T(8,128)(2,1)} async-done(((bf16[8,384,2048]{2,1,0:T(8,128)(2,1)}), bf16[8,384,2048]{2,1,0:T(8,128)(2,1)}, u32[]{:S(2)}, u32[]{:S(2)}) %all-to-all-start.3) | async-done | bytes 12582944 | tf_op jit(solution)/shard_map/all_to_all | solution.py:287
  1061.6 5.4 all-to-all-start.1
  1067.0 3.2 fusion.126
  1076.7 19.3 gather_fusion.1
  1096.0 11.7 reshape.354
  1107.7 9.8 reduce_sum.142
  1117.5 5.5 fusion.42
  1123.1 52.1 %all-reduce.14.cloned.1.call-done = f32[256,2048]{1,0:T(8,128)} async-done(((f32[256,2048]{1,0:T(8,128)}), f32[256,2048]{1,0:T(8,128)}) %all-reduce.14.cloned.1.call-update) | async-done | bytes 2097168 | tf_op jit(solution)/shard_map/psum | solution.py:295
  1175.2 2.9 multiply_reduce_fusion.2
  1185.3 6.5 multiply_reduce_fusion.1
  1197.7 3.9 pad_maximum_fusion
  1201.8 3.9 convolution_convert_fusion.3
  1210.7 196.4 %all-to-all-done.1 = bf16[8,384,2048]{2,1,0:T(8,128)(2,1)} async-done(((bf16[8,384,2048]{2,1,0:T(8,128)(2,1)}), bf16[8,384,2048]{2,1,0:T(8,128)(2,1)}, u32[]{:S(2)}, u32[]{:S(2)}) %all-to-all-start.1) | async-done | bytes 12582944 | tf_op jit(solution)/shard_map/all_to_all | solution.py:213
  1407.1 19.6 gather_fusion
  1426.7 11.8 reshape.353
  1438.5 9.5 multiply_reduce_fusion
  1454.1 4.4 fusion.72
  1461.3 2.7 convolution_convert_fusion.9
  1464.1 3.7 convolution_convert_fusion.6
  1467.9 3.9 convolution_convert_fusion.1
  1471.8 43.7 %reduce-scatter.5.cloned.1.call-done = f32[256,64]{0,1:T(8,128)} async-done(((f32[2048,64]{0,1:T(8,128)}), f32[256,64]{0,1:T(8,128)}) %reduce-scatter.5.cloned.1.call-update) | async-done | bytes 65552 | tf_op jit(solution)/shard_map/reduce_scatter | solution.py:335
  1516.3 10.7 psum.120
  1527.3 2.7 convolution_convert_fusion.8
  1530.0 43.6 %all-reduce.18.cloned.1.call-done = (bf16[256,2048]{1,0:T(8,128)(2,1)}, bf16[256,2048]{1,0:T(8,128)(2,1)}, bf16[256,512]{0,1:T(8,128)(2,1)}) async-done(((bf16[256,2048]{1,0:T(8,128)(2,1)}, bf16[256,2048]{1,0:T(8,128)(2,1)}, bf16[256,512]{0,1:T(8,128)(2,1)}), (bf16[256,2048]{1,0:T(8,128)(2,1)}, bf16[256,2048]{1,0:T(8,128)(2,1)}, bf16[256,512]{0,1:T(8,128)(2,1)})) %all-reduce.18.cloned.1.call-update) | async-done | bytes 2359312 | tf_op jit(solution)/shard_map/psum | solution.py:221
  1576.3 3.5 convolution_convert_fusion.5
  1579.8 10.1 convolution_bitcast_fusion
  1589.9 10.5 convolution_bitcast_fusion.1
  1600.4 10.6 fusion.29
  1611.1 2.7 fusion.50
  1613.8 24.1 %all-reduce.4 = (bf16[2048]{0:T(1024)(128)(2,1)S(1)}, bf16[512]{0:T(512)(128)(2,1)S(1)}, bf16[2048]{0:T(1024)(128)(2,1)S(1)}) all-reduce(bf16[2048]{0:T(1024)(128)(2,1)S(1)} %get-tuple-element.17, bf16[512]{0:T(512)(128)(2,1)S(1)} %get-tuple-element.19, ...), channel_id=1, replica_groups=mesh['expert'=8,'tensor'=4] {'expert'}, use_global_device_ids=true, to_apply=%region_28.29 | all-reduce | flops 4608 | bytes 18432 | tf_op jit(solution)/shard_map/psum | solution.py:369
  1639.7 6.2 fusion.52
  1645.9 466.5 %all-reduce.16.cloned.1.call-done = (bf16[2048,768]{1,0:T(8,128)(2,1)}, bf16[2048,576]{0,1:T(8,128)(2,1)}, bf16[512,1024]{1,0:T(8,128)(2,1)}, bf16[512,2048]{1,0...) async-done(((bf16[2048,768]{1,0:T(8,128)(2,1)}, bf16[2048,576]{0,1:T(8,128)(2,1)}, bf16[512,1024]{1,0:T(8,128)(2,1)}, ...) | async-done | bytes 17301520 | tf_op jit(solution)/shard_map/psum | solution.py:370
  2112.4 2.9 convert_element_type.249
  2115.4 3.2 convert_element_type.243
  2118.6 2.5 convert_element_type.251
  2121.1 2.8 convert_element_type.245
  2123.9 3.3 convert_element_type.255
  2127.2 3.3 convert_element_type.257
  2130.5 3.3 convert_element_type.259
  (268 shorter events, 67.6 us)
Async XLA Ops:
  7.2 42.2 %copy-start = (bf16[2048,768]{1,0:T(8,128)(2,1)S(1)}, bf16[2048,768]{1,0:T(8,128)(2,1)}, u32[]{:S(2)}) copy-start(bf16[2048,768]{1,0:T(8,128)(2,1)} %param.20) | copy-start | bytes 9437188
  7.2 61.8 %all-gather.2.cloned.1.call-start = ((), (), s32[]{:S(2)}) async-start(), calls=%async_computation.6 | async-start | bytes 2359296 | tf_op jit(solution)/shard_map/all_gather | solution.py:101
  9.5 3.8 copy-start.67
  9.5 39.9 %copy-start.63 = (f32[256]{0:T(256)}, f32[256]{0:T(256)S(1)}, u32[]{:S(2)}) copy-start(f32[256]{0:T(256)S(1)} %fusion.110) | copy-start | bytes 3076
  9.5 4.7 copy-start.59
  9.5 39.9 %copy-start.57 = (f32[2048]{0:T(1024)S(1)}, f32[2048]{0:T(1024)}, u32[]{:S(2)}) copy-start(f32[2048]{0:T(1024)} %param.19) | copy-start | bytes 24580
  14.1 121.6 %all-reduce.12.cloned.1.call-start = ((), (), s32[]{:S(2)}) async-start(), calls=%async_computation.7 | async-start | bytes 4194304 | tf_op jit(solution)/shard_map/psum | solution.py:117
  16.1 36.0 %copy-start.53 = (f32[256,32]{0,1:T(8,128)}, f32[256,32]{0,1:T(8,128)S(1)}, u32[]{:S(2)}) copy-start(f32[256,32]{0,1:T(8,128)S(1)} %get-tuple-element.50) | copy-start | bytes 98308
  16.1 36.0 %copy-start.55 = (f32[256,32]{0,1:T(8,128)}, f32[256,32]{0,1:T(8,128)S(1)}, u32[]{:S(2)}) copy-start(f32[256,32]{0,1:T(8,128)S(1)} %get-tuple-element.51) | copy-start | bytes 98308
  49.4 25.3 %copy-start.35 = (bf16[2048,64]{0,1:T(8,128)(2,1)}, bf16[2048,64]{0,1:T(8,128)(2,1)S(1)}, u32[]{:S(2)}) copy-start(bf16[2048,64]{0,1:T(8,128)(2,1)S(1)} %all_gather.9) | copy-start | bytes 786436
  53.1 21.6 %copy-start.49 = (bf16[256,4,32]{0,2,1:T(8,128)(2,1)}, bf16[256,4,32]{0,2,1:T(8,128)(2,1)S(1)}, u32[]{:S(2)}) copy-start(bf16[256,4,32]{0,2,1:T(8,128)(2,1)S(1)} %get-tuple-element.42) | copy-start | bytes 196612
  53.1 21.6 %copy-start.51 = (bf16[256,4,32]{0,2,1:T(8,128)(2,1)}, bf16[256,4,32]{0,2,1:T(8,128)(2,1)S(1)}, u32[]{:S(2)}) copy-start(bf16[256,4,32]{0,2,1:T(8,128)(2,1)S(1)} %get-tuple-element.43) | copy-start | bytes 196612
  69.0 4.3 copy-start.21
  73.3 5.2 copy-start.17
  77.3 3.3 copy-start.1
  77.3 3.4 copy-start.65
  80.6 3.1 copy-start.14
  85.9 53.4 %copy-start.60 = (f32[2048]{0:T(1024)S(1)}, f32[2048]{0:T(1024)}, u32[]{:S(2)}) copy-start(f32[2048]{0:T(1024)} %param.25) | copy-start | bytes 24580
  175.2 5.5 copy-start.83
  175.2 278.5 %all-to-all-start = ((bf16[8,384,2048]{2,1,0:T(8,128)(2,1)}), bf16[8,384,2048]{2,1,0:T(8,128)(2,1)}, u32[]{:S(2)}, u32[]{:S(2)}) async-start(bf16[8,384,2048]{2,1,0:T(8,128)(2,1)} %bitcast.181), calls=%async_computation | async-start | bytes 25165824 | tf_op jit(solution)/shard_map/all_to_all | solution.py:141
  180.9 5.4 copy-start.44
  453.7 277.5 %all-to-all-start.2 = ((bf16[8,384,2048]{2,1,0:T(8,128)(2,1)}), bf16[8,384,2048]{2,1,0:T(8,128)(2,1)}, u32[]{:S(2)}, u32[]{:S(2)}) async-start(bf16[8,384,2048]{2,1,0:T(8,128)(2,1)} %bitcast.182), calls=%async_computation.2 | async-start | bytes 25165824 | tf_op jit(solution)/shard_map/all_to_all | solution.py:262
  459.2 12.0 copy-start.30
  731.2 14.9 copy-start.31
  746.1 11.8 copy-start.18
  784.7 276.9 %all-to-all-start.3 = ((bf16[8,384,2048]{2,1,0:T(8,128)(2,1)}), bf16[8,384,2048]{2,1,0:T(8,128)(2,1)}, u32[]{:S(2)}, u32[]{:S(2)}) async-start(bf16[8,384,2048]{2,1,0:T(8,128)(2,1)} %bitcast.183), calls=%async_computation.3 | async-start | bytes 25165824 | tf_op jit(solution)/shard_map/all_to_all | solution.py:287
  1061.6 345.5 %all-to-all-start.1 = ((bf16[8,384,2048]{2,1,0:T(8,128)(2,1)}), bf16[8,384,2048]{2,1,0:T(8,128)(2,1)}, u32[]{:S(2)}, u32[]{:S(2)}) async-start(bf16[8,384,2048]{2,1,0:T(8,128)(2,1)} %bitcast.180), calls=%async_computation.1 | async-start | bytes 25165824 | tf_op jit(solution)/shard_map/all_to_all | solution.py:213
  1066.9 108.2 %all-reduce.14.cloned.1.call-start = ((), (), s32[]{:S(2)}) async-start(), calls=%async_computation.8 | async-start | bytes 4194304 | tf_op jit(solution)/shard_map/psum | solution.py:295
  1067.0 3.3 copy-start.9
  1067.0 3.3 copy-start.29
  1117.5 5.6 copy-start.66
  1117.5 5.6 copy-start.70
  1117.5 57.7 %copy-start.61 = (f32[2048]{0:T(1024)S(1)}, f32[2048]{0:T(1024)}, u32[]{:S(2)}) copy-start(f32[2048]{0:T(1024)} %param.25) | copy-start | bytes 24580
  1117.5 57.7 %copy-start.72 = (f32[256]{0:T(256)S(1)}, f32[256]{0:T(256)}, u32[]{:S(2)}) copy-start(f32[256]{0:T(256)} %copy-done.71) | copy-start | bytes 3076
  1123.0 55.1 %copy-start.82 = (f32[256]{0:T(256)S(1)}, f32[256]{0:T(256)}, u32[]{:S(2)}) copy-start(f32[256]{0:T(256)} %copy-done.81) | copy-start | bytes 3076
  1123.0 338.3 %reduce-scatter.3.cloned.1.call-start = ((), (), s32[]{:S(2)}) async-start(), calls=%async_computation.9 | async-start | bytes 9437184 | tf_op jit(solution)/shard_map/reduce_scatter | solution.py:334
  1178.3 3.7 copy-start.15
  1185.3 6.5 slice-start
  1185.3 6.6 slice-start.1
  1201.5 313.9 %reduce-scatter.5.cloned.1.call-start = ((), (), s32[]{:S(2)}) async-start(), calls=%async_computation.10 | async-start | bytes 589824 | tf_op jit(solution)/shard_map/reduce_scatter | solution.py:335
  1201.8 3.9 copy-start.10
  1426.7 11.8 copy-start.45
  1438.5 9.6 copy-start.25
  1438.5 9.6 copy-start.33
  1453.9 119.7 %all-reduce.18.cloned.1.call-start = ((), (), s32[]{:S(2)}) async-start(), calls=%async_computation.12 | async-start | bytes 4718592 | tf_op jit(solution)/shard_map/psum | solution.py:221
  1464.0 3.8 copy-start.58
  1464.0 3.8 copy-start.64
  1464.1 648.4 %all-reduce.16.cloned.1.call-start = ((), (), s32[]{:S(2)}) async-start(), calls=%async_computation.11 | async-start | bytes 34603008 | tf_op jit(solution)/shard_map/psum | solution.py:370
  1464.1 3.7 copy-start.6
  1467.8 59.2 %copy-start.76 = (f32[256]{0:T(256)S(1)}, f32[256]{0:T(256)}, u32[]{:S(2)}) copy-start(f32[256]{0:T(256)} %copy-done.75) | copy-start | bytes 3076
  1467.8 59.2 %copy-start.85 = (f32[32]{0:T(128)S(1)}, f32[32]{0:T(128)}, u32[]{:S(2)}) copy-start(f32[32]{0:T(128)} %copy-done.84) | copy-start | bytes 388
  1467.9 59.4 %copy-start.39 = (bf16[256,512]{0,1:T(8,128)(2,1)S(1)}, bf16[256,512]{0,1:T(8,128)(2,1)}, u32[]{:S(2)}) copy-start(bf16[256,512]{0,1:T(8,128)(2,1)} %multiply_convert_fusion.5) | copy-start | bytes 786436
  1467.9 105.7 %copy-start.68 = (f32[512]{0:T(512)S(1)}, f32[512]{0:T(512)}, u32[]{:S(2)}) copy-start(f32[512]{0:T(512)} %param.22) | copy-start | bytes 6148
  1467.9 105.7 %copy-start.74 = (f32[256]{0:T(256)S(1)}, f32[256]{0:T(256)}, u32[]{:S(2)}) copy-start(f32[256]{0:T(256)} %copy-done.73) | copy-start | bytes 3076
  1471.8 103.2 %copy-start.80 = (f32[256]{0:T(256)S(1)}, f32[256]{0:T(256)}, u32[]{:S(2)}) copy-start(f32[256]{0:T(256)} %copy-done.79) | copy-start | bytes 3076
  1579.8 10.1 copy-start.19
  1589.9 10.5 copy-start.86
  1600.4 10.7 copy-start.7
  1600.4 10.7 copy-start.40
  1600.4 10.7 copy-start.48
  1611.1 28.6 %copy-start.78 = (f32[256]{0:T(256)S(1)}, f32[256]{0:T(256)}, u32[]{:S(2)}) copy-start(f32[256]{0:T(256)} %copy-done.77) | copy-start | bytes 3076
  2115.4 3.2 copy-start.41
  2123.9 3.3 copy-start.27
  2127.2 3.3 copy-start.26
  (36 other events, 63.9 us)
Sparse Core Ops, SparseCore 0:
  14.2 54.7 all-gather.1
  86.0 49.7 all-reduce.11
  1123.1 51.9 all-reduce.13
  1201.7 244.7 reduce-scatter.2
  1454.0 61.3 reduce-scatter.4
  1518.4 55.0 all-reduce.17
  1580.4 531.9 all-reduce.15
where the time goes:
time: 2150 us; the launch traced here: 2140 us
  waiting for transfers between devices  1610 us (75%)
  matrix products  188 us (9%)
  local copies, waits for them, and re-layouts  156 us (7%)
  other arithmetic  80.3 us (4%)
  blocking collectives  68 us (3%)
  starting transfers between devices  22.4 us (1%)
    psum x1, waiting for transfers between devices, shards(): lax.psum(grad_query_weight.astype(jnp.bfloat16), 'expert')  466 us
    all_to_all x1, waiting for transfers between devices, shards(): lax.all_to_all(grad_rows.reshape(groups, -1, model_width), 'expert', spli...  257 us
    all_to_all x1, waiting for transfers between devices, shards(): lax.all_to_all(grad_buffer, 'expert', split_axis=0, concat_axis=0, tiled=...  249 us
    all_to_all x1, waiting for transfers between devices, dispatch(): lax.all_to_all(buffer, 'expert', split_axis=0, concat_axis=0, tiled=True)  239 us
    all_to_all x1, waiting for transfers between devices, shards(): lax.all_to_all(expert_out.reshape(groups, -1, model_width), 'expert', spl...  196 us
    psum x1, waiting for transfers between devices, shards(): grad_moe_in = lax.psum(grad_moe_part + routed_grad, 'tensor')  52.1 us
    psum x1, waiting for transfers between devices, attention_pass(): lax.psum(jnp.dot(merged, output_weight, preferred_element_type=jnp.float3...  48.6 us
    reduce_scatter x1, waiting for transfers between devices, shards(): lax.psum_scatter(grad_k_rope, 'expert', scatter_dimension=0, tiled=True)  43.7 us
  transfers between devices with their start and end apart: 11, of which 10 were waited for; matrix products, arithmetic and copies ran while one was open for 13% of the time, Pallas kernels for 0%

commit v1 on v0

v1 whole, which is shorter than its diff:
```python
import functools
from functools import partial

import jax
import jax.numpy as jnp
from jax import lax
from jax.experimental import pallas as pl
from jax.experimental.pallas import tpu as pltpu
from jax.sharding import PartitionSpec as P

NOPE = 128
ROPE = 64
VDIM = 128
LATENT = 512
TOP = 6
EXP_DEV = 2
ALL = ("expert", "tensor")
MESH = pl.DeviceIdType.MESH

epsilon = 1e-06
masked_out = -1e30


class Grid:
    def __init__(self, expert, tensor):
        self.na = 4 if expert % 4 == 0 else 1
        self.nb = expert // self.na
        self.ny = tensor // 2
        self.size = expert * tensor

    def here(self):
        e, t = lax.axis_index("expert"), lax.axis_index("tensor")
        return (lax.div(e, self.nb), lax.rem(e, self.nb), lax.div(t, 2), lax.rem(t, 2))

    def device(self, a, b, y, c):
        return {"expert": a * self.nb + b, "tensor": y * 2 + c}

    def block(self, a, b, y, c):
        return ((a * self.nb + b) * self.ny + y) * 2 + c


def wrap(i, n):
    return lax.rem(i, n)


def greet(grid):
    a, b, y, c = grid.here()
    barrier = pltpu.get_barrier_semaphore()
    others = (
        [grid.device(wrap(a + i, grid.na), b, y, c) for i in range(1, grid.na)]
        + [grid.device(a, wrap(b + i, grid.nb), y, c) for i in range(1, grid.nb)]
        + [grid.device(a, b, wrap(y + i, grid.ny), c) for i in range(1, grid.ny)]
        + [grid.device(a, b, y, 1 - c)]
    )
    for other in others:
        pl.semaphore_signal(barrier, inc=1, device_id=other, device_id_type=MESH)
    pl.semaphore_wait(barrier, len(others))


def gather_kernel(grid, x_ref, out_ref, own_sem, send_sem, recv_sem, core_send, core_recv):
    na, nb, ny = grid.na, grid.nb, grid.ny
    a, b, y, c = grid.here()
    half = x_ref.shape[0] // 2
    greet(grid)
    waits = []

    def dst(bb, yy, cc, aa, h):
        return out_ref.at[grid.block(aa, bb, yy, cc), pl.ds(h * half, half)]

    def slot(bb, yy, aa, h):
        return ((bb * ny + yy) * na + aa) * 2 + h

    def push(src, bb, yy, aa, h, where, kind):
        copy = pltpu.make_async_remote_copy(
            src_ref=src,
            dst_ref=dst(bb, yy, c, aa, h),
            send_sem=core_send.at[slot(bb, yy, aa, h)] if kind == "c" else send_sem.at[len(waits)],
            recv_sem=(core_recv if kind == "c" else recv_sem).at[slot(bb, yy, aa, h)],
            device_id=where,
            device_id_type=MESH,
        )
        copy.start()
        if kind != "c":
            waits.append(copy)
        else:
            core_waits.append(copy)

    core_waits = []

    def onward(src, bb, yy, aa, h, dims):
        for d in dims:
            if d == "a":
                for i in range(1, na):
                    push(src, bb, yy, aa, h, grid.device(wrap(a + i, na), b, y, c), d)
            if d == "b":
                for i in range(1, nb):
                    push(src, bb, yy, aa, h, grid.device(a, wrap(b + i, nb), y, c), d)
            if d == "y":
                for i in range(1, ny):
                    push(src, bb, yy, aa, h, grid.device(a, b, wrap(y + i, ny), c), d)
        push(src, bb, yy, aa, h, grid.device(a, b, y, 1 - c), "c")

    def landed(bb, yy, cc, aa, h, sem):
        ref = dst(bb, yy, cc, aa, h)
        pltpu.make_async_copy(ref, ref, sem.at[slot(bb, yy, aa, h)]).wait()
        return ref

    own = pltpu.make_async_copy(x_ref, out_ref.at[grid.block(a, b, y, c)], own_sem)
    own.start()
    orders = (("b", "y"), ("y", "b"))
    for h in range(2):
        onward(x_ref.at[pl.ds(h * half, half)], b, y, a, h, ("a",) + orders[h])
    for i in range(1, na):
        aa = wrap(a + na - i, na)
        for h in range(2):
            onward(landed(b, y, c, aa, h, recv_sem), b, y, aa, h, orders[h])
    for i in range(na):
        aa = wrap(a + na - i, na)
        for h in range(2):
            n1 = (nb, ny)[h]
            for j in range(1, n1):
                bb, yy = (wrap(b + nb - j, nb), y) if h == 0 else (b, wrap(y + ny - j, ny))
                onward(landed(bb, yy, c, aa, h, recv_sem), bb, yy, aa, h, orders[h][1:])
    for i in range(na):
        aa = wrap(a + na - i, na)
        for h in range(2):
            for j in range(nb):
                for k in range(1, ny):
                    if h == 0:
                        bb, yy = wrap(b + nb - j, nb), wrap(y + ny - k, ny)
                        onward(landed(bb, yy, c, aa, h, recv_sem), bb, yy, aa, h, ())
            for j in range(ny):
                for k in range(1, nb):
                    if h == 1:
                        bb, yy = wrap(b + nb - k, nb), wrap(y + ny - j, ny)
                        onward(landed(bb, yy, c, aa, h, recv_sem), bb, yy, aa, h, ())
    for j in range(nb):
        for k in range(ny):
            for i in range(na):
                for h in range(2):
                    landed(wrap(b + nb - j, nb), wrap(y + ny - k, ny), 1 - c, wrap(a + na - i, na), h, core_recv)
    own.wait()
    for copy in waits + core_waits:
        copy.wait_send()


def gather_all(grid, x, collective_id):
    r, n = x.shape
    blocks = grid.na * grid.nb * grid.ny
    sends = 2 * (grid.na - 1 + grid.na * (grid.nb - 1) + grid.na * (grid.ny - 1)) + 2 * grid.na * ((grid.nb - 1) * (grid.ny - 1))
    return pl.pallas_call(
        functools.partial(gather_kernel, grid),
        out_shape=jax.ShapeDtypeStruct((grid.size, r, n), x.dtype),
        in_specs=[pl.BlockSpec(memory_space=pl.ANY)],
        out_specs=pl.BlockSpec(memory_space=pl.ANY),
        scratch_shapes=[
            pltpu.SemaphoreType.DMA,
            pltpu.SemaphoreType.DMA((sends,)),
            pltpu.SemaphoreType.DMA((2 * blocks,)),
            pltpu.SemaphoreType.DMA((2 * blocks,)),
            pltpu.SemaphoreType.DMA((2 * blocks,)),
        ],
        compiler_params=pltpu.CompilerParams(collective_id=collective_id, has_side_effects=True),
    )(x)


def scatter_kernel(grid, pieces, p_ref, out_ref, acc, core_in, d1_in0, d1_in1, d2_in0, d2_in1, a_in,
                   load_sem, core_s, core_r, s10, r10, s11, r11, s20, r20, s21, r21, sa, ra):
    na, nb, ny = grid.na, grid.nb, grid.ny
    a, b, y, c = grid.here()
    half = p_ref.shape[4] // 2
    width = p_ref.shape[5] // pieces
    greet(grid)
    pending = []

    def send(src, dst, ss, rs, where):
        copy = pltpu.make_async_remote_copy(src_ref=src, dst_ref=dst, send_sem=ss, recv_sem=rs, device_id=where, device_id_type=MESH)
        copy.start()
        pending.append(copy)

    def await_in(ref, sem):
        pltpu.make_async_copy(ref, ref, sem).wait()

    def add(dst, src):
        dst[...] = (dst[...].astype(jnp.float32) + src[...].astype(jnp.float32)).astype(dst.dtype)

    def cols(p):
        return pl.ds(p * width, width)

    spots = [(j, k) for j in reversed(range(nb)) for k in reversed(range(ny))]
    loads = {}
    for p in range(pieces):
        for n, (j, k) in enumerate(spots):
            bb, yy = wrap(b + j, nb), wrap(y + k, ny)
            send(p_ref.at[:, bb, yy, 1 - c, :, cols(p)], core_in.at[p, j, k], core_s.at[p, n], core_r.at[p, n],
                 grid.device(a, b, y, 1 - c))
            load = pltpu.make_async_copy(p_ref.at[:, bb, yy, c, :, cols(p)], acc.at[p, j, k], load_sem.at[p, n])
            load.start()
            loads[p, n] = load
    rows = (pl.ds(0, half), pl.ds(half, half))
    for p in range(pieces):
        for n, (j, k) in enumerate(spots):
            loads[p, n].wait()
            await_in(core_in.at[p, j, k], core_r.at[p, n])
            for i in range(na):
                add(acc.at[p, j, k, i], core_in.at[p, j, k, i])
            if k:
                send(acc.at[p, j, k, :, rows[0]], d1_in0.at[p, j, k - 1], s10.at[p, j, k - 1], r10.at[p, j, k - 1],
                     grid.device(a, b, wrap(y + k, ny), c))
            if j:
                send(acc.at[p, j, k, :, rows[1]], d1_in1.at[p, k, j - 1], s11.at[p, k, j - 1], r11.at[p, k, j - 1],
                     grid.device(a, wrap(b + j, nb), y, c))
    for p in range(pieces):
        for j in reversed(range(nb)):
            for k in range(1, ny):
                await_in(d1_in0.at[p, j, k - 1], r10.at[p, j, k - 1])
                for i in range(na):
                    add(acc.at[p, j, 0, i, rows[0]], d1_in0.at[p, j, k - 1, i])
            if j:
                send(acc.at[p, j, 0, :, rows[0]], d2_in0.at[p, j - 1], s20.at[p, j - 1], r20.at[p, j - 1],
                     grid.device(a, wrap(b + j, nb), y, c))
        for k in reversed(range(ny)):
            for j in range(1, nb):
                await_in(d1_in1.at[p, k, j - 1], r11.at[p, k, j - 1])
                for i in range(na):
                    add(acc.at[p, 0, k, i, rows[1]], d1_in1.at[p, k, j - 1, i])
            if k:
                send(acc.at[p, 0, k, :, rows[1]], d2_in1.at[p, k - 1], s21.at[p, k - 1], r21.at[p, k - 1],
                     grid.device(a, b, wrap(y + k, ny), c))
    for p in range(pieces):
        for j in range(1, nb):
            await_in(d2_in0.at[p, j - 1], r20.at[p, j - 1])
            for i in range(na):
                add(acc.at[p, 0, 0, i, rows[0]], d2_in0.at[p, j - 1, i])
        for k in range(1, ny):
            await_in(d2_in1.at[p, k - 1], r21.at[p, k - 1])
            for i in range(na):
                add(acc.at[p, 0, 0, i, rows[1]], d2_in1.at[p, k - 1, i])
        for i in range(1, na):
            aa = wrap(a + i, na)
            send(acc.at[p, 0, 0, aa], a_in.at[p, i - 1], sa.at[p, i - 1], ra.at[p, i - 1], grid.device(aa, b, y, c))
    for p in range(pieces):
        total = acc[p, 0, 0, a].astype(jnp.float32)
        for i in range(1, na):
            await_in(a_in.at[p, i - 1], ra.at[p, i - 1])
            total = total + a_in[p, i - 1].astype(jnp.float32)
        out_ref[:, cols(p)] = total.astype(out_ref.dtype)
    for copy in pending:
        copy.wait_send()


def scatter_all(grid, p, dtype, collective_id, pieces=2):
    r, n = p.shape[0] // grid.size, p.shape[1]
    na, nb, ny = grid.na, grid.nb, grid.ny
    half, width = r // 2, n // pieces
    sems = lambda *s: pltpu.SemaphoreType.DMA(s)
    vm = lambda *s: pltpu.VMEM(s, jnp.bfloat16)
    return pl.pallas_call(
        functools.partial(scatter_kernel, grid, pieces),
        out_shape=jax.ShapeDtypeStruct((r, n), dtype),
        in_specs=[pl.BlockSpec(memory_space=pl.ANY)],
        out_specs=pl.BlockSpec(memory_space=pltpu.VMEM),
        scratch_shapes=[
            vm(pieces, nb, ny, na, r, width),
            vm(pieces, nb, ny, na, r, width),
            vm(pieces, nb, ny - 1, na, half, width),
            vm(pieces, ny, nb - 1, na, half, width),
            vm(pieces, nb - 1, na, half, width),
            vm(pieces, ny - 1, na, half, width),
            vm(pieces, na - 1, r, width),
            sems(pieces, nb * ny), sems(pieces, nb * ny), sems(pieces, nb * ny),
            sems(pieces, nb, ny - 1), sems(pieces, nb, ny - 1),
            sems(pieces, ny, nb - 1), sems(pieces, ny, nb - 1),
            sems(pieces, nb - 1), sems(pieces, nb - 1),
            sems(pieces, ny - 1), sems(pieces, ny - 1),
            sems(pieces, na - 1), sems(pieces, na - 1),
        ],
        compiler_params=pltpu.CompilerParams(collective_id=collective_id, has_side_effects=True, vmem_limit_bytes=40 << 20),
    )(p.reshape(na, nb, ny, 2, r, n))


def greet_tensor(grid):
    a, b, y, c = grid.here()
    barrier = pltpu.get_barrier_semaphore()
    others = [grid.device(a, b, wrap(y + i, grid.ny), c) for i in range(1, grid.ny)]
    others.append(grid.device(a, b, y, 1 - c))
    for other in others:
        pl.semaphore_signal(barrier, inc=1, device_id=other, device_id_type=MESH)
    pl.semaphore_wait(barrier, len(others))


def tensor_scatter_kernel(grid, p_ref, out_ref, acc, core_in, y_in, core_s, core_r, ys, yr):
    ny = grid.ny
    a, b, y, c = grid.here()
    greet_tensor(grid)
    pending = []
    for k in reversed(range(ny)):
        copy = pltpu.make_async_remote_copy(
            src_ref=p_ref.at[wrap(y + k, ny), 1 - c], dst_ref=core_in.at[k], send_sem=core_s.at[k], recv_sem=core_r.at[k],
            device_id=grid.device(a, b, y, 1 - c), device_id_type=MESH,
        )
        copy.start()
        pending.append(copy)
    for k in reversed(range(ny)):
        pltpu.make_async_copy(core_in.at[k], core_in.at[k], core_r.at[k]).wait()
        total = p_ref[wrap(y + k, ny), c].astype(jnp.float32) + core_in[k].astype(jnp.float32)
        if k:
            acc[k - 1] = total.astype(acc.dtype)
            copy = pltpu.make_async_remote_copy(
                src_ref=acc.at[k - 1], dst_ref=y_in.at[k - 1], send_sem=ys.at[k - 1], recv_sem=yr.at[k - 1],
                device_id=grid.device(a, b, wrap(y + k, ny), c), device_id_type=MESH,
            )
            copy.start()
            pending.append(copy)
        else:
            out_ref[...] = total
    for k in range(1, ny):
        pltpu.make_async_copy(y_in.at[k - 1], y_in.at[k - 1], yr.at[k - 1]).wait()
        out_ref[...] += y_in[k - 1].astype(jnp.float32)
    for copy in pending:
        copy.wait_send()


def tensor_scatter(grid, p, collective_id):
    ny = grid.ny
    r, n = p.shape[0] // (2 * ny), p.shape[1]
    return pl.pallas_call(
        functools.partial(tensor_scatter_kernel, grid),
        out_shape=jax.ShapeDtypeStruct((r, n), jnp.float32),
        in_specs=[pl.BlockSpec(memory_space=pltpu.VMEM)],
        out_specs=pl.BlockSpec(memory_space=pltpu.VMEM),
        scratch_shapes=[
            pltpu.VMEM((max(ny - 1, 1), r, n), p.dtype),
            pltpu.VMEM((ny, r, n), p.dtype),
            pltpu.VMEM((max(ny - 1, 1), r, n), p.dtype),
            pltpu.SemaphoreType.DMA((ny,)),
            pltpu.SemaphoreType.DMA((ny,)),
            pltpu.SemaphoreType.DMA((max(ny - 1, 1),)),
            pltpu.SemaphoreType.DMA((max(ny - 1, 1),)),
        ],
        compiler_params=pltpu.CompilerParams(
            collective_id=collective_id, has_side_effects=True, vmem_limit_bytes=16 << 20
        ),
    )(p.reshape(ny, 2, r, n))


def tensor_gather_kernel(grid, x_ref, out_ref, own_sem, ys, yr, core_s, core_r):
    ny = grid.ny
    a, b, y, c = grid.here()
    greet_tensor(grid)
    own = pltpu.make_async_copy(x_ref, out_ref.at[y, c], own_sem)
    own.start()
    pending = []

    def push(src, spot, ss, rs, where):
        copy = pltpu.make_async_remote_copy(
            src_ref=src, dst_ref=out_ref.at[spot, c], send_sem=ss, recv_sem=rs, device_id=where, device_id_type=MESH
        )
        copy.start()
        pending.append(copy)

    for k in range(1, ny):
        push(x_ref, y, ys.at[k], yr.at[k], grid.device(a, b, wrap(y + k, ny), c))
    push(x_ref, y, core_s.at[0], core_r.at[0], grid.device(a, b, y, 1 - c))
    for k in range(1, ny):
        spot = wrap(y + ny - k, ny)
        ref = out_ref.at[spot, c]
        pltpu.make_async_copy(ref, ref, yr.at[k]).wait()
        push(ref, spot, core_s.at[k], core_r.at[k], grid.device(a, b, y, 1 - c))
    for k in range(ny):
        ref = out_ref.at[wrap(y + ny - k, ny), 1 - c]
        pltpu.make_async_copy(ref, ref, core_r.at[k]).wait()
    own.wait()
    for copy in pending:
        copy.wait_send()


def tensor_gather(grid, x, collective_id):
    ny = grid.ny
    r, n = x.shape
    out = pl.pallas_call(
        functools.partial(tensor_gather_kernel, grid),
        out_shape=jax.ShapeDtypeStruct((ny, 2, r, n), x.dtype),
        in_specs=[pl.BlockSpec(memory_space=pltpu.VMEM)],
        out_specs=pl.BlockSpec(memory_space=pltpu.VMEM),
        scratch_shapes=[pltpu.SemaphoreType.DMA] + [pltpu.SemaphoreType.DMA((ny,))] * 4,
        compiler_params=pltpu.CompilerParams(
            collective_id=collective_id, has_side_effects=True, vmem_limit_bytes=16 << 20
        ),
    )(x)
    return out.reshape(2 * ny * r, n)


def rms_scale(values, gain_vec):
    return (
        values * lax.rsqrt(jnp.mean(values * values, axis=-1, keepdims=True) + epsilon) * gain_vec
    )


def rotate(values, places):
    halfway = values.shape[-1] // 2
    frequency = 10000.0 ** (-jnp.arange(halfway, dtype=jnp.float32) / halfway)
    angles = places.astype(jnp.float32)[:, None] * frequency[None, :]
    cosine = jnp.cos(angles)
    sine_part = jnp.sin(angles)
    if values.ndim == 3:
        cosine = cosine[:, None, :]
        sine_part = sine_part[:, None, :]
    first_half = values[..., :halfway]
    second = values[..., halfway:]
    return jnp.concatenate(
        [first_half * cosine - second * sine_part, second * cosine + first_half * sine_part],
        axis=-1,
    )


def seq_places(segments):
    total_rows = segments.shape[0]
    ordinal = jnp.arange(total_rows, dtype=jnp.int32)
    starts = jnp.concatenate(
        [jnp.ones((1,), jnp.int32), (segments[1:] != segments[:-1]).astype(jnp.int32)]
    )
    seg_start = lax.cummax(jnp.where(starts > 0, ordinal, 0), axis=0)
    return jnp.where(segments == 0, ordinal, total_rows // 2 + ordinal - seg_start)


def silu_product(gate_pre, up_pre):
    return jax.nn.silu(gate_pre) * up_pre


def score_block(queries, key_plain, rope_all, visible):
    scale_factor = (NOPE + ROPE) ** (-0.5)
    raw_scores = jnp.einsum(
        "thc,shc->hts", queries[..., :NOPE], key_plain, preferred_element_type=jnp.float32
    )
    raw_scores = raw_scores + jnp.einsum(
        "thr,sr->hts", queries[..., NOPE:], rope_all, preferred_element_type=jnp.float32
    )
    return jnp.where(visible[None], scale_factor * raw_scores, masked_out)


def dot(left_side, right_side):
    return jnp.dot(left_side, right_side, preferred_element_type=jnp.float32)


def pad_columns(values):
    return jnp.pad(values, ((0, 0), (0, -values.shape[1] % 128)))


def low(values):
    return values.astype(jnp.bfloat16)


def shards(
    grid,
    hidden_in,
    attn_gain,
    query_weight,
    latent_weight,
    latent_gain,
    expand_weight,
    output_weight,
    moe_gain,
    shared_gate,
    shared_up,
    shared_down,
    expert_gate,
    expert_up,
    expert_down,
    gate_values,
    expert_routes,
    segments,
    cotangent,
):
    tok_rows, model_width = hidden_in.shape
    groups = lax.axis_size("expert")
    parts = lax.axis_size("tensor")
    device = lax.axis_index("expert")
    part = lax.axis_index("tensor")
    total_rows = segments.shape[0]
    few = tok_rows // parts
    start_row = device * tok_rows
    scale_factor = (NOPE + ROPE) ** (-0.5)

    def quarter(values):
        return lax.dynamic_slice_in_dim(values, part * few, few)

    def own_group(values):
        return lax.dynamic_slice_in_dim(values, start_row, tok_rows)

    places = own_group(seq_places(segments))
    own_seg = own_group(segments)
    own_ordinal = start_row + jnp.arange(tok_rows, dtype=jnp.int32)
    key_ordinal = jnp.arange(total_rows, dtype=jnp.int32)
    visible = (key_ordinal[None, :] <= own_ordinal[:, None]) & (
        (segments[None, :] == own_seg[:, None]) | (segments[None, :] == 0)
    )
    experts_all = EXP_DEV * groups
    cot_all = lax.all_gather(quarter(cotangent), ALL, axis=0, tiled=True)

    hidden_f = hidden_in.astype(jnp.float32)
    normed = low(rms_scale(hidden_f, attn_gain))
    compressed = dot(normed, latent_weight)
    latents = low(rms_scale(compressed[:, :LATENT], latent_gain))
    key_rope = low(rotate(compressed[:, LATENT:], places))
    onehot = expert_routes[:, :, None] == jnp.arange(experts_all, dtype=jnp.int32)
    gate_rows = jnp.sum(jnp.where(onehot, gate_values[:, :, None], 0.0), axis=1)
    gate_high = low(gate_rows)
    gate_low = low(gate_rows - gate_high.astype(jnp.float32))
    packed = pad_columns(jnp.concatenate([latents, key_rope, gate_high, gate_low], axis=1))
    packed_all = gather_all(grid, quarter(packed), 0).reshape(total_rows, -1)
    latents_all = packed_all[:, :LATENT]
    rope_all = packed_all[:, LATENT : LATENT + ROPE]
    first_gate = LATENT + ROPE + EXP_DEV * device
    gates_own = lax.dynamic_slice_in_dim(packed_all, first_gate, EXP_DEV, axis=1).astype(
        jnp.float32
    ) + lax.dynamic_slice_in_dim(packed_all, first_gate + experts_all, EXP_DEV, axis=1).astype(
        jnp.float32
    )
    q_raw = dot(normed, query_weight)
    heads_here = q_raw.shape[1] // (NOPE + ROPE)
    q_raw = q_raw.reshape(tok_rows, heads_here, NOPE + ROPE)
    queries = low(
        jnp.concatenate([q_raw[..., :NOPE], rotate(q_raw[..., NOPE:], places)], axis=-1)
    )
    expanded = low(dot(latents_all, expand_weight)).reshape(
        total_rows, heads_here, NOPE + VDIM
    )
    key_plain, value_part = expanded[..., :NOPE], expanded[..., NOPE:]
    scores = score_block(queries, key_plain, rope_all, visible)
    peak = jnp.max(scores, axis=-1, keepdims=True)
    weights = jnp.exp(scores - peak)
    total_weight = jnp.sum(weights, axis=-1, keepdims=True)
    log_total = peak + jnp.log(total_weight)
    context = jnp.einsum(
        "hts,shv->thv", low(weights / total_weight), value_part, preferred_element_type=jnp.float32
    )
    merged = low(context).reshape(tok_rows, heads_here * VDIM)
    attn_out = tensor_scatter(grid, low(dot(merged, output_weight)), 1)
    residual = quarter(hidden_f) + attn_out
    moe_in = low(rms_scale(residual, moe_gain))
    moe_all = gather_all(grid, moe_in, 2).reshape(total_rows, model_width)
    normed_later, _ = lax.optimization_barrier((quarter(normed), moe_all[:8]))
    normed_all = lax.all_gather(normed_later, ALL, axis=0, tiled=True)

    hidden_here = expert_gate.shape[2]
    eg = jnp.einsum("td,kdf->tkf", moe_all, expert_gate, preferred_element_type=jnp.float32)
    eu = jnp.einsum("td,kdf->tkf", moe_all, expert_up, preferred_element_type=jnp.float32)
    active, pull_expert = jax.vjp(silu_product, eg, eu)
    gated = low(gates_own[:, :, None] * active)
    d_active = jnp.einsum("td,kfd->tkf", cot_all, expert_down, preferred_element_type=jnp.float32)
    d_eg, d_eu = pull_expert(gates_own[:, :, None] * d_active)
    d_eg, d_eu = low(d_eg), low(d_eu)
    sg = dot(moe_all, shared_gate)
    su = dot(moe_all, shared_up)
    shared_act, pull_shared = jax.vjp(silu_product, sg, su)
    shared_act = low(shared_act)
    d_sg, d_su = pull_shared(dot(cot_all, shared_down.T))
    d_sg, d_su = low(d_sg), low(d_su)

    grad_in = jnp.einsum("tkf,kdf->td", d_eg, expert_gate, preferred_element_type=jnp.float32)
    grad_in = grad_in + jnp.einsum(
        "tkf,kdf->td", d_eu, expert_up, preferred_element_type=jnp.float32
    )
    grad_in_shared = dot(own_group(d_sg), shared_gate.T) + dot(own_group(d_su), shared_up.T)
    grad_in = lax.dynamic_update_slice_in_dim(
        grad_in, own_group(grad_in) + grad_in_shared, start_row, 0
    )
    grad_moe_in = scatter_all(grid, low(grad_in), jnp.float32, 3)
    out_rows = jnp.einsum("tkf,kfd->td", gated, expert_down, preferred_element_type=jnp.float32)
    out_shared = dot(own_group(shared_act), shared_down)
    out_rows = lax.dynamic_update_slice_in_dim(
        out_rows, own_group(out_rows) + out_shared, start_row, 0
    )
    moe_out = lax.psum_scatter(low(out_rows), ALL, scatter_dimension=0, tiled=True)
    layer_out = low(residual + moe_out.astype(jnp.float32))
    layer_out = tensor_gather(grid, layer_out, 4)

    grad_expert_gate = jnp.einsum("td,tkf->kdf", moe_all, d_eg, preferred_element_type=jnp.float32)
    grad_expert_up = jnp.einsum("td,tkf->kdf", moe_all, d_eu, preferred_element_type=jnp.float32)
    grad_expert_down = jnp.einsum("tkf,td->kfd", gated, cot_all, preferred_element_type=jnp.float32)
    grad_shared_gate = dot(moe_all.T, d_sg)
    grad_shared_up = dot(moe_all.T, d_su)
    grad_shared_down = dot(shared_act.T, cot_all)

    _, pull_moe = jax.vjp(rms_scale, residual, moe_gain)
    grad_residual, grad_moe_gain = pull_moe(grad_moe_in)
    grad_residual = grad_residual + quarter(cotangent).astype(jnp.float32)
    grad_res_low = tensor_gather(grid, low(grad_residual), 5)
    grad_output_weight = dot(merged.T, grad_res_low)
    grad_context = low(dot(grad_res_low, output_weight.T)).reshape(tok_rows, heads_here, VDIM)
    scores = score_block(queries, key_plain, rope_all, visible)
    probs = jnp.exp(scores - log_total)
    grad_probs = jnp.einsum(
        "thv,shv->hts", grad_context, value_part, preferred_element_type=jnp.float32
    )
    grad_values = jnp.einsum(
        "hts,thv->shv", low(probs), grad_context, preferred_element_type=jnp.float32
    )
    grad_scores = low(probs * (grad_probs - jnp.sum(probs * grad_probs, axis=-1, keepdims=True)))
    grad_q_plain = scale_factor * jnp.einsum(
        "hts,shc->thc", grad_scores, key_plain, preferred_element_type=jnp.float32
    )
    grad_q_rope = scale_factor * jnp.einsum(
        "hts,sr->thr", grad_scores, rope_all, preferred_element_type=jnp.float32
    )
    grad_k_plain = scale_factor * jnp.einsum(
        "hts,thc->shc", grad_scores, queries[..., :NOPE], preferred_element_type=jnp.float32
    )
    grad_k_rope = scale_factor * jnp.einsum(
        "hts,thr->sr", grad_scores, queries[..., NOPE:], preferred_element_type=jnp.float32
    )
    grad_expanded = low(
        jnp.concatenate([grad_k_plain, grad_values], axis=-1).reshape(
            total_rows, heads_here * (NOPE + VDIM)
        )
    )
    grad_expand_weight = dot(latents_all.T, grad_expanded)
    grad_keys = jnp.concatenate([dot(grad_expanded, expand_weight.T), grad_k_rope], axis=1)
    grad_keys = scatter_all(grid, pad_columns(low(grad_keys)), jnp.float32, 6, pieces=1)
    _, pull_qrope = jax.vjp(partial(rotate, places=places), q_raw[..., NOPE:])
    (grad_q_turned,) = pull_qrope(grad_q_rope)
    grad_q_low = low(
        jnp.concatenate([grad_q_plain, grad_q_turned], axis=-1).reshape(tok_rows, -1)
    )
    grad_q_all = lax.all_gather(grad_q_low, "expert", axis=0, tiled=True)
    grad_normed = tensor_scatter(grid, low(dot(grad_q_low, query_weight.T)), 7)

    places_few = quarter(places)
    compressed_few = quarter(compressed)
    _, pull_latent = jax.vjp(rms_scale, compressed_few[:, :LATENT], latent_gain)
    grad_plain_latent, grad_latent_gain = pull_latent(grad_keys[:, :LATENT])
    _, pull_krope = jax.vjp(partial(rotate, places=places_few), compressed_few[:, LATENT:])
    (grad_k_turned,) = pull_krope(grad_keys[:, LATENT : LATENT + ROPE])
    grad_comp_low = low(jnp.concatenate([grad_plain_latent, grad_k_turned], axis=-1))
    grad_comp_all = gather_all(grid, pad_columns(grad_comp_low), 8).reshape(total_rows, -1)
    grad_comp_all = grad_comp_all[:, : LATENT + ROPE]
    grad_latent_weight = dot(normed_all.T, grad_comp_all)
    grad_query_weight = dot(normed_all.T, grad_q_all)
    grad_normed = grad_normed + dot(grad_comp_low, latent_weight.T)
    _, pull_input = jax.vjp(rms_scale, quarter(hidden_f), attn_gain)
    grad_input_norm, grad_attn_gain = pull_input(grad_normed)
    grad_hidden = tensor_gather(grid, low(grad_residual + grad_input_norm), 9).astype(jnp.float32)

    gains = lax.psum(jnp.concatenate([grad_attn_gain, grad_latent_gain, grad_moe_gain]), ALL)
    grad_output_weight = lax.psum(low(grad_output_weight), "expert").astype(jnp.float32)
    grad_expand_weight = lax.psum(low(grad_expand_weight), "expert").astype(jnp.float32)
    return (
        layer_out,
        grad_hidden,
        gains[:model_width],
        grad_query_weight,
        grad_latent_weight,
        gains[model_width : model_width + LATENT],
        grad_expand_weight,
        grad_output_weight,
        gains[model_width + LATENT :],
        grad_shared_gate,
        grad_shared_up,
        grad_shared_down,
        grad_expert_gate,
        grad_expert_up,
        grad_expert_down,
    )


def solution(mesh):
    grid = Grid(mesh.shape["expert"], mesh.shape["tensor"])
    placed = (
        P("expert", None),
        P(),
        P(None, "tensor"),
        P(),
        P(),
        P(None, "tensor"),
        P("tensor", None),
        P(),
        P(None, "tensor"),
        P(None, "tensor"),
        P("tensor", None),
        P("expert", None, "tensor"),
        P("expert", None, "tensor"),
        P("expert", "tensor", None),
        P("expert", None),
        P("expert", None),
        P(),
        P("expert", None),
    )
    return jax.shard_map(
        partial(shards, grid),
        mesh=mesh,
        in_specs=placed,
        out_specs=(
            P("expert", None),
            P("expert", None),
            P(),
            P(None, "tensor"),
            P(),
            P(),
            P(None, "tensor"),
            P("tensor", None),
            P(),
            P(None, "tensor"),
            P(None, "tensor"),
            P("tensor", None),
            P("expert", None, "tensor"),
            P("expert", None, "tensor"),
            P("expert", "tensor", None),
        ),
        check_vma=False,
    )
```

time: 2150 us -> 766 us (0.36)
  waiting for transfers between devices: 1610 us -> 99.8 us
  Pallas kernels: 0 us -> 272 us
  local copies, waits for them, and re-layouts: 156 us -> 38.4 us
  matrix products: 188 us -> 243 us
  other arithmetic: 80.3 us -> 48.4 us
  blocking collectives: 68 us -> 39.9 us
  starting transfers between devices: 22.4 us -> 0.61 us
    all_to_all x4 -> x0, waiting for transfers between devices: 942 us -> none  [the longest x1 257 us: shards(): lax.all_to_all(grad_rows.reshape(groups, -1, model_width), 'expert', spli...]
    psum x4 -> x1, waiting for transfers between devices: 611 us -> 0.01 us  [shards(): lax.psum(low(grad_expand_weight), 'expert').astype(jnp.float32)]
    pallas_call x0 -> x10, Pallas kernels: none -> 272 us  [the longest x3 122 us: gather_all(): pl.pallas_call(functools.partial(gather_kernel, grid), out_shape=jax.Shap...]
    reduce_scatter x2 -> x1, waiting for transfers between devices: 43.7 us -> 99.7 us  [shards(): lax.psum_scatter(low(out_rows), ALL, scatter_dimension=0, tiled=True)]
    convert_element_type x6 -> x2, local copies, waits for them, and re-layouts: 52.2 us -> 0.84 us  [the longest x1 0.73 us: low(): return values.astype(jnp.bfloat16)]
    dot_general x33, matrix products: 176 us -> 227 us  [the longest x21 114 us: dot(): return jnp.dot(left_side, right_side, preferred_element_type=jnp.float32)]
    gather x2 -> x0, local copies, waits for them, and re-layouts: 38.9 us -> none  [the longest x1 19.6 us: shards(): returned[targets].astype(jnp.float32)]
    scatter x2 -> x0, local copies, waits for them, and re-layouts: 35 us -> none  [the longest x1 17.7 us: dispatch(): jnp.zeros((experts_all * capacity, model_width), jnp.bfloat16).at[targets]]
  transfers between devices with their start and end apart: 11 -> 5, of which waited for: 10 -> 1; matrix products, arithmetic and copies ran while one was open for 13% -> 40% of each run, Pallas kernels for 0% -> 33%
where the time goes in v1:
time: 766 us; the launch traced here: 758 us
  Pallas kernels  272 us (36%)
  matrix products  243 us (32%)
  waiting for transfers between devices  99.8 us (13%)
  other arithmetic  48.4 us (6%)
  blocking collectives  39.9 us (5%)
  local copies, waits for them, and re-layouts  38.4 us (5%)
  between operations  15.3 us (2%)
    pallas_call x3, Pallas kernels, gather_all(): pl.pallas_call(functools.partial(gather_kernel, grid), out_shape=jax.Shap...  122 us
    dot_general x21, matrix products, dot(): return jnp.dot(left_side, right_side, preferred_element_type=jnp.float32)  114 us
    pallas_call x2, Pallas kernels, scatter_all(): pl.pallas_call(functools.partial(scatter_kernel, grid, pieces), out_shape...  102 us
    reduce_scatter x1, waiting for transfers between devices, shards(): lax.psum_scatter(low(out_rows), ALL, scatter_dimension=0, tiled=True)  99.7 us
    psum x1, blocking collectives, shards(): lax.psum(jnp.concatenate([grad_attn_gain, grad_latent_gain, grad_moe_gain...  39.9 us
    pallas_call x3, Pallas kernels, tensor_gather(): pl.pallas_call(functools.partial(tensor_gather_kernel, grid), out_shape=j...  28 us
    unnamed x158, local copies, waits for them, and re-layouts  25 us
    convert_element_type x10, other arithmetic, low(): return values.astype(jnp.bfloat16)  20.7 us
  transfers between devices with their start and end apart: 5, of which 1 were waited for; matrix products, arithmetic and copies ran while one was open for 40% of the time, Pallas kernels for 33%

profile of v1, /device:TPU:0, one launch (start us, length us, event | category | flops | bytes accessed | tf_op | source)
XLA Modules:
  0.0 757.5 jit_solution(3996573159458755003)
XLA Ops:
  7.3 1.8 constant_dynamic-slice_fusion
  10.7 1.6 multiply_convert_fusion.6
  14.0 2.8 convert_element_type.138
  18.4 3.0 fusion.88
  23.3 1.9 multiply_convert_fusion.8
  25.2 2.3 multiply_cosine_fusion
  29.9 30.3 %shard_map.289 = bf16[32,64,640]{2,1,0:T(8,128)(2,1)} custom-call(bf16[64,640]{1,0:T(8,128)(2,1)} %pad_dynamic-slice_fusion.x_ref), custom_call_target="tpu_custom_call" | custom-call | tf_op jit(solution)/shard_map/pallas_call | solution.py:151
  60.2 2.7 constant_dynamic-slice_fusion.3
  65.4 6.3 convolution_convert_fusion
  71.8 2.3 fusion.89
  74.2 3.1 fusion.35
  79.1 3.8 fusion.87
  84.2 3.0 copy-done.4
  88.2 2.2 fusion.51
  91.2 10.2 %shard_map.290 = f32[64,2048]{1,0:T(8,128)S(1)} custom-call(bf16[2,2,64,2048]{3,2,1,0:T(8,128)(2,1)S(1)} %bitcast.137), custom_call_target="tpu_custom_call" | custom-call | tf_op jit(solution)/shard_map/pallas_call | solution.py:327
  104.3 59.2 %shard_map.291 = bf16[32,64,2048]{2,1,0:T(8,128)(2,1)} custom-call(bf16[64,2048]{1,0:T(8,128)(2,1)} %multiply_convert_fusion.7.x_ref), custom_call_target="tpu_custom_call" | custom-call | tf_op jit(solution)/shard_map/pallas_call | solution.py:151
  163.5 11.3 %fusion.90 = f32[2048,2,352]{0,2,1:T(8,128)} fusion(bf16[2048,2048,1]{1,0,2:T(8,128)(2,1)} %bitcast.146, bf16[2,2048,352]{1,2,0:T(8,128)(2,1)} %param.29), kind=kOutput, calls=%fused_computation.174 | convolution fusion | flops 5905580032 | bytes 17039360 | tf_op jit(solution)/shard_map/td,kdf->tkf/dot_general | solution.py:547
  174.8 8.0 %fusion.91 = f32[2048,2,352]{0,2,1:T(8,128)} fusion(bf16[2048,2048,1]{1,0,2:T(8,128)(2,1)S(1)} %bitcast.150, bf16[2,2048,352]{1,2,0:T(8,128)(2,1)S(1)} %copy-done.65), kind=kOutput, calls=%fused_computation.175 | convolution fusion | flops 5905580032 | bytes 17039360 | tf_op jit(solution)/shard_map/td,kdf->tkf/dot_general | solution.py:548
  182.8 8.4 %fusion.92 = f32[2048,704]{0,1:T(8,128)} fusion(bf16[2048,2048]{1,0:T(8,128)(2,1)S(1)} %bitcast.151, bf16[2048,704]{0,1:T(8,128)(2,1)S(1)} %copy-done.20), kind=kOutput, calls=%fused_computation.176 | convolution fusion | flops 5905580032 | bytes 17039360 | tf_op jit(solution)/shard_map/dot_general | solution.py:443
  191.2 8.0 %fusion.93 = f32[2048,704]{0,1:T(8,128)} fusion(bf16[2048,2048]{1,0:T(8,128)(2,1)S(1)} %bitcast.152, bf16[2048,704]{0,1:T(8,128)(2,1)S(1)} %copy-done.18), kind=kOutput, calls=%fused_computation.177 | convolution fusion | flops 5905580032 | bytes 17039360 | tf_op jit(solution)/shard_map/dot_general | solution.py:443
  199.2 15.2 %multiply_convert_fusion.1 = (bf16[2048,704]{0,1:T(8,128)(2,1)S(1)}, bf16[2048,704]{0,1:T(8,128)(2,1)S(1)}, bf16[2048,704]{0,1:T(8,128)(2,1)}) fusion(f32[2048,704]{0,1:T(8,128)} %fusion.92, f32[2048,704]{0,1:T(8,128)} %fusion.93, bf16[2048,2048]{1,0:T(8,128)(2,1)} %all-gather.4.cloned.1.call-done, bf16[704,2048]{1,0:T(8,128)(2,1)} %param.28), kind=kOutput, calls=%fused_computation.24 | convolution fusion | flops 5928648704 | bytes 31457280 | tf_op jit(solution)/shard_map/dot_general | solution.py:443
  215.5 2.9 copy-done.67
  218.4 16.4 %multiply_convert_fusion.2 = (bf16[2048,2,352]{0,2,1:T(8,128)(2,1)}, bf16[2048,2,352]{0,2,1:T(8,128)(2,1)}, bf16[2048,2,352]{0,2,1:T(8,128)(2,1)}) fusion(f32[2048,2]{0,1:T(2,128)S(1)} %convert_add_fusion, f32[2048,2,352]{0,2,1:T(8,128)} %fusion.90, f32[2048,2,352]{0,2,1:T(8,128)} %fusion.91, bf16[2,352,2048]{2,1,0:T(8,128)(2,1)S(1)} %copy-done.67, ...), kind=kOutput, calls=%fused_computation.25 | convolution fusion | flops 5931532288 | bytes 31473664 | tf_op jit(solution)/shard_map/td,kfd->tkf/dot_general | solution.py:551
  234.8 12.3 %fusion.94 = f32[2048,2048,1]{1,0,2:T(8,128)} fusion(bf16[2048,2,352]{0,2,1:T(8,128)(2,1)} %get-tuple-element.28, bf16[2,2048,352]{1,2,0:T(8,128)(2,1)S(1)} %copy-done.64), kind=kOutput, calls=%fused_computation.178 | convolution fusion | flops 5905580032 | bytes 22544384 | tf_op jit(solution)/shard_map/tkf,kdf->td/dot_general | solution.py:561
  247.2 14.7 %bitcast_add_fusion = f32[2048,2048]{1,0:T(8,128)} fusion(f32[2048,2048,1]{1,0,2:T(8,128)} %fusion.94, bf16[2048,2,352]{0,2,1:T(8,128)(2,1)} %get-tuple-element.27, bf16[2,2048,352]{1,2,0:T(8,128)(2,1)S(1)} %copy-done.66), kind=kOutput, calls=%fused_computation | convolution fusion | flops 5909774336 | bytes 39321600 | tf_op jit(solution)/shard_map/tkf,kdf->td/dot_general | solution.py:562
  261.9 4.0 fusion.29
  265.9 6.6 convert_element_type.162
  272.5 69.8 %shard_map.293 = f32[64,2048]{1,0:T(8,128)S(1)} custom-call(bf16[4,2,2,2,64,2048]{5,4,3,2,1,0:T(8,128)(2,1)S(1)} %bitcast.132), custom_call_target="tpu_custom_call" | custom-call | tf_op jit(solution)/shard_map/pallas_call | solution.py:258
  344.3 9.5 %shard_map.294 = bf16[2,2,64,2048]{3,2,1,0:T(8,128)(2,1)S(1)} custom-call(bf16[64,2048]{1,0:T(8,128)(2,1)S(1)} %fusion.85.x_ref), custom_call_target="tpu_custom_call" | custom-call | tf_op jit(solution)/shard_map/pallas_call | solution.py:381
  357.3 3.3 convolution_convert_fusion.2
  360.6 5.4 multiply_reduce_fusion
  367.2 1.9 multiply_convert_fusion
  371.1 1.6 fusion.25
  373.3 2.0 copy-done.15
  375.3 3.4 fusion.45
  379.1 3.9 fusion.60
  383.1 3.2 fusion.57
  390.1 9.8 %convolution_bitcast_fusion = f32[2048,2048]{1,0:T(8,128)S(1)} fusion(bf16[2048,2,352]{0,2,1:T(8,128)(2,1)} %get-tuple-element.29, bf16[2,352,2048]{2,1,0:T(8,128)(2,1)} %param.31), kind=kOutput, calls=%fused_computation.3 | convolution fusion | flops 5905580032 | bytes 22544384 | tf_op jit(solution)/shard_map/tkf,kfd->td/dot_general | solution.py:570
  399.8 2.2 fusion.24
  402.0 4.3 convert_element_type.155
  408.4 10.2 %shard_map.295 = f32[64,2048]{1,0:T(8,128)S(1)} custom-call(bf16[2,2,64,2048]{3,2,1,0:T(8,128)(2,1)S(1)} %bitcast.138), custom_call_target="tpu_custom_call" | custom-call | tf_op jit(solution)/shard_map/pallas_call | solution.py:327
  420.3 2.4 convolution_convert_fusion.1
  422.7 1.6 pad_maximum_fusion.1
  424.2 4.3 copy.126
  428.6 2.0 pad.27.clone
  430.6 31.8 %shard_map.296 = f32[64,640]{1,0:T(8,128)S(1)} custom-call(bf16[4,2,2,2,64,640]{5,4,3,2,1,0:T(8,128)(2,1)S(1)} %bitcast.133), custom_call_target="tpu_custom_call" | custom-call | tf_op jit(solution)/shard_map/pallas_call | solution.py:258
  465.6 32.5 %shard_map.298 = bf16[32,64,640]{2,1,0:T(8,128)(2,1)} custom-call(bf16[64,640]{1,0:T(8,128)(2,1)} %pad.30.x_ref), custom_call_target="tpu_custom_call" | custom-call | tf_op jit(solution)/shard_map/pallas_call | solution.py:151
  498.0 3.4 multiply_reduce_fusion.3
  501.5 39.9 %psum.21 = f32[4608]{0:T(1024)S(1)} all-reduce(f32[4608]{0:T(1024)S(1)} %pad_maximum_fusion.7), channel_id=1, replica_groups=mesh['expert'=8,'tensor'=4] {'expert','tensor'}, use_global_device_ids=true, to_apply=%region_18.19 | all-reduce | flops 4608 | bytes 36864 | tf_op jit(solution)/shard_map/psum | solution.py:645
  542.6 11.1 %convolution_bitcast_fusion.2 = f32[2,2048,352]{1,2,0:T(8,128)} fusion(bf16[2048,2,352]{0,2,1:T(8,128)(2,1)} %get-tuple-element.28, bf16[2048,2048,1]{1,0,2:T(8,128)(2,1)} %bitcast.147), kind=kOutput, calls=%fused_computation.39 | convolution fusion | flops 5905580032 | bytes 17039360 | tf_op jit(solution)/shard_map/td,tkf->kdf/dot_general | solution.py:579
  553.7 10.2 %convolution_bitcast_fusion.1 = f32[2,2048,352]{1,2,0:T(8,128)} fusion(bf16[2048,2,352]{0,2,1:T(8,128)(2,1)S(1)} %copy-done.69, bf16[2048,2048,1]{1,0,2:T(8,128)(2,1)} %bitcast.148), kind=kOutput, calls=%fused_computation.38 | convolution fusion | flops 5905580032 | bytes 17039360 | tf_op jit(solution)/shard_map/td,tkf->kdf/dot_general | solution.py:580
  563.9 10.1 %fusion = f32[2,352,2048]{2,1,0:T(8,128)} fusion(bf16[2048,2,352]{0,2,1:T(8,128)(2,1)S(1)} %copy-done.70, bf16[2048,2048]{1,0:T(8,128)(2,1)} %all-gather.4.cloned.1.call-done), kind=kOutput, calls=%fused_computation.4 | convolution fusion | flops 5905580032 | bytes 17039360 | tf_op jit(solution)/shard_map/tkf,td->kfd/dot_general | solution.py:581
  574.0 9.9 %fusion.30 = f32[2048,576]{0,1:T(8,128)} fusion(bf16[2048,2048]{1,0:T(8,128)(2,1)} %all-gather.6.cloned.1.call-done, bf16[2048,640]{1,0:T(8,128)(2,1)} %bitcast.165), kind=kOutput, calls=%fused_computation.50 | convolution fusion | flops 4831838208 | bytes 15728640 | tf_op jit(solution)/shard_map/dot_general | solution.py:443
  583.9 10.5 %fusion.97 = f32[2048,704]{0,1:T(8,128)} fusion(bf16[2048,704]{0,1:T(8,128)(2,1)S(1)} %copy-done.47, bf16[2048,2048]{1,0:T(8,128)(2,1)} %bitcast.149), kind=kOutput, calls=%fused_computation.181 | convolution fusion | flops 5905580032 | bytes 17039360 | tf_op jit(solution)/shard_map/dot_general | solution.py:443
  594.5 7.9 %fusion.98 = f32[2048,704]{0,1:T(8,128)} fusion(bf16[2048,704]{0,1:T(8,128)(2,1)S(1)} %copy-done.45, bf16[2048,2048]{1,0:T(8,128)(2,1)S(1)} %bitcast.155), kind=kOutput, calls=%fused_computation.182 | convolution fusion | flops 5905580032 | bytes 17039360 | tf_op jit(solution)/shard_map/dot_general | solution.py:443
  602.4 7.9 %fusion.96 = f32[704,2048]{1,0:T(8,128)} fusion(bf16[2048,704]{0,1:T(8,128)(2,1)S(1)} %copy-done.43, bf16[2048,2048]{1,0:T(8,128)(2,1)S(1)} %bitcast.173), kind=kOutput, calls=%fused_computation.180 | convolution fusion | flops 5905580032 | bytes 17039360 | tf_op jit(solution)/shard_map/dot_general | solution.py:443
  610.3 3.0 convert_element_type.176
  613.2 2.5 convert_element_type.178
  615.8 11.9 %fusion.95 = f32[2048,768]{1,0:T(8,128)} fusion(bf16[2048,2048]{1,0:T(8,128)(2,1)} %all-gather.6.cloned.1.call-done, bf16[2048,768]{0,1:T(8,128)(2,1)} %all-gather.8.cloned.1.call-done), kind=kOutput, calls=%fused_computation.179 | convolution fusion | flops 6442450944 | bytes 17825792 | tf_op jit(solution)/shard_map/dot_general | solution.py:443
  627.6 99.7 %reduce-scatter.2.cloned.1.call-done = bf16[64,2048]{1,0:T(8,128)(2,1)} async-done(((bf16[2048,2048]{1,0:T(8,128)(2,1)}), bf16[64,2048]{1,0:T(8,128)(2,1)}) %reduce-scatter.2.cloned.1.call-update) | async-done | bytes 262160 | tf_op jit(solution)/shard_map/reduce_scatter | solution.py:575
  727.4 2.0 fusion.63
  729.4 7.7 %shard_map.292 = bf16[2,2,64,2048]{3,2,1,0:T(8,128)(2,1)S(1)} custom-call(bf16[64,2048]{1,0:T(8,128)(2,1)S(1)} %get-tuple-element.41.x_ref), custom_call_target="tpu_custom_call" | custom-call | tf_op jit(solution)/shard_map/pallas_call | solution.py:381
  737.0 10.9 %shard_map.297 = bf16[2,2,64,2048]{3,2,1,0:T(8,128)(2,1)S(1)} custom-call(bf16[64,2048]{1,0:T(8,128)(2,1)S(1)} %get-tuple-element.40.x_ref), custom_call_target="tpu_custom_call" | custom-call | tf_op jit(solution)/shard_map/pallas_call | solution.py:381
  748.0 1.6 bitcast_convert_fusion
  (233 shorter events, 42.8 us)
Async XLA Ops:
  7.2 64.6 %copy-start = (bf16[2048,768]{1,0:T(8,128)(2,1)S(1)}, bf16[2048,768]{1,0:T(8,128)(2,1)}, u32[]{:S(2)}) copy-start(bf16[2048,768]{1,0:T(8,128)(2,1)} %param.20) | copy-start | bytes 9437188
  7.2 9.7 %copy-start.53 = (f32[256,6]{0,1:T(8,128)S(1)}, f32[256,6]{0,1:T(8,128)}, u32[]{:S(2)}) copy-start(f32[256,6]{0,1:T(8,128)} %param.32) | copy-start | bytes 18436
  7.2 9.6 %copy-start.54 = (s32[256,6]{0,1:T(8,128)S(1)}, s32[256,6]{0,1:T(8,128)}, u32[]{:S(2)}) copy-start(s32[256,6]{0,1:T(8,128)} %param.33) | copy-start | bytes 18436
  7.2 192.0 %all-gather.4.cloned.1.call-start = ((), (), s32[]{:S(2)}) async-start(), calls=%async_computation.2 | async-start | bytes 8650752 | tf_op jit(solution)/shard_map/all_gather | solution.py:499
  9.1 564.9 %all-gather.6.cloned.1.call-start = ((), (), s32[]{:S(2)}) async-start(), calls=%async_computation.3 | async-start | bytes 8650752 | tf_op jit(solution)/shard_map/all_gather | solution.py:544
  14.0 8.4 %copy-start.39 = (s32[2048]{0:T(1024)S(1)}, s32[2048]{0:T(1024)}, u32[]{:S(2)}) copy-start(s32[2048]{0:T(1024)} %param.34) | copy-start | bytes 24580
  14.0 9.3 %copy-start.48 = (f32[512]{0:T(512)S(1)}, f32[512]{0:T(512)}, u32[]{:S(2)}) copy-start(f32[512]{0:T(512)} %param.22) | copy-start | bytes 6148
  14.0 596.3 %all-reduce.10.cloned.1.call-start = ((), (), s32[]{:S(2)}) async-start(), calls=%async_computation.5 | async-start | bytes 6291456 | tf_op jit(solution)/shard_map/psum | solution.py:647
  16.9 11.2 %copy-start.58 = (f32[32]{0:T(128)}, f32[32]{0:T(128)S(1)}, u32[]{:S(2)}) copy-start(f32[32]{0:T(128)S(1)} %multiply_power_fusion) | copy-start | bytes 388
  23.1 5.0 copy-start.50
  65.4 6.3 copy-start.26
  74.2 4.2 copy-start.60
  78.4 4.5 copy-start.29
  78.4 4.5 copy-start.31
  82.9 4.3 copy-start.4
  82.9 5.2 copy-start.12
  90.4 12.2 %copy-start.28 = (bf16[4,128,256]{2,1,0:T(8,128)(2,1)}, bf16[4,128,256]{2,1,0:T(8,128)(2,1)S(1)}, u32[]{:S(2)}) copy-start(bf16[4,128,256]{2,1,0:T(8,128)(2,1)S(1)} %fusion.51) | copy-start | bytes 786436
  90.4 13.0 %copy-start.40 = (f32[2048]{0:T(1024)S(1)}, f32[2048]{0:T(1024)}, u32[]{:S(2)}) copy-start(f32[2048]{0:T(1024)} %param.25) | copy-start | bytes 24580
  102.7 239.9 %copy-start.51 = (f32[64]{0:T(128)}, f32[64]{0:T(128)S(1)}, u32[]{:S(2)}) copy-start(f32[64]{0:T(128)S(1)} %fusion.80) | copy-start | bytes 772
  163.5 11.3 %copy-start.11 = (bf16[32,64,2048]{2,1,0:T(8,128)(2,1)S(1)}, bf16[32,64,2048]{2,1,0:T(8,128)(2,1)}, u32[]{:S(2)}) copy-start(bf16[32,64,2048]{2,1,0:T(8,128)(2,1)} %shard_map.291) | copy-start | bytes 25165828
  163.5 11.3 %copy-start.65 = (bf16[2,2048,352]{1,2,0:T(8,128)(2,1)S(1)}, bf16[2,2048,352]{1,2,0:T(8,128)(2,1)}, u32[]{:S(2)}) copy-start(bf16[2,2048,352]{1,2,0:T(8,128)(2,1)} %param.30) | copy-start | bytes 8650756
  174.8 8.0 %copy-start.20 = (bf16[2048,704]{0,1:T(8,128)(2,1)S(1)}, bf16[2048,704]{0,1:T(8,128)(2,1)}, u32[]{:S(2)}) copy-start(bf16[2048,704]{0,1:T(8,128)(2,1)} %param.26) | copy-start | bytes 8650756
  182.8 8.4 %copy-start.18 = (bf16[2048,704]{0,1:T(8,128)(2,1)S(1)}, bf16[2048,704]{0,1:T(8,128)(2,1)}, u32[]{:S(2)}) copy-start(bf16[2048,704]{0,1:T(8,128)(2,1)} %param.27) | copy-start | bytes 8650756
  199.2 15.3 %copy-start.21 = (bf16[2048,704]{0,1:T(8,128)(2,1)S(1)}, bf16[2048,704]{0,1:T(8,128)(2,1)}, u32[]{:S(2)}) copy-start(bf16[2048,704]{0,1:T(8,128)(2,1)} %param.26) | copy-start | bytes 8650756
  214.5 20.3 %copy-start.46 = (bf16[2048,704]{0,1:T(8,128)(2,1)}, bf16[2048,704]{0,1:T(8,128)(2,1)S(1)}, u32[]{:S(2)}) copy-start(bf16[2048,704]{0,1:T(8,128)(2,1)S(1)} %get-tuple-element.31) | copy-start | bytes 8650756
  214.5 47.4 %copy-start.44 = (bf16[2048,704]{0,1:T(8,128)(2,1)}, bf16[2048,704]{0,1:T(8,128)(2,1)S(1)}, u32[]{:S(2)}) copy-start(bf16[2048,704]{0,1:T(8,128)(2,1)S(1)} %get-tuple-element.30) | copy-start | bytes 8650756
  214.5 3.9 copy-start.67
  218.4 16.4 %copy-start.64 = (bf16[2,2048,352]{1,2,0:T(8,128)(2,1)S(1)}, bf16[2,2048,352]{1,2,0:T(8,128)(2,1)}, u32[]{:S(2)}) copy-start(bf16[2,2048,352]{1,2,0:T(8,128)(2,1)} %param.29) | copy-start | bytes 8650756
  234.8 12.3 %copy-start.66 = (bf16[2,2048,352]{1,2,0:T(8,128)(2,1)S(1)}, bf16[2,2048,352]{1,2,0:T(8,128)(2,1)}, u32[]{:S(2)}) copy-start(bf16[2,2048,352]{1,2,0:T(8,128)(2,1)} %param.30) | copy-start | bytes 8650756
  247.2 14.7 %copy-start.19 = (bf16[2048,704]{0,1:T(8,128)(2,1)S(1)}, bf16[2048,704]{0,1:T(8,128)(2,1)}, u32[]{:S(2)}) copy-start(bf16[2048,704]{0,1:T(8,128)(2,1)} %param.27) | copy-start | bytes 8650756
  272.5 69.9 %copy-start.9 = (f32[64,2048]{1,0:T(8,128)S(1)}, f32[64,2048]{1,0:T(8,128)}, u32[]{:S(2)}) copy-start(f32[64,2048]{1,0:T(8,128)} %copy-done.8) | copy-start | bytes 1572868
  272.5 82.3 %copy-start.24 = (bf16[512,2048]{1,0:T(8,128)(2,1)S(1)}, bf16[512,2048]{1,0:T(8,128)(2,1)}, u32[]{:S(2)}) copy-start(bf16[512,2048]{1,0:T(8,128)(2,1)} %param.24) | copy-start | bytes 6291460
  342.5 18.1 %copy-start.55 = (f32[64]{0:T(128)}, f32[64]{0:T(128)S(1)}, u32[]{:S(2)}) copy-start(f32[64]{0:T(128)S(1)} %get-tuple-element.57) | copy-start | bytes 772
  360.6 5.4 slice-start
  360.6 6.5 slice-start.1
  378.6 4.4 copy-start.36
  378.6 4.4 copy-start.38
  378.7 237.1 %all-gather.8.cloned.1.call-start = ((), (), s32[]{:S(2)}) async-start(), calls=%async_computation.4 | async-start | bytes 3538944 | tf_op jit(solution)/shard_map/all_gather | solution.py:626
  379.1 4.0 copy-start.6
  387.1 340.2 %reduce-scatter.2.cloned.1.call-start = ((), (), s32[]{:S(2)}) async-start(), calls=%async_computation.1 | async-start | bytes 8650752 | tf_op jit(solution)/shard_map/reduce_scatter | solution.py:575
  390.1 9.8 %copy-start.17 = (bf16[704,2048]{1,0:T(8,128)(2,1)S(1)}, bf16[704,2048]{1,0:T(8,128)(2,1)}, u32[]{:S(2)}) copy-start(bf16[704,2048]{1,0:T(8,128)(2,1)} %param.28) | copy-start | bytes 8650756
  407.3 12.1 %copy-start.7 = (bf16[4,256,2048]{2,1,0:T(8,128)(2,1)S(1)}, bf16[4,256,2048]{2,1,0:T(8,128)(2,1)}, u32[]{:S(2)}) copy-start(bf16[4,256,2048]{2,1,0:T(8,128)(2,1)} %copy-done.5) | copy-start | bytes 12582916
  407.3 12.1 %copy-start.30 = (bf16[256,4,32]{0,2,1:T(8,128)(2,1)S(1)}, bf16[256,4,32]{0,2,1:T(8,128)(2,1)}, u32[]{:S(2)}) copy-start(bf16[256,4,32]{0,2,1:T(8,128)(2,1)} %copy-done.29) | copy-start | bytes 196612
  407.3 12.1 %copy-start.32 = (bf16[256,4,32]{0,2,1:T(8,128)(2,1)S(1)}, bf16[256,4,32]{0,2,1:T(8,128)(2,1)}, u32[]{:S(2)}) copy-start(bf16[256,4,32]{0,2,1:T(8,128)(2,1)} %copy-done.31) | copy-start | bytes 196612
  408.3 11.9 %copy-start.16 = (bf16[2048,4,256]{0,2,1:T(8,128)(2,1)S(1)}, bf16[2048,4,256]{0,2,1:T(8,128)(2,1)}, u32[]{:S(2)}) copy-start(bf16[2048,4,256]{0,2,1:T(8,128)(2,1)} %copy-done.15) | copy-start | bytes 12582916
  408.4 11.9 %copy-start.68 = (bf16[512,1024]{1,0:T(8,128)(2,1)S(1)}, bf16[512,1024]{1,0:T(8,128)(2,1)}, u32[]{:S(2)}) copy-start(bf16[512,1024]{1,0:T(8,128)(2,1)} %param.23) | copy-start | bytes 3145732
  428.6 33.9 %copy-start.59 = (f32[32]{0:T(128)S(1)}, f32[32]{0:T(128)}, u32[]{:S(2)}) copy-start(f32[32]{0:T(128)} %copy-done.58) | copy-start | bytes 388
  428.6 33.9 %copy-start.63 = (f32[64]{0:T(128)S(1)}, f32[64]{0:T(128)}, u32[]{:S(2)}) copy-start(f32[64]{0:T(128)} %dynamic-slice_convert_fusion.1) | copy-start | bytes 772
  428.6 34.2 %copy-start.49 = (f32[512]{0:T(512)S(1)}, f32[512]{0:T(512)}, u32[]{:S(2)}) copy-start(f32[512]{0:T(512)} %param.22) | copy-start | bytes 6148
  428.6 34.2 %copy-start.57 = (f32[64]{0:T(128)S(1)}, f32[64]{0:T(128)}, u32[]{:S(2)}) copy-start(f32[64]{0:T(128)} %fusion.81) | copy-start | bytes 772
  428.6 35.3 %copy-start.62 = (f32[64]{0:T(128)S(1)}, f32[64]{0:T(128)}, u32[]{:S(2)}) copy-start(f32[64]{0:T(128)} %copy-done.61) | copy-start | bytes 772
  430.6 67.4 %copy-start.42 = (f32[2048]{0:T(1024)S(1)}, f32[2048]{0:T(1024)}, u32[]{:S(2)}) copy-start(f32[2048]{0:T(1024)} %param.19) | copy-start | bytes 24580
  542.6 11.1 %copy-start.69 = (bf16[2048,2,352]{0,2,1:T(8,128)(2,1)S(1)}, bf16[2048,2,352]{0,2,1:T(8,128)(2,1)}, u32[]{:S(2)}) copy-start(bf16[2048,2,352]{0,2,1:T(8,128)(2,1)} %get-tuple-element.27) | copy-start | bytes 8650756
  553.7 10.2 %copy-start.70 = (bf16[2048,2,352]{0,2,1:T(8,128)(2,1)S(1)}, bf16[2048,2,352]{0,2,1:T(8,128)(2,1)}, u32[]{:S(2)}) copy-start(bf16[2048,2,352]{0,2,1:T(8,128)(2,1)} %get-tuple-element.29) | copy-start | bytes 8650756
  574.0 9.9 %copy-start.47 = (bf16[2048,704]{0,1:T(8,128)(2,1)S(1)}, bf16[2048,704]{0,1:T(8,128)(2,1)}, u32[]{:S(2)}) copy-start(bf16[2048,704]{0,1:T(8,128)(2,1)} %copy-done.46) | copy-start | bytes 8650756
  574.0 20.4 %slice-start.2 = ((s8[8388608]{0:T(1024)(128)(4,1)}), s8[4194304]{0:T(1024)(128)(4,1)S(1)}, s32[]{:S(2)}) async-start(s8[8388608]{0:T(1024)(128)(4,1)} %bitcast.153), calls=%async_computation.8 | async-start | bytes 8388608
  583.9 10.5 %slice-start.3 = ((s8[8388608]{0:T(1024)(128)(4,1)}), s8[4194304]{0:T(1024)(128)(4,1)S(1)}, s32[]{:S(2)}) async-start(s8[8388608]{0:T(1024)(128)(4,1)} %bitcast.153), calls=%async_computation.9 | async-start | bytes 8388608
  583.9 10.5 %copy-start.45 = (bf16[2048,704]{0,1:T(8,128)(2,1)S(1)}, bf16[2048,704]{0,1:T(8,128)(2,1)}, u32[]{:S(2)}) copy-start(bf16[2048,704]{0,1:T(8,128)(2,1)} %copy-done.44) | copy-start | bytes 8650756
  583.9 18.5 %slice-start.4 = ((s8[8388608]{0:T(1024)(128)(4,1)}), s8[4194304]{0:T(1024)(128)(4,1)S(1)}, s32[]{:S(2)}) async-start(s8[8388608]{0:T(1024)(128)(4,1)} %bitcast.172), calls=%async_computation.10 | async-start | bytes 8388608
  594.4 7.9 %copy-start.43 = (bf16[2048,704]{0,1:T(8,128)(2,1)S(1)}, bf16[2048,704]{0,1:T(8,128)(2,1)}, u32[]{:S(2)}) copy-start(bf16[2048,704]{0,1:T(8,128)(2,1)} %get-tuple-element.32) | copy-start | bytes 8650756
  594.5 7.9 %slice-start.5 = ((s8[8388608]{0:T(1024)(128)(4,1)}), s8[4194304]{0:T(1024)(128)(4,1)S(1)}, s32[]{:S(2)}) async-start(s8[8388608]{0:T(1024)(128)(4,1)} %bitcast.172), calls=%async_computation.11 | async-start | bytes 8388608
  615.8 111.6 %copy-start.41 = (f32[2048]{0:T(1024)S(1)}, f32[2048]{0:T(1024)}, u32[]{:S(2)}) copy-start(f32[2048]{0:T(1024)} %param.25) | copy-start | bytes 24580
  615.8 111.6 %copy-start.52 = (f32[64]{0:T(128)S(1)}, f32[64]{0:T(128)}, u32[]{:S(2)}) copy-start(f32[64]{0:T(128)} %copy-done.51) | copy-start | bytes 772
  615.8 111.6 %copy-start.56 = (f32[64]{0:T(128)S(1)}, f32[64]{0:T(128)}, u32[]{:S(2)}) copy-start(f32[64]{0:T(128)} %copy-done.55) | copy-start | bytes 772
  (18 other events, 32.7 us)
Sparse Core Ops, SparseCore 0:
  11.5 86.5 all-gather.3
  100.9 91.4 all-gather.5
  378.8 135.5 all-reduce.9
  516.4 61.4 all-gather.7
  580.2 147.1 reduce-scatter.1

commit v2 on v1

--- a/solution.py
+++ b/solution.py
@@ -391,6 +391,644 @@
     return out.reshape(2 * ny * r, n)
 
 
+def dot_rows(left_side, right_side):
+    return lax.dot_general(
+        left_side, right_side, (((1,), (1,)), ((), ())), preferred_element_type=jnp.float32
+    )
+
+
+def dot_plain(left_side, right_side):
+    return jnp.dot(left_side, right_side, preferred_element_type=jnp.float32)
+
+
+def round_up(value, unit):
+    return -(-value // unit) * unit
+
+
+def experts_kernel(
+    grid,
+    pieces,
+    x_ref,
+    dz_ref,
+    gate_ref,
+    eg_hbm,
+    eu_hbm,
+    ed_hbm,
+    sg_hbm,
+    su_hbm,
+    sd_hbm,
+    all_ref,
+    grad_ref,
+    y_ref,
+    gated_ref,
+    dcat_ref,
+    act_ref,
+    dsg_ref,
+    dsu_ref,
+    raw,
+    egu,
+    ed,
+    sg,
+    su,
+    sd,
+    dabuf,
+    xbuf,
+    dzbuf,
+    gated,
+    dcat,
+    act,
+    dsg,
+    dsu,
+    ybuf,
+    dx,
+    dx_out,
+    core_in,
+    d1_in0,
+    d1_in1,
+    d2_in0,
+    d2_in1,
+    a_in,
+    raw_sem,
+    weight_sem,
+    own_sem,
+    x_sem,
+    dz_sem,
+    out_sem,
+    fill_sem,
+    send_sem,
+    recv_sem,
+    share_send,
+    share_recv,
+    core_s,
+    core_r,
+    s10,
+    r10,
+    s11,
+    r11,
+    s20,
+    r20,
+    s21,
+    r21,
+    sa,
+    ra,
+):
+    na, nb, ny = grid.na, grid.nb, grid.ny
+    a, b, y, c = grid.here()
+    r, n = x_ref.shape
+    half, width, rows = r // 2, n // pieces, na * r
+    pairs = nb * ny
+    steps = 2 * pairs
+    device = a * nb + b
+    f, fs = eg_hbm.shape[2], sg_hbm.shape[1]
+    wide = egu.shape[1] // (2 * EXP_DEV)
+    ef = EXP_DEV * wide
+    f32, bf = jnp.float32, jnp.bfloat16
+
+    def raw_load(src):
+        return pltpu.make_async_copy(src, raw, raw_sem)
+
+    loads = [
+        pltpu.make_async_copy(ed_hbm.at[e], ed.at[pl.ds(e * wide, f)], weight_sem.at[e])
+        for e in range(EXP_DEV)
+    ]
+    loads += [
+        pltpu.make_async_copy(src, dst, weight_sem.at[EXP_DEV + i])
+        for i, (src, dst) in enumerate(((sd_hbm, sd.at[pl.ds(0, fs)]), (sg_hbm, sg), (su_hbm, su)))
+    ]
+    for load in loads:
+        load.start()
+    raw_load(eg_hbm).start()
+    greet(grid)
+
+    counts = [0]
+
+    def place(bb, yy, cc, aa, h):
+        return all_ref.at[aa, bb, yy, cc, pl.ds(h * half, half)]
+
+    def slot(bb, yy, aa, h):
+        return ((bb * ny + yy) * na + aa) * 2 + h
+
+    def push(src, bb, yy, aa, h, where, send, recv):
+        pltpu.make_async_remote_copy(
+            src_ref=src,
+            dst_ref=place(bb, yy, c, aa, h),
+            send_sem=send,
+            recv_sem=recv.at[slot(bb, yy, aa, h)],
+            device_id=where,
+            device_id_type=MESH,
+        ).start()
+
+    def line(i):
+        if na != 4:
+            return wrap(a + i, na)
+        if i == 0:
+            return a
+        if i == 1:
+            return a + 1 - 2 * lax.rem(a, 2)
+        return (i - lax.div(a, 2)) if i == 2 else (3 - 3 * lax.div(a, 2))
+
+    def onward(src, bb, yy, aa, h, dims):
+        for d in dims:
+            size = {"a": na, "b": nb, "y": ny}[d]
+            for i in range(1, size):
+                where = {
+                    "a": lambda: grid.device(line(i), b, y, c),
+                    "b": lambda: grid.device(a, wrap(b + i, nb), y, c),
+                    "y": lambda: grid.device(a, b, wrap(y + i, ny), c),
+                }[d]()
+                push(src, bb, yy, aa, h, where, send_sem.at[counts[0]], recv_sem)
+                counts[0] += 1
+        push(
+            src, bb, yy, aa, h, grid.device(a, b, y, 1 - c), share_send.at[slot(bb, yy, aa, h)], share_recv
+        )
+
+    def landed(bb, yy, cc, aa, h, sem):
+        ref = place(bb, yy, cc, aa, h)
+        pltpu.make_async_copy(ref, ref, sem.at[slot(bb, yy, aa, h)]).wait()
+        return ref
+
+    orders = (("b", "y"), ("y", "b"))
+
+    def relay(j, k, i, h, dims):
+        bb, yy, aa = wrap(b + j, nb), wrap(y + k, ny), line(i)
+        onward(landed(bb, yy, c, aa, h, recv_sem), bb, yy, aa, h, dims)
+
+    own = pltpu.make_async_copy(x_ref, all_ref.at[a, b, y, c], own_sem)
+    own.start()
+    for h in range(2):
+        onward(x_ref.at[pl.ds(h * half, half)], b, y, a, h, ("a",) + orders[h])
+
+    hooks = {}
+    early = []
+    for i in range(na):
+        if i:
+            early += [(0, 0, i, h, orders[h]) for h in range(2)]
+        if i:
+            early += [(j, 0, i - 1, 0, orders[0][1:]) for j in range(1, nb)]
+            early += [(0, k, i - 1, 1, orders[1][1:]) for k in range(1, ny)]
+    early += [(j, 0, na - 1, 0, orders[0][1:]) for j in range(1, nb)]
+    early += [(0, k, na - 1, 1, orders[1][1:]) for k in range(1, ny)]
+    for m, event in enumerate(early):
+        place_at = 1 + m * (2 * steps - 1) // len(early)
+        hooks.setdefault(("early", place_at // 2, place_at % 2), []).append(event)
+    for pair in range(1, pairs):
+        j, k = pair // ny, pair % ny
+        late = [(j, k, i, h, ()) for i in range(na) for h in range(2) if (k if h == 0 else j)]
+        for m, event in enumerate(late):
+            hooks.setdefault(("main", pair, m * 3 // len(late)), []).append(event)
+
+    def hook(stage, step, spot):
+        for (when_stage, when, when_spot), events in hooks.items():
+            if when_stage == stage and when_spot == spot:
+
+                @pl.when(step == when)
+                def _():
+                    for event in events:
+                        relay(*event)
+
+    def spots(step):
+        pair, l = lax.div(step, 2), 1 - lax.rem(step, 2)
+        j, k = lax.div(pair, ny), lax.rem(pair, ny)
+        return j, k, l, wrap(b + j, nb), wrap(y + k, ny), wrap(c + l, 2)
+
+    def flat(value):
+        return value.reshape(rows, value.shape[-1])
+
+    def fold(value):
+        return value.reshape(na, r, value.shape[-1])
+
+    def dz_load(step):
+        _, _, _, bb, yy, cc = spots(step)
+        s = lax.rem(step, 2)
+        return pltpu.make_async_copy(dz_ref.at[:, bb, yy, cc], dzbuf.at[s], dz_sem.at[s])
+
+    dz_load(a * 0).start()
+    for e in range(EXP_DEV):
+        ed[e * wide + f : (e + 1) * wide] = jnp.zeros((wide - f, n), bf)
+    if sd.shape[0] > fs:
+        sd[fs:] = jnp.zeros((sd.shape[0] - fs, n), bf)
+    for load in loads[: EXP_DEV + 1]:
+        load.wait()
+
+    def early_body(step, carry):
+        s = lax.rem(step, 2)
+
+        @pl.when(step + 1 < steps)
+        def _():
+            dz_load(step + 1).start()
+
+        dz_load(step).wait()
+        dz = flat(dzbuf[s])
+        dabuf[step, :, :ef] = dot_rows(dz, ed[...]).astype(bf)
+        hook("early", step, 0)
+        dabuf[step, :, ef:] = dot_rows(dz, sd[...]).astype(bf)
+        hook("early", step, 1)
+        return carry
+
+    lax.fori_loop(0, steps, early_body, 0)
+    for part, src in enumerate((eg_hbm, eu_hbm)):
+        raw_load(src).wait()
+        for e in range(EXP_DEV):
+            at = part * ef + e * wide
+            if wide > f:
+                egu[:, at + wide - 128 : at + wide] = jnp.zeros((n, 128), bf)
+            egu[:, at : at + f] = raw[e]
+        if part == 0:
+            raw_load(eu_hbm).start()
+    for load in loads[EXP_DEV + 1 :]:
+        load.wait()
+    own.wait()
+
+    def x_load(step):
+        _, _, _, bb, yy, cc = spots(step)
+        return pltpu.make_async_copy(all_ref.at[:, bb, yy, cc], xbuf.at[0], x_sem.at[0])
+
+    def stores(step):
+        _, _, _, bb, yy, cc = spots(step)
+        s = lax.rem(step, 2)
+        return [
+            pltpu.make_async_copy(gated.at[s], gated_ref.at[:, bb, yy, cc], out_sem.at[s, 0]),
+            pltpu.make_async_copy(dcat.at[s], dcat_ref.at[:, bb, yy, cc], out_sem.at[s, 1]),
+        ]
+
+    def remote(src, dst, ss, rs, where):
+        return pltpu.make_async_remote_copy(
+            src_ref=src, dst_ref=dst, send_sem=ss, recv_sem=rs, device_id=where, device_id_type=MESH
+        )
+
+    def cols(p):
+        return pl.ds(p * width, width)
+
+    upper = (pl.ds(0, half), pl.ds(half, half))
+
+    def send_core(pair):
+        j, k = lax.div(pair, ny), lax.rem(pair, ny)
+        return remote(
+            dx_out.at[lax.rem(pair, 2)], core_in.at[j, k], core_s.at[lax.rem(pair, 2)],
+            core_r.at[j, k], grid.device(a, b, y, 1 - c),
+        )
+
+    def send_10(p, j, k):
+        return remote(
+            dx.at[j, k, :, upper[0], cols(p)], d1_in0.at[p, j, k - 1], s10.at[p, j, k - 1],
+            r10.at[p, j, k - 1], grid.device(a, b, wrap(y + k, ny), c),
+        )
+
+    def send_11(p, j, k):
+        return remote(
+            dx.at[j, k, :, upper[1], cols(p)], d1_in1.at[p, k, j - 1], s11.at[p, k, j - 1],
+            r11.at[p, k, j - 1], grid.device(a, wrap(b + j, nb), y, c),
+        )
+
+    def await_in(ref, sem):
+        pltpu.make_async_copy(ref, ref, sem).wait()
+
+    def add(dst, src):
+        dst[...] = (dst[...].astype(f32) + src[...].astype(f32)).astype(dst.dtype)
+
+    def shared_front(step, x, s):
+        g = dot_plain(x, sg[...])
+        u = dot_plain(x, su[...])
+        d = dabuf[step, :, ef : ef + fs].astype(f32)
+        sig = 1.0 / (1.0 + jnp.exp(-g))
+        swish = g * sig
+        act[s] = fold((swish * u).astype(bf))
+        dsg[s] = fold((d * u * (sig + swish * (1.0 - sig))).astype(bf))
+        dsu[s] = fold((d * swish).astype(bf))
+
+    def is_mine(bb, yy, cc):
+        return lax.rem((bb * ny + yy) * 2 + cc, na * nb) == device
+
+    chunk = min(n, 1024)
+
+    def main_body(step, carry):
+        j, k, l, bb, yy, cc = spots(step)
+        s = lax.rem(step, 2)
+
+        @pl.when(l == 1)
+        def _():
+            for i in range(na):
+                for h in range(2):
+                    landed(bb, yy, cc, line(i), h, share_recv)
+
+        x_load(step).start()
+
+        @pl.when(step >= 2)
+        def _():
+            for store in stores(step - 2):
+                store.wait()
+
+        x_load(step).wait()
+        x = flat(xbuf[0])
+        g = dot_plain(x, egu[:, :ef])
+        u = dot_plain(x, egu[:, ef:])
+        for e in range(EXP_DEV):
+            at = pl.ds(e * wide, wide)
+            scale = flat(gate_ref[e, :, bb, yy, cc])
+            ge, ue = g[:, e * wide : (e + 1) * wide], u[:, e * wide : (e + 1) * wide]
+            d = dabuf[step, :, at].astype(f32) * scale
+            sig = 1.0 / (1.0 + jnp.exp(-ge))
+            swish = ge * sig
+            gated[s, :, :, at] = fold((scale * (swish * ue)).astype(bf))
+            dcat[s, :, :, at] = fold((d * ue * (sig + swish * (1.0 - sig))).astype(bf))
+            dcat[s, :, :, pl.ds(ef + e * wide, wide)] = fold((d * swish).astype(bf))
+        hook("main", step, 0)
+        mine = is_mine(bb, yy, cc)
+
+        @pl.when(mine)
+        def _():
+            shared_front(step, x, 0)
+
+        hook("main", step, 1)
+
+        def column(target):
+            for q in range(n // chunk):
+                at = pl.ds(q * chunk, chunk)
+                total = dot_rows(flat(dcat[s]), egu[at])
+                target[:, :, at] = fold(total.astype(bf))
+
+            @pl.when(mine)
+            def _():
+                for q in range(n // chunk):
+                    at = pl.ds(q * chunk, chunk)
+                    more = dot_rows(flat(dsg[0]), sg[at]) + dot_rows(flat(dsu[0]), su[at])
+                    target[:, :, at] = fold((flat(target[:, :, at]).astype(f32) + more).astype(bf))
+
+        for store in stores(step):
+            store.start()
+
+        @pl.when(l == 1)
+        def _():
+            pair = lax.div(step, 2)
+
+            @pl.when(pair >= 2)
+            def _():
+                send_core(pair - 2).wait_send()
+
+            column(dx_out.at[lax.rem(pair, 2)])
+            send_core(pair).start()
+
+        @pl.when(l == 0)
+        def _():
+            column(dx.at[j, k])
+            await_in(core_in.at[j, k], core_r.at[j, k])
+
+            def one(i, carry):
+                add(dx.at[j, k, i], core_in.at[j, k, i])
+                return carry
+
+            lax.fori_loop(0, na, one, 0)
+
+            @pl.when(k > 0)
+            def _():
+                for p in range(pieces):
+                    send_10(p, j, k).start()
+
+            @pl.when(j > 0)
+            def _():
+                for p in range(pieces):
+                    send_11(p, j, k).start()
+
+        hook("main", step, 2)
+        return carry
+
+    lax.fori_loop(0, steps, main_body, 0)
+    for step in (steps - 2, steps - 1):
+        for store in stores(a * 0 + step):
+            store.wait()
+
+    def send_20(p, j):
+        return remote(
+            dx.at[j, 0, :, upper[0], cols(p)], d2_in0.at[p, j - 1], s20.at[p, j - 1],
+            r20.at[p, j - 1], grid.device(a, wrap(b + j, nb), y, c),
+        )
+
+    def send_21(p, k):
+        return remote(
+            dx.at[0, k, :, upper[1], cols(p)], d2_in1.at[p, k - 1], s21.at[p, k - 1],
+            r21.at[p, k - 1], grid.device(a, b, wrap(y + k, ny), c),
+        )
+
+    def send_a(p, i):
+        return remote(
+            dx.at[0, 0, wrap(a + i, na), :, cols(p)], a_in.at[p, i - 1], sa.at[p, i - 1],
+            ra.at[p, i - 1], grid.device(wrap(a + i, na), b, y, c),
+        )
+
+    def sum_first(p):
+        for j in reversed(range(nb)):
+            for k in range(1, ny):
+                await_in(d1_in0.at[p, j, k - 1], r10.at[p, j, k - 1])
+                for i in range(na):
+                    add(dx.at[j, 0, i, upper[0], cols(p)], d1_in0.at[p, j, k - 1, i])
+            if j:
+                send_20(p, j).start()
+        for k in reversed(range(ny)):
+            for j in range(1, nb):
+                await_in(d1_in1.at[p, k, j - 1], r11.at[p, k, j - 1])
+                for i in range(na):
+                    add(dx.at[0, k, i, upper[1], cols(p)], d1_in1.at[p, k, j - 1, i])
+            if k:
+                send_21(p, k).start()
+
+    def sum_second(p):
+        for j in range(1, nb):
+            await_in(d2_in0.at[p, j - 1], r20.at[p, j - 1])
+            for i in range(na):
+                add(dx.at[0, 0, i, upper[0], cols(p)], d2_in0.at[p, j - 1, i])
+        for k in range(1, ny):
+            await_in(d2_in1.at[p, k - 1], r21.at[p, k - 1])
+            for i in range(na):
+                add(dx.at[0, 0, i, upper[1], cols(p)], d2_in1.at[p, k - 1, i])
+        for i in range(1, na):
+            send_a(p, i).start()
+
+    def sum_last(p):
+        total = dx[0, 0, a, :, cols(p)].astype(f32)
+        for i in range(1, na):
+            await_in(a_in.at[p, i - 1], ra.at[p, i - 1])
+            total = total + a_in[p, i - 1].astype(f32)
+        grad_ref[:, cols(p)] = total
+
+    work = [(sum_first, p) for p in range(pieces)] + [(sum_second, p) for p in range(pieces)]
+    turns = {}
+    for m, item in enumerate(work):
+        turns.setdefault(min(steps - 1, 1 + m * (steps - 1) // len(work)), []).append(item)
+
+    def fill_loads(step):
+        _, _, _, bb, yy, cc = spots(step)
+        s = lax.rem(step, 2)
+        return [
+            pltpu.make_async_copy(all_ref.at[:, bb, yy, cc], xbuf.at[s], x_sem.at[s]),
+            pltpu.make_async_copy(gated_ref.at[:, bb, yy, cc], gated.at[s], fill_sem.at[s]),
+        ]
+
+    def fill_stores(step):
+        _, _, _, bb, yy, cc = spots(step)
+        s = lax.rem(step, 2)
+        pairs_of = [
+            (act.at[s], act_ref.at[:, bb, yy, cc]),
+            (dsg.at[s], dsg_ref.at[:, bb, yy, cc]),
+            (dsu.at[s], dsu_ref.at[:, bb, yy, cc]),
+            (ybuf.at[s], y_ref.at[:, bb, yy, cc]),
+        ]
+        return [
+            pltpu.make_async_copy(src, dst, out_sem.at[s, i])
+            for i, (src, dst) in enumerate(pairs_of)
+        ]
+
+    for load in fill_loads(a * 0):
+        load.start()
+
+    def fill_body(step, carry):
+        j, k, l, bb, yy, cc = spots(step)
+        s = lax.rem(step, 2)
+
+        @pl.when(step + 1 < steps)
+        def _():
+            for load in fill_loads(step + 1):
+                load.start()
+
+        @pl.when(step >= 2)
+        def _():
+            for store in fill_stores(step - 2):
+                store.wait()
+
+        for load in fill_loads(step):
+            load.wait()
+        x = flat(xbuf[s])
+        shared_front(step, x, s)
+        for q in range(n // chunk):
+            at = pl.ds(q * chunk, chunk)
+            ybuf[s, :, :, at] = fold(dot_plain(flat(gated[s]), ed[:, at]).astype(bf))
+
+        @pl.when(is_mine(bb, yy, cc))
+        def _():
+            for q in range(n // chunk):
+                at = pl.ds(q * chunk, chunk)
+                more = dot_plain(flat(act[s]), sd[:fs, at])
+                ybuf[s, :, :, at] = fold((flat(ybuf[s, :, :, at]).astype(f32) + more).astype(bf))
+
+        for store in fill_stores(step):
+            store.start()
+        for when, items in turns.items():
+
+            @pl.when(step == when)
+            def _():
+                for item, p in items:
+                    item(p)
+
+        return carry
+
+    lax.fori_loop(0, steps, fill_body, 0)
+    for p in range(pieces):
+        sum_last(p)
+
+    for step in (steps - 2, steps - 1):
+        for store in fill_stores(a * 0 + step):
+            store.wait()
+    some = place(b, y, c, a, 0)
+    for i in range(counts[0]):
+        pltpu.make_async_copy(some, some, send_sem.at[i]).wait()
+    for i in range(2 * na * pairs):
+        pltpu.make_async_copy(some, some, share_send.at[i]).wait()
+    for pair in range(max(0, pairs - 2), pairs):
+        send_core(a * 0 + pair).wait_send()
+    for p in range(pieces):
+        for j in range(nb):
+            for k in range(ny):
+                if k:
+                    send_10(p, j, k).wait_send()
+                if j:
+                    send_11(p, j, k).wait_send()
+        for j in range(1, nb):
+            send_20(p, j).wait_send()
+        for k in range(1, ny):
+            send_21(p, k).wait_send()
+        for i in range(1, na):
+            send_a(p, i).wait_send()
+
+
+def experts_call(
+    grid, x, dz, gates, expert_gate, expert_up, expert_down, shared_gate, shared_up, shared_down,
+    collective_id, pieces=2,
+):
+    r, n = x.shape
+    na, nb, ny = grid.na, grid.nb, grid.ny
+    f, fs = expert_gate.shape[2], shared_gate.shape[1]
+    wide, wide_s = round_up(f, 128), round_up(fs, 128)
+    ef = EXP_DEV * wide
+    half, width, rows = r // 2, n // pieces, na * r
+    steps = 2 * nb * ny
+    lay = (na, nb, ny, 2, r)
+    bf = jnp.bfloat16
+    sems = lambda *s: pltpu.SemaphoreType.DMA(s)
+    vm = lambda *s: pltpu.VMEM(s, bf)
+    sends = 2 * (na - 1 + na * (nb - 1) + na * (ny - 1) + na * (nb - 1) * (ny - 1))
+    any_space = pl.BlockSpec(memory_space=pl.ANY)
+    in_vmem = pl.BlockSpec(memory_space=pltpu.VMEM)
+    outs = pl.pallas_call(
+        functools.partial(experts_kernel, grid, pieces),
+        out_shape=[
+            jax.ShapeDtypeStruct(lay + (n,), bf),
+            jax.ShapeDtypeStruct((r, n), jnp.float32),
+            jax.ShapeDtypeStruct(lay + (n,), bf),
+            jax.ShapeDtypeStruct(lay + (ef,), bf),
+            jax.ShapeDtypeStruct(lay + (2 * ef,), bf),
+            jax.ShapeDtypeStruct(lay + (fs,), bf),
+            jax.ShapeDtypeStruct(lay + (fs,), bf),
+            jax.ShapeDtypeStruct(lay + (fs,), bf),
+        ],
+        in_specs=[any_space, any_space, in_vmem] + [any_space] * 6,
+        out_specs=[any_space, in_vmem] + [any_space] * 6,
+        scratch_shapes=[
+            vm(EXP_DEV, n, f), vm(n, 2 * ef), vm(ef, n), vm(n, fs), vm(n, fs), vm(wide_s, n),
+            vm(steps, rows, ef + wide_s),
+            vm(2, na, r, n), vm(2, na, r, n),
+            vm(2, na, r, ef), vm(2, na, r, 2 * ef),
+            vm(2, na, r, fs), vm(2, na, r, fs), vm(2, na, r, fs),
+            vm(2, na, r, n),
+            vm(nb, ny, na, r, n),
+            vm(2, na, r, n),
+            vm(nb, ny, na, r, n),
+            vm(pieces, nb, ny - 1, na, half, width),
+            vm(pieces, ny, nb - 1, na, half, width),
+            vm(pieces, nb - 1, na, half, width),
+            vm(pieces, ny - 1, na, half, width),
+            vm(pieces, na - 1, r, width),
+            pltpu.SemaphoreType.DMA, sems(EXP_DEV + 3), pltpu.SemaphoreType.DMA, sems(2), sems(2),
+            sems(2, 4), sems(2),
+            sems(sends), sems(2 * na * nb * ny), sems(2 * na * nb * ny), sems(2 * na * nb * ny),
+            sems(2), sems(nb, ny),
+            sems(pieces, nb, ny - 1), sems(pieces, nb, ny - 1),
+            sems(pieces, ny, nb - 1), sems(pieces, ny, nb - 1),
+            sems(pieces, nb - 1), sems(pieces, nb - 1),
+            sems(pieces, ny - 1), sems(pieces, ny - 1),
+            sems(pieces, na - 1), sems(pieces, na - 1),
+        ],
+        compiler_params=pltpu.CompilerParams(
+            collective_id=collective_id, has_side_effects=True, vmem_limit_bytes=63 << 20
+        ),
+    )(
+        x,
+        dz.reshape(lay + (n,)),
+        gates.reshape((EXP_DEV,) + lay + (1,)),
+        expert_gate, expert_up, expert_down, shared_gate, shared_up, shared_down,
+    )
+    tokens = grid.size * r
+    rows_all, grad, out_rows, gated, dcat, act, d_sg, d_su = outs
+    return (
+        rows_all.reshape(tokens, n),
+        grad,
+        out_rows.reshape(tokens, n),
+        gated.reshape(tokens, ef),
+        dcat.reshape(tokens, 2 * ef),
+        act.reshape(tokens, fs),
+        d_sg.reshape(tokens, fs),
+        d_su.reshape(tokens, fs),
+    )
+
+
 def rms_scale(values, gain_vec):
     return (
         values * lax.rsqrt(jnp.mean(values * values, axis=-1, keepdims=True) + epsilon) * gain_vec
@@ -539,46 +1177,25 @@
     attn_out = tensor_scatter(grid, low(dot(merged, output_weight)), 1)
     residual = quarter(hidden_f) + attn_out
     moe_in = low(rms_scale(residual, moe_gain))
-    moe_all = gather_all(grid, moe_in, 2).reshape(total_rows, model_width)
+    gates_mine = jnp.swapaxes(gates_own, 0, 1)[:, :, None]
+    moe_all, grad_moe_in, out_rows, gated, d_cat, shared_act, d_sg, d_su = experts_call(
+        grid, moe_in, cot_all, gates_mine, expert_gate, expert_up, expert_down,
+        shared_gate, shared_up, shared_down, 2,
+    )
     normed_later, _ = lax.optimization_barrier((quarter(normed), moe_all[:8]))
     normed_all = lax.all_gather(normed_later, ALL, axis=0, tiled=True)
+    moe_out = scatter_all(grid, out_rows, jnp.float32, 3)
+    layer_out = low(residual + moe_out)
+    layer_out = tensor_gather(grid, layer_out, 4)
 
     hidden_here = expert_gate.shape[2]
-    eg = jnp.einsum("td,kdf->tkf", moe_all, expert_gate, preferred_element_type=jnp.float32)
-    eu = jnp.einsum("td,kdf->tkf", moe_all, expert_up, preferred_element_type=jnp.float32)
-    active, pull_expert = jax.vjp(silu_product, eg, eu)
-    gated = low(gates_own[:, :, None] * active)
-    d_active = jnp.einsum("td,kfd->tkf", cot_all, expert_down, preferred_element_type=jnp.float32)
-    d_eg, d_eu = pull_expert(gates_own[:, :, None] * d_active)
-    d_eg, d_eu = low(d_eg), low(d_eu)
-    sg = dot(moe_all, shared_gate)
-    su = dot(moe_all, shared_up)
-    shared_act, pull_shared = jax.vjp(silu_product, sg, su)
-    shared_act = low(shared_act)
-    d_sg, d_su = pull_shared(dot(cot_all, shared_down.T))
-    d_sg, d_su = low(d_sg), low(d_su)
-
-    grad_in = jnp.einsum("tkf,kdf->td", d_eg, expert_gate, preferred_element_type=jnp.float32)
-    grad_in = grad_in + jnp.einsum(
-        "tkf,kdf->td", d_eu, expert_up, preferred_element_type=jnp.float32
-    )
-    grad_in_shared = dot(own_group(d_sg), shared_gate.T) + dot(own_group(d_su), shared_up.T)
-    grad_in = lax.dynamic_update_slice_in_dim(
-        grad_in, own_group(grad_in) + grad_in_shared, start_row, 0
-    )
-    grad_moe_in = scatter_all(grid, low(grad_in), jnp.float32, 3)
-    out_rows = jnp.einsum("tkf,kfd->td", gated, expert_down, preferred_element_type=jnp.float32)
-    out_shared = dot(own_group(shared_act), shared_down)
-    out_rows = lax.dynamic_update_slice_in_dim(
-        out_rows, own_group(out_rows) + out_shared, start_row, 0
-    )
-    moe_out = lax.psum_scatter(low(out_rows), ALL, scatter_dimension=0, tiled=True)
-    layer_out = low(residual + moe_out.astype(jnp.float32))
-    layer_out = tensor_gather(grid, layer_out, 4)
-
-    grad_expert_gate = jnp.einsum("td,tkf->kdf", moe_all, d_eg, preferred_element_type=jnp.float32)
-    grad_expert_up = jnp.einsum("td,tkf->kdf", moe_all, d_eu, preferred_element_type=jnp.float32)
-    grad_expert_down = jnp.einsum("tkf,td->kfd", gated, cot_all, preferred_element_type=jnp.float32)
+    wide = gated.shape[1] // EXP_DEV
+    part_of = lambda e, first=0: slice(first + e * wide, first + e * wide + hidden_here)
+    grad_expert_gate = jnp.stack([dot(moe_all.T, d_cat[:, part_of(e)]) for e in range(EXP_DEV)])
+    grad_expert_up = jnp.stack(
+        [dot(moe_all.T, d_cat[:, part_of(e, EXP_DEV * wide)]) for e in range(EXP_DEV)]
+    )
+    grad_expert_down = jnp.stack([dot(gated[:, part_of(e)].T, cot_all) for e in range(EXP_DEV)])
     grad_shared_gate = dot(moe_all.T, d_sg)
     grad_shared_up = dot(moe_all.T, d_su)
     grad_shared_down = dot(shared_act.T, cot_all)

time: 766 us -> 739 us (0.965)
  matrix products: 243 us -> 139 us
  Pallas kernels: 272 us -> 355 us
  waiting for transfers between devices: 99.8 us -> 82.2 us
  local copies, waits for them, and re-layouts: 38.4 us -> 52.6 us
    pallas_call x0 -> x1, Pallas kernels: none -> 154 us  [experts_call(): pl.pallas_call(functools.partial(experts_kernel, grid, pieces), out_shape...]
    dot_general x9 -> x0, matrix products: 104 us -> none  [the longest x1 16.4 us: shards(): jnp.einsum('td,kfd->tkf', cot_all, expert_down, preferred_element_type=jn...]
    reduce_scatter x1 -> x0, waiting for transfers between devices: 99.7 us -> none  [shards(): lax.psum_scatter(low(out_rows), ALL, scatter_dimension=0, tiled=True)]
    pallas_call x3 -> x2, Pallas kernels: 122 us -> 59.1 us  [gather_all(): pl.pallas_call(functools.partial(gather_kernel, grid), out_shape=jax.Shap...]
    all_gather x1, waiting for transfers between devices: 0.01 us -> 59.3 us  [shards(): grad_q_all = lax.all_gather(grad_q_low, 'expert', axis=0, tiled=True)]
    psum x1, waiting for transfers between devices: 0.01 us -> 22.9 us  [shards(): lax.psum(low(grad_expand_weight), 'expert').astype(jnp.float32)]
    pallas_call x2, Pallas kernels: 102 us -> 84.8 us  [scatter_all(): pl.pallas_call(functools.partial(scatter_kernel, grid, pieces), out_shape...]
    convert_element_type x10 -> x8, other arithmetic: 20.7 us -> 7.01 us  [low(): return values.astype(jnp.bfloat16)]
  transfers between devices with their start and end apart: 5 -> 4, of which waited for: 1 -> 2; matrix products, arithmetic and copies ran while one was open for 40% -> 28% of each run, Pallas kernels for 33% -> 49%
where the time goes in v2:
time: 739 us; the launch traced here: 729 us
  Pallas kernels  355 us (48%)
  matrix products  139 us (19%)
  waiting for transfers between devices  82.2 us (11%)
  local copies, waits for them, and re-layouts  52.6 us (7%)
  other arithmetic  43.5 us (6%)
  blocking collectives  40.8 us (6%)
  between operations  15 us (2%)
    pallas_call x1, Pallas kernels, experts_call(): pl.pallas_call(functools.partial(experts_kernel, grid, pieces), out_shape...  154 us
    dot_general x21, matrix products, dot(): return jnp.dot(left_side, right_side, preferred_element_type=jnp.float32)  118 us
    pallas_call x2, Pallas kernels, scatter_all(): pl.pallas_call(functools.partial(scatter_kernel, grid, pieces), out_shape...  84.8 us
    all_gather x1, waiting for transfers between devices, shards(): grad_q_all = lax.all_gather(grad_q_low, 'expert', axis=0, tiled=True)  59.3 us
    pallas_call x2, Pallas kernels, gather_all(): pl.pallas_call(functools.partial(gather_kernel, grid), out_shape=jax.Shap...  59.1 us
    psum x1, blocking collectives, shards(): lax.psum(jnp.concatenate([grad_attn_gain, grad_latent_gain, grad_moe_gain...  40.8 us
    unnamed x150, local copies, waits for them, and re-layouts  37.3 us
    pallas_call x3, Pallas kernels, tensor_gather(): pl.pallas_call(functools.partial(tensor_gather_kernel, grid), out_shape=j...  31.3 us
  transfers between devices with their start and end apart: 4, of which 2 were waited for; matrix products, arithmetic and copies ran while one was open for 28% of the time, Pallas kernels for 49%

profile of v2, /device:TPU:0, one launch (start us, length us, event | category | flops | bytes accessed | tf_op | source)
XLA Modules:
  0.0 728.9 jit_solution(18057898077829022023)
XLA Ops:
  7.3 1.8 constant_dynamic-slice_fusion.3
  9.2 1.5 multiply_reduce_fusion.1
  10.7 1.6 multiply_convert_fusion.2
  16.1 2.2 fusion.72
  23.0 29.3 %shard_map.289 = bf16[32,64,640]{2,1,0:T(8,128)(2,1)} custom-call(bf16[64,640]{1,0:T(8,128)(2,1)} %pad_dynamic-slice_fusion.x_ref), custom_call_target="tpu_custom_call" | custom-call | tf_op jit(solution)/shard_map/pallas_call | solution.py:151
  52.4 4.6 fusion.73
  57.1 3.7 convolution_convert_fusion
  63.0 1.6 convert_element_type.111
  64.5 2.5 fusion.71
  67.0 1.8 fusion.2
  68.8 1.5 copy-done.1
  70.3 2.2 fusion.42
  73.3 16.0 %shard_map.290 = f32[64,2048]{1,0:T(8,128)S(1)} custom-call(bf16[2,2,64,2048]{3,2,1,0:T(8,128)(2,1)S(1)} %bitcast.123), custom_call_target="tpu_custom_call" | custom-call | tf_op jit(solution)/shard_map/pallas_call | solution.py:327
  93.3 3.3 reshape_broadcast_in_dim.4.gate_ref
  96.6 2.8 copy.128.eg_hbm
  99.3 4.8 copy.129.eu_hbm
  104.1 2.8 copy.130.sg_hbm
  106.9 4.6 copy.131.su_hbm
  116.4 153.5 %shard_map.291 = (bf16[4,2,2,2,64,2048]{5,4,3,2,1,0:T(8,128)(2,1)}, f32[64,2048]{1,0:T(8,128)}, bf16[4,2,2,2,64,2048]{5,4,3,2,1,0:T(8,128)(2,1)}, bf16[4,2,2,2,6...) custom-call(bf16[64,2048]{1,0:T(8,128)(2,1)} %multiply_convert_fusio, ...), custom_call_target="tpu_custom_call" | custom-call | tf_op jit(solution)/shard_map/pallas_call | solution.py:970
  269.9 1.8 multiply_reduce_fusion.2
  273.1 10.9 %shard_map.294 = bf16[2,2,64,2048]{3,2,1,0:T(8,128)(2,1)S(1)} custom-call(bf16[64,2048]{1,0:T(8,128)(2,1)S(1)} %fusion.69.x_ref), custom_call_target="tpu_custom_call" | custom-call | tf_op jit(solution)/shard_map/pallas_call | solution.py:381
  284.0 2.3 convolution_convert_fusion.5
  286.5 5.4 multiply_reduce_fusion
  293.0 1.9 multiply_convert_fusion
  294.9 3.1 fusion.51
  298.8 1.5 fusion.48
  300.4 3.1 convolution_convert_fusion.4
  303.5 10.2 %shard_map.295 = f32[64,2048]{1,0:T(8,128)S(1)} custom-call(bf16[2,2,64,2048]{3,2,1,0:T(8,128)(2,1)S(1)} %bitcast.124), custom_call_target="tpu_custom_call" | custom-call | tf_op jit(solution)/shard_map/pallas_call | solution.py:327
  313.8 3.4 fusion.11
  317.4 1.6 fusion.12
  319.6 1.6 copy-done.3
  323.2 2.3 convolution_convert_fusion.1
  325.6 1.7 pad_maximum_fusion.4
  327.2 4.3 copy.150
  331.6 2.0 pad.27.clone
  333.6 28.1 %shard_map.296 = f32[64,640]{1,0:T(8,128)S(1)} custom-call(bf16[4,2,2,2,64,640]{5,4,3,2,1,0:T(8,128)(2,1)S(1)} %bitcast.119), custom_call_target="tpu_custom_call" | custom-call | tf_op jit(solution)/shard_map/pallas_call | solution.py:258
  361.7 3.4 copy-done
  365.1 56.7 %shard_map.292 = f32[64,2048]{1,0:T(8,128)S(1)} custom-call(bf16[4,2,2,2,64,2048]{5,4,3,2,1,0:T(8,128)(2,1)S(1)} %copy-done), custom_call_target="tpu_custom_call" | custom-call | tf_op jit(solution)/shard_map/pallas_call | solution.py:258
  426.4 10.5 %shard_map.293 = bf16[2,2,64,2048]{3,2,1,0:T(8,128)(2,1)S(1)} custom-call(bf16[64,2048]{1,0:T(8,128)(2,1)S(1)} %get-tuple-element.51.x_ref), custom_call_target="tpu_custom_call" | custom-call | tf_op jit(solution)/shard_map/pallas_call | solution.py:381
  436.9 9.9 %shard_map.297 = bf16[2,2,64,2048]{3,2,1,0:T(8,128)(2,1)S(1)} custom-call(bf16[64,2048]{1,0:T(8,128)(2,1)S(1)} %get-tuple-element.50.x_ref), custom_call_target="tpu_custom_call" | custom-call | tf_op jit(solution)/shard_map/pallas_call | solution.py:381
  446.8 40.8 %psum.21 = f32[4608]{0:T(1024)S(1)} all-reduce(f32[4608]{0:T(1024)S(1)} %pad_maximum_fusion.10), channel_id=1, replica_groups=mesh['expert'=8,'tensor'=4] {'expert','tensor'}, use_global_device_ids=true, to_apply=%region_17.18 | all-reduce | flops 4608 | bytes 36864 | tf_op jit(solution)/shard_map/psum | solution.py:1262
  490.8 2.0 convolution_convert_fusion.2
  492.8 6.2 fusion.36
  499.0 8.7 %convolution_bitcast_fusion.6 = f32[1,2048,352]{1,2,0:T(8,128)} fusion(bf16[2048,2048]{1,0:T(8,128)(2,1)} %bitcast.153, bf16[2048,1536]{1,0:T(8,128)(2,1)} %bitcast.161), kind=kOutput, calls=%fused_computation.28 | convolution fusion | flops 2952790016 | bytes 12845056 | tf_op jit(solution)/shard_map/dot_general | solution.py:1081
  508.0 1.6 bitcast_convert_fusion
  509.6 10.0 %convolution_bitcast_fusion.7 = f32[1,2048,352]{1,2,0:T(8,128)} fusion(bf16[2048,2048]{1,0:T(8,128)(2,1)} %bitcast.154, bf16[2048,1536]{1,0:T(8,128)(2,1)} %bitcast.162), kind=kOutput, calls=%fused_computation.29 | convolution fusion | flops 2952790016 | bytes 12845056 | tf_op jit(solution)/shard_map/dot_general | solution.py:1081
  519.6 4.8 convolution_bitcast_fusion.4
  524.4 4.8 convolution_bitcast_fusion.5
  529.9 29.8 %shard_map.298 = bf16[32,64,640]{2,1,0:T(8,128)(2,1)} custom-call(bf16[64,640]{1,0:T(8,128)(2,1)} %pad.30.x_ref), custom_call_target="tpu_custom_call" | custom-call | tf_op jit(solution)/shard_map/pallas_call | solution.py:151
  559.7 6.7 convolution_bitcast_fusion.2
  566.4 5.8 convolution_bitcast_fusion.3
  572.3 3.3 pad_maximum_fusion.2
  575.6 1.4 copy-done.16
  577.1 6.1 pad_maximum_fusion
  583.1 1.5 copy-done.56
  584.6 8.2 %fusion.75 = f32[704,2048]{1,0:T(8,128)} fusion(bf16[2048,704]{1,0:T(8,128)(2,1)S(1)} %bitcast.167, bf16[2048,2048]{1,0:T(8,128)(2,1)S(1)} %bitcast.136), kind=kOutput, calls=%fused_computation.156 | convolution fusion | flops 5905580032 | bytes 17039360 | tf_op jit(solution)/shard_map/dot_general | solution.py:1081
  592.8 9.9 %fusion.15 = f32[2048,576]{0,1:T(8,128)} fusion(bf16[2048,2048]{1,0:T(8,128)(2,1)} %all-gather.6.cloned.1.call-done, bf16[2048,640]{1,0:T(8,128)(2,1)} %bitcast.146), kind=kOutput, calls=%fused_computation.32 | convolution fusion | flops 4831838208 | bytes 15728640 | tf_op jit(solution)/shard_map/dot_general | solution.py:1081
  602.7 10.5 %convolution_bitcast_fusion.1 = f32[2048,704]{0,1:T(8,128)} fusion(bf16[4,2,2,2,64,2048]{5,4,3,2,1,0:T(8,128)(2,1)} %get-tuple-element.25, bf16[4,2,2,2,64,704]{5,4,3,2,1,0:T(8,128)(2,1)S(1)} %copy-done.55), kind=kOutput, calls=%fused_computation.20 | convolution fusion | flops 5905580032 | bytes 17039360 | tf_op jit(solution)/shard_map/dot_general | solution.py:1081
  613.3 8.4 %convolution_bitcast_fusion = f32[2048,704]{0,1:T(8,128)} fusion(bf16[4,2,2,2,64,2048]{5,4,3,2,1,0:T(8,128)(2,1)S(1)} %bitcast.160, bf16[4,2,2,2,64,704]{5,4,3,2,1,0:T(8,128)(2,1)S(1)} %copy-done.54), kind=kOutput, calls=%fused_computation.19 | convolution fusion | flops 5905580032 | bytes 17039360 | tf_op jit(solution)/shard_map/dot_general | solution.py:1081
  621.7 22.9 %all-reduce.10.cloned.1.call-done = (bf16[512,1024]{1,0:T(8,128)(2,1)}, bf16[512,2048]{1,0:T(8,128)(2,1)}) async-done(((bf16[512,1024]{1,0:T(8,128)(2,1)}, bf16[512,2048]{1,0:T(8,128)(2,1)}), (bf16[512,1024]{1,0:T(8,128)(2,1)}, bf16[512,2048]{1,0:T(8,128)(2,1)})) %all-reduce.10.cloned.1.call-update) | async-done | bytes 3145744 | tf_op jit(solution)/shard_map/psum | solution.py:1264
  644.6 2.9 convert_element_type.140
  647.5 2.5 convert_element_type.142
  650.1 59.3 %all-gather.8.cloned.1.call-done = bf16[2048,768]{0,1:T(8,128)(2,1)} async-done(((bf16[256,768]{0,1:T(8,128)(2,1)}), bf16[2048,768]{0,1:T(8,128)(2,1)}) %all-gather.8.cloned.1.call-update) | async-done | bytes 3145744 | tf_op jit(solution)/shard_map/all_gather | solution.py:1243
  709.3 11.8 %fusion.74 = f32[2048,768]{1,0:T(8,128)} fusion(bf16[2048,2048]{1,0:T(8,128)(2,1)} %all-gather.6.cloned.1.call-done, bf16[2048,768]{0,1:T(8,128)(2,1)} %all-gather.8.cloned.1.call-done), kind=kOutput, calls=%fused_computation.155 | convolution fusion | flops 6442450944 | bytes 17825792 | tf_op jit(solution)/shard_map/dot_general | solution.py:1081
  (217 shorter events, 36.3 us)
Async XLA Ops:
  7.2 7.4 %copy-start.43 = (f32[256,6]{0,1:T(8,128)S(1)}, f32[256,6]{0,1:T(8,128)}, u32[]{:S(2)}) copy-start(f32[256,6]{0,1:T(8,128)} %param.32) | copy-start | bytes 18436
  7.2 7.4 %copy-start.44 = (s32[256,6]{0,1:T(8,128)S(1)}, s32[256,6]{0,1:T(8,128)}, u32[]{:S(2)}) copy-start(s32[256,6]{0,1:T(8,128)} %param.33) | copy-start | bytes 18436
  7.2 8.9 %copy-start.19 = (bf16[2048,576]{0,1:T(8,128)(2,1)S(1)}, bf16[2048,576]{0,1:T(8,128)(2,1)}, u32[]{:S(2)}) copy-start(bf16[2048,576]{0,1:T(8,128)(2,1)} %param.21) | copy-start | bytes 7077892
  7.2 109.2 %all-gather.4.cloned.1.call-start = ((), (), s32[]{:S(2)}) async-start(), calls=%async_computation | async-start | bytes 8650752 | tf_op jit(solution)/shard_map/all_gather | solution.py:1137
  9.1 583.7 %all-gather.6.cloned.1.call-start = ((), (), s32[]{:S(2)}) async-start(), calls=%async_computation.1 | async-start | bytes 8650752 | tf_op jit(solution)/shard_map/all_gather | solution.py:1186
  10.7 7.8 %copy-start.34 = (s32[2048]{0:T(1024)S(1)}, s32[2048]{0:T(1024)}, u32[]{:S(2)}) copy-start(s32[2048]{0:T(1024)} %param.34) | copy-start | bytes 24580
  10.7 9.3 %copy-start.39 = (f32[512]{0:T(512)S(1)}, f32[512]{0:T(512)}, u32[]{:S(2)}) copy-start(f32[512]{0:T(512)} %param.22) | copy-start | bytes 6148
  14.0 630.6 %all-reduce.10.cloned.1.call-start = ((), (), s32[]{:S(2)}) async-start(), calls=%async_computation.3 | async-start | bytes 6291456 | tf_op jit(solution)/shard_map/psum | solution.py:1264
  18.4 4.6 copy-start.10
  52.4 4.7 copy-start.5
  57.0 5.9 copy-start.31
  57.1 3.7 copy-start.11
  60.8 8.0 %copy-start.6 = (bf16[2048,1024]{0,1:T(8,128)(2,1)}, bf16[2048,1024]{0,1:T(8,128)(2,1)S(1)}, u32[]{:S(2)}) copy-start(bf16[2048,1024]{0,1:T(8,128)(2,1)S(1)} %convolution_convert_fusion) | copy-start | bytes 12582916
  63.0 4.0 copy-start.27
  63.0 4.0 copy-start.29
  67.0 3.3 copy-start.1
  70.3 2.2 copy-start.22
  90.6 6.0 copy-start.13
  99.3 4.8 copy-start.14
  106.9 8.7 %copy-start.35 = (f32[2048]{0:T(1024)S(1)}, f32[2048]{0:T(1024)}, u32[]{:S(2)}) copy-start(f32[2048]{0:T(1024)} %param.25) | copy-start | bytes 24580
  112.5 157.4 %copy-start.51 = (f32[64]{0:T(128)}, f32[64]{0:T(128)S(1)}, u32[]{:S(2)}) copy-start(f32[64]{0:T(128)S(1)} %multiply_reduce_fusion.11) | copy-start | bytes 772
  115.0 156.7 %copy-start.46 = (f32[64]{0:T(128)}, f32[64]{0:T(128)S(1)}, u32[]{:S(2)}) copy-start(f32[64]{0:T(128)S(1)} %get-tuple-element.45) | copy-start | bytes 772
  115.0 156.7 %copy-start.41 = (f32[64]{0:T(128)}, f32[64]{0:T(128)S(1)}, u32[]{:S(2)}) copy-start(f32[64]{0:T(128)S(1)} %fusion.64) | copy-start | bytes 772
  286.5 5.5 slice-start
  286.5 6.5 slice-start.1
  294.9 5.4 copy-start.2
  294.9 3.1 copy-start.32
  294.9 3.9 copy-start.7
  300.4 16.8 %copy-start.24 = (bf16[256,4,192]{0,2,1:T(8,128)(2,1)}, bf16[256,4,192]{0,2,1:T(8,128)(2,1)S(1)}, u32[]{:S(2)}) copy-start(bf16[256,4,192]{0,2,1:T(8,128)(2,1)S(1)} %pad_maximum_fusion.5) | copy-start | bytes 1179652
  300.4 16.8 %slice-start.2 = ((s8[8388608]{0:T(1024)(128)(4,1)}), s8[4194304]{0:T(1024)(128)(4,1)S(1)}, s32[]{:S(2)}) async-start(s8[8388608]{0:T(1024)(128)(4,1)} %bitcast.127), calls=%async_computation.6 | async-start | bytes 8388608
  313.8 3.6 slice-start.3
  321.2 4.3 copy-start.12
  361.7 3.4 copy-start
  365.1 56.7 %copy-start.49 = (f32[32]{0:T(128)S(1)}, f32[32]{0:T(128)}, u32[]{:S(2)}) copy-start(f32[32]{0:T(128)} %multiply_power_fusion) | copy-start | bytes 388
  365.1 56.7 %copy-start.53 = (f32[64]{0:T(128)S(1)}, f32[64]{0:T(128)}, u32[]{:S(2)}) copy-start(f32[64]{0:T(128)} %dynamic-slice_convert_fusion.1) | copy-start | bytes 772
  365.1 57.1 %copy-start.48 = (f32[64]{0:T(128)S(1)}, f32[64]{0:T(128)}, u32[]{:S(2)}) copy-start(f32[64]{0:T(128)} %fusion.65) | copy-start | bytes 772
  365.1 58.2 %copy-start.52 = (f32[64]{0:T(128)S(1)}, f32[64]{0:T(128)}, u32[]{:S(2)}) copy-start(f32[64]{0:T(128)} %copy-done.51) | copy-start | bytes 772
  365.1 59.2 %copy-start.8 = (f32[256,2048]{1,0:T(8,128)S(1)}, f32[256,2048]{1,0:T(8,128)}, u32[]{:S(2)}) copy-start(f32[256,2048]{1,0:T(8,128)} %convert_element_type.111) | copy-start | bytes 6291460
  365.1 59.2 %copy-start.20 = (bf16[2048,576]{0,1:T(8,128)(2,1)S(1)}, bf16[2048,576]{0,1:T(8,128)(2,1)}, u32[]{:S(2)}) copy-start(bf16[2048,576]{0,1:T(8,128)(2,1)} %param.21) | copy-start | bytes 7077892
  365.1 59.2 %copy-start.37 = (f32[2048]{0:T(1024)S(1)}, f32[2048]{0:T(1024)}, u32[]{:S(2)}) copy-start(f32[2048]{0:T(1024)} %param.19) | copy-start | bytes 24580
  421.8 3.2 copy-start.47
  421.8 3.3 copy-start.9
  421.8 3.3 copy-start.42
  422.1 14.7 %copy-start.33 = (bf16[64,64]{1,0:T(8,128)(2,1)}, bf16[64,64]{1,0:T(8,128)(2,1)S(1)}, u32[]{:S(2)}) copy-start(bf16[64,64]{1,0:T(8,128)(2,1)S(1)} %add_convert_fusion.4) | copy-start | bytes 24580
  424.3 22.5 %copy-start.38 = (f32[2048]{0:T(1024)S(1)}, f32[2048]{0:T(1024)}, u32[]{:S(2)}) copy-start(f32[2048]{0:T(1024)} %get-tuple-element.33) | copy-start | bytes 24580
  424.3 66.5 %copy-start.26 = (bf16[4,128,256]{2,1,0:T(8,128)(2,1)S(1)}, bf16[4,128,256]{2,1,0:T(8,128)(2,1)}, u32[]{:S(2)}) copy-start(bf16[4,128,256]{2,1,0:T(8,128)(2,1)} %copy-done.25) | copy-start | bytes 786436
  507.7 201.6 %all-gather.8.cloned.1.call-start = ((), (), s32[]{:S(2)}) async-start(), calls=%async_computation.2 | async-start | bytes 3538944 | tf_op jit(solution)/shard_map/all_gather | solution.py:1243
  508.0 11.6 %slice-start.6 = ((s8[8388608]{0:T(1024)(128)(4,1)}), s8[4194304]{0:T(1024)(128)(4,1)S(1)}, s32[]{:S(2)}) async-start(s8[8388608]{0:T(1024)(128)(4,1)} %bitcast.155), calls=%async_computation.10 | async-start | bytes 8388608
  508.0 11.6 %slice-start.10 = ((s8[6291456]{0:T(1024)(128)(4,1)}), s8[4194304]{0:T(1024)(128)(4,1)S(1)}, s32[]{:S(2)}) async-start(s8[6291456]{0:T(1024)(128)(4,1)} %bitcast.163), calls=%async_computation.14 | async-start | bytes 8388608
  509.6 10.0 %slice-start.7 = ((s8[8388608]{0:T(1024)(128)(4,1)}), s8[4194304]{0:T(1024)(128)(4,1)S(1)}, s32[]{:S(2)}) async-start(s8[8388608]{0:T(1024)(128)(4,1)} %bitcast.155), calls=%async_computation.11 | async-start | bytes 8388608
  509.6 10.0 %slice-start.11 = ((s8[6291456]{0:T(1024)(128)(4,1)}), s8[2097152]{0:T(1024)(128)(4,1)S(1)}, s32[]{:S(2)}) async-start(s8[6291456]{0:T(1024)(128)(4,1)} %bitcast.163), calls=%async_computation.15 | async-start | bytes 4194304
  559.7 6.7 copy-start.57
  566.4 9.2 %copy-start.17 = (f32[1,2048,352]{1,2,0:T(8,128)S(1)}, f32[1,2048,352]{1,2,0:T(8,128)}, u32[]{:S(2)}) copy-start(f32[1,2048,352]{1,2,0:T(8,128)} %convolution_bitcast_fusion.4) | copy-start | bytes 8650756
  566.4 9.2 %copy-start.18 = (f32[1,2048,352]{1,2,0:T(8,128)S(1)}, f32[1,2048,352]{1,2,0:T(8,128)}, u32[]{:S(2)}) copy-start(f32[1,2048,352]{1,2,0:T(8,128)} %convolution_bitcast_fusion.5) | copy-start | bytes 8650756
  572.2 3.4 copy-start.15
  572.3 4.8 copy-start.16
  572.3 10.9 %slice-start.4 = ((s8[8388608]{0:T(1024)(128)(4,1)}), s8[4194304]{0:T(1024)(128)(4,1)S(1)}, s32[]{:S(2)}) async-start(s8[8388608]{0:T(1024)(128)(4,1)} %bitcast.135), calls=%async_computation.8 | async-start | bytes 8388608
  577.0 6.1 slice-start.5
  577.0 7.6 %copy-start.56 = (bf16[4,2,2,2,64,704]{5,4,3,2,1,0:T(8,128)(2,1)S(1)}, bf16[4,2,2,2,64,704]{5,4,3,2,1,0:T(8,128)(2,1)}, u32[]{:S(2)}) copy-start(bf16[4,2,2,2,64,704]{5,4,3,2,1,0:T(8,128)(2,1)} %get-tuple-element.28) | copy-start | bytes 8650756
  592.8 9.9 %copy-start.55 = (bf16[4,2,2,2,64,704]{5,4,3,2,1,0:T(8,128)(2,1)S(1)}, bf16[4,2,2,2,64,704]{5,4,3,2,1,0:T(8,128)(2,1)}, u32[]{:S(2)}) copy-start(bf16[4,2,2,2,64,704]{5,4,3,2,1,0:T(8,128)(2,1)} %get-tuple-element.26) | copy-start | bytes 8650756
  592.8 20.5 %slice-start.8 = ((s8[8388608]{0:T(1024)(128)(4,1)}), s8[4194304]{0:T(1024)(128)(4,1)S(1)}, s32[]{:S(2)}) async-start(s8[8388608]{0:T(1024)(128)(4,1)} %bitcast.159), calls=%async_computation.12 | async-start | bytes 8388608
  602.7 10.6 %slice-start.9 = ((s8[8388608]{0:T(1024)(128)(4,1)}), s8[4194304]{0:T(1024)(128)(4,1)S(1)}, s32[]{:S(2)}) async-start(s8[8388608]{0:T(1024)(128)(4,1)} %bitcast.159), calls=%async_computation.13 | async-start | bytes 8388608
  602.7 10.6 %copy-start.54 = (bf16[4,2,2,2,64,704]{5,4,3,2,1,0:T(8,128)(2,1)S(1)}, bf16[4,2,2,2,64,704]{5,4,3,2,1,0:T(8,128)(2,1)}, u32[]{:S(2)}) copy-start(bf16[4,2,2,2,64,704]{5,4,3,2,1,0:T(8,128)(2,1)} %get-tuple-element.27) | copy-start | bytes 8650756
  644.6 2.9 copy-start.21
  (11 other events, 16.4 us)
Sparse Core Ops, SparseCore 0:
  11.5 89.3 all-gather.3
  103.8 96.4 all-gather.5
  507.8 136.7 all-reduce.9
  647.3 62.0 all-gather.7

commit v3 on v2

--- a/solution.py
+++ b/solution.py
@@ -1,4 +1,5 @@
 import functools
+import math
 from functools import partial
 
 import jax
@@ -57,7 +58,9 @@
     pl.semaphore_wait(barrier, len(others))
 
 
-def gather_kernel(grid, x_ref, out_ref, own_sem, send_sem, recv_sem, core_send, core_recv):
+def gather_kernel(
+    grid, x_ref, out_ref, own_sem, send_sem, recv_sem, core_send, core_recv, extra=()
+):
     na, nb, ny = grid.na, grid.nb, grid.ny
     a, b, y, c = grid.here()
     half = x_ref.shape[0] // 2
@@ -110,6 +113,8 @@
     orders = (("b", "y"), ("y", "b"))
     for h in range(2):
         onward(x_ref.at[pl.ds(h * half, half)], b, y, a, h, ("a",) + orders[h])
+    for one in extra:
+        one.start()
     for i in range(1, na):
         aa = wrap(a + na - i, na)
         for h in range(2):
@@ -134,6 +139,9 @@
                     if h == 1:
                         bb, yy = wrap(b + nb - k, nb), wrap(y + ny - j, ny)
                         onward(landed(bb, yy, c, aa, h, recv_sem), bb, yy, aa, h, ())
+    for i in range(1, na):
+        for one in extra:
+            one.middle(i)
     for j in range(nb):
         for k in range(ny):
             for i in range(na):
@@ -142,12 +150,18 @@
     own.wait()
     for copy in waits + core_waits:
         copy.wait_send()
+    for one in extra:
+        one.last()
+
+
+def gather_sends(grid):
+    na, nb, ny = grid.na, grid.nb, grid.ny
+    return 2 * (na - 1 + na * (nb - 1) + na * (ny - 1) + na * (nb - 1) * (ny - 1))
 
 
 def gather_all(grid, x, collective_id):
     r, n = x.shape
     blocks = grid.na * grid.nb * grid.ny
-    sends = 2 * (grid.na - 1 + grid.na * (grid.nb - 1) + grid.na * (grid.ny - 1)) + 2 * grid.na * ((grid.nb - 1) * (grid.ny - 1))
     return pl.pallas_call(
         functools.partial(gather_kernel, grid),
         out_shape=jax.ShapeDtypeStruct((grid.size, r, n), x.dtype),
@@ -155,7 +169,7 @@
         out_specs=pl.BlockSpec(memory_space=pl.ANY),
         scratch_shapes=[
             pltpu.SemaphoreType.DMA,
-            pltpu.SemaphoreType.DMA((sends,)),
+            pltpu.SemaphoreType.DMA((gather_sends(grid),)),
             pltpu.SemaphoreType.DMA((2 * blocks,)),
             pltpu.SemaphoreType.DMA((2 * blocks,)),
             pltpu.SemaphoreType.DMA((2 * blocks,)),
@@ -420,16 +434,11 @@
     all_ref,
     grad_ref,
     y_ref,
-    gated_ref,
-    dcat_ref,
-    act_ref,
-    dsg_ref,
-    dsu_ref,
-    raw,
+    acts_ref,
+    gates,
     egu,
     ed,
-    sg,
-    su,
+    sgu,
     sd,
     dabuf,
     xbuf,
@@ -437,8 +446,7 @@
     gated,
     dcat,
     act,
-    dsg,
-    dsu,
+    dsh,
     ybuf,
     dx,
     dx_out,
@@ -448,7 +456,7 @@
     d2_in0,
     d2_in1,
     a_in,
-    raw_sem,
+    gate_sem,
     weight_sem,
     own_sem,
     x_sem,
@@ -479,25 +487,24 @@
     pairs = nb * ny
     steps = 2 * pairs
     device = a * nb + b
-    f, fs = eg_hbm.shape[2], sg_hbm.shape[1]
-    wide = egu.shape[1] // (2 * EXP_DEV)
+    f, fs = ed_hbm.shape[1], sd_hbm.shape[0]
+    wide, wide_s = egu.shape[0] // (2 * EXP_DEV), sd.shape[0]
     ef = EXP_DEV * wide
+    columns = columns_of(ef, wide_s)
     f32, bf = jnp.float32, jnp.bfloat16
-
-    def raw_load(src):
-        return pltpu.make_async_copy(src, raw, raw_sem)
-
+    fills = [(ed_hbm.at[e], ed, e * wide, f, wide) for e in range(EXP_DEV)]
+    fills += [(sd_hbm, sd, 0, fs, wide_s)]
+    fills += [(eg_hbm.at[e], egu, e * wide, f, wide) for e in range(EXP_DEV)]
+    fills += [(eu_hbm.at[e], egu, ef + e * wide, f, wide) for e in range(EXP_DEV)]
+    fills += [(sg_hbm, sgu, 0, fs, wide_s), (su_hbm, sgu, wide_s, fs, wide_s)]
     loads = [
-        pltpu.make_async_copy(ed_hbm.at[e], ed.at[pl.ds(e * wide, f)], weight_sem.at[e])
-        for e in range(EXP_DEV)
-    ]
-    loads += [
-        pltpu.make_async_copy(src, dst, weight_sem.at[EXP_DEV + i])
-        for i, (src, dst) in enumerate(((sd_hbm, sd.at[pl.ds(0, fs)]), (sg_hbm, sg), (su_hbm, su)))
+        pltpu.make_async_copy(src, dst.at[pl.ds(at, real)], weight_sem.at[i])
+        for i, (src, dst, at, real, _) in enumerate(fills)
     ]
     for load in loads:
         load.start()
-    raw_load(eg_hbm).start()
+    gate_load = pltpu.make_async_copy(gate_ref.at[:, :, :, :, :, pl.ds(LATENT, 128)], gates, gate_sem)
+    gate_load.start()
     greet(grid)
 
     counts = [0]
@@ -603,10 +610,9 @@
         return pltpu.make_async_copy(dz_ref.at[:, bb, yy, cc], dzbuf.at[s], dz_sem.at[s])
 
     dz_load(a * 0).start()
-    for e in range(EXP_DEV):
-        ed[e * wide + f : (e + 1) * wide] = jnp.zeros((wide - f, n), bf)
-    if sd.shape[0] > fs:
-        sd[fs:] = jnp.zeros((sd.shape[0] - fs, n), bf)
+    for _, dst, at, real, padded in fills:
+        if padded > real:
+            dst[at + real : at + padded] = jnp.zeros((padded - real, n), bf)
     for load in loads[: EXP_DEV + 1]:
         load.wait()
 
@@ -626,18 +632,10 @@
         return carry
 
     lax.fori_loop(0, steps, early_body, 0)
-    for part, src in enumerate((eg_hbm, eu_hbm)):
-        raw_load(src).wait()
-        for e in range(EXP_DEV):
-            at = part * ef + e * wide
-            if wide > f:
-                egu[:, at + wide - 128 : at + wide] = jnp.zeros((n, 128), bf)
-            egu[:, at : at + f] = raw[e]
-        if part == 0:
-            raw_load(eu_hbm).start()
     for load in loads[EXP_DEV + 1 :]:
         load.wait()
     own.wait()
+    gate_load.wait()
 
     def x_load(step):
         _, _, _, bb, yy, cc = spots(step)
@@ -647,8 +645,12 @@
         _, _, _, bb, yy, cc = spots(step)
         s = lax.rem(step, 2)
         return [
-            pltpu.make_async_copy(gated.at[s], gated_ref.at[:, bb, yy, cc], out_sem.at[s, 0]),
-            pltpu.make_async_copy(dcat.at[s], dcat_ref.at[:, bb, yy, cc], out_sem.at[s, 1]),
+            pltpu.make_async_copy(
+                gated.at[s], acts_ref.at[:, bb, yy, cc, :, pl.ds(columns[2], ef)], out_sem.at[s, 0]
+            ),
+            pltpu.make_async_copy(
+                dcat.at[s], acts_ref.at[:, bb, yy, cc, :, pl.ds(columns[0], 2 * ef)], out_sem.at[s, 1]
+            ),
         ]
 
     def remote(src, dst, ss, rs, where):
@@ -687,14 +689,14 @@
         dst[...] = (dst[...].astype(f32) + src[...].astype(f32)).astype(dst.dtype)
 
     def shared_front(step, x, s):
-        g = dot_plain(x, sg[...])
-        u = dot_plain(x, su[...])
-        d = dabuf[step, :, ef : ef + fs].astype(f32)
+        g = dot_rows(x, sgu[:wide_s])
+        u = dot_rows(x, sgu[wide_s:])
+        d = dabuf[step, :, ef:].astype(f32)
         sig = 1.0 / (1.0 + jnp.exp(-g))
         swish = g * sig
         act[s] = fold((swish * u).astype(bf))
-        dsg[s] = fold((d * u * (sig + swish * (1.0 - sig))).astype(bf))
-        dsu[s] = fold((d * swish).astype(bf))
+        dsh[s, :, :, :wide_s] = fold((d * u * (sig + swish * (1.0 - sig))).astype(bf))
+        dsh[s, :, :, wide_s:] = fold((d * swish).astype(bf))
 
     def is_mine(bb, yy, cc):
         return lax.rem((bb * ny + yy) * 2 + cc, na * nb) == device
@@ -720,11 +722,15 @@
 
         x_load(step).wait()
         x = flat(xbuf[0])
-        g = dot_plain(x, egu[:, :ef])
-        u = dot_plain(x, egu[:, ef:])
+        g = dot_rows(x, egu[:ef])
+        u = dot_rows(x, egu[ef:])
+        gate = flat(gates[:, bb, yy, cc]).astype(f32)
+        lane = lax.broadcasted_iota(jnp.int32, gate.shape, 1) - (ROPE + EXP_DEV * device)
+        experts_all = EXP_DEV * na * nb
         for e in range(EXP_DEV):
             at = pl.ds(e * wide, wide)
-            scale = flat(gate_ref[e, :, bb, yy, cc])
+            hit = (lane == e) | (lane == e + experts_all)
+            scale = jnp.sum(jnp.where(hit, gate, 0.0), axis=-1, keepdims=True)
             ge, ue = g[:, e * wide : (e + 1) * wide], u[:, e * wide : (e + 1) * wide]
             d = dabuf[step, :, at].astype(f32) * scale
             sig = 1.0 / (1.0 + jnp.exp(-ge))
@@ -744,14 +750,14 @@
         def column(target):
             for q in range(n // chunk):
                 at = pl.ds(q * chunk, chunk)
-                total = dot_rows(flat(dcat[s]), egu[at])
+                total = dot_plain(flat(dcat[s]), egu[:, at])
                 target[:, :, at] = fold(total.astype(bf))
 
             @pl.when(mine)
             def _():
                 for q in range(n // chunk):
                     at = pl.ds(q * chunk, chunk)
-                    more = dot_rows(flat(dsg[0]), sg[at]) + dot_rows(flat(dsu[0]), su[at])
+                    more = dot_plain(flat(dsh[0]), sgu[:, at])
                     target[:, :, at] = fold((flat(target[:, :, at]).astype(f32) + more).astype(bf))
 
         for store in stores(step):
@@ -860,16 +866,17 @@
         s = lax.rem(step, 2)
         return [
             pltpu.make_async_copy(all_ref.at[:, bb, yy, cc], xbuf.at[s], x_sem.at[s]),
-            pltpu.make_async_copy(gated_ref.at[:, bb, yy, cc], gated.at[s], fill_sem.at[s]),
+            pltpu.make_async_copy(
+                acts_ref.at[:, bb, yy, cc, :, pl.ds(columns[2], ef)], gated.at[s], fill_sem.at[s]
+            ),
         ]
 
     def fill_stores(step):
         _, _, _, bb, yy, cc = spots(step)
         s = lax.rem(step, 2)
         pairs_of = [
-            (act.at[s], act_ref.at[:, bb, yy, cc]),
-            (dsg.at[s], dsg_ref.at[:, bb, yy, cc]),
-            (dsu.at[s], dsu_ref.at[:, bb, yy, cc]),
+            (act.at[s], acts_ref.at[:, bb, yy, cc, :, pl.ds(columns[3], wide_s)]),
+            (dsh.at[s], acts_ref.at[:, bb, yy, cc, :, pl.ds(columns[1], 2 * wide_s)]),
             (ybuf.at[s], y_ref.at[:, bb, yy, cc]),
         ]
         return [
@@ -906,7 +913,7 @@
         def _():
             for q in range(n // chunk):
                 at = pl.ds(q * chunk, chunk)
-                more = dot_plain(flat(act[s]), sd[:fs, at])
+                more = dot_plain(flat(act[s]), sd[:, at])
                 ybuf[s, :, :, at] = fold((flat(ybuf[s, :, :, at]).astype(f32) + more).astype(bf))
 
         for store in fill_stores(step):
@@ -949,13 +956,17 @@
             send_a(p, i).wait_send()
 
 
+def columns_of(ef, wide_s):
+    return (0, 2 * ef, 2 * ef + 2 * wide_s, 3 * ef + 2 * wide_s, 3 * ef + 3 * wide_s)
+
+
 def experts_call(
     grid, x, dz, gates, expert_gate, expert_up, expert_down, shared_gate, shared_up, shared_down,
     collective_id, pieces=2,
 ):
     r, n = x.shape
     na, nb, ny = grid.na, grid.nb, grid.ny
-    f, fs = expert_gate.shape[2], shared_gate.shape[1]
+    f, fs = expert_down.shape[1], shared_down.shape[0]
     wide, wide_s = round_up(f, 128), round_up(fs, 128)
     ef = EXP_DEV * wide
     half, width, rows = r // 2, n // pieces, na * r
@@ -973,20 +984,16 @@
             jax.ShapeDtypeStruct(lay + (n,), bf),
             jax.ShapeDtypeStruct((r, n), jnp.float32),
             jax.ShapeDtypeStruct(lay + (n,), bf),
-            jax.ShapeDtypeStruct(lay + (ef,), bf),
-            jax.ShapeDtypeStruct(lay + (2 * ef,), bf),
-            jax.ShapeDtypeStruct(lay + (fs,), bf),
-            jax.ShapeDtypeStruct(lay + (fs,), bf),
-            jax.ShapeDtypeStruct(lay + (fs,), bf),
+            jax.ShapeDtypeStruct(lay + (columns_of(ef, wide_s)[-1],), bf),
         ],
-        in_specs=[any_space, any_space, in_vmem] + [any_space] * 6,
-        out_specs=[any_space, in_vmem] + [any_space] * 6,
+        in_specs=[any_space] * 9,
+        out_specs=[any_space, in_vmem] + [any_space] * 2,
         scratch_shapes=[
-            vm(EXP_DEV, n, f), vm(n, 2 * ef), vm(ef, n), vm(n, fs), vm(n, fs), vm(wide_s, n),
+            vm(*lay, 128), vm(2 * ef, n), vm(ef, n), vm(2 * wide_s, n), vm(wide_s, n),
             vm(steps, rows, ef + wide_s),
             vm(2, na, r, n), vm(2, na, r, n),
             vm(2, na, r, ef), vm(2, na, r, 2 * ef),
-            vm(2, na, r, fs), vm(2, na, r, fs), vm(2, na, r, fs),
+            vm(2, na, r, wide_s), vm(2, na, r, 2 * wide_s),
             vm(2, na, r, n),
             vm(nb, ny, na, r, n),
             vm(2, na, r, n),
@@ -996,7 +1003,7 @@
             vm(pieces, nb - 1, na, half, width),
             vm(pieces, ny - 1, na, half, width),
             vm(pieces, na - 1, r, width),
-            pltpu.SemaphoreType.DMA, sems(EXP_DEV + 3), pltpu.SemaphoreType.DMA, sems(2), sems(2),
+            pltpu.SemaphoreType.DMA, sems(3 * EXP_DEV + 3), pltpu.SemaphoreType.DMA, sems(2), sems(2),
             sems(2, 4), sems(2),
             sems(sends), sems(2 * na * nb * ny), sems(2 * na * nb * ny), sems(2 * na * nb * ny),
             sems(2), sems(nb, ny),
@@ -1012,21 +1019,643 @@
     )(
         x,
         dz.reshape(lay + (n,)),
-        gates.reshape((EXP_DEV,) + lay + (1,)),
-        expert_gate, expert_up, expert_down, shared_gate, shared_up, shared_down,
+        gates.reshape(lay + (gates.shape[-1],)),
+        jnp.swapaxes(expert_gate, 1, 2), jnp.swapaxes(expert_up, 1, 2), expert_down,
+        shared_gate.T, shared_up.T, shared_down,
     )
     tokens = grid.size * r
-    rows_all, grad, out_rows, gated, dcat, act, d_sg, d_su = outs
-    return (
-        rows_all.reshape(tokens, n),
-        grad,
-        out_rows.reshape(tokens, n),
-        gated.reshape(tokens, ef),
-        dcat.reshape(tokens, 2 * ef),
-        act.reshape(tokens, fs),
-        d_sg.reshape(tokens, fs),
-        d_su.reshape(tokens, fs),
-    )
+    rows_all, grad, out_rows, acts = outs
+    return rows_all.reshape(tokens, n), grad, out_rows.reshape(tokens, n), acts.reshape(tokens, -1)
+
+
+class TensorReduce:
+    count = 8
+
+    @staticmethod
+    def scratch(grid, r, width):
+        ny = grid.ny
+        sems = lambda *s: pltpu.SemaphoreType.DMA(s)
+        vm = lambda *s: pltpu.VMEM(s, jnp.bfloat16)
+        return [
+            vm(ny, r, width), vm(ny, r, width), vm(ny - 1, r, width),
+            sems(ny), sems(ny), sems(ny), sems(ny - 1), sems(ny - 1),
+        ]
+
+    def __init__(self, grid, source, out, scratch):
+        self.grid, self.source, self.out = grid, source, out
+        (
+            self.acc, self.core_in, self.y_in, self.load_sem, self.core_s, self.core_r, self.ys, self.yr,
+        ) = scratch
+        self.spot = grid.here()
+
+    def load(self, k):
+        g, (a, b, y, c) = self.grid, self.spot
+        return pltpu.make_async_copy(self.source.at[wrap(y + k, g.ny), c], self.acc.at[k], self.load_sem.at[k])
+
+    def core_copy(self, k):
+        g, (a, b, y, c) = self.grid, self.spot
+        return pltpu.make_async_remote_copy(
+            src_ref=self.source.at[wrap(y + k, g.ny), 1 - c], dst_ref=self.core_in.at[k],
+            send_sem=self.core_s.at[k], recv_sem=self.core_r.at[k],
+            device_id=g.device(a, b, y, 1 - c), device_id_type=MESH,
+        )
+
+    def y_copy(self, k):
+        g, (a, b, y, c) = self.grid, self.spot
+        return pltpu.make_async_remote_copy(
+            src_ref=self.acc.at[k], dst_ref=self.y_in.at[k - 1], send_sem=self.ys.at[k - 1],
+            recv_sem=self.yr.at[k - 1], device_id=g.device(a, b, wrap(y + k, g.ny), c), device_id_type=MESH,
+        )
+
+    def start(self):
+        for k in reversed(range(self.grid.ny)):
+            self.core_copy(k).start()
+            self.load(k).start()
+
+    def middle(self):
+        f32 = jnp.float32
+        for k in reversed(range(self.grid.ny)):
+            self.load(k).wait()
+            ref = self.core_in.at[k]
+            pltpu.make_async_copy(ref, ref, self.core_r.at[k]).wait()
+            total = self.acc[k].astype(f32) + self.core_in[k].astype(f32)
+            self.acc[k] = total.astype(self.acc.dtype)
+            if k:
+                self.y_copy(k).start()
+
+    def last(self):
+        total = self.acc[0].astype(jnp.float32)
+        for k in range(1, self.grid.ny):
+            ref = self.y_in.at[k - 1]
+            pltpu.make_async_copy(ref, ref, self.yr.at[k - 1]).wait()
+            total = total + self.y_in[k - 1].astype(jnp.float32)
+        self.out[...] = total
+
+    def finish(self):
+        for k in range(self.grid.ny):
+            self.core_copy(k).wait_send()
+            if k:
+                self.y_copy(k).wait_send()
+
+
+class TensorGather:
+    count = 5
+
+    @staticmethod
+    def scratch(grid):
+        return [pltpu.SemaphoreType.DMA((1,))] + [pltpu.SemaphoreType.DMA((grid.ny,))] * 4
+
+    def __init__(self, grid, x, out, scratch):
+        self.grid, self.x, self.out = grid, x, out
+        self.own_sem, self.ys, self.yr, self.core_s, self.core_r = scratch
+        self.spot = grid.here()
+
+    def own(self):
+        return pltpu.make_async_copy(self.x, self.out.at[self.spot[2], self.spot[3]], self.own_sem.at[0])
+
+    def y_copy(self, k):
+        g, (a, b, y, c) = self.grid, self.spot
+        return pltpu.make_async_remote_copy(
+            src_ref=self.x, dst_ref=self.out.at[y, c], send_sem=self.ys.at[k], recv_sem=self.yr.at[k],
+            device_id=g.device(a, b, wrap(y + k, g.ny), c), device_id_type=MESH,
+        )
+
+    def core_copy(self, k):
+        g, (a, b, y, c) = self.grid, self.spot
+        spot = wrap(y + g.ny - k, g.ny)
+        return pltpu.make_async_remote_copy(
+            src_ref=self.x if k == 0 else self.out.at[spot, c], dst_ref=self.out.at[spot, c],
+            send_sem=self.core_s.at[k], recv_sem=self.core_r.at[k],
+            device_id=g.device(a, b, y, 1 - c), device_id_type=MESH,
+        )
+
+    def start(self):
+        self.own().start()
+        for k in range(1, self.grid.ny):
+            self.y_copy(k).start()
+        self.core_copy(0).start()
+
+    def middle(self, i):
+        if i == 1:
+            for k in range(1, self.grid.ny):
+                pltpu.make_async_copy(self.x, self.x, self.yr.at[k]).wait()
+                self.core_copy(k).start()
+
+    def last(self):
+        self.own().wait()
+        for k in range(self.grid.ny):
+            pltpu.make_async_copy(self.x, self.x, self.core_r.at[k]).wait()
+        for k in range(self.grid.ny):
+            if k:
+                self.y_copy(k).wait_send()
+            self.core_copy(k).wait_send()
+
+
+class PlaneReduce:
+    count = 9
+
+    @staticmethod
+    def scratch(grid, r, width):
+        na, nb = grid.na, grid.nb
+        sems = lambda *s: pltpu.SemaphoreType.DMA(s)
+        vm = lambda *s: pltpu.VMEM(s, jnp.bfloat16)
+        return [
+            vm(na, r, width), vm(nb - 1, na, r, width), vm(na - 1, r, width),
+            sems(1), sems(nb - 1), sems(nb - 1), sems(na - 1), sems(na - 1), sems(1),
+        ]
+
+    def __init__(self, grid, source, out, scratch):
+        self.grid, self.source, self.out = grid, source, out
+        self.acc, self.b_in, self.a_in, self.load_sem, self.sb, self.rb, self.sa, self.ra, _ = scratch
+        self.spot = grid.here()
+
+    def load(self):
+        return pltpu.make_async_copy(self.source.at[:, self.spot[1]], self.acc, self.load_sem.at[0])
+
+    def copy_b(self, i):
+        g, (a, b, y, c) = self.grid, self.spot
+        return pltpu.make_async_remote_copy(
+            src_ref=self.source.at[:, wrap(b + i, g.nb)], dst_ref=self.b_in.at[i - 1],
+            send_sem=self.sb.at[i - 1], recv_sem=self.rb.at[i - 1],
+            device_id=g.device(a, wrap(b + i, g.nb), y, c), device_id_type=MESH,
+        )
+
+    def copy_a(self, i):
+        g, (a, b, y, c) = self.grid, self.spot
+        return pltpu.make_async_remote_copy(
+            src_ref=self.acc.at[wrap(a + i, g.na)], dst_ref=self.a_in.at[i - 1],
+            send_sem=self.sa.at[i - 1], recv_sem=self.ra.at[i - 1],
+            device_id=g.device(wrap(a + i, g.na), b, y, c), device_id_type=MESH,
+        )
+
+    def start(self):
+        for i in range(1, self.grid.nb):
+            self.copy_b(i).start()
+        self.load().start()
+
+    def middle(self):
+        f32 = jnp.float32
+        self.load().wait()
+        for i in range(1, self.grid.nb):
+            ref = self.b_in.at[i - 1]
+            pltpu.make_async_copy(ref, ref, self.rb.at[i - 1]).wait()
+
+            def one(m, carry):
+                self.acc[m] = (self.acc[m].astype(f32) + ref[m].astype(f32)).astype(self.acc.dtype)
+                return carry
+
+            lax.fori_loop(0, self.grid.na, one, 0)
+        for i in range(1, self.grid.na):
+            self.copy_a(i).start()
+
+    def last(self):
+        total = self.acc[self.spot[0]].astype(jnp.float32)
+        for i in range(1, self.grid.na):
+            ref = self.a_in.at[i - 1]
+            pltpu.make_async_copy(ref, ref, self.ra.at[i - 1]).wait()
+            total = total + self.a_in[i - 1].astype(jnp.float32)
+        self.out[...] = total.astype(self.out.dtype)
+
+    def finish(self):
+        for i in range(1, self.grid.nb):
+            self.copy_b(i).wait_send()
+        for i in range(1, self.grid.na):
+            self.copy_a(i).wait_send()
+
+
+class PlaneGather:
+    count = 5
+
+    @staticmethod
+    def scratch(grid):
+        na, nb = grid.na, grid.nb
+        sems = lambda *s: pltpu.SemaphoreType.DMA(s)
+        return [sems(1), sems(na - 1), sems(na, nb - 1), sems(na), sems(na, nb - 1)]
+
+    def __init__(self, grid, x, out, scratch):
+        self.grid, self.x, self.out = grid, x, out
+        self.own_sem, self.sa, self.sb, self.ra, self.rb = scratch
+        self.spot = grid.here()
+
+    def own(self):
+        return pltpu.make_async_copy(self.x, self.out.at[self.spot[0], self.spot[1]], self.own_sem.at[0])
+
+    def copy_a(self, i):
+        g, (a, b, y, c) = self.grid, self.spot
+        return pltpu.make_async_remote_copy(
+            src_ref=self.x, dst_ref=self.out.at[a, b], send_sem=self.sa.at[i - 1], recv_sem=self.ra.at[i],
+            device_id=g.device(wrap(a + i, g.na), b, y, c), device_id_type=MESH,
+        )
+
+    def copy_b(self, i, k):
+        g, (a, b, y, c) = self.grid, self.spot
+        aa = wrap(a + g.na - i, g.na)
+        return pltpu.make_async_remote_copy(
+            src_ref=self.x if i == 0 else self.out.at[aa, b], dst_ref=self.out.at[aa, b],
+            send_sem=self.sb.at[i, k - 1], recv_sem=self.rb.at[i, k - 1],
+            device_id=g.device(a, wrap(b + k, g.nb), y, c), device_id_type=MESH,
+        )
+
+    def start(self):
+        self.own().start()
+        for i in range(1, self.grid.na):
+            self.copy_a(i).start()
+        for k in range(1, self.grid.nb):
+            self.copy_b(0, k).start()
+
+    def middle(self, i):
+        ref = self.out.at[wrap(self.spot[0] + self.grid.na - i, self.grid.na), self.spot[1]]
+        pltpu.make_async_copy(ref, ref, self.ra.at[i]).wait()
+        for k in range(1, self.grid.nb):
+            self.copy_b(i, k).start()
+
+    def last(self):
+        self.own().wait()
+        ref = self.x
+        for i in range(self.grid.na):
+            for k in range(1, self.grid.nb):
+                pltpu.make_async_copy(ref, ref, self.rb.at[i, k - 1]).wait()
+        for i in range(1, self.grid.na):
+            self.copy_a(i).wait_send()
+        for i in range(self.grid.na):
+            for k in range(1, self.grid.nb):
+                self.copy_b(i, k).wait_send()
+
+
+def last_kernel(grid, x_ref, w_ref, t_ref, out_ref, w_out, t_out, own_sem, ss, rs, cs, cr, *scratch):
+    gathers = [
+        TensorGather(grid, t_ref, t_out, scratch[: TensorGather.count]),
+        PlaneGather(grid, w_ref, w_out, scratch[TensorGather.count :]),
+    ]
+    gather_kernel(grid, x_ref, out_ref, own_sem, ss, rs, cs, cr, gathers)
+
+
+def last_call(grid, x, w, t, collective_id):
+    r, n = x.shape
+    blocks = grid.na * grid.nb * grid.ny
+    any_space = pl.BlockSpec(memory_space=pl.ANY)
+    outs = pl.pallas_call(
+        functools.partial(last_kernel, grid),
+        out_shape=[
+            jax.ShapeDtypeStruct((grid.size, r, n), x.dtype),
+            jax.ShapeDtypeStruct((grid.na, grid.nb) + w.shape, w.dtype),
+            jax.ShapeDtypeStruct((grid.ny, 2) + t.shape, t.dtype),
+        ],
+        in_specs=[any_space] * 3,
+        out_specs=[any_space] * 3,
+        scratch_shapes=[
+            pltpu.SemaphoreType.DMA,
+            pltpu.SemaphoreType.DMA((gather_sends(grid),)),
+            pltpu.SemaphoreType.DMA((2 * blocks,)),
+            pltpu.SemaphoreType.DMA((2 * blocks,)),
+            pltpu.SemaphoreType.DMA((2 * blocks,)),
+        ]
+        + TensorGather.scratch(grid)
+        + PlaneGather.scratch(grid),
+        compiler_params=pltpu.CompilerParams(collective_id=collective_id, has_side_effects=True),
+    )(x, w, t)
+    whole = lambda v: v.reshape(-1, v.shape[-1])
+    return outs[0], whole(outs[1]), whole(outs[2])
+
+
+class Reduce:
+    @staticmethod
+    def scratch(grid, r, width):
+        na, nb, ny = grid.na, grid.nb, grid.ny
+        head = Reduce.head(r)
+        sems = lambda *s: pltpu.SemaphoreType.DMA(s)
+        vm = lambda *s: pltpu.VMEM(s, jnp.bfloat16)
+        return [
+            vm(nb, ny, na, r, width), vm(nb, ny, na, r, width),
+            vm(nb, ny - 1, na, head, width), vm(ny, nb - 1, na, r - head, width),
+            vm(nb - 1, na, head, width), vm(ny - 1, na, r - head, width), vm(na - 1, r, width),
+            sems(nb, ny), sems(nb, ny), sems(nb, ny),
+            sems(nb, ny - 1), sems(nb, ny - 1), sems(ny, nb - 1), sems(ny, nb - 1),
+            sems(nb - 1), sems(nb - 1), sems(ny - 1), sems(ny - 1), sems(na - 1), sems(na - 1),
+        ]
+
+    count = 20
+
+    @staticmethod
+    def head(r):
+        return max(16, r * 3 // 4 // 16 * 16)
+
+    def __init__(self, grid, source, out, scratch):
+        self.grid, self.source, self.out = grid, source, out
+        (
+            self.acc, self.core_in, self.in10, self.in11, self.in20, self.in21, self.a_in,
+            self.load_sem, self.core_s, self.core_r, self.s10, self.r10, self.s11, self.r11,
+            self.s20, self.r20, self.s21, self.r21, self.sa, self.ra,
+        ) = scratch
+        self.spot = grid.here()
+        r = self.acc.shape[3]
+        head = Reduce.head(r)
+        self.upper = (pl.ds(0, head), pl.ds(head, r - head))
+        self.spots = [(j, k) for j in reversed(range(grid.nb)) for k in reversed(range(grid.ny))]
+
+    def remote(self, src, dst, ss, rs, where):
+        return pltpu.make_async_remote_copy(
+            src_ref=src, dst_ref=dst, send_sem=ss, recv_sem=rs, device_id=where, device_id_type=MESH
+        )
+
+    def core_copy(self, j, k):
+        g, (a, b, y, c) = self.grid, self.spot
+        return self.remote(
+            self.source.at[:, wrap(b + j, g.nb), wrap(y + k, g.ny), 1 - c], self.core_in.at[j, k],
+            self.core_s.at[j, k], self.core_r.at[j, k], g.device(a, b, y, 1 - c),
+        )
+
+    def load(self, j, k):
+        g, (a, b, y, c) = self.grid, self.spot
+        return pltpu.make_async_copy(
+            self.source.at[:, wrap(b + j, g.nb), wrap(y + k, g.ny), c], self.acc.at[j, k], self.load_sem.at[j, k]
+        )
+
+    def copy10(self, j, k):
+        g, (a, b, y, c) = self.grid, self.spot
+        return self.remote(
+            self.acc.at[j, k, :, self.upper[0]], self.in10.at[j, k - 1], self.s10.at[j, k - 1],
+            self.r10.at[j, k - 1], g.device(a, b, wrap(y + k, g.ny), c),
+        )
+
+    def copy11(self, j, k):
+        g, (a, b, y, c) = self.grid, self.spot
+        return self.remote(
+            self.acc.at[j, k, :, self.upper[1]], self.in11.at[k, j - 1], self.s11.at[k, j - 1],
+            self.r11.at[k, j - 1], g.device(a, wrap(b + j, g.nb), y, c),
+        )
+
+    def copy20(self, j):
+        g, (a, b, y, c) = self.grid, self.spot
+        return self.remote(
+            self.acc.at[j, 0, :, self.upper[0]], self.in20.at[j - 1], self.s20.at[j - 1],
+            self.r20.at[j - 1], g.device(a, wrap(b + j, g.nb), y, c),
+        )
+
+    def copy21(self, k):
+        g, (a, b, y, c) = self.grid, self.spot
+        return self.remote(
+            self.acc.at[0, k, :, self.upper[1]], self.in21.at[k - 1], self.s21.at[k - 1],
+            self.r21.at[k - 1], g.device(a, b, wrap(y + k, g.ny), c),
+        )
+
+    def copy_a(self, i):
+        g, (a, b, y, c) = self.grid, self.spot
+        return self.remote(
+            self.acc.at[0, 0, wrap(a + i, g.na)], self.a_in.at[i - 1], self.sa.at[i - 1],
+            self.ra.at[i - 1], g.device(wrap(a + i, g.na), b, y, c),
+        )
+
+    def add(self, into, rows, ref, sem):
+        pltpu.make_async_copy(ref, ref, sem).wait()
+        f32 = jnp.float32
+
+        def one(i, carry):
+            total = into[i, rows].astype(f32) + ref[i].astype(f32)
+            into[i, rows] = total.astype(into.dtype)
+            return carry
+
+        lax.fori_loop(0, self.grid.na, one, 0)
+
+    def start(self):
+        for j, k in self.spots:
+            self.core_copy(j, k).start()
+            self.load(j, k).start()
+
+    def core(self):
+        whole = pl.ds(0, self.acc.shape[3])
+        for j, k in self.spots:
+            self.load(j, k).wait()
+            self.add(self.acc.at[j, k], whole, self.core_in.at[j, k], self.core_r.at[j, k])
+            if k:
+                self.copy10(j, k).start()
+            if j:
+                self.copy11(j, k).start()
+
+    def first(self):
+        nb, ny = self.grid.nb, self.grid.ny
+        for j in reversed(range(nb)):
+            for k in range(1, ny):
+                self.add(self.acc.at[j, 0], self.upper[0], self.in10.at[j, k - 1], self.r10.at[j, k - 1])
+            if j:
+                self.copy20(j).start()
+        for k in reversed(range(ny)):
+            for j in range(1, nb):
+                self.add(self.acc.at[0, k], self.upper[1], self.in11.at[k, j - 1], self.r11.at[k, j - 1])
+            if k:
+                self.copy21(k).start()
+
+    def second(self):
+        for j in range(1, self.grid.nb):
+            self.add(self.acc.at[0, 0], self.upper[0], self.in20.at[j - 1], self.r20.at[j - 1])
+        for k in range(1, self.grid.ny):
+            self.add(self.acc.at[0, 0], self.upper[1], self.in21.at[k - 1], self.r21.at[k - 1])
+        for i in range(1, self.grid.na):
+            self.copy_a(i).start()
+
+    def last(self):
+        total = self.acc[0, 0, self.spot[0]].astype(jnp.float32)
+        for i in range(1, self.grid.na):
+            pltpu.make_async_copy(self.a_in.at[i - 1], self.a_in.at[i - 1], self.ra.at[i - 1]).wait()
+            total = total + self.a_in[i - 1].astype(jnp.float32)
+        self.out[...] = total.astype(self.out.dtype)
+
+    def finish(self):
+        for j, k in self.spots:
+            self.core_copy(j, k).wait_send()
+            if k:
+                self.copy10(j, k).wait_send()
+            if j:
+                self.copy11(j, k).wait_send()
+        for j in range(1, self.grid.nb):
+            self.copy20(j).wait_send()
+        for k in range(1, self.grid.ny):
+            self.copy21(k).wait_send()
+        for i in range(1, self.grid.na):
+            self.copy_a(i).wait_send()
+
+
+W_PIECES = 3
+
+
+def gradients_kernel(grid, pieces, unit, places, *refs):
+    (y_ref, k_ref, w_ref, t_ref, q_ref, x_ref, dz_ref, acts_ref), refs = refs[:8], refs[8:]
+    (y_out, k_out, w_out, t_out, q_out), refs = refs[:5], refs[5:]
+    outs, refs = refs[:6], refs[6:]
+    (big, left, right, big_sem, left_sem, out_sem), refs = refs[:6], refs[6:]
+    width = y_ref.shape[-1] // pieces
+    sources = [(k_ref, k_out)]
+    for p in range(pieces):
+        at = pl.ds(p * width, width)
+        sources.append((y_ref.at[:, :, :, :, :, at], y_out.at[:, at]))
+    sums = [
+        Reduce(grid, src, out, refs[m * Reduce.count : (m + 1) * Reduce.count])
+        for m, (src, out) in enumerate(sources)
+    ]
+    refs = refs[len(sums) * Reduce.count :]
+    w_width = w_ref.shape[-1] // W_PIECES
+    flat_sums = []
+    for p in range(W_PIECES):
+        at = pl.ds(p * w_width, w_width)
+        part = refs[p * PlaneReduce.count : (p + 1) * PlaneReduce.count]
+        flat_sums.append(PlaneReduce(grid, w_ref.at[:, :, :, at], w_out.at[:, at], part))
+    refs = refs[W_PIECES * PlaneReduce.count :]
+    flat_sums.append(TensorReduce(grid, t_ref, t_out, refs[: TensorReduce.count]))
+    q_gather = PlaneGather(grid, q_ref, q_out, refs[TensorReduce.count :])
+    tiles = len(places)
+    turn = sum(1 for place in places if place[0] != 2 and place[0] != 5)
+    slots = big.shape[0]
+
+    def left_load(m):
+        s = lax.rem(m, 2)
+        at = pl.ds(pl.multiple_of(m * unit, unit), unit)
+        return pltpu.make_async_copy(acts_ref.at[:, at], left.at[s], left_sem.at[s])
+
+    big_loads = [
+        pltpu.make_async_copy(src, big.at[s % slots], big_sem.at[s]) for s, src in enumerate((x_ref, dz_ref))
+    ]
+    big_loads[0].start()
+    greet(grid)
+    for one in sums + flat_sums + [q_gather]:
+        one.start()
+    left_load(grid.here()[0] * 0).start()
+    if slots > 1:
+        big_loads[1].start()
+    big_loads[0].wait()
+
+    stages = [[one.core, one.first, one.second] for one in sums]
+    work = []
+    for beat in range(len(sums) + 2):
+        for back in range(3):
+            if 0 <= beat - back < len(sums):
+                work.append(stages[beat - back][back])
+    for p, one in enumerate(flat_sums):
+        work.insert(min(len(work), 3 + 3 * p), one.middle)
+    for i in range(1, grid.na):
+        work.insert(min(len(work), 3 + 3 * i), functools.partial(q_gather.middle, i))
+    turns = {}
+    for n, item in enumerate(work):
+        turns.setdefault(n * tiles // len(work), []).append(item)
+
+    def store(m):
+        which, head, first, rows = places[m]
+        dst = outs[which]
+        dst = dst.at[pl.ds(first, rows)] if head is None else dst.at[head, pl.ds(first, rows)]
+        return pltpu.make_async_copy(right.at[m % 2, pl.ds(0, rows)], dst, out_sem.at[m % 2])
+
+    def tile_body(m, carry):
+        s = lax.rem(m, 2)
+
+        @pl.when(m + 1 < tiles)
+        def _():
+            left_load(m + 1).start()
+
+        for n in range(2, tiles):
+
+            @pl.when(m == n)
+            def _():
+                store(n - 2).wait()
+
+        @pl.when(m == turn)
+        def _():
+            if slots == 1:
+                big_loads[1].start()
+            big_loads[1].wait()
+
+        left_load(m).wait()
+        operand = big.at[lax.div(m, turn) if slots > 1 else 0]
+        right[s] = lax.dot_general(
+            left[s], operand[...], (((0,), (0,)), ((), ())), preferred_element_type=jnp.float32
+        ).astype(right.dtype)
+        for n in range(tiles):
+
+            @pl.when(m == n)
+            def _():
+                store(n).start()
+                for item in turns.get(n, ()):
+                    item()
+
+        return carry
+
+    lax.fori_loop(0, tiles, tile_body, 0)
+    for one in sums + flat_sums:
+        one.last()
+    for n in range(max(0, tiles - 2), tiles):
+        store(n).wait()
+    for one in sums + flat_sums:
+        one.finish()
+    q_gather.last()
+
+
+def gradients_call(grid, out_rows, key_rows, weight_rows, tensor_rows, query_rows, x, dz, acts, f, fs, collective_id, pieces=4):
+    tokens, n = x.shape
+    r = tokens // grid.size
+    lay = (grid.na, grid.nb, grid.ny, 2, r)
+    wide, wide_s = round_up(f, 128), round_up(fs, 128)
+    unit = math.gcd(wide, wide_s)
+    places = []
+    for which, heads, real, padded in (
+        (0, EXP_DEV, f, wide), (1, EXP_DEV, f, wide), (3, 0, fs, wide_s), (4, 0, fs, wide_s),
+        (2, EXP_DEV, f, wide), (5, 0, fs, wide_s),
+    ):
+        for head in range(max(heads, 1)):
+            for first in range(0, padded, unit):
+                places.append((which, head if heads else None, first, min(unit, real - first)))
+    slots = 2 if 2 * tokens * n * 2 <= (24 << 20) else 1
+    any_space = pl.BlockSpec(memory_space=pl.ANY)
+    in_vmem = pl.BlockSpec(memory_space=pltpu.VMEM)
+    f32 = jnp.float32
+    scratch = [
+        pltpu.VMEM((slots, tokens, n), x.dtype),
+        pltpu.VMEM((2, tokens, unit), x.dtype),
+        pltpu.VMEM((2, unit, n), x.dtype),
+        pltpu.SemaphoreType.DMA((2,)),
+        pltpu.SemaphoreType.DMA((2,)),
+        pltpu.SemaphoreType.DMA((2,)),
+    ]
+    kw = key_rows.shape[1]
+    for width in [kw] + [n // pieces] * pieces:
+        scratch += Reduce.scratch(grid, r, width)
+    wr, ww = weight_rows.shape[0] // (grid.na * grid.nb), weight_rows.shape[1]
+    scratch += PlaneReduce.scratch(grid, wr, ww // W_PIECES) * W_PIECES
+    tr, tw = tensor_rows.shape[0] // (2 * grid.ny), tensor_rows.shape[1]
+    scratch += TensorReduce.scratch(grid, tr, tw) + PlaneGather.scratch(grid)
+    outs = pl.pallas_call(
+        functools.partial(gradients_kernel, grid, pieces, unit, places),
+        out_shape=[
+            jax.ShapeDtypeStruct((r, n), f32),
+            jax.ShapeDtypeStruct((r, kw), f32),
+            jax.ShapeDtypeStruct((wr, ww), x.dtype),
+            jax.ShapeDtypeStruct((tr, tw), f32),
+            jax.ShapeDtypeStruct((grid.na, grid.nb) + query_rows.shape, x.dtype),
+            jax.ShapeDtypeStruct((EXP_DEV, f, n), x.dtype),
+            jax.ShapeDtypeStruct((EXP_DEV, f, n), x.dtype),
+            jax.ShapeDtypeStruct((EXP_DEV, f, n), x.dtype),
+            jax.ShapeDtypeStruct((fs, n), x.dtype),
+            jax.ShapeDtypeStruct((fs, n), x.dtype),
+            jax.ShapeDtypeStruct((fs, n), x.dtype),
+        ],
+        in_specs=[any_space] * 8,
+        out_specs=[in_vmem] * 4 + [any_space] * 7,
+        scratch_shapes=scratch,
+        compiler_params=pltpu.CompilerParams(
+            collective_id=collective_id, has_side_effects=True, vmem_limit_bytes=62 << 20
+        ),
+    )(
+        out_rows.reshape(lay + (n,)),
+        key_rows.reshape(lay + (kw,)),
+        weight_rows.reshape(grid.na, grid.nb, wr, ww),
+        tensor_rows.reshape(grid.ny, 2, tr, tw),
+        query_rows,
+        x,
+        dz,
+        acts,
+    )
+    y_sum, k_sum, w_sum, t_sum, q_all = outs[:5]
+    eg, eu, ed, sg, su, sd = (out.astype(f32) for out in outs[5:])
+    q_all = q_all.reshape(tokens, -1)
+    weights = (jnp.swapaxes(eg, 1, 2), jnp.swapaxes(eu, 1, 2), ed, sg.T, su.T, sd)
+    return y_sum, k_sum, w_sum, t_sum, q_all, weights
 
 
 def rms_scale(values, gain_vec):
@@ -1149,12 +1778,6 @@
     packed_all = gather_all(grid, quarter(packed), 0).reshape(total_rows, -1)
     latents_all = packed_all[:, :LATENT]
     rope_all = packed_all[:, LATENT : LATENT + ROPE]
-    first_gate = LATENT + ROPE + EXP_DEV * device
-    gates_own = lax.dynamic_slice_in_dim(packed_all, first_gate, EXP_DEV, axis=1).astype(
-        jnp.float32
-    ) + lax.dynamic_slice_in_dim(packed_all, first_gate + experts_all, EXP_DEV, axis=1).astype(
-        jnp.float32
-    )
     q_raw = dot(normed, query_weight)
     heads_here = q_raw.shape[1] // (NOPE + ROPE)
     q_raw = q_raw.reshape(tok_rows, heads_here, NOPE + ROPE)
@@ -1177,34 +1800,19 @@
     attn_out = tensor_scatter(grid, low(dot(merged, output_weight)), 1)
     residual = quarter(hidden_f) + attn_out
     moe_in = low(rms_scale(residual, moe_gain))
-    gates_mine = jnp.swapaxes(gates_own, 0, 1)[:, :, None]
-    moe_all, grad_moe_in, out_rows, gated, d_cat, shared_act, d_sg, d_su = experts_call(
-        grid, moe_in, cot_all, gates_mine, expert_gate, expert_up, expert_down,
+    moe_all, grad_moe_in, out_rows, acts = experts_call(
+        grid, moe_in, cot_all, packed_all, expert_gate, expert_up, expert_down,
         shared_gate, shared_up, shared_down, 2,
     )
-    normed_later, _ = lax.optimization_barrier((quarter(normed), moe_all[:8]))
+    normed_later, _ = lax.optimization_barrier((quarter(normed), moe_in[:8]))
     normed_all = lax.all_gather(normed_later, ALL, axis=0, tiled=True)
-    moe_out = scatter_all(grid, out_rows, jnp.float32, 3)
-    layer_out = low(residual + moe_out)
-    layer_out = tensor_gather(grid, layer_out, 4)
-
-    hidden_here = expert_gate.shape[2]
-    wide = gated.shape[1] // EXP_DEV
-    part_of = lambda e, first=0: slice(first + e * wide, first + e * wide + hidden_here)
-    grad_expert_gate = jnp.stack([dot(moe_all.T, d_cat[:, part_of(e)]) for e in range(EXP_DEV)])
-    grad_expert_up = jnp.stack(
-        [dot(moe_all.T, d_cat[:, part_of(e, EXP_DEV * wide)]) for e in range(EXP_DEV)]
-    )
-    grad_expert_down = jnp.stack([dot(gated[:, part_of(e)].T, cot_all) for e in range(EXP_DEV)])
-    grad_shared_gate = dot(moe_all.T, d_sg)
-    grad_shared_up = dot(moe_all.T, d_su)
-    grad_shared_down = dot(shared_act.T, cot_all)
-
+
+    grad_moe_in, normed_all = lax.optimization_barrier((grad_moe_in, normed_all))
     _, pull_moe = jax.vjp(rms_scale, residual, moe_gain)
     grad_residual, grad_moe_gain = pull_moe(grad_moe_in)
     grad_residual = grad_residual + quarter(cotangent).astype(jnp.float32)
     grad_res_low = tensor_gather(grid, low(grad_residual), 5)
-    grad_output_weight = dot(merged.T, grad_res_low)
+    output_part = low(dot(merged.T, grad_res_low))
     grad_context = low(dot(grad_res_low, output_weight.T)).reshape(tok_rows, heads_here, VDIM)
     scores = score_block(queries, key_plain, rope_all, visible)
     probs = jnp.exp(scores - log_total)
@@ -1232,17 +1840,25 @@
             total_rows, heads_here * (NOPE + VDIM)
         )
     )
-    grad_expand_weight = dot(latents_all.T, grad_expanded)
+    expand_part = low(dot(latents_all.T, grad_expanded))
     grad_keys = jnp.concatenate([dot(grad_expanded, expand_weight.T), grad_k_rope], axis=1)
-    grad_keys = scatter_all(grid, pad_columns(low(grad_keys)), jnp.float32, 6, pieces=1)
     _, pull_qrope = jax.vjp(partial(rotate, places=places), q_raw[..., NOPE:])
     (grad_q_turned,) = pull_qrope(grad_q_rope)
     grad_q_low = low(
         jnp.concatenate([grad_q_plain, grad_q_turned], axis=-1).reshape(tok_rows, -1)
     )
-    grad_q_all = lax.all_gather(grad_q_low, "expert", axis=0, tiled=True)
-    grad_normed = tensor_scatter(grid, low(dot(grad_q_low, query_weight.T)), 7)
-
+    normed_rows = low(dot(grad_q_low, query_weight.T))
+
+    weight_rows = jnp.concatenate(
+        [output_part.reshape(LATENT, -1), expand_part], axis=1
+    )
+    moe_out, grad_keys, weight_rows, grad_normed, grad_q_all, expert_grads = gradients_call(
+        grid, out_rows, pad_columns(low(grad_keys)), weight_rows, normed_rows, grad_q_low, moe_all, cot_all, acts,
+        expert_down.shape[1], shared_down.shape[0], 3,
+    )
+    grad_expert_gate, grad_expert_up, grad_expert_down = expert_grads[:3]
+    grad_shared_gate, grad_shared_up, grad_shared_down = expert_grads[3:]
+    layer_out = low(residual + moe_out)
     places_few = quarter(places)
     compressed_few = quarter(compressed)
     _, pull_latent = jax.vjp(rms_scale, compressed_few[:, :LATENT], latent_gain)
@@ -1250,18 +1866,31 @@
     _, pull_krope = jax.vjp(partial(rotate, places=places_few), compressed_few[:, LATENT:])
     (grad_k_turned,) = pull_krope(grad_keys[:, LATENT : LATENT + ROPE])
     grad_comp_low = low(jnp.concatenate([grad_plain_latent, grad_k_turned], axis=-1))
-    grad_comp_all = gather_all(grid, pad_columns(grad_comp_low), 8).reshape(total_rows, -1)
-    grad_comp_all = grad_comp_all[:, : LATENT + ROPE]
-    grad_latent_weight = dot(normed_all.T, grad_comp_all)
-    grad_query_weight = dot(normed_all.T, grad_q_all)
     grad_normed = grad_normed + dot(grad_comp_low, latent_weight.T)
     _, pull_input = jax.vjp(rms_scale, quarter(hidden_f), attn_gain)
     grad_input_norm, grad_attn_gain = pull_input(grad_normed)
-    grad_hidden = tensor_gather(grid, low(grad_residual + grad_input_norm), 9).astype(jnp.float32)
-
-    gains = lax.psum(jnp.concatenate([grad_attn_gain, grad_latent_gain, grad_moe_gain]), ALL)
-    grad_output_weight = lax.psum(low(grad_output_weight), "expert").astype(jnp.float32)
-    grad_expand_weight = lax.psum(low(grad_expand_weight), "expert").astype(jnp.float32)
+    gains = jnp.concatenate([grad_attn_gain, grad_latent_gain, grad_moe_gain])
+    gains = jnp.pad(gains, (0, -gains.shape[0] % few)).reshape(few, -1)
+    gains_high = low(gains)
+    gains_low = low(gains - gains_high.astype(jnp.float32))
+    spread = gains.shape[1]
+    both = jnp.concatenate([layer_out, low(grad_residual + grad_input_norm)], axis=1)
+    last, weight_rows, both = last_call(
+        grid,
+        pad_columns(jnp.concatenate([grad_comp_low, gains_high, gains_low], axis=1)),
+        weight_rows,
+        both,
+        8,
+    )
+    grad_comp_all = last.reshape(total_rows, -1)[:, : LATENT + ROPE]
+    gains = jnp.sum(last[:, :, LATENT + ROPE : LATENT + ROPE + 2 * spread].astype(jnp.float32), axis=0)
+    gains = (gains[:, :spread] + gains[:, spread:]).reshape(-1)
+    grad_latent_weight = dot(normed_all.T, grad_comp_all)
+    grad_query_weight = dot(normed_all.T, grad_q_all)
+    layer_out, grad_hidden = both[:, :model_width], both[:, model_width:].astype(jnp.float32)
+    split = weight_rows.shape[1] - expand_weight.shape[1]
+    grad_output_weight = weight_rows[:, :split].reshape(output_weight.shape).astype(jnp.float32)
+    grad_expand_weight = weight_rows[:, split:].astype(jnp.float32)
     return (
         layer_out,
         grad_hidden,
@@ -1271,7 +1900,7 @@
         gains[model_width : model_width + LATENT],
         grad_expand_weight,
         grad_output_weight,
-        gains[model_width + LATENT :],
+        gains[model_width + LATENT : 2 * model_width + LATENT],
         grad_shared_gate,
         grad_shared_up,
         grad_shared_down,

time: 739 us -> 561 us (0.76)
  matrix products: 139 us -> 65 us
  waiting for transfers between devices: 82.2 us -> 8.51 us
  blocking collectives: 40.8 us -> 0 us
  local copies, waits for them, and re-layouts: 52.6 us -> 18.7 us
  Pallas kernels: 355 us -> 383 us
  other arithmetic: 43.5 us -> 59.3 us
    pallas_call x2, Pallas kernels: 84.8 us -> 185 us  [the longest x1 123 us: gradients_call(): pl.pallas_call(functools.partial(gradients_kernel, grid, pieces, unit, pl...]
    dot_general x21 -> x12, matrix products: 118 us -> 43.9 us  [dot(): return jnp.dot(left_side, right_side, preferred_element_type=jnp.float32)]
    all_gather x1 -> x0, waiting for transfers between devices: 59.3 us -> none  [shards(): grad_q_all = lax.all_gather(grad_q_low, 'expert', axis=0, tiled=True)]
    psum x1 -> x0, blocking collectives: 40.8 us -> none  [shards(): lax.psum(jnp.concatenate([grad_attn_gain, grad_latent_gain, grad_moe_gain...]
    unnamed x150 -> x113, local copies, waits for them, and re-layouts: 37.3 us -> 7.43 us
    pallas_call x2 -> x1, Pallas kernels: 59.1 us -> 30.3 us  [gather_all(): pl.pallas_call(functools.partial(gather_kernel, grid), out_shape=jax.Shap...]
    psum x1 -> x0, waiting for transfers between devices: 22.9 us -> none  [shards(): lax.psum(low(grad_expand_weight), 'expert').astype(jnp.float32)]
    pallas_call x3 -> x1, Pallas kernels: 31.3 us -> 11.1 us  [tensor_gather(): pl.pallas_call(functools.partial(tensor_gather_kernel, grid), out_shape=j...]
  transfers between devices with their start and end apart: 4 -> 2, of which waited for: 2 -> 1; matrix products, arithmetic and copies ran while one was open for 28% -> 6% of each run, Pallas kernels for 49% -> 34%
where the time goes in v3:
time: 561 us; the launch traced here: 550 us
  Pallas kernels  383 us (68%)
  matrix products  65 us (12%)
  other arithmetic  59.3 us (11%)
  local copies, waits for them, and re-layouts  18.7 us (3%)
  between operations  15.4 us (3%)
  waiting for transfers between devices  8.51 us (2%)
    pallas_call x1, Pallas kernels, experts_call(): pl.pallas_call(functools.partial(experts_kernel, grid, pieces), out_shape...  141 us
    pallas_call x1, Pallas kernels, gradients_call(): pl.pallas_call(functools.partial(gradients_kernel, grid, pieces, unit, pl...  123 us
    pallas_call x1, Pallas kernels, last_call(): pl.pallas_call(functools.partial(last_kernel, grid), out_shape=[jax.Shape...  61.8 us
    dot_general x12, matrix products, dot(): return jnp.dot(left_side, right_side, preferred_element_type=jnp.float32)  43.9 us
    pallas_call x1, Pallas kernels, gather_all(): pl.pallas_call(functools.partial(gather_kernel, grid), out_shape=jax.Shap...  30.3 us
    pallas_call x1, Pallas kernels, tensor_scatter(): pl.pallas_call(functools.partial(tensor_scatter_kernel, grid), out_shape=...  16.2 us
  transfers between devices with their start and end apart: 2, of which 1 were waited for; matrix products, arithmetic and copies ran while one was open for 6% of the time, Pallas kernels for 34%

profile of v3, /device:TPU:0, one launch (start us, length us, event | category | flops | bytes accessed | tf_op | source)
XLA Modules:
  0.0 549.9 jit_solution(5456778571757438934)
XLA Ops:
  7.3 1.7 constant_dynamic-slice_fusion.1
  9.1 1.5 multiply_reduce_fusion.1
  10.6 1.6 multiply_convert_fusion.2
  12.2 0.8 constant_dynamic-slice_fusion
  13.4 1.6 convert_element_type.123
  17.0 2.7 fusion.77
  21.4 30.3 %shard_map.289 = bf16[32,64,640]{2,1,0:T(8,128)(2,1)} custom-call(bf16[64,640]{1,0:T(8,128)(2,1)} %pad_dynamic-slice_fusion.x_ref), custom_call_target="tpu_custom_call" | custom-call | tf_op jit(solution)/shard_map/pallas_call | solution.py:165
  52.5 3.6 fusion.78
  56.2 1.5 fusion.19
  57.8 2.4 convolution_convert_fusion
  60.2 1.3 fusion.20
  61.5 2.5 fusion.76
  64.0 1.5 fusion.2
  65.5 2.4 copy-done
  67.9 2.2 fusion.36
  70.1 0.7 convolution_convert_fusion.3
  70.9 16.2 %shard_map.290 = f32[64,2048]{1,0:T(8,128)S(1)} custom-call(bf16[2,2,64,2048]{3,2,1,0:T(8,128)(2,1)S(1)} %bitcast.98), custom_call_target="tpu_custom_call" | custom-call | tf_op jit(solution)/shard_map/pallas_call | solution.py:341
  87.2 1.3 dynamic-slice_convert_fusion.1
  89.0 1.3 multiply_reduce_fusion.7
  91.4 0.8 multiply_convert_fusion.3.x_ref
  92.3 8.5 %all-gather.3.cloned.1.call-done.refs_6_ = bf16[2048,2048]{1,0:T(8,128)(2,1)} async-done(((bf16[64,2048]{1,0:T(8,128)(2,1)}), bf16[2048,2048]{1,0:T(8,128)(2,1)}) %all-gather.3.cloned.1.call-update) | async-done | bytes 8388624 | tf_op jit(solution)/shard_map/all_gather | solution.py:1766
  100.7 140.6 %shard_map.291 = (bf16[4,2,2,2,64,2048]{5,4,3,2,1,0:T(8,128)(2,1)}, f32[64,2048]{1,0:T(8,128)}, bf16[4,2,2,2,64,2048]{5,4,3,2,1,0:T(8,128)(2,1)}, bf16[4,2,2,2,64,4608]{5,4,3,2,1,0:T(8,128)(2,1)}) custom-call(bf16[64,2048]{1,0:T(8,128)(2,1)} %multiply_convert_fusion.3.x_ref, bf16[4,2,2,2,64,2048]{5,4,3,2,1,0:T(8,128)(2,1)} %bitcast.101, ...), custom_call_target="tpu_custom_call" | custom-call | tf_op jit(solution)/shard_map/pallas_call | solution.py:981
  241.4 1.3 multiply_reduce_fusion.6
  242.7 1.3 fusion.74.x_ref
  244.0 11.1 %shard_map.292 = bf16[2,2,64,2048]{3,2,1,0:T(8,128)(2,1)S(1)} custom-call(bf16[64,2048]{1,0:T(8,128)(2,1)S(1)} %fusion.74.x_ref), custom_call_target="tpu_custom_call" | custom-call | tf_op jit(solution)/shard_map/pallas_call | solution.py:395
  255.2 2.3 convolution_convert_fusion.5
  257.7 5.3 multiply_reduce_fusion
  263.0 5.1 fusion.12
  268.2 2.0 multiply_convert_fusion
  270.2 0.8 fusion.18
  271.3 0.9 fusion.11
  273.4 3.7 convolution_convert_fusion.1
  277.1 3.4 fusion.30
  280.5 2.0 convolution_convert_fusion.2
  282.5 1.4 fusion.45
  284.0 1.5 fusion.42
  285.8 2.0 convolution_convert_fusion.4
  287.9 0.9 copy.113.refs_4_
  288.8 1.7 pad_maximum_fusion.2
  290.5 2.6 copy.123
  293.1 3.6 pad.25.clone
  296.7 1.9 pad_maximum_fusion.1
  298.6 123.0 %shard_map.293 = (f32[64,2048]{1,0:T(8,128)}, f32[64,640]{1,0:T(8,128)}, bf16[64,3072]{1,0:T(8,128)(2,1)}, f32[64,2048]{1,0:T(8,128)}, bf16[4,2,256,768]{3,2,1,0...) custom-call(bf16[4,2,2,2,64,2048]{5,4,3,2,1,0:T(8,128)(2,1)} %get-tu, ...), custom_call_target="tpu_custom_call" | custom-call | tf_op jit(solution)/shard_map/pallas_call | solution.py:1623
  421.7 1.2 multiply_reduce_fusion.10
  423.0 1.0 fusion.64
  424.0 1.1 fusion.53
  425.2 2.6 multiply_reduce_fusion.2
  428.0 0.7 fusion.56.x_ref
  428.7 1.5 add_convert_fusion
  430.2 0.8 pad_maximum_fusion.3.t_ref
  431.0 61.8 %shard_map.294 = (bf16[32,64,768]{2,1,0:T(8,128)(2,1)}, bf16[4,2,64,3072]{3,2,1,0:T(8,128)(2,1)}, bf16[2,2,64,4096]{3,2,1,0:T(8,128)(2,1)}) custom-call(bf16[64,768]{1,0:T(8,128)(2,1)} %fusion.56.x_ref, bf16[64,3072]{1,0:T(8,128)(2,1)} %get-tuple-element.42.w_ref, bf16[64,4096]{1,0:T(8,128)(2,1)} %pad_maximum_fusion.3.t_ref), custom_call_target="tpu_custom_call" | custom-call | tf_op jit(solution)/shard_map/pallas_call | solution.py:1297
  492.8 1.8 convert_reduce_fusion
  496.0 2.9 slice_convert_fusion.1
  498.9 2.5 slice_convert_fusion
  501.4 1.9 slice_convert_fusion.2
  503.4 1.1 copy-done.49
  504.5 11.2 %fusion.79 = f32[2048,768]{1,0:T(8,128)} fusion(bf16[2048,2048]{1,0:T(8,128)(2,1)} %all-gather.5.cloned.1.call-done, bf16[2048,768]{1,0:T(8,128)(2,1)S(1)} %bitcast.137), kind=kOutput, calls=%fused_computation.157 | convolution fusion | flops 6442450944 | bytes 17825792 | tf_op jit(solution)/shard_map/dot_general | solution.py:1710
  515.7 7.1 %fusion.15 = f32[2048,576]{0,1:T(8,128)} fusion(bf16[2048,2048]{1,0:T(8,128)(2,1)S(1)} %bitcast.136, bf16[2048,768]{1,0:T(8,128)(2,1)S(1)} %bitcast.134), kind=kOutput, calls=%fused_computation.26 | convolution fusion | flops 4831838208 | bytes 15728640 | tf_op jit(solution)/shard_map/dot_general | solution.py:1710
  522.8 3.3 convert_bitcast_fusion.3
  526.1 3.3 convert_bitcast_fusion.2
  529.4 3.3 convert_element_type.156
  532.7 3.3 convert_bitcast_fusion.1
  536.1 3.3 convert_bitcast_fusion
  539.4 3.3 convert_element_type.157
  (164 shorter events, 10.4 us)
Async XLA Ops:
  7.2 6.2 %copy-start.3 = (bf16[256,2048]{1,0:T(8,128)(2,1)S(1)}, bf16[256,2048]{1,0:T(8,128)(2,1)}, u32[]{:S(2)}) copy-start(bf16[256,2048]{1,0:T(8,128)(2,1)} %param.18) | copy-start | bytes 3145732
  7.2 5.8 %copy-start.37 = (f32[256,6]{0,1:T(8,128)S(1)}, f32[256,6]{0,1:T(8,128)}, u32[]{:S(2)}) copy-start(f32[256,6]{0,1:T(8,128)} %param.32) | copy-start | bytes 18436
  7.2 5.8 %copy-start.38 = (s32[256,6]{0,1:T(8,128)S(1)}, s32[256,6]{0,1:T(8,128)}, u32[]{:S(2)}) copy-start(s32[256,6]{0,1:T(8,128)} %param.33) | copy-start | bytes 18436
  7.2 7.8 %copy-start.27 = (s32[2048]{0:T(1024)S(1)}, s32[2048]{0:T(1024)}, u32[]{:S(2)}) copy-start(s32[2048]{0:T(1024)} %param.34) | copy-start | bytes 24580
  7.2 93.5 %all-gather.3.cloned.1.call-start = ((), (), s32[]{:S(2)}) async-start(), calls=%async_computation | async-start | bytes 8650752 | tf_op jit(solution)/shard_map/all_gather | solution.py:1766
  9.0 232.3 %all-gather.5.cloned.1.call-start = ((), (), s32[]{:S(2)}) async-start(), calls=%async_computation.1 | async-start | bytes 8650752 | tf_op jit(solution)/shard_map/all_gather | solution.py:1808
  12.2 7.5 %copy-start.20 = (bf16[256,2048]{1,0:T(8,128)(2,1)}, bf16[256,2048]{1,0:T(8,128)(2,1)S(1)}, u32[]{:S(2)}) copy-start(bf16[256,2048]{1,0:T(8,128)(2,1)S(1)} %multiply_convert_fusion.2) | copy-start | bytes 3145732
  13.4 7.0 %copy-start.32 = (f32[512]{0:T(512)S(1)}, f32[512]{0:T(512)}, u32[]{:S(2)}) copy-start(f32[512]{0:T(512)} %param.22) | copy-start | bytes 6148
  16.2 5.2 copy-start.43
  16.9 2.9 copy-start.36
  19.7 67.4 %copy-start.8 = (f32[256,576]{1,0:T(8,128)}, f32[256,576]{1,0:T(8,128)S(1)}, u32[]{:S(2)}) copy-start(f32[256,576]{1,0:T(8,128)S(1)} %fusion.77) | copy-start | bytes 1769476
  51.7 6.0 %copy-start.1 = (bf16[32,64,640]{2,1,0:T(8,128)(2,1)S(1)}, bf16[32,64,640]{2,1,0:T(8,128)(2,1)}, u32[]{:S(2)}) copy-start(bf16[32,64,640]{2,1,0:T(8,128)(2,1)} %shard_map.289) | copy-start | bytes 7864324
  52.4 3.8 copy-start.26
  52.5 5.3 copy-start.50
  56.2 4.0 copy-start.9
  60.2 5.3 copy-start.5
  64.0 3.9 copy-start
  67.9 2.2 copy-start.19
  70.1 0.8 copy-start.22
  70.1 21.3 %copy-start.28 = (f32[2048]{0:T(1024)S(1)}, f32[2048]{0:T(1024)}, u32[]{:S(2)}) copy-start(f32[2048]{0:T(1024)} %param.25) | copy-start | bytes 24580
  87.2 3.1 copy-start.45
  90.3 151.0 %copy-start.40 = (f32[64]{0:T(128)}, f32[64]{0:T(128)S(1)}, u32[]{:S(2)}) copy-start(f32[64]{0:T(128)S(1)} %get-tuple-element.69) | copy-start | bytes 772
  90.8 151.9 %copy-start.34 = (f32[64]{0:T(128)}, f32[64]{0:T(128)S(1)}, u32[]{:S(2)}) copy-start(f32[64]{0:T(128)S(1)} %get-tuple-element.91) | copy-start | bytes 772
  241.3 16.3 %copy-start.31 = (f32[4,256]{1,0:T(4,128)S(1)}, f32[4,256]{1,0:T(4,128)}, u32[]{:S(2)}) copy-start(f32[4,256]{1,0:T(4,128)} %log_add_fusion) | copy-start | bytes 12292
  257.6 10.5 %slice-start = ((s8[8388608]{0:T(1024)(128)(4,1)}), s8[4194304]{0:T(1024)(128)(4,1)S(1)}, s32[]{:S(2)}) async-start(s8[8388608]{0:T(1024)(128)(4,1)} %bitcast.99), calls=%async_computation.2 | async-start | bytes 8388608
  257.7 10.5 %slice-start.1 = ((s8[8388608]{0:T(1024)(128)(4,1)}), s8[4194304]{0:T(1024)(128)(4,1)S(1)}, s32[]{:S(2)}) async-start(s8[8388608]{0:T(1024)(128)(4,1)} %bitcast.99), calls=%async_computation.3 | async-start | bytes 8388608
  270.2 1.1 copy-start.10
  272.2 1.2 copy-start.51
  273.4 3.7 copy-start.2
  277.1 3.4 copy-start.23
  280.5 3.5 copy-start.6
  284.0 1.9 copy-start.48
  293.1 3.6 copy-start.4
  293.1 3.6 copy-start.21
  298.6 123.1 %copy-start.33 = (f32[512]{0:T(512)S(1)}, f32[512]{0:T(512)}, u32[]{:S(2)}) copy-start(f32[512]{0:T(512)} %param.22) | copy-start | bytes 6148
  298.6 123.1 %copy-start.42 = (f32[64]{0:T(128)S(1)}, f32[64]{0:T(128)}, u32[]{:S(2)}) copy-start(f32[64]{0:T(128)} %fusion.69) | copy-start | bytes 772
  298.6 124.4 %copy-start.44 = (f32[32]{0:T(128)S(1)}, f32[32]{0:T(128)}, u32[]{:S(2)}) copy-start(f32[32]{0:T(128)} %copy-done.43) | copy-start | bytes 388
  298.6 124.4 %copy-start.47 = (f32[64]{0:T(128)S(1)}, f32[64]{0:T(128)}, u32[]{:S(2)}) copy-start(f32[64]{0:T(128)} %dynamic-slice_convert_fusion.1) | copy-start | bytes 772
  298.6 125.4 %copy-start.46 = (f32[64]{0:T(128)S(1)}, f32[64]{0:T(128)}, u32[]{:S(2)}) copy-start(f32[64]{0:T(128)} %copy-done.45) | copy-start | bytes 772
  298.6 126.6 %copy-start.30 = (f32[2048]{0:T(1024)S(1)}, f32[2048]{0:T(1024)}, u32[]{:S(2)}) copy-start(f32[2048]{0:T(1024)} %param.19) | copy-start | bytes 24580
  298.6 126.6 %copy-start.39 = (f32[64]{0:T(128)S(1)}, f32[64]{0:T(128)}, u32[]{:S(2)}) copy-start(f32[64]{0:T(128)} %get-tuple-element.92) | copy-start | bytes 772
  421.6 6.3 %copy-start.41 = (f32[64]{0:T(128)S(1)}, f32[64]{0:T(128)}, u32[]{:S(2)}) copy-start(f32[64]{0:T(128)} %copy-done.40) | copy-start | bytes 772
  421.6 7.1 %copy-start.7 = (f32[64,2048]{1,0:T(8,128)S(1)}, f32[64,2048]{1,0:T(8,128)}, u32[]{:S(2)}) copy-start(f32[64,2048]{1,0:T(8,128)} %get-tuple-element.37) | copy-start | bytes 1572868
  421.7 7.1 %copy-start.24 = (f32[64,2048]{1,0:T(8,128)S(1)}, f32[64,2048]{1,0:T(8,128)}, u32[]{:S(2)}) copy-start(f32[64,2048]{1,0:T(8,128)} %get-tuple-element.43) | copy-start | bytes 1572868
  421.7 7.1 %copy-start.29 = (f32[2048]{0:T(1024)S(1)}, f32[2048]{0:T(1024)}, u32[]{:S(2)}) copy-start(f32[2048]{0:T(1024)} %param.25) | copy-start | bytes 24580
  421.7 7.1 %copy-start.35 = (f32[64]{0:T(128)S(1)}, f32[64]{0:T(128)}, u32[]{:S(2)}) copy-start(f32[64]{0:T(128)} %copy-done.34) | copy-start | bytes 772
  492.8 6.1 %copy-start.11 = (bf16[4,2,64,3072]{3,2,1,0:T(8,128)(2,1)S(1)}, bf16[4,2,64,3072]{3,2,1,0:T(8,128)(2,1)}, u32[]{:S(2)}) copy-start(bf16[4,2,64,3072]{3,2,1,0:T(8,128)(2,1)} %get-tuple-element.48) | copy-start | bytes 9437188
  496.0 5.5 copy-start.18
  501.4 3.0 copy-start.49
  501.4 14.3 %slice-start.2 = ((s8[8388608]{0:T(1024)(128)(4,1)}), s8[4194304]{0:T(1024)(128)(4,1)S(1)}, s32[]{:S(2)}) async-start(s8[8388608]{0:T(1024)(128)(4,1)} %bitcast.135), calls=%async_computation.4 | async-start | bytes 8388608
  504.5 11.2 %copy-start.25 = (bf16[32,64,768]{2,1,0:T(8,128)(2,1)S(1)}, bf16[32,64,768]{2,1,0:T(8,128)(2,1)}, u32[]{:S(2)}) copy-start(bf16[32,64,768]{2,1,0:T(8,128)(2,1)} %get-tuple-element.45) | copy-start | bytes 9437188
  504.5 11.2 %slice-start.3 = ((s8[8388608]{0:T(1024)(128)(4,1)}), s8[4194304]{0:T(1024)(128)(4,1)S(1)}, s32[]{:S(2)}) async-start(s8[8388608]{0:T(1024)(128)(4,1)} %bitcast.135), calls=%async_computation.5 | async-start | bytes 8388608
  515.7 7.1 %copy-start.17 = (bf16[704,2048]{1,0:T(8,128)(2,1)S(1)}, bf16[704,2048]{1,0:T(8,128)(2,1)}, u32[]{:S(2)}) copy-start(bf16[704,2048]{1,0:T(8,128)(2,1)} %get-tuple-element.49) | copy-start | bytes 8650756
  522.8 3.3 copy-start.16
  526.1 3.3 copy-start.15
  529.4 3.3 copy-start.14
  532.7 3.3 copy-start.13
  536.1 3.3 copy-start.12
Sparse Core Ops, SparseCore 0:
  11.5 89.1 all-gather.2
  104.1 96.7 all-gather.4

commit v4 on v3

--- a/solution.py
+++ b/solution.py
@@ -403,6 +403,302 @@
         ),
     )(x)
     return out.reshape(2 * ny * r, n)
+
+
+class TensorReduce:
+    count = 8
+
+    @staticmethod
+    def scratch(grid, r, width):
+        ny = grid.ny
+        sems = lambda *s: pltpu.SemaphoreType.DMA(s)
+        vm = lambda *s: pltpu.VMEM(s, jnp.bfloat16)
+        return [
+            vm(ny, r, width), vm(ny, r, width), vm(ny - 1, r, width),
+            sems(ny), sems(ny), sems(ny), sems(ny - 1), sems(ny - 1),
+        ]
+
+    def __init__(self, grid, source, out, scratch):
+        self.grid, self.source, self.out = grid, source, out
+        (
+            self.acc, self.core_in, self.y_in, self.load_sem, self.core_s, self.core_r, self.ys, self.yr,
+        ) = scratch
+        self.spot = grid.here()
+
+    def load(self, k):
+        g, (a, b, y, c) = self.grid, self.spot
+        return pltpu.make_async_copy(self.source.at[wrap(y + k, g.ny), c], self.acc.at[k], self.load_sem.at[k])
+
+    def core_copy(self, k):
+        g, (a, b, y, c) = self.grid, self.spot
+        return pltpu.make_async_remote_copy(
+            src_ref=self.source.at[wrap(y + k, g.ny), 1 - c], dst_ref=self.core_in.at[k],
+            send_sem=self.core_s.at[k], recv_sem=self.core_r.at[k],
+            device_id=g.device(a, b, y, 1 - c), device_id_type=MESH,
+        )
+
+    def y_copy(self, k):
+        g, (a, b, y, c) = self.grid, self.spot
+        return pltpu.make_async_remote_copy(
+            src_ref=self.acc.at[k], dst_ref=self.y_in.at[k - 1], send_sem=self.ys.at[k - 1],
+            recv_sem=self.yr.at[k - 1], device_id=g.device(a, b, wrap(y + k, g.ny), c), device_id_type=MESH,
+        )
+
+    def start(self):
+        for k in reversed(range(self.grid.ny)):
+            self.core_copy(k).start()
+            self.load(k).start()
+
+    def middle(self):
+        f32 = jnp.float32
+        for k in reversed(range(self.grid.ny)):
+            self.load(k).wait()
+            ref = self.core_in.at[k]
+            pltpu.make_async_copy(ref, ref, self.core_r.at[k]).wait()
+            total = self.acc[k].astype(f32) + self.core_in[k].astype(f32)
+            self.acc[k] = total.astype(self.acc.dtype)
+            if k:
+                self.y_copy(k).start()
+
+    def last(self):
+        total = self.acc[0].astype(jnp.float32)
+        for k in range(1, self.grid.ny):
+            ref = self.y_in.at[k - 1]
+            pltpu.make_async_copy(ref, ref, self.yr.at[k - 1]).wait()
+            total = total + self.y_in[k - 1].astype(jnp.float32)
+        self.out[...] = total
+
+    def finish(self):
+        for k in range(self.grid.ny):
+            self.core_copy(k).wait_send()
+            if k:
+                self.y_copy(k).wait_send()
+
+
+class TensorGather:
+    count = 5
+
+    @staticmethod
+    def scratch(grid):
+        return [pltpu.SemaphoreType.DMA((1,))] + [pltpu.SemaphoreType.DMA((grid.ny,))] * 4
+
+    def __init__(self, grid, x, out, scratch):
+        self.grid, self.x, self.out = grid, x, out
+        self.own_sem, self.ys, self.yr, self.core_s, self.core_r = scratch
+        self.spot = grid.here()
+
+    def own(self):
+        return pltpu.make_async_copy(self.x, self.out.at[self.spot[2], self.spot[3]], self.own_sem.at[0])
+
+    def y_copy(self, k):
+        g, (a, b, y, c) = self.grid, self.spot
+        return pltpu.make_async_remote_copy(
+            src_ref=self.x, dst_ref=self.out.at[y, c], send_sem=self.ys.at[k], recv_sem=self.yr.at[k],
+            device_id=g.device(a, b, wrap(y + k, g.ny), c), device_id_type=MESH,
+        )
+
+    def core_copy(self, k):
+        g, (a, b, y, c) = self.grid, self.spot
+        spot = wrap(y + g.ny - k, g.ny)
+        return pltpu.make_async_remote_copy(
+            src_ref=self.x if k == 0 else self.out.at[spot, c], dst_ref=self.out.at[spot, c],
+            send_sem=self.core_s.at[k], recv_sem=self.core_r.at[k],
+            device_id=g.device(a, b, y, 1 - c), device_id_type=MESH,
+        )
+
+    def start(self):
+        self.own().start()
+        for k in range(1, self.grid.ny):
+            self.y_copy(k).start()
+        self.core_copy(0).start()
+
+    def middle(self, i):
+        if i == 1:
+            for k in range(1, self.grid.ny):
+                pltpu.make_async_copy(self.x, self.x, self.yr.at[k]).wait()
+                self.core_copy(k).start()
+
+    def last(self):
+        self.own().wait()
+        for k in range(self.grid.ny):
+            pltpu.make_async_copy(self.x, self.x, self.core_r.at[k]).wait()
+        for k in range(self.grid.ny):
+            if k:
+                self.y_copy(k).wait_send()
+            self.core_copy(k).wait_send()
+
+
+class PlaneReduce:
+    count = 9
+
+    @staticmethod
+    def scratch(grid, r, width):
+        na, nb = grid.na, grid.nb
+        sems = lambda *s: pltpu.SemaphoreType.DMA(s)
+        vm = lambda *s: pltpu.VMEM(s, jnp.bfloat16)
+        return [
+            vm(na, r, width), vm(nb - 1, na, r, width), vm(na - 1, r, width),
+            sems(1), sems(nb - 1), sems(nb - 1), sems(na - 1), sems(na - 1), sems(1),
+        ]
+
+    def __init__(self, grid, source, out, scratch):
+        self.grid, self.source, self.out = grid, source, out
+        self.acc, self.b_in, self.a_in, self.load_sem, self.sb, self.rb, self.sa, self.ra, _ = scratch
+        self.spot = grid.here()
+
+    def load(self):
+        return pltpu.make_async_copy(self.source.at[:, self.spot[1]], self.acc, self.load_sem.at[0])
+
+    def copy_b(self, i):
+        g, (a, b, y, c) = self.grid, self.spot
+        return pltpu.make_async_remote_copy(
+            src_ref=self.source.at[:, wrap(b + i, g.nb)], dst_ref=self.b_in.at[i - 1],
+            send_sem=self.sb.at[i - 1], recv_sem=self.rb.at[i - 1],
+            device_id=g.device(a, wrap(b + i, g.nb), y, c), device_id_type=MESH,
+        )
+
+    def copy_a(self, i):
+        g, (a, b, y, c) = self.grid, self.spot
+        return pltpu.make_async_remote_copy(
+            src_ref=self.acc.at[wrap(a + i, g.na)], dst_ref=self.a_in.at[i - 1],
+            send_sem=self.sa.at[i - 1], recv_sem=self.ra.at[i - 1],
+            device_id=g.device(wrap(a + i, g.na), b, y, c), device_id_type=MESH,
+        )
+
+    def start(self):
+        for i in range(1, self.grid.nb):
+            self.copy_b(i).start()
+        self.load().start()
+
+    def middle(self):
+        f32 = jnp.float32
+        self.load().wait()
+        for i in range(1, self.grid.nb):
+            ref = self.b_in.at[i - 1]
+            pltpu.make_async_copy(ref, ref, self.rb.at[i - 1]).wait()
+
+            def one(m, carry):
+                self.acc[m] = (self.acc[m].astype(f32) + ref[m].astype(f32)).astype(self.acc.dtype)
+                return carry
+
+            lax.fori_loop(0, self.grid.na, one, 0)
+        for i in range(1, self.grid.na):
+            self.copy_a(i).start()
+
+    def last(self):
+        total = self.acc[self.spot[0]].astype(jnp.float32)
+        for i in range(1, self.grid.na):
+            ref = self.a_in.at[i - 1]
+            pltpu.make_async_copy(ref, ref, self.ra.at[i - 1]).wait()
+            total = total + self.a_in[i - 1].astype(jnp.float32)
+        self.out[...] = total.astype(self.out.dtype)
+
+    def finish(self):
+        for i in range(1, self.grid.nb):
+            self.copy_b(i).wait_send()
+        for i in range(1, self.grid.na):
+            self.copy_a(i).wait_send()
+
+
+class PlaneGather:
+    count = 5
+
+    @staticmethod
+    def scratch(grid):
+        na, nb = grid.na, grid.nb
+        sems = lambda *s: pltpu.SemaphoreType.DMA(s)
+        return [sems(1), sems(na - 1), sems(na, nb - 1), sems(na), sems(na, nb - 1)]
+
+    def __init__(self, grid, x, out, scratch):
+        self.grid, self.x, self.out = grid, x, out
+        self.own_sem, self.sa, self.sb, self.ra, self.rb = scratch
+        self.spot = grid.here()
+
+    def own(self):
+        return pltpu.make_async_copy(self.x, self.out.at[self.spot[0], self.spot[1]], self.own_sem.at[0])
+
+    def copy_a(self, i):
+        g, (a, b, y, c) = self.grid, self.spot
+        return pltpu.make_async_remote_copy(
+            src_ref=self.x, dst_ref=self.out.at[a, b], send_sem=self.sa.at[i - 1], recv_sem=self.ra.at[i],
+            device_id=g.device(wrap(a + i, g.na), b, y, c), device_id_type=MESH,
+        )
+
+    def copy_b(self, i, k):
+        g, (a, b, y, c) = self.grid, self.spot
+        aa = wrap(a + g.na - i, g.na)
+        return pltpu.make_async_remote_copy(
+            src_ref=self.x if i == 0 else self.out.at[aa, b], dst_ref=self.out.at[aa, b],
+            send_sem=self.sb.at[i, k - 1], recv_sem=self.rb.at[i, k - 1],
+            device_id=g.device(a, wrap(b + k, g.nb), y, c), device_id_type=MESH,
+        )
+
+    def start(self):
+        self.own().start()
+        for i in range(1, self.grid.na):
+            self.copy_a(i).start()
+        for k in range(1, self.grid.nb):
+            self.copy_b(0, k).start()
+
+    def middle(self, i):
+        ref = self.out.at[wrap(self.spot[0] + self.grid.na - i, self.grid.na), self.spot[1]]
+        pltpu.make_async_copy(ref, ref, self.ra.at[i]).wait()
+        for k in range(1, self.grid.nb):
+            self.copy_b(i, k).start()
+
+    def last(self):
+        self.own().wait()
+        ref = self.x
+        for i in range(self.grid.na):
+            for k in range(1, self.grid.nb):
+                pltpu.make_async_copy(ref, ref, self.rb.at[i, k - 1]).wait()
+        for i in range(1, self.grid.na):
+            self.copy_a(i).wait_send()
+        for i in range(self.grid.na):
+            for k in range(1, self.grid.nb):
+                self.copy_b(i, k).wait_send()
+
+
+def last_kernel(
+    grid, x_ref, w_ref, o_ref, t_ref, out_ref, w_out, o_out, t_out, own_sem, ss, rs, cs, cr, *scratch
+):
+    plane = TensorGather.count + PlaneGather.count
+    gathers = [
+        TensorGather(grid, t_ref, t_out, scratch[: TensorGather.count]),
+        PlaneGather(grid, o_ref, o_out, scratch[TensorGather.count : plane]),
+        PlaneGather(grid, w_ref, w_out, scratch[plane:]),
+    ]
+    gather_kernel(grid, x_ref, out_ref, own_sem, ss, rs, cs, cr, gathers)
+
+
+def last_call(grid, x, w, o, t, collective_id):
+    r, n = x.shape
+    blocks = grid.na * grid.nb * grid.ny
+    any_space = pl.BlockSpec(memory_space=pl.ANY)
+    plane = (grid.na, grid.nb)
+    outs = pl.pallas_call(
+        functools.partial(last_kernel, grid),
+        out_shape=[
+            jax.ShapeDtypeStruct((grid.size, r, n), x.dtype),
+            jax.ShapeDtypeStruct(plane + w.shape, w.dtype),
+            jax.ShapeDtypeStruct(plane + o.shape, o.dtype),
+            jax.ShapeDtypeStruct((grid.ny, 2) + t.shape, t.dtype),
+        ],
+        in_specs=[any_space] * 4,
+        out_specs=[any_space] * 4,
+        scratch_shapes=[
+            pltpu.SemaphoreType.DMA,
+            pltpu.SemaphoreType.DMA((gather_sends(grid),)),
+            pltpu.SemaphoreType.DMA((2 * blocks,)),
+            pltpu.SemaphoreType.DMA((2 * blocks,)),
+            pltpu.SemaphoreType.DMA((2 * blocks,)),
+        ]
+        + TensorGather.scratch(grid)
+        + PlaneGather.scratch(grid) * 2,
+        compiler_params=pltpu.CompilerParams(collective_id=collective_id, has_side_effects=True),
+    )(x, w, o, t)
+    whole = lambda v: v.reshape(-1, v.shape[-1])
+    return outs[0], whole(outs[1]), whole(outs[2]), whole(outs[3])
 
 
 def dot_rows(left_side, right_side):
@@ -1028,296 +1324,6 @@
     return rows_all.reshape(tokens, n), grad, out_rows.reshape(tokens, n), acts.reshape(tokens, -1)
 
 
-class TensorReduce:
-    count = 8
-
-    @staticmethod
-    def scratch(grid, r, width):
-        ny = grid.ny
-        sems = lambda *s: pltpu.SemaphoreType.DMA(s)
-        vm = lambda *s: pltpu.VMEM(s, jnp.bfloat16)
-        return [
-            vm(ny, r, width), vm(ny, r, width), vm(ny - 1, r, width),
-            sems(ny), sems(ny), sems(ny), sems(ny - 1), sems(ny - 1),
-        ]
-
-    def __init__(self, grid, source, out, scratch):
-        self.grid, self.source, self.out = grid, source, out
-        (
-            self.acc, self.core_in, self.y_in, self.load_sem, self.core_s, self.core_r, self.ys, self.yr,
-        ) = scratch
-        self.spot = grid.here()
-
-    def load(self, k):
-        g, (a, b, y, c) = self.grid, self.spot
-        return pltpu.make_async_copy(self.source.at[wrap(y + k, g.ny), c], self.acc.at[k], self.load_sem.at[k])
-
-    def core_copy(self, k):
-        g, (a, b, y, c) = self.grid, self.spot
-        return pltpu.make_async_remote_copy(
-            src_ref=self.source.at[wrap(y + k, g.ny), 1 - c], dst_ref=self.core_in.at[k],
-            send_sem=self.core_s.at[k], recv_sem=self.core_r.at[k],
-            device_id=g.device(a, b, y, 1 - c), device_id_type=MESH,
-        )
-
-    def y_copy(self, k):
-        g, (a, b, y, c) = self.grid, self.spot
-        return pltpu.make_async_remote_copy(
-            src_ref=self.acc.at[k], dst_ref=self.y_in.at[k - 1], send_sem=self.ys.at[k - 1],
-            recv_sem=self.yr.at[k - 1], device_id=g.device(a, b, wrap(y + k, g.ny), c), device_id_type=MESH,
-        )
-
-    def start(self):
-        for k in reversed(range(self.grid.ny)):
-            self.core_copy(k).start()
-            self.load(k).start()
-
-    def middle(self):
-        f32 = jnp.float32
-        for k in reversed(range(self.grid.ny)):
-            self.load(k).wait()
-            ref = self.core_in.at[k]
-            pltpu.make_async_copy(ref, ref, self.core_r.at[k]).wait()
-            total = self.acc[k].astype(f32) + self.core_in[k].astype(f32)
-            self.acc[k] = total.astype(self.acc.dtype)
-            if k:
-                self.y_copy(k).start()
-
-    def last(self):
-        total = self.acc[0].astype(jnp.float32)
-        for k in range(1, self.grid.ny):
-            ref = self.y_in.at[k - 1]
-            pltpu.make_async_copy(ref, ref, self.yr.at[k - 1]).wait()
-            total = total + self.y_in[k - 1].astype(jnp.float32)
-        self.out[...] = total
-
-    def finish(self):
-        for k in range(self.grid.ny):
-            self.core_copy(k).wait_send()
-            if k:
-                self.y_copy(k).wait_send()
-
-
-class TensorGather:
-    count = 5
-
-    @staticmethod
-    def scratch(grid):
-        return [pltpu.SemaphoreType.DMA((1,))] + [pltpu.SemaphoreType.DMA((grid.ny,))] * 4
-
-    def __init__(self, grid, x, out, scratch):
-        self.grid, self.x, self.out = grid, x, out
-        self.own_sem, self.ys, self.yr, self.core_s, self.core_r = scratch
-        self.spot = grid.here()
-
-    def own(self):
-        return pltpu.make_async_copy(self.x, self.out.at[self.spot[2], self.spot[3]], self.own_sem.at[0])
-
-    def y_copy(self, k):
-        g, (a, b, y, c) = self.grid, self.spot
-        return pltpu.make_async_remote_copy(
-            src_ref=self.x, dst_ref=self.out.at[y, c], send_sem=self.ys.at[k], recv_sem=self.yr.at[k],
-            device_id=g.device(a, b, wrap(y + k, g.ny), c), device_id_type=MESH,
-        )
-
-    def core_copy(self, k):
-        g, (a, b, y, c) = self.grid, self.spot
-        spot = wrap(y + g.ny - k, g.ny)
-        return pltpu.make_async_remote_copy(
-            src_ref=self.x if k == 0 else self.out.at[spot, c], dst_ref=self.out.at[spot, c],
-            send_sem=self.core_s.at[k], recv_sem=self.core_r.at[k],
-            device_id=g.device(a, b, y, 1 - c), device_id_type=MESH,
-        )
-
-    def start(self):
-        self.own().start()
-        for k in range(1, self.grid.ny):
-            self.y_copy(k).start()
-        self.core_copy(0).start()
-
-    def middle(self, i):
-        if i == 1:
-            for k in range(1, self.grid.ny):
-                pltpu.make_async_copy(self.x, self.x, self.yr.at[k]).wait()
-                self.core_copy(k).start()
-
-    def last(self):
-        self.own().wait()
-        for k in range(self.grid.ny):
-            pltpu.make_async_copy(self.x, self.x, self.core_r.at[k]).wait()
-        for k in range(self.grid.ny):
-            if k:
-                self.y_copy(k).wait_send()
-            self.core_copy(k).wait_send()
-
-
-class PlaneReduce:
-    count = 9
-
-    @staticmethod
-    def scratch(grid, r, width):
-        na, nb = grid.na, grid.nb
-        sems = lambda *s: pltpu.SemaphoreType.DMA(s)
-        vm = lambda *s: pltpu.VMEM(s, jnp.bfloat16)
-        return [
-            vm(na, r, width), vm(nb - 1, na, r, width), vm(na - 1, r, width),
-            sems(1), sems(nb - 1), sems(nb - 1), sems(na - 1), sems(na - 1), sems(1),
-        ]
-
-    def __init__(self, grid, source, out, scratch):
-        self.grid, self.source, self.out = grid, source, out
-        self.acc, self.b_in, self.a_in, self.load_sem, self.sb, self.rb, self.sa, self.ra, _ = scratch
-        self.spot = grid.here()
-
-    def load(self):
-        return pltpu.make_async_copy(self.source.at[:, self.spot[1]], self.acc, self.load_sem.at[0])
-
-    def copy_b(self, i):
-        g, (a, b, y, c) = self.grid, self.spot
-        return pltpu.make_async_remote_copy(
-            src_ref=self.source.at[:, wrap(b + i, g.nb)], dst_ref=self.b_in.at[i - 1],
-            send_sem=self.sb.at[i - 1], recv_sem=self.rb.at[i - 1],
-            device_id=g.device(a, wrap(b + i, g.nb), y, c), device_id_type=MESH,
-        )
-
-    def copy_a(self, i):
-        g, (a, b, y, c) = self.grid, self.spot
-        return pltpu.make_async_remote_copy(
-            src_ref=self.acc.at[wrap(a + i, g.na)], dst_ref=self.a_in.at[i - 1],
-            send_sem=self.sa.at[i - 1], recv_sem=self.ra.at[i - 1],
-            device_id=g.device(wrap(a + i, g.na), b, y, c), device_id_type=MESH,
-        )
-
-    def start(self):
-        for i in range(1, self.grid.nb):
-            self.copy_b(i).start()
-        self.load().start()
-
-    def middle(self):
-        f32 = jnp.float32
-        self.load().wait()
-        for i in range(1, self.grid.nb):
-            ref = self.b_in.at[i - 1]
-            pltpu.make_async_copy(ref, ref, self.rb.at[i - 1]).wait()
-
-            def one(m, carry):
-                self.acc[m] = (self.acc[m].astype(f32) + ref[m].astype(f32)).astype(self.acc.dtype)
-                return carry
-
-            lax.fori_loop(0, self.grid.na, one, 0)
-        for i in range(1, self.grid.na):
-            self.copy_a(i).start()
-
-    def last(self):
-        total = self.acc[self.spot[0]].astype(jnp.float32)
-        for i in range(1, self.grid.na):
-            ref = self.a_in.at[i - 1]
-            pltpu.make_async_copy(ref, ref, self.ra.at[i - 1]).wait()
-            total = total + self.a_in[i - 1].astype(jnp.float32)
-        self.out[...] = total.astype(self.out.dtype)
-
-    def finish(self):
-        for i in range(1, self.grid.nb):
-            self.copy_b(i).wait_send()
-        for i in range(1, self.grid.na):
-            self.copy_a(i).wait_send()
-
-
-class PlaneGather:
-    count = 5
-
-    @staticmethod
-    def scratch(grid):
-        na, nb = grid.na, grid.nb
-        sems = lambda *s: pltpu.SemaphoreType.DMA(s)
-        return [sems(1), sems(na - 1), sems(na, nb - 1), sems(na), sems(na, nb - 1)]
-
-    def __init__(self, grid, x, out, scratch):
-        self.grid, self.x, self.out = grid, x, out
-        self.own_sem, self.sa, self.sb, self.ra, self.rb = scratch
-        self.spot = grid.here()
-
-    def own(self):
-        return pltpu.make_async_copy(self.x, self.out.at[self.spot[0], self.spot[1]], self.own_sem.at[0])
-
-    def copy_a(self, i):
-        g, (a, b, y, c) = self.grid, self.spot
-        return pltpu.make_async_remote_copy(
-            src_ref=self.x, dst_ref=self.out.at[a, b], send_sem=self.sa.at[i - 1], recv_sem=self.ra.at[i],
-            device_id=g.device(wrap(a + i, g.na), b, y, c), device_id_type=MESH,
-        )
-
-    def copy_b(self, i, k):
-        g, (a, b, y, c) = self.grid, self.spot
-        aa = wrap(a + g.na - i, g.na)
-        return pltpu.make_async_remote_copy(
-            src_ref=self.x if i == 0 else self.out.at[aa, b], dst_ref=self.out.at[aa, b],
-            send_sem=self.sb.at[i, k - 1], recv_sem=self.rb.at[i, k - 1],
-            device_id=g.device(a, wrap(b + k, g.nb), y, c), device_id_type=MESH,
-        )
-
-    def start(self):
-        self.own().start()
-        for i in range(1, self.grid.na):
-            self.copy_a(i).start()
-        for k in range(1, self.grid.nb):
-            self.copy_b(0, k).start()
-
-    def middle(self, i):
-        ref = self.out.at[wrap(self.spot[0] + self.grid.na - i, self.grid.na), self.spot[1]]
-        pltpu.make_async_copy(ref, ref, self.ra.at[i]).wait()
-        for k in range(1, self.grid.nb):
-            self.copy_b(i, k).start()
-
-    def last(self):
-        self.own().wait()
-        ref = self.x
-        for i in range(self.grid.na):
-            for k in range(1, self.grid.nb):
-                pltpu.make_async_copy(ref, ref, self.rb.at[i, k - 1]).wait()
-        for i in range(1, self.grid.na):
-            self.copy_a(i).wait_send()
-        for i in range(self.grid.na):
-            for k in range(1, self.grid.nb):
-                self.copy_b(i, k).wait_send()
-
-
-def last_kernel(grid, x_ref, w_ref, t_ref, out_ref, w_out, t_out, own_sem, ss, rs, cs, cr, *scratch):
-    gathers = [
-        TensorGather(grid, t_ref, t_out, scratch[: TensorGather.count]),
-        PlaneGather(grid, w_ref, w_out, scratch[TensorGather.count :]),
-    ]
-    gather_kernel(grid, x_ref, out_ref, own_sem, ss, rs, cs, cr, gathers)
-
-
-def last_call(grid, x, w, t, collective_id):
-    r, n = x.shape
-    blocks = grid.na * grid.nb * grid.ny
-    any_space = pl.BlockSpec(memory_space=pl.ANY)
-    outs = pl.pallas_call(
-        functools.partial(last_kernel, grid),
-        out_shape=[
-            jax.ShapeDtypeStruct((grid.size, r, n), x.dtype),
-            jax.ShapeDtypeStruct((grid.na, grid.nb) + w.shape, w.dtype),
-            jax.ShapeDtypeStruct((grid.ny, 2) + t.shape, t.dtype),
-        ],
-        in_specs=[any_space] * 3,
-        out_specs=[any_space] * 3,
-        scratch_shapes=[
-            pltpu.SemaphoreType.DMA,
-            pltpu.SemaphoreType.DMA((gather_sends(grid),)),
-            pltpu.SemaphoreType.DMA((2 * blocks,)),
-            pltpu.SemaphoreType.DMA((2 * blocks,)),
-            pltpu.SemaphoreType.DMA((2 * blocks,)),
-        ]
-        + TensorGather.scratch(grid)
-        + PlaneGather.scratch(grid),
-        compiler_params=pltpu.CompilerParams(collective_id=collective_id, has_side_effects=True),
-    )(x, w, t)
-    whole = lambda v: v.reshape(-1, v.shape[-1])
-    return outs[0], whole(outs[1]), whole(outs[2])
-
-
 class Reduce:
     @staticmethod
     def scratch(grid, r, width):
@@ -1475,7 +1481,7 @@
             self.copy_a(i).wait_send()
 
 
-W_PIECES = 3
+W_PIECES = 1
 
 
 def gradients_kernel(grid, pieces, unit, places, *refs):
@@ -1658,6 +1664,529 @@
     return y_sum, k_sum, w_sum, t_sum, q_all, weights
 
 
+class GatherAll:
+    @staticmethod
+    def scratch(grid):
+        blocks = 2 * grid.na * grid.nb * grid.ny
+        sems = lambda n: pltpu.SemaphoreType.DMA((n,))
+        return [sems(1), sems(gather_sends(grid)), sems(blocks), sems(blocks), sems(blocks)]
+
+    def __init__(self, grid, x, out, scratch, halves=2):
+        self.grid, self.x, self.out, self.halves = grid, x, out, halves
+        self.own_sem, self.sends, self.recvs, self.share_s, self.share_r = scratch
+        self.spot = grid.here()
+        self.half = x.shape[0] // halves
+        self.count = 0
+        na, nb, ny = grid.na, grid.nb, grid.ny
+        self.orders = (("b", "y"), ("y", "b"))
+        near = [(0, k, 0, 0, ()) for k in range(1, ny)] + [(0, k, 0, 1, ("b",)) for k in range(1, ny)]
+        first = [(0, 0, i, h, self.orders[h]) for i in range(1, na) for h in range(2)]
+        second = []
+        for i in range(na):
+            second += [(j, 0, i, 0, ("y",)) for j in range(1, nb)]
+            second += [(0, k, i, 1, ("b",)) for k in range(1, ny) if i]
+        third = []
+        for i in range(na):
+            third += [(0, k, i, 0, ()) for k in range(1, ny) if i]
+            third += [(j, 0, i, 1, ()) for j in range(1, nb)]
+        for i in range(na):
+            third += [(j, k, i, h, ()) for j in range(1, nb) for k in range(1, ny) for h in range(2)]
+        self.near = [event for event in near if event[3] < halves]
+        self.others = [event for event in first + second + third if event[3] < halves]
+
+    def line(self, i):
+        a = self.spot[0]
+        if self.grid.na != 4:
+            return wrap(a + i, self.grid.na)
+        if i == 0:
+            return a
+        if i == 1:
+            return a + 1 - 2 * lax.rem(a, 2)
+        return (i - lax.div(a, 2)) if i == 2 else (3 - 3 * lax.div(a, 2))
+
+    def place(self, bb, yy, cc, aa, h):
+        return self.out.at[aa, bb, yy, cc, pl.ds(h * self.half, self.half)]
+
+    def slot(self, bb, yy, aa, h):
+        return ((bb * self.grid.ny + yy) * self.grid.na + aa) * 2 + h
+
+    def push(self, src, bb, yy, aa, h, where, send, recv):
+        pltpu.make_async_remote_copy(
+            src_ref=src, dst_ref=self.place(bb, yy, self.spot[3], aa, h), send_sem=send,
+            recv_sem=recv.at[self.slot(bb, yy, aa, h)], device_id=where, device_id_type=MESH,
+        ).start()
+
+    def onward(self, src, bb, yy, aa, h, dims):
+        g, (a, b, y, c) = self.grid, self.spot
+        for d in dims:
+            for i in range(1, {"a": g.na, "b": g.nb, "y": g.ny}[d]):
+                if d == "a":
+                    where = g.device(self.line(i), b, y, c)
+                elif d == "b":
+                    where = g.device(a, wrap(b + i, g.nb), y, c)
+                else:
+                    where = g.device(a, b, wrap(y + i, g.ny), c)
+                self.push(src, bb, yy, aa, h, where, self.sends.at[self.count], self.recvs)
+                self.count += 1
+        where = g.device(a, b, y, 1 - c)
+        self.push(src, bb, yy, aa, h, where, self.share_s.at[self.slot(bb, yy, aa, h)], self.share_r)
+
+    def landed(self, bb, yy, cc, aa, h, sem):
+        ref = self.place(bb, yy, cc, aa, h)
+        pltpu.make_async_copy(ref, ref, sem.at[self.slot(bb, yy, aa, h)]).wait()
+        return ref
+
+    def own(self):
+        a, b, y, c = self.spot
+        return pltpu.make_async_copy(self.x, self.out.at[a, b, y, c], self.own_sem.at[0])
+
+    def start(self):
+        a, b, y, c = self.spot
+        self.own().start()
+        for h in range(self.halves):
+            src = self.x.at[pl.ds(h * self.half, self.half)]
+            self.onward(src, b, y, a, h, ("y", "a", "b") if h == 0 else ("y", "b", "a"))
+
+    def relay(self, j, k, i, h, dims):
+        g, (a, b, y, c) = self.grid, self.spot
+        bb, yy, aa = wrap(b + j, g.nb), wrap(y + k, g.ny), self.line(i)
+        self.onward(self.landed(bb, yy, c, aa, h, self.recvs), bb, yy, aa, h, dims)
+
+    def shared(self, j, k, i):
+        g, (a, b, y, c) = self.grid, self.spot
+        for h in range(self.halves):
+            self.landed(wrap(b + j, g.nb), wrap(y + k, g.ny), 1 - c, self.line(i), h, self.share_r)
+
+    def group(self):
+        for event in self.near:
+            self.relay(*event)
+        for k in range(self.grid.ny):
+            self.shared(0, k, 0)
+        self.own().wait()
+
+    def finish(self):
+        g, (a, b, y, c) = self.grid, self.spot
+        for j in range(g.nb):
+            for k in range(g.ny):
+                for i in range(g.na):
+                    if i or j:
+                        self.shared(j, k, i)
+        some = self.place(b, y, c, a, 0)
+        for i in range(self.count):
+            pltpu.make_async_copy(some, some, self.sends.at[i]).wait()
+        for i in range(g.na * g.nb * g.ny):
+            for h in range(self.halves):
+                pltpu.make_async_copy(some, some, self.share_s.at[2 * i + h]).wait()
+
+
+def turn_back(values, cosines, sines):
+    quarter = ROPE // 2
+    lane = lax.broadcasted_iota(jnp.int32, values.shape, 1)
+    swapped = jnp.where(
+        lane < quarter,
+        pltpu.roll(values, values.shape[1] - quarter, 1),
+        pltpu.roll(values, quarter, 1),
+    )
+    return values * cosines + swapped * sines
+
+
+def attention_back_kernel(
+    grid,
+    pieces,
+    x_ref,
+    wo_hbm,
+    q_hbm,
+    kv_hbm,
+    packed_hbm,
+    we_hbm,
+    ctx_ref,
+    log_ref,
+    seg_ref,
+    own_seg_ref,
+    cos_ref,
+    sin_ref,
+    dq_ref,
+    keys_ref,
+    part_ref,
+    wo_ref,
+    wo,
+    q,
+    kv,
+    packed,
+    we,
+    grads,
+    kcat,
+    bias,
+    dkv,
+    drope,
+    wo_part,
+    load_sem,
+    *scratch,
+):
+    f32, bf = jnp.float32, jnp.bfloat16
+    rows, tokens = q.shape[0], kv.shape[0]
+    heads = q.shape[1] // 256
+    scale = (NOPE + ROPE) ** (-0.5)
+    a, b, y, c = grid.here()
+    pairs = ((wo_hbm, wo), (q_hbm, q), (kv_hbm, kv), (packed_hbm, packed), (we_hbm, we))
+    loads = [pltpu.make_async_copy(src, dst, load_sem.at[i]) for i, (src, dst) in enumerate(pairs)]
+    for load in loads:
+        load.start()
+    greet(grid)
+    group = TensorGather(grid, x_ref, grads, scratch[: TensorGather.count])
+    group.start()
+    sums = []
+    width = wo.shape[1] // pieces
+    for p in range(pieces):
+        first = TensorGather.count + p * PlaneReduce.count
+        at = pl.ds(p * width, width)
+        sums.append(
+            PlaneReduce(
+                grid, wo_part.at[:, :, :, at], wo_ref.at[:, at], scratch[first : first + PlaneReduce.count]
+            )
+        )
+    first_row = (a * grid.nb + b) * rows
+    ordinal = first_row + lax.broadcasted_iota(jnp.int32, (rows, tokens), 0)
+    key = lax.broadcasted_iota(jnp.int32, (rows, tokens), 1)
+    seg = seg_ref[...]
+    seen = (key <= ordinal) & ((seg == own_seg_ref[...]) | (seg == 0))
+    bias[...] = jnp.where(seen, 0.0, masked_out)
+    for load in loads:
+        load.wait()
+    kcat[:, NOPE:] = packed[:, LATENT : LATENT + 128]
+    lane = lax.broadcasted_iota(jnp.int32, (tokens, 128), 1)
+    kcat[:, NOPE:] = jnp.where(lane < ROPE, kcat[:, NOPE:].astype(f32), 0.0).astype(bf)
+
+    group.middle(1)
+    group.last()
+    rows_in = grads[...].reshape(rows, grads.shape[-1])
+    for p in range(pieces):
+        at = pl.ds(p * width, width)
+        wo_part[:, :, :, at] = (
+            lax.dot_general(
+                ctx_ref[...], rows_in[:, p * width : (p + 1) * width], (((0,), (0,)), ((), ())),
+                preferred_element_type=f32,
+            )
+            .astype(bf)
+            .reshape(wo_part.shape[:3] + (width,))
+        )
+        sums[p].start()
+    dctx = dot_rows(rows_in, wo[...]).astype(bf)
+
+    points = 3 * heads + 1
+    at_point = {}
+    for p in range(pieces):
+        at_point.setdefault((p + 1) * points // (pieces + 2), []).append(sums[p].middle)
+    done = [0]
+
+    def hook():
+        for event in at_point.get(done[0], ()):
+            event()
+        done[0] += 1
+
+    hook()
+    for h in range(heads):
+        qh = q[:, h * 256 : (h + 1) * 256]
+        kcat[:, :NOPE] = kv[:, h * 256 : h * 256 + NOPE]
+        s = dot_rows(qh, kcat[...]) * scale + bias[...]
+        p = jnp.exp(s - log_ref[h])
+        dh = dctx[:, h * VDIM : (h + 1) * VDIM]
+        dp = dot_rows(dh, kv[:, h * 256 + NOPE : (h + 1) * 256])
+        ds = (p * (dp - jnp.sum(p * dp, axis=-1, keepdims=True))).astype(bf)
+        p = p.astype(bf)
+        hook()
+        dq = dot_plain(ds, kcat[...]) * scale
+        dq_ref[:, h * 256 : h * 256 + NOPE] = dq[:, :NOPE].astype(bf)
+        dq_ref[:, h * 256 + NOPE : (h + 1) * 256] = turn_back(
+            dq[:, NOPE:], cos_ref[...], sin_ref[...]
+        ).astype(bf)
+        hook()
+        dkv[:, h * 256 + NOPE : (h + 1) * 256] = lax.dot_general(
+            p, dh, (((0,), (0,)), ((), ())), preferred_element_type=f32
+        ).astype(bf)
+        dk = scale * lax.dot_general(ds, qh, (((0,), (0,)), ((), ())), preferred_element_type=f32)
+        dkv[:, h * 256 : h * 256 + NOPE] = dk[:, :NOPE].astype(bf)
+        if h == 0:
+            drope[...] = dk[:, NOPE:]
+        else:
+            drope[...] += dk[:, NOPE:]
+        hook()
+    keys_ref[:, :LATENT] = dot_rows(dkv[...], we[...]).astype(bf)
+    keys_ref[:, LATENT:] = drope[...].astype(bf)
+    part_ref[...] = lax.dot_general(
+        packed[:, :LATENT], dkv[...], (((0,), (0,)), ((), ())), preferred_element_type=f32
+    ).astype(bf)
+    for one in sums:
+        one.last()
+    for one in sums:
+        one.finish()
+
+
+def attention_back_call(
+    grid, x, wo, q, kv, packed, we, context, log_total, seg, own_seg, cosines, sines, collective_id, pieces=4
+):
+    r, n = x.shape
+    rows, tokens, heads = q.shape[0], kv.shape[0], q.shape[1] // 256
+    bf, f32 = jnp.bfloat16, jnp.float32
+    any_space = pl.BlockSpec(memory_space=pl.ANY)
+    in_vmem = pl.BlockSpec(memory_space=pltpu.VMEM)
+    share = wo.shape[0] // (grid.na * grid.nb)
+    return pl.pallas_call(
+        functools.partial(attention_back_kernel, grid, pieces),
+        out_shape=[
+            jax.ShapeDtypeStruct(q.shape, bf),
+            jax.ShapeDtypeStruct((tokens, LATENT + 128), bf),
+            jax.ShapeDtypeStruct(we.shape, bf),
+            jax.ShapeDtypeStruct((share, n), bf),
+        ],
+        in_specs=[any_space] * 6 + [in_vmem] * 6,
+        out_specs=[in_vmem] * 4,
+        scratch_shapes=[
+            pltpu.VMEM(wo.shape, bf),
+            pltpu.VMEM(q.shape, bf),
+            pltpu.VMEM(kv.shape, bf),
+            pltpu.VMEM(packed.shape, bf),
+            pltpu.VMEM(we.shape, bf),
+            pltpu.VMEM((grid.ny, 2, r, n), bf),
+            pltpu.VMEM((tokens, 256), bf),
+            pltpu.VMEM((rows, tokens), f32),
+            pltpu.VMEM(kv.shape, bf),
+            pltpu.VMEM((tokens, 128), f32),
+            pltpu.VMEM((grid.na, grid.nb, share, n), bf),
+            pltpu.SemaphoreType.DMA((5,)),
+        ]
+        + TensorGather.scratch(grid)
+        + PlaneReduce.scratch(grid, share, n // pieces) * pieces,
+        compiler_params=pltpu.CompilerParams(
+            collective_id=collective_id, has_side_effects=True, vmem_limit_bytes=62 << 20
+        ),
+    )(x, wo, q, kv, packed, we, context, log_total, seg, own_seg, cosines, sines)
+
+
+def first_kernel(
+    grid,
+    hidden_ref,
+    gain_ref,
+    wl_hbm,
+    lgain_ref,
+    wq_hbm,
+    gate_ref,
+    route_ref,
+    cos_ref,
+    sin_ref,
+    packed_ref,
+    q_ref,
+    normed_ref,
+    comp_ref,
+    wl,
+    wq,
+    normed,
+    mine,
+    load_sem,
+    *scratch,
+):
+    f32, bf = jnp.float32, jnp.bfloat16
+    rows, few = hidden_ref.shape[0], mine.shape[0]
+    heads = q_ref.shape[1] // 256
+    a, b, y, c = grid.here()
+    pairs = ((wl_hbm, wl.at[pl.ds(0, LATENT + ROPE)]), (wq_hbm, wq))
+    loads = [pltpu.make_async_copy(src, dst, load_sem.at[i]) for i, (src, dst) in enumerate(pairs)]
+    for load in loads:
+        load.start()
+    wl[LATENT + ROPE :] = jnp.zeros((wl.shape[0] - LATENT - ROPE, wl.shape[1]), bf)
+    greet(grid)
+    at = pl.ds(pl.multiple_of((y * 2 + c) * few, few), few)
+
+    def rms(v, gain):
+        return v * lax.rsqrt(jnp.mean(v * v, axis=-1, keepdims=True) + epsilon) * gain
+
+    normed_few = rms(hidden_ref[at].astype(f32), gain_ref[...]).astype(bf)
+    normed_ref[...] = normed_few
+    loads[0].wait()
+    comp = dot_rows(normed_few, wl[...])
+    comp_ref[...] = comp
+    mine[:, :LATENT] = rms(comp[:, :LATENT], lgain_ref[...]).astype(bf)
+    tail = turn_back(comp[:, LATENT:], cos_ref[at], -sin_ref[at])
+    lane = lax.broadcasted_iota(jnp.int32, tail.shape, 1) - ROPE
+    routes, gates = route_ref[at], gate_ref[at]
+    for k in range(TOP):
+        expert, gate = routes[:, k : k + 1], gates[:, k : k + 1]
+        high = gate.astype(bf).astype(f32)
+        tail += jnp.where(lane == expert, high, 0.0)
+        tail += jnp.where(lane == expert + EXP_DEV * grid.na * grid.nb, gate - high, 0.0)
+    mine[:, LATENT:] = tail.astype(bf)
+    gather = GatherAll(grid, mine, packed_ref, scratch, halves=1)
+    gather.start()
+    normed[...] = rms(hidden_ref[...].astype(f32), gain_ref[...]).astype(bf)
+    loads[1].wait()
+    gather.group()
+    for event in gather.others[: len(gather.others) // 3]:
+        gather.relay(*event)
+    raw = dot_plain(normed[...], wq[...])
+    total = raw.shape[1]
+    for h in range(heads):
+        step = h * (NOPE + ROPE)
+        moved = raw if step == 0 else pltpu.roll(raw, total - step, 1)
+        q_ref[:, h * 256 : h * 256 + NOPE] = moved[:, :NOPE].astype(bf)
+        q_ref[:, h * 256 + NOPE : (h + 1) * 256] = turn_back(
+            moved[:, NOPE : NOPE + 128], cos_ref[...], -sin_ref[...]
+        ).astype(bf)
+    for event in gather.others[len(gather.others) // 3 :]:
+        gather.relay(*event)
+    gather.finish()
+
+
+def first_call(
+    grid, hidden, attn_gain, latent_weight, latent_gain, query_weight, gates, routes, cosines, sines,
+    collective_id,
+):
+    rows, n = hidden.shape
+    few = rows // (2 * grid.ny)
+    heads = query_weight.shape[1] // (NOPE + ROPE)
+    bf, f32 = jnp.bfloat16, jnp.float32
+    any_space = pl.BlockSpec(memory_space=pl.ANY)
+    in_vmem = pl.BlockSpec(memory_space=pltpu.VMEM)
+    width = LATENT + 128
+    outs = pl.pallas_call(
+        functools.partial(first_kernel, grid),
+        out_shape=[
+            jax.ShapeDtypeStruct((grid.na, grid.nb, grid.ny, 2, few, width), bf),
+            jax.ShapeDtypeStruct((rows, heads * 256), bf),
+            jax.ShapeDtypeStruct((few, n), bf),
+            jax.ShapeDtypeStruct((few, width), f32),
+        ],
+        in_specs=[in_vmem, in_vmem, any_space, in_vmem, any_space] + [in_vmem] * 4,
+        out_specs=[any_space] + [in_vmem] * 3,
+        scratch_shapes=[
+            pltpu.VMEM((width, n), bf),
+            pltpu.VMEM(query_weight.shape, bf),
+            pltpu.VMEM((rows, n), bf),
+            pltpu.VMEM((few, width), bf),
+            pltpu.SemaphoreType.DMA((2,)),
+        ]
+        + GatherAll.scratch(grid),
+        compiler_params=pltpu.CompilerParams(
+            collective_id=collective_id, has_side_effects=True, vmem_limit_bytes=40 << 20
+        ),
+    )(
+        hidden, attn_gain[None], latent_weight.T, latent_gain[None], query_weight, gates, routes,
+        cosines, sines,
+    )
+    return outs[0].reshape(-1, width), outs[1], outs[2], outs[3]
+
+
+def attention_kernel(
+    grid,
+    hidden_ref,
+    gain_ref,
+    q_hbm,
+    packed_hbm,
+    we_hbm,
+    wo_hbm,
+    seg_ref,
+    own_seg_ref,
+    kv_ref,
+    log_ref,
+    ctx_ref,
+    res_ref,
+    moe_ref,
+    q,
+    packed,
+    we,
+    wo,
+    kv,
+    kcat,
+    bias,
+    part,
+    total,
+    load_sem,
+    kv_sem,
+    *scratch,
+):
+    f32, bf = jnp.float32, jnp.bfloat16
+    rows, tokens = q.shape[0], kv.shape[0]
+    heads = q.shape[1] // 256
+    few = res_ref.shape[0]
+    scale = (NOPE + ROPE) ** (-0.5)
+    a, b, y, c = grid.here()
+    pairs = ((packed_hbm, packed), (we_hbm, we), (q_hbm, q), (wo_hbm, wo))
+    loads = [pltpu.make_async_copy(src, dst, load_sem.at[i]) for i, (src, dst) in enumerate(pairs)]
+    for load in loads:
+        load.start()
+    greet_tensor(grid)
+    ordinal = (a * grid.nb + b) * rows + lax.broadcasted_iota(jnp.int32, (rows, tokens), 0)
+    key = lax.broadcasted_iota(jnp.int32, (rows, tokens), 1)
+    seg = seg_ref[...]
+    seen = (key <= ordinal) & ((seg == own_seg_ref[...]) | (seg == 0))
+    bias[...] = jnp.where(seen, 0.0, masked_out)
+    for load in loads:
+        load.wait()
+    lane = lax.broadcasted_iota(jnp.int32, (tokens, 128), 1)
+    kcat[:, NOPE:] = jnp.where(lane < ROPE, packed[:, LATENT:].astype(f32), 0.0).astype(bf)
+    kv[...] = dot_plain(packed[:, :LATENT], we[...]).astype(bf)
+    store = pltpu.make_async_copy(kv, kv_ref, kv_sem)
+    store.start()
+    for h in range(heads):
+        kcat[:, :NOPE] = kv[:, h * 256 : h * 256 + NOPE]
+        s = dot_rows(q[:, h * 256 : (h + 1) * 256], kcat[...]) * scale + bias[...]
+        peak = jnp.max(s, axis=-1, keepdims=True)
+        w = jnp.exp(s - peak)
+        tot = jnp.sum(w, axis=-1, keepdims=True)
+        log_ref[h] = peak + jnp.log(tot)
+        p = (w * (1.0 / tot)).astype(bf)
+        ctx_ref[:, h * VDIM : (h + 1) * VDIM] = dot_plain(
+            p, kv[:, h * 256 + NOPE : (h + 1) * 256]
+        ).astype(bf)
+    part[...] = dot_plain(ctx_ref[...], wo[...]).astype(bf).reshape(part.shape)
+    reduce = TensorReduce(grid, part, total, scratch)
+    reduce.start()
+    reduce.middle()
+    reduce.last()
+    residual = hidden_ref[...].astype(f32) + total[...]
+    res_ref[...] = residual
+    inverse = lax.rsqrt(jnp.mean(residual * residual, axis=-1, keepdims=True) + epsilon)
+    moe_ref[...] = (residual * inverse * gain_ref[...]).astype(bf)
+    store.wait()
+    reduce.finish()
+
+
+def attention_call(grid, hidden, gain, q, packed, we, wo, seg, own_seg, collective_id):
+    few, n = hidden.shape
+    rows, tokens, heads = q.shape[0], packed.shape[0], q.shape[1] // 256
+    bf, f32 = jnp.bfloat16, jnp.float32
+    any_space = pl.BlockSpec(memory_space=pl.ANY)
+    in_vmem = pl.BlockSpec(memory_space=pltpu.VMEM)
+    return pl.pallas_call(
+        functools.partial(attention_kernel, grid),
+        out_shape=[
+            jax.ShapeDtypeStruct((tokens, heads * 256), bf),
+            jax.ShapeDtypeStruct((heads, rows, 1), f32),
+            jax.ShapeDtypeStruct((rows, heads * VDIM), bf),
+            jax.ShapeDtypeStruct((few, n), f32),
+            jax.ShapeDtypeStruct((few, n), bf),
+        ],
+        in_specs=[in_vmem] * 2 + [any_space] * 4 + [in_vmem] * 2,
+        out_specs=[any_space] + [in_vmem] * 4,
+        scratch_shapes=[
+            pltpu.VMEM(q.shape, bf),
+            pltpu.VMEM(packed.shape, bf),
+            pltpu.VMEM(we.shape, bf),
+            pltpu.VMEM(wo.shape, bf),
+            pltpu.VMEM((tokens, heads * 256), bf),
+            pltpu.VMEM((tokens, 256), bf),
+            pltpu.VMEM((rows, tokens), f32),
+            pltpu.VMEM((grid.ny, 2, few, n), bf),
+            pltpu.VMEM((few, n), f32),
+            pltpu.SemaphoreType.DMA((4,)),
+            pltpu.SemaphoreType.DMA,
+        ]
+        + TensorReduce.scratch(grid, few, n),
+        compiler_params=pltpu.CompilerParams(
+            collective_id=collective_id, has_side_effects=True, vmem_limit_bytes=62 << 20
+        ),
+    )(hidden, gain[None], q, packed, we, wo, seg, own_seg)
+
+
 def rms_scale(values, gain_vec):
     return (
         values * lax.rsqrt(jnp.mean(values * values, axis=-1, keepdims=True) + epsilon) * gain_vec
@@ -1757,117 +2286,71 @@
 
     places = own_group(seq_places(segments))
     own_seg = own_group(segments)
-    own_ordinal = start_row + jnp.arange(tok_rows, dtype=jnp.int32)
-    key_ordinal = jnp.arange(total_rows, dtype=jnp.int32)
-    visible = (key_ordinal[None, :] <= own_ordinal[:, None]) & (
-        (segments[None, :] == own_seg[:, None]) | (segments[None, :] == 0)
+    halfway = ROPE // 2
+    frequency = 10000.0 ** (-jnp.arange(halfway, dtype=jnp.float32) / halfway)
+    angles = places.astype(jnp.float32)[:, None] * frequency[None, :]
+    nothing = jnp.zeros((tok_rows, 128 - ROPE), jnp.float32)
+    cosines, sines = jnp.cos(angles), jnp.sin(angles)
+    cosines = jnp.concatenate([cosines, cosines, nothing], axis=1)
+    sines = jnp.concatenate([sines, -sines, nothing], axis=1)
+    hidden_few = quarter(hidden_in)
+    cot_all = lax.all_gather(quarter(cotangent), ALL, axis=0, tiled=True)
+
+    packed_all, queries, normed_few, compressed = first_call(
+        grid, hidden_in, attn_gain, latent_weight, latent_gain, query_weight, gate_values,
+        expert_routes, cosines, sines, 0,
     )
-    experts_all = EXP_DEV * groups
-    cot_all = lax.all_gather(quarter(cotangent), ALL, axis=0, tiled=True)
-
-    hidden_f = hidden_in.astype(jnp.float32)
-    normed = low(rms_scale(hidden_f, attn_gain))
-    compressed = dot(normed, latent_weight)
-    latents = low(rms_scale(compressed[:, :LATENT], latent_gain))
-    key_rope = low(rotate(compressed[:, LATENT:], places))
-    onehot = expert_routes[:, :, None] == jnp.arange(experts_all, dtype=jnp.int32)
-    gate_rows = jnp.sum(jnp.where(onehot, gate_values[:, :, None], 0.0), axis=1)
-    gate_high = low(gate_rows)
-    gate_low = low(gate_rows - gate_high.astype(jnp.float32))
-    packed = pad_columns(jnp.concatenate([latents, key_rope, gate_high, gate_low], axis=1))
-    packed_all = gather_all(grid, quarter(packed), 0).reshape(total_rows, -1)
-    latents_all = packed_all[:, :LATENT]
-    rope_all = packed_all[:, LATENT : LATENT + ROPE]
-    q_raw = dot(normed, query_weight)
-    heads_here = q_raw.shape[1] // (NOPE + ROPE)
-    q_raw = q_raw.reshape(tok_rows, heads_here, NOPE + ROPE)
-    queries = low(
-        jnp.concatenate([q_raw[..., :NOPE], rotate(q_raw[..., NOPE:], places)], axis=-1)
+    expanded, log_total, merged, residual, moe_in = attention_call(
+        grid, hidden_few, moe_gain, queries, packed_all, expand_weight, output_weight,
+        segments[None, :], own_seg[:, None], 1,
     )
-    expanded = low(dot(latents_all, expand_weight)).reshape(
-        total_rows, heads_here, NOPE + VDIM
-    )
-    key_plain, value_part = expanded[..., :NOPE], expanded[..., NOPE:]
-    scores = score_block(queries, key_plain, rope_all, visible)
-    peak = jnp.max(scores, axis=-1, keepdims=True)
-    weights = jnp.exp(scores - peak)
-    total_weight = jnp.sum(weights, axis=-1, keepdims=True)
-    log_total = peak + jnp.log(total_weight)
-    context = jnp.einsum(
-        "hts,shv->thv", low(weights / total_weight), value_part, preferred_element_type=jnp.float32
-    )
-    merged = low(context).reshape(tok_rows, heads_here * VDIM)
-    attn_out = tensor_scatter(grid, low(dot(merged, output_weight)), 1)
-    residual = quarter(hidden_f) + attn_out
-    moe_in = low(rms_scale(residual, moe_gain))
+    hidden_f = hidden_few.astype(jnp.float32)
+
     moe_all, grad_moe_in, out_rows, acts = experts_call(
         grid, moe_in, cot_all, packed_all, expert_gate, expert_up, expert_down,
         shared_gate, shared_up, shared_down, 2,
     )
-    normed_later, _ = lax.optimization_barrier((quarter(normed), moe_in[:8]))
+    normed_later, _ = lax.optimization_barrier((normed_few, moe_in[:8]))
     normed_all = lax.all_gather(normed_later, ALL, axis=0, tiled=True)
 
-    grad_moe_in, normed_all = lax.optimization_barrier((grad_moe_in, normed_all))
     _, pull_moe = jax.vjp(rms_scale, residual, moe_gain)
     grad_residual, grad_moe_gain = pull_moe(grad_moe_in)
     grad_residual = grad_residual + quarter(cotangent).astype(jnp.float32)
-    grad_res_low = tensor_gather(grid, low(grad_residual), 5)
-    output_part = low(dot(merged.T, grad_res_low))
-    grad_context = low(dot(grad_res_low, output_weight.T)).reshape(tok_rows, heads_here, VDIM)
-    scores = score_block(queries, key_plain, rope_all, visible)
-    probs = jnp.exp(scores - log_total)
-    grad_probs = jnp.einsum(
-        "thv,shv->hts", grad_context, value_part, preferred_element_type=jnp.float32
+    grad_q, key_rows, expand_part, output_rows = attention_back_call(
+        grid,
+        low(grad_residual),
+        output_weight,
+        queries,
+        expanded,
+        packed_all,
+        expand_weight,
+        merged,
+        log_total,
+        segments[None, :],
+        own_seg[:, None],
+        cosines,
+        sines,
+        5,
     )
-    grad_values = jnp.einsum(
-        "hts,thv->shv", low(probs), grad_context, preferred_element_type=jnp.float32
-    )
-    grad_scores = low(probs * (grad_probs - jnp.sum(probs * grad_probs, axis=-1, keepdims=True)))
-    grad_q_plain = scale_factor * jnp.einsum(
-        "hts,shc->thc", grad_scores, key_plain, preferred_element_type=jnp.float32
-    )
-    grad_q_rope = scale_factor * jnp.einsum(
-        "hts,sr->thr", grad_scores, rope_all, preferred_element_type=jnp.float32
-    )
-    grad_k_plain = scale_factor * jnp.einsum(
-        "hts,thc->shc", grad_scores, queries[..., :NOPE], preferred_element_type=jnp.float32
-    )
-    grad_k_rope = scale_factor * jnp.einsum(
-        "hts,thr->sr", grad_scores, queries[..., NOPE:], preferred_element_type=jnp.float32
-    )
-    grad_expanded = low(
-        jnp.concatenate([grad_k_plain, grad_values], axis=-1).reshape(
-            total_rows, heads_here * (NOPE + VDIM)
-        )
-    )
-    expand_part = low(dot(latents_all.T, grad_expanded))
-    grad_keys = jnp.concatenate([dot(grad_expanded, expand_weight.T), grad_k_rope], axis=1)
-    _, pull_qrope = jax.vjp(partial(rotate, places=places), q_raw[..., NOPE:])
-    (grad_q_turned,) = pull_qrope(grad_q_rope)
-    grad_q_low = low(
-        jnp.concatenate([grad_q_plain, grad_q_turned], axis=-1).reshape(tok_rows, -1)
-    )
+    grad_q_low = grad_q.reshape(tok_rows, -1, 256)[:, :, : NOPE + ROPE].reshape(tok_rows, -1)
     normed_rows = low(dot(grad_q_low, query_weight.T))
 
-    weight_rows = jnp.concatenate(
-        [output_part.reshape(LATENT, -1), expand_part], axis=1
-    )
     moe_out, grad_keys, weight_rows, grad_normed, grad_q_all, expert_grads = gradients_call(
-        grid, out_rows, pad_columns(low(grad_keys)), weight_rows, normed_rows, grad_q_low, moe_all, cot_all, acts,
+        grid, out_rows, key_rows, expand_part, normed_rows, grad_q_low, moe_all, cot_all, acts,
         expert_down.shape[1], shared_down.shape[0], 3,
     )
     grad_expert_gate, grad_expert_up, grad_expert_down = expert_grads[:3]
     grad_shared_gate, grad_shared_up, grad_shared_down = expert_grads[3:]
     layer_out = low(residual + moe_out)
     places_few = quarter(places)
-    compressed_few = quarter(compressed)
+    compressed_few = compressed[:, : LATENT + ROPE]
     _, pull_latent = jax.vjp(rms_scale, compressed_few[:, :LATENT], latent_gain)
     grad_plain_latent, grad_latent_gain = pull_latent(grad_keys[:, :LATENT])
     _, pull_krope = jax.vjp(partial(rotate, places=places_few), compressed_few[:, LATENT:])
     (grad_k_turned,) = pull_krope(grad_keys[:, LATENT : LATENT + ROPE])
     grad_comp_low = low(jnp.concatenate([grad_plain_latent, grad_k_turned], axis=-1))
     grad_normed = grad_normed + dot(grad_comp_low, latent_weight.T)
-    _, pull_input = jax.vjp(rms_scale, quarter(hidden_f), attn_gain)
+    _, pull_input = jax.vjp(rms_scale, hidden_f, attn_gain)
     grad_input_norm, grad_attn_gain = pull_input(grad_normed)
     gains = jnp.concatenate([grad_attn_gain, grad_latent_gain, grad_moe_gain])
     gains = jnp.pad(gains, (0, -gains.shape[0] % few)).reshape(few, -1)
@@ -1875,10 +2358,11 @@
     gains_low = low(gains - gains_high.astype(jnp.float32))
     spread = gains.shape[1]
     both = jnp.concatenate([layer_out, low(grad_residual + grad_input_norm)], axis=1)
-    last, weight_rows, both = last_call(
+    last, weight_rows, output_rows, both = last_call(
         grid,
         pad_columns(jnp.concatenate([grad_comp_low, gains_high, gains_low], axis=1)),
         weight_rows,
+        output_rows,
         both,
         8,
     )
@@ -1888,9 +2372,8 @@
     grad_latent_weight = dot(normed_all.T, grad_comp_all)
     grad_query_weight = dot(normed_all.T, grad_q_all)
     layer_out, grad_hidden = both[:, :model_width], both[:, model_width:].astype(jnp.float32)
-    split = weight_rows.shape[1] - expand_weight.shape[1]
-    grad_output_weight = weight_rows[:, :split].reshape(output_weight.shape).astype(jnp.float32)
-    grad_expand_weight = weight_rows[:, split:].astype(jnp.float32)
+    grad_output_weight = output_rows.astype(jnp.float32)
+    grad_expand_weight = weight_rows.astype(jnp.float32)
     return (
         layer_out,
         grad_hidden,

time: 561 us -> 535 us (0.954)
  the two profiles are of different devices: /device:TPU:0 before, /device:TPU:18 now
where the time goes in v4:
time: 535 us; the launch traced here: 525 us
  Pallas kernels  407 us (76%)
  other arithmetic  42 us (8%)
  matrix products  24.5 us (5%)
  local copies, waits for them, and re-layouts  19.2 us (4%)
  waiting for transfers between devices  16.6 us (3%)
  between operations  14.8 us (3%)
    pallas_call x1, Pallas kernels, experts_call(): pl.pallas_call(functools.partial(experts_kernel, grid, pieces), out_shape...  141 us
    pallas_call x1, Pallas kernels, gradients_call(): pl.pallas_call(functools.partial(gradients_kernel, grid, pieces, unit, pl...  97.4 us
    pallas_call x1, Pallas kernels, last_call(): pl.pallas_call(functools.partial(last_kernel, grid), out_shape=[jax.Shape...  65.2 us
    pallas_call x1, Pallas kernels, attention_back_call(): pl.pallas_call(functools.partial(attention_back_kernel, grid, pieces), ou...  49 us
    pallas_call x1, Pallas kernels, attention_call(): pl.pallas_call(functools.partial(attention_kernel, grid), out_shape=[jax....  28.3 us
    pallas_call x1, Pallas kernels, first_call(): pl.pallas_call(functools.partial(first_kernel, grid), out_shape=[jax.Shap...  26.5 us
    dot_general x4, matrix products, dot(): return jnp.dot(left_side, right_side, preferred_element_type=jnp.float32)  24.5 us
    all_gather x1, waiting for transfers between devices, shards(): cot_all = lax.all_gather(quarter(cotangent), ALL, axis=0, tiled=True)  16.5 us
  transfers between devices with their start and end apart: 2, of which 1 were waited for; matrix products, arithmetic and copies ran while one was open for 11% of the time, Pallas kernels for 78%

profile of v4, /device:TPU:18, one launch (start us, length us, event | category | flops | bytes accessed | tf_op | source)
XLA Modules:
  0.0 524.6 jit_solution(12260082521820410938)
XLA Ops:
  7.2 1.7 constant_dynamic-slice_fusion
  8.9 0.0 all-gather.5.cloned.1.call-start
  9.0 0.8 copy.42.gate_ref
  9.8 0.8 copy.43.route_ref
  10.6 0.9 slice_compare_fusion
  11.5 0.1 add_select_fusion
  11.6 0.3 reduce-window.9
  11.9 0.1 slice.71
  12.0 0.1 pad.29.clone
  12.1 0.1 slice_reduce_fusion
  12.2 0.8 fusion.27
  13.0 0.1 dynamic-slice_convert_fusion
  13.0 0.5 multiply_sine_fusion
  13.6 0.1 maximum_maximum_fusion.1
  13.8 1.7 copy-done.1
  15.5 1.9 copy-done.2
  17.4 1.2 copy-done.4
  18.6 0.7 copy-done.7
  19.3 0.7 copy-done.9
  20.0 26.5 %shard_map.289 = (bf16[4,2,2,2,64,640]{5,4,3,2,1,0:T(8,128)(2,1)S(1)}, bf16[256,1024]{1,0:T(8,128)(2,1)S(1)}, bf16[64,2048]{1,0:T(8,128)(2,1)}, f32[64,640]{1,0:T(8,128)S(1)}) custom-call(bf16[256,2048]{1,0:T(8,128)(2,1)S(1)} %copy-done.4, f32[1,2048]{1,0:T(1,128)S(1)} %bitcast.53, bf16[576,2048]{1,0:T(8,128)(2,1)S(1)} %bitcast.52, f32[1,512]{1,0:T(1,128)S(1)} %bitcast.54, ...), custom_call_target="tpu_custom_call" | custom-call | tf_op jit(solution)/shard_map/pallas_call | solution.py:2050
  46.5 1.5 copy-done
  48.0 0.8 copy-done.3
  48.8 0.8 dynamic_slice.20
  49.6 0.8 copy.44.own_seg_ref
  50.4 1.8 fusion.5
  52.2 28.3 %shard_map.290 = (bf16[2048,1024]{1,0:T(8,128)(2,1)}, f32[4,256,1]{2,1,0:T(8,128)}, bf16[256,512]{1,0:T(8,128)(2,1)}, f32[64,2048]{1,0:T(8,128)}, bf16[64,2048]{1,0:T(8,128)(2,1)}) custom-call(bf16[64,2048]{1,0:T(8,128)(2,1)} %get-tuple-element.88.hidden_ref, f32[1,2048]{1,0:T(1,128)} %bitcast.72, bf16[256,1024]{1,0:T(8,128)(2,1)} %copy-done.3, ...), custom_call_target="tpu_custom_call" | custom-call | tf_op jit(solution)/shard_map/pallas_call | solution.py:2159
  80.5 0.1 dynamic-slice_convert_fusion.1
  80.6 0.1 multiply_reduce_fusion.5
  80.7 1.2 multiply_reduce_fusion.2
  81.9 16.5 %all-gather.3.cloned.1.call-done.refs_6_ = bf16[2048,2048]{1,0:T(8,128)(2,1)} async-done(((bf16[64,2048]{1,0:T(8,128)(2,1)}), bf16[2048,2048]{1,0:T(8,128)(2,1)}) %all-gather.3.cloned.1.call-update) | async-done | bytes 8388624 | tf_op jit(solution)/shard_map/all_gather | solution.py:2297
  98.5 141.0 %shard_map.291 = (bf16[4,2,2,2,64,2048]{5,4,3,2,1,0:T(8,128)(2,1)}, f32[64,2048]{1,0:T(8,128)}, bf16[4,2,2,2,64,2048]{5,4,3,2,1,0:T(8,128)(2,1)}, bf16[4,2,2,2,64,4608]{5,4,3,2,1,0:T(8,128)(2,1)}) custom-call(bf16[64,2048]{1,0:T(8,128)(2,1)} %get-tuple-element.49.x_ref, bf16[4,2,2,2,64,2048]{5,4,3,2,1,0:T(8,128)(2,1)} %bitcast.55, ...), custom_call_target="tpu_custom_call" | custom-call | tf_op jit(solution)/shard_map/pallas_call | solution.py:1277
  239.5 1.3 multiply_reduce_fusion.1
  240.8 2.0 fusion.33.x_ref
  242.8 49.0 %shard_map.292 = (bf16[256,1024]{1,0:T(8,128)(2,1)}, bf16[2048,640]{1,0:T(8,128)(2,1)}, bf16[512,1024]{1,0:T(8,128)(2,1)}, bf16[64,2048]{1,0:T(8,128)(2,1)}) custom-call(bf16[64,2048]{1,0:T(8,128)(2,1)} %fusion.33.x_ref, bf16[512,2048]{1,0:T(8,128)(2,1)} %wo_hbm.3, bf16[256,1024]{1,0:T(8,128)(2,1)} %copy-done.3, ...), custom_call_target="tpu_custom_call" | custom-call | tf_op jit(solution)/shard_map/pallas_call | solution.py:1934
  291.8 1.2 copy.48
  293.1 0.9 copy.47.refs_4_
  294.0 3.9 convolution_convert_fusion
  297.9 97.4 %shard_map.293 = (f32[64,2048]{1,0:T(8,128)}, f32[64,640]{1,0:T(8,128)}, bf16[64,1024]{1,0:T(8,128)(2,1)}, f32[64,2048]{1,0:T(8,128)}, bf16[4,2,256,768]{3,2,1,0...) custom-call(bf16[4,2,2,2,64,2048]{5,4,3,2,1,0:T(8,128)(2,1)} %get-tu, ...), custom_call_target="tpu_custom_call" | custom-call | tf_op jit(solution)/shard_map/pallas_call | solution.py:1629
  395.4 1.1 fusion.25
  396.4 0.1 add_convert_fusion.1
  396.5 1.1 multiply_reduce_fusion.4
  397.6 1.0 fusion.13
  398.7 2.5 fusion.8
  401.2 0.1 reshape.174
  401.3 0.7 fusion.16.x_ref
  402.0 1.3 add_convert_fusion
  403.4 0.8 pad_maximum_fusion.t_ref
  404.2 65.2 %shard_map.294 = (bf16[32,64,768]{2,1,0:T(8,128)(2,1)}, bf16[4,2,64,1024]{3,2,1,0:T(8,128)(2,1)}, bf16[4,2,64,2048]{3,2,1,0:T(8,128)(2,1)}, bf16[2,2,64,4096]{3,2,1,0:T(8,128)(2,1)}) custom-call(bf16[64,768]{1,0:T(8,128)(2,1)} %fusion.16.x_ref, bf16[64,1024]{1,0:T(8,128)(2,1)} %get-tuple-element.64.w_ref, bf16[64,2048]{1,0:T(8,128)(2,1)} %get-tuple-element.65.o_ref, ...), custom_call_target="tpu_custom_call" | custom-call | tf_op jit(solution)/shard_map/pallas_call | solution.py:679
  469.4 1.6 convert_reduce_fusion
  471.1 0.1 slice_add_fusion
  471.1 0.1 reshape.176
  471.2 0.6 slice.80
  471.8 3.3 convert_element_type.82
  475.1 3.3 convert_element_type.83
  478.4 0.6 fusion.34
  479.0 1.6 bitcast_convert_fusion.1
  480.7 1.9 slice_convert_fusion
  482.6 0.4 copy-done.20
  483.1 2.8 bitcast_convert_fusion
  485.9 1.4 copy-done.19
  487.3 5.9 %convert_bitcast_fusion.2 = (f32[2048,704]{0,1:T(8,128)}, f32[2048,704]{0,1:T(8,128)}) fusion(bf16[704,2048]{1,0:T(8,128)(2,1)S(1)} %copy-done.19, bf16[704,2048]{1,0:T(8,128)(2,1)S(1)} %copy-done.18), kind=kLoop, calls=%fused_computation.2 | loop fusion | flops 2883584 | bytes 17301504 | tf_op jit(solution)/shard_map/transpose | solution.py:1663
  493.2 5.9 %convert_bitcast_fusion = (f32[2,2048,352]{1,2,0:T(8,128)}, f32[2,2048,352]{1,2,0:T(8,128)}) fusion(bf16[2,352,2048]{2,1,0:T(8,128)(2,1)S(1)} %copy-done.17, bf16[2,352,2048]{2,1,0:T(8,128)(2,1)S(1)} %copy-done.16), kind=kLoop, calls=%fused_computation | loop fusion | flops 2883584 | bytes 17301504 | tf_op jit(solution)/shard_map/transpose | solution.py:1663
  499.2 11.3 %fusion.35 = f32[2048,768]{1,0:T(8,128)} fusion(bf16[2048,2048]{1,0:T(8,128)(2,1)} %all-gather.5.cloned.1.call-done, bf16[2048,768]{1,0:T(8,128)(2,1)S(1)} %bitcast.74), kind=kOutput, calls=%fused_computation.87 | convolution fusion | flops 6442450944 | bytes 17825792 | tf_op jit(solution)/shard_map/dot_general | solution.py:2239
  510.5 6.8 %fusion = f32[2048,576]{0,1:T(8,128)} fusion(bf16[2048,2048]{1,0:T(8,128)(2,1)S(1)} %copy-done.26, bf16[2048,768]{1,0:T(8,128)(2,1)S(1)} %bitcast.69), kind=kOutput, calls=%fused_computation.4 | convolution fusion | flops 4831838208 | bytes 15728640 | tf_op jit(solution)/shard_map/dot_general | solution.py:2239
  (63 shorter events, 0.3 us)
Async XLA Ops:
  7.2 91.3 %all-gather.3.cloned.1.call-start = ((), (), s32[]{:S(2)}) async-start(), calls=%async_computation | async-start | bytes 8650752 | tf_op jit(solution)/shard_map/all_gather | solution.py:2297
  8.9 490.2 %all-gather.5.cloned.1.call-start = ((), (), s32[]{:S(2)}) async-start(), calls=%async_computation.1 | async-start | bytes 8650752 | tf_op jit(solution)/shard_map/all_gather | solution.py:2314
  13.7 32.8 %copy-start.5 = (f32[256,128]{1,0:T(8,128)}, f32[256,128]{1,0:T(8,128)S(1)}, u32[]{:S(2)}) copy-start(f32[256,128]{1,0:T(8,128)S(1)} %get-tuple-element.100.sin_ref) | copy-start | bytes 393220
  13.7 32.8 %copy-start.6 = (f32[256,128]{1,0:T(8,128)}, f32[256,128]{1,0:T(8,128)S(1)}, u32[]{:S(2)}) copy-start(f32[256,128]{1,0:T(8,128)S(1)} %get-tuple-element.101.cos_ref) | copy-start | bytes 393220
  13.8 1.8 copy-start.1
  15.5 1.9 copy-start.2
  17.4 1.2 copy-start.4
  18.6 0.7 copy-start.7
  19.3 0.7 copy-start.9
  46.5 1.5 copy-start
  48.0 0.8 copy-start.3
  98.5 141.0 %copy-start.11 = (f32[64,2048]{1,0:T(8,128)S(1)}, f32[64,2048]{1,0:T(8,128)}, u32[]{:S(2)}) copy-start(f32[64,2048]{1,0:T(8,128)} %get-tuple-element.52) | copy-start | bytes 1572868
  98.5 141.0 %copy-start.25 = (f32[2048]{0:T(1024)S(1)}, f32[2048]{0:T(1024)}, u32[]{:S(2)}) copy-start(f32[2048]{0:T(1024)} %param.25) | copy-start | bytes 24580
  297.9 98.6 %copy-start.10 = (f32[512]{0:T(512)S(1)}, f32[512]{0:T(512)}, u32[]{:S(2)}) copy-start(f32[512]{0:T(512)} %param.22) | copy-start | bytes 6148
  297.9 100.7 %copy-start.8 = (f32[2048]{0:T(1024)S(1)}, f32[2048]{0:T(1024)}, u32[]{:S(2)}) copy-start(f32[2048]{0:T(1024)} %param.19) | copy-start | bytes 24580
  297.9 100.7 %copy-start.13 = (bf16[64,2048]{1,0:T(8,128)(2,1)S(1)}, bf16[64,2048]{1,0:T(8,128)(2,1)}, u32[]{:S(2)}) copy-start(bf16[64,2048]{1,0:T(8,128)(2,1)} %get-tuple-element.88.hidden_ref) | copy-start | bytes 786436
  395.4 6.7 %copy-start.12 = (f32[64,2048]{1,0:T(8,128)S(1)}, f32[64,2048]{1,0:T(8,128)}, u32[]{:S(2)}) copy-start(f32[64,2048]{1,0:T(8,128)} %get-tuple-element.51) | copy-start | bytes 1572868
  395.4 6.7 %copy-start.23 = (f32[64,2048]{1,0:T(8,128)S(1)}, f32[64,2048]{1,0:T(8,128)}, u32[]{:S(2)}) copy-start(f32[64,2048]{1,0:T(8,128)} %get-tuple-element.66) | copy-start | bytes 1572868
  403.4 68.4 %copy-start.15 = (bf16[704,2048]{1,0:T(8,128)(2,1)S(1)}, bf16[704,2048]{1,0:T(8,128)(2,1)}, u32[]{:S(2)}) copy-start(bf16[704,2048]{1,0:T(8,128)(2,1)} %get-tuple-element.75) | copy-start | bytes 8650756
  471.8 3.3 copy-start.14
  475.1 3.9 copy-start.22
  478.4 2.2 copy-start.21
  480.7 2.4 copy-start.20
  483.1 2.8 copy-start.18
  483.1 4.2 copy-start.19
  487.3 5.9 %copy-start.16 = (bf16[2,352,2048]{2,1,0:T(8,128)(2,1)S(1)}, bf16[2,352,2048]{2,1,0:T(8,128)(2,1)}, u32[]{:S(2)}) copy-start(bf16[2,352,2048]{2,1,0:T(8,128)(2,1)} %get-tuple-element.76) | copy-start | bytes 8650756
  487.3 5.9 %copy-start.17 = (bf16[2,352,2048]{2,1,0:T(8,128)(2,1)S(1)}, bf16[2,352,2048]{2,1,0:T(8,128)(2,1)}, u32[]{:S(2)}) copy-start(bf16[2,352,2048]{2,1,0:T(8,128)(2,1)} %get-tuple-element.77) | copy-start | bytes 8650756
  493.2 5.9 %copy-start.27 = (bf16[4,2,256,768]{3,2,1,0:T(8,128)(2,1)S(1)}, bf16[4,2,256,768]{3,2,1,0:T(8,128)(2,1)}, u32[]{:S(2)}) copy-start(bf16[4,2,256,768]{3,2,1,0:T(8,128)(2,1)} %get-tuple-element.70) | copy-start | bytes 9437188
  499.2 11.3 %copy-start.24 = (bf16[32,64,768]{2,1,0:T(8,128)(2,1)S(1)}, bf16[32,64,768]{2,1,0:T(8,128)(2,1)}, u32[]{:S(2)}) copy-start(bf16[32,64,768]{2,1,0:T(8,128)(2,1)} %get-tuple-element.68) | copy-start | bytes 9437188
  499.2 11.3 %copy-start.26 = (bf16[2048,2048]{1,0:T(8,128)(2,1)S(1)}, bf16[2048,2048]{1,0:T(8,128)(2,1)}, u32[]{:S(2)}) copy-start(bf16[2048,2048]{1,0:T(8,128)(2,1)} %all-gather.5.cloned.1.call-done) | copy-start | bytes 25165828
Sparse Core Ops, SparseCore 0:
  11.5 86.9 all-gather.2
  101.3 91.9 all-gather.4

commit v5 on v4

--- a/solution.py
+++ b/solution.py
@@ -38,6 +38,10 @@
 
     def block(self, a, b, y, c):
         return ((a * self.nb + b) * self.ny + y) * 2 + c
+
+
+def microseconds(time):
+    return pl.CostEstimate(flops=time * 1000**3, bytes_accessed=0, transcendentals=0)
 
 
 def wrap(i, n):
@@ -659,33 +663,22 @@
                 self.copy_b(i, k).wait_send()
 
 
-def last_kernel(
-    grid, x_ref, w_ref, o_ref, t_ref, out_ref, w_out, o_out, t_out, own_sem, ss, rs, cs, cr, *scratch
-):
-    plane = TensorGather.count + PlaneGather.count
-    gathers = [
-        TensorGather(grid, t_ref, t_out, scratch[: TensorGather.count]),
-        PlaneGather(grid, o_ref, o_out, scratch[TensorGather.count : plane]),
-        PlaneGather(grid, w_ref, w_out, scratch[plane:]),
-    ]
-    gather_kernel(grid, x_ref, out_ref, own_sem, ss, rs, cs, cr, gathers)
-
-
-def last_call(grid, x, w, o, t, collective_id):
+def last_kernel(grid, x_ref, t_ref, out_ref, t_out, own_sem, ss, rs, cs, cr, *scratch):
+    gather_kernel(grid, x_ref, out_ref, own_sem, ss, rs, cs, cr, [TensorGather(grid, t_ref, t_out, scratch)])
+
+
+def last_call(grid, x, t, collective_id):
     r, n = x.shape
     blocks = grid.na * grid.nb * grid.ny
     any_space = pl.BlockSpec(memory_space=pl.ANY)
-    plane = (grid.na, grid.nb)
     outs = pl.pallas_call(
         functools.partial(last_kernel, grid),
         out_shape=[
             jax.ShapeDtypeStruct((grid.size, r, n), x.dtype),
-            jax.ShapeDtypeStruct(plane + w.shape, w.dtype),
-            jax.ShapeDtypeStruct(plane + o.shape, o.dtype),
             jax.ShapeDtypeStruct((grid.ny, 2) + t.shape, t.dtype),
         ],
-        in_specs=[any_space] * 4,
-        out_specs=[any_space] * 4,
+        in_specs=[any_space] * 2,
+        out_specs=[any_space] * 2,
         scratch_shapes=[
             pltpu.SemaphoreType.DMA,
             pltpu.SemaphoreType.DMA((gather_sends(grid),)),
@@ -693,12 +686,11 @@
             pltpu.SemaphoreType.DMA((2 * blocks,)),
             pltpu.SemaphoreType.DMA((2 * blocks,)),
         ]
-        + TensorGather.scratch(grid)
-        + PlaneGather.scratch(grid) * 2,
+        + TensorGather.scratch(grid),
+        cost_estimate=microseconds(32),
         compiler_params=pltpu.CompilerParams(collective_id=collective_id, has_side_effects=True),
-    )(x, w, o, t)
-    whole = lambda v: v.reshape(-1, v.shape[-1])
-    return outs[0], whole(outs[1]), whole(outs[2]), whole(outs[3])
+    )(x, t)
+    return outs[0], outs[1].reshape(-1, t.shape[-1])
 
 
 def dot_rows(left_side, right_side):
@@ -1309,6 +1301,7 @@
             sems(pieces, ny - 1), sems(pieces, ny - 1),
             sems(pieces, na - 1), sems(pieces, na - 1),
         ],
+        cost_estimate=microseconds(130),
         compiler_params=pltpu.CompilerParams(
             collective_id=collective_id, has_side_effects=True, vmem_limit_bytes=63 << 20
         ),
@@ -1333,8 +1326,8 @@
         vm = lambda *s: pltpu.VMEM(s, jnp.bfloat16)
         return [
             vm(nb, ny, na, r, width), vm(nb, ny, na, r, width),
-            vm(nb, ny - 1, na, head, width), vm(ny, nb - 1, na, r - head, width),
-            vm(nb - 1, na, head, width), vm(ny - 1, na, r - head, width), vm(na - 1, r, width),
+            vm(nb, ny - 1, na, head, width), vm(ny, nb - 1, na, max(16, r - head), width),
+            vm(nb - 1, na, head, width), vm(ny - 1, na, max(16, r - head), width), vm(na - 1, r, width),
             sems(nb, ny), sems(nb, ny), sems(nb, ny),
             sems(nb, ny - 1), sems(nb, ny - 1), sems(ny, nb - 1), sems(ny, nb - 1),
             sems(nb - 1), sems(nb - 1), sems(ny - 1), sems(ny - 1), sems(na - 1), sems(na - 1),
@@ -1344,7 +1337,17 @@
 
     @staticmethod
     def head(r):
-        return max(16, r * 3 // 4 // 16 * 16)
+        return r
+
+    @staticmethod
+    def schedule(sums):
+        stages = [[one.core, one.first, one.second] for one in sums]
+        work = []
+        for beat in range(len(sums) + 2):
+            for back in range(3):
+                if 0 <= beat - back < len(sums):
+                    work.append(stages[beat - back][back])
+        return work
 
     def __init__(self, grid, source, out, scratch):
         self.grid, self.source, self.out = grid, source, out
@@ -1356,7 +1359,8 @@
         self.spot = grid.here()
         r = self.acc.shape[3]
         head = Reduce.head(r)
-        self.upper = (pl.ds(0, head), pl.ds(head, r - head))
+        self.both = head < r
+        self.upper = (pl.ds(0, head), pl.ds(head, r - head) if self.both else None)
         self.spots = [(j, k) for j in reversed(range(grid.nb)) for k in reversed(range(grid.ny))]
 
     def remote(self, src, dst, ss, rs, where):
@@ -1435,7 +1439,7 @@
             self.add(self.acc.at[j, k], whole, self.core_in.at[j, k], self.core_r.at[j, k])
             if k:
                 self.copy10(j, k).start()
-            if j:
+            if j and self.both:
                 self.copy11(j, k).start()
 
     def first(self):
@@ -1445,7 +1449,7 @@
                 self.add(self.acc.at[j, 0], self.upper[0], self.in10.at[j, k - 1], self.r10.at[j, k - 1])
             if j:
                 self.copy20(j).start()
-        for k in reversed(range(ny)):
+        for k in reversed(range(ny if self.both else 0)):
             for j in range(1, nb):
                 self.add(self.acc.at[0, k], self.upper[1], self.in11.at[k, j - 1], self.r11.at[k, j - 1])
             if k:
@@ -1454,7 +1458,7 @@
     def second(self):
         for j in range(1, self.grid.nb):
             self.add(self.acc.at[0, 0], self.upper[0], self.in20.at[j - 1], self.r20.at[j - 1])
-        for k in range(1, self.grid.ny):
+        for k in range(1, self.grid.ny if self.both else 0):
             self.add(self.acc.at[0, 0], self.upper[1], self.in21.at[k - 1], self.r21.at[k - 1])
         for i in range(1, self.grid.na):
             self.copy_a(i).start()
@@ -1471,11 +1475,11 @@
             self.core_copy(j, k).wait_send()
             if k:
                 self.copy10(j, k).wait_send()
-            if j:
+            if j and self.both:
                 self.copy11(j, k).wait_send()
         for j in range(1, self.grid.nb):
             self.copy20(j).wait_send()
-        for k in range(1, self.grid.ny):
+        for k in range(1, self.grid.ny if self.both else 0):
             self.copy21(k).wait_send()
         for i in range(1, self.grid.na):
             self.copy_a(i).wait_send()
@@ -1529,12 +1533,7 @@
         big_loads[1].start()
     big_loads[0].wait()
 
-    stages = [[one.core, one.first, one.second] for one in sums]
-    work = []
-    for beat in range(len(sums) + 2):
-        for back in range(3):
-            if 0 <= beat - back < len(sums):
-                work.append(stages[beat - back][back])
+    work = Reduce.schedule(sums)
     for p, one in enumerate(flat_sums):
         work.insert(min(len(work), 3 + 3 * p), one.middle)
     for i in range(1, grid.na):
@@ -1644,6 +1643,7 @@
         in_specs=[any_space] * 8,
         out_specs=[in_vmem] * 4 + [any_space] * 7,
         scratch_shapes=scratch,
+        cost_estimate=microseconds(90),
         compiler_params=pltpu.CompilerParams(
             collective_id=collective_id, has_side_effects=True, vmem_limit_bytes=62 << 20
         ),
@@ -1957,39 +1957,65 @@
         ]
         + TensorGather.scratch(grid)
         + PlaneReduce.scratch(grid, share, n // pieces) * pieces,
+        cost_estimate=microseconds(50),
         compiler_params=pltpu.CompilerParams(
             collective_id=collective_id, has_side_effects=True, vmem_limit_bytes=62 << 20
         ),
     )(x, wo, q, kv, packed, we, context, log_total, seg, own_seg, cosines, sines)
 
 
-def first_kernel(
+def front_kernel(
     grid,
     hidden_ref,
     gain_ref,
-    wl_hbm,
     lgain_ref,
-    wq_hbm,
+    mgain_ref,
     gate_ref,
     route_ref,
     cos_ref,
     sin_ref,
-    packed_ref,
-    q_ref,
+    seg_ref,
+    own_seg_ref,
+    cot_hbm,
+    wl_hbm,
+    wq_hbm,
+    we_hbm,
+    wo_hbm,
+    packed_hbm,
+    cot_all,
+    kv_ref,
+    q,
     normed_ref,
     comp_ref,
+    log_ref,
+    ctx_ref,
+    res_ref,
+    moe_ref,
     wl,
     wq,
+    we,
+    wo,
     normed,
     mine,
+    packed,
+    kv,
+    kcat,
+    bias,
+    part,
+    total,
     load_sem,
+    kv_sem,
+    packed_sem,
     *scratch,
 ):
     f32, bf = jnp.float32, jnp.bfloat16
-    rows, few = hidden_ref.shape[0], mine.shape[0]
-    heads = q_ref.shape[1] // 256
+    rows, few, tokens = hidden_ref.shape[0], mine.shape[0], kv.shape[0]
+    heads = q.shape[1] // 256
+    scale = (NOPE + ROPE) ** (-0.5)
     a, b, y, c = grid.here()
-    pairs = ((wl_hbm, wl.at[pl.ds(0, LATENT + ROPE)]), (wq_hbm, wq))
+    pairs = (
+        (wl_hbm, wl.at[pl.ds(0, LATENT + ROPE)]), (wq_hbm, wq), (we_hbm, we), (wo_hbm, wo),
+    )
     loads = [pltpu.make_async_copy(src, dst, load_sem.at[i]) for i, (src, dst) in enumerate(pairs)]
     for load in loads:
         load.start()
@@ -2000,7 +2026,8 @@
     def rms(v, gain):
         return v * lax.rsqrt(jnp.mean(v * v, axis=-1, keepdims=True) + epsilon) * gain
 
-    normed_few = rms(hidden_ref[at].astype(f32), gain_ref[...]).astype(bf)
+    hidden_few = hidden_ref[at].astype(f32)
+    normed_few = rms(hidden_few, gain_ref[...]).astype(bf)
     normed_ref[...] = normed_few
     loads[0].wait()
     comp = dot_rows(normed_few, wl[...])
@@ -2015,117 +2042,58 @@
         tail += jnp.where(lane == expert, high, 0.0)
         tail += jnp.where(lane == expert + EXP_DEV * grid.na * grid.nb, gate - high, 0.0)
     mine[:, LATENT:] = tail.astype(bf)
-    gather = GatherAll(grid, mine, packed_ref, scratch, halves=1)
+    gather = GatherAll(grid, mine, packed_hbm, scratch[:5], halves=1)
     gather.start()
+    cots = GatherAll(grid, cot_hbm.at[at], cot_all, scratch[5:10])
+    cots.start()
     normed[...] = rms(hidden_ref[...].astype(f32), gain_ref[...]).astype(bf)
     loads[1].wait()
     gather.group()
-    for event in gather.others[: len(gather.others) // 3]:
+    third = len(gather.others) // 3
+    for event in gather.others[:third]:
         gather.relay(*event)
     raw = dot_plain(normed[...], wq[...])
-    total = raw.shape[1]
+    width = raw.shape[1]
     for h in range(heads):
         step = h * (NOPE + ROPE)
-        moved = raw if step == 0 else pltpu.roll(raw, total - step, 1)
-        q_ref[:, h * 256 : h * 256 + NOPE] = moved[:, :NOPE].astype(bf)
-        q_ref[:, h * 256 + NOPE : (h + 1) * 256] = turn_back(
+        moved = raw if step == 0 else pltpu.roll(raw, width - step, 1)
+        q[:, h * 256 : h * 256 + NOPE] = moved[:, :NOPE].astype(bf)
+        q[:, h * 256 + NOPE : (h + 1) * 256] = turn_back(
             moved[:, NOPE : NOPE + 128], cos_ref[...], -sin_ref[...]
         ).astype(bf)
-    for event in gather.others[len(gather.others) // 3 :]:
+    for event in gather.others[third:]:
         gather.relay(*event)
-    gather.finish()
-
-
-def first_call(
-    grid, hidden, attn_gain, latent_weight, latent_gain, query_weight, gates, routes, cosines, sines,
-    collective_id,
-):
-    rows, n = hidden.shape
-    few = rows // (2 * grid.ny)
-    heads = query_weight.shape[1] // (NOPE + ROPE)
-    bf, f32 = jnp.bfloat16, jnp.float32
-    any_space = pl.BlockSpec(memory_space=pl.ANY)
-    in_vmem = pl.BlockSpec(memory_space=pltpu.VMEM)
-    width = LATENT + 128
-    outs = pl.pallas_call(
-        functools.partial(first_kernel, grid),
-        out_shape=[
-            jax.ShapeDtypeStruct((grid.na, grid.nb, grid.ny, 2, few, width), bf),
-            jax.ShapeDtypeStruct((rows, heads * 256), bf),
-            jax.ShapeDtypeStruct((few, n), bf),
-            jax.ShapeDtypeStruct((few, width), f32),
-        ],
-        in_specs=[in_vmem, in_vmem, any_space, in_vmem, any_space] + [in_vmem] * 4,
-        out_specs=[any_space] + [in_vmem] * 3,
-        scratch_shapes=[
-            pltpu.VMEM((width, n), bf),
-            pltpu.VMEM(query_weight.shape, bf),
-            pltpu.VMEM((rows, n), bf),
-            pltpu.VMEM((few, width), bf),
-            pltpu.SemaphoreType.DMA((2,)),
-        ]
-        + GatherAll.scratch(grid),
-        compiler_params=pltpu.CompilerParams(
-            collective_id=collective_id, has_side_effects=True, vmem_limit_bytes=40 << 20
-        ),
-    )(
-        hidden, attn_gain[None], latent_weight.T, latent_gain[None], query_weight, gates, routes,
-        cosines, sines,
-    )
-    return outs[0].reshape(-1, width), outs[1], outs[2], outs[3]
-
-
-def attention_kernel(
-    grid,
-    hidden_ref,
-    gain_ref,
-    q_hbm,
-    packed_hbm,
-    we_hbm,
-    wo_hbm,
-    seg_ref,
-    own_seg_ref,
-    kv_ref,
-    log_ref,
-    ctx_ref,
-    res_ref,
-    moe_ref,
-    q,
-    packed,
-    we,
-    wo,
-    kv,
-    kcat,
-    bias,
-    part,
-    total,
-    load_sem,
-    kv_sem,
-    *scratch,
-):
-    f32, bf = jnp.float32, jnp.bfloat16
-    rows, tokens = q.shape[0], kv.shape[0]
-    heads = q.shape[1] // 256
-    few = res_ref.shape[0]
-    scale = (NOPE + ROPE) ** (-0.5)
-    a, b, y, c = grid.here()
-    pairs = ((packed_hbm, packed), (we_hbm, we), (q_hbm, q), (wo_hbm, wo))
-    loads = [pltpu.make_async_copy(src, dst, load_sem.at[i]) for i, (src, dst) in enumerate(pairs)]
-    for load in loads:
-        load.start()
-    greet_tensor(grid)
+    early = 2 * (grid.na - 1)
+    for event in cots.near + cots.others[:early]:
+        cots.relay(*event)
     ordinal = (a * grid.nb + b) * rows + lax.broadcasted_iota(jnp.int32, (rows, tokens), 0)
     key = lax.broadcasted_iota(jnp.int32, (rows, tokens), 1)
     seg = seg_ref[...]
     seen = (key <= ordinal) & ((seg == own_seg_ref[...]) | (seg == 0))
     bias[...] = jnp.where(seen, 0.0, masked_out)
-    for load in loads:
-        load.wait()
+    gather.finish()
+    load = pltpu.make_async_copy(packed_hbm, packed, packed_sem)
+    load.start()
+
+    passing = [functools.partial(cots.relay, *event) for event in cots.others[early:]]
+    at_point = {}
+    for m, event in enumerate(passing):
+        at_point.setdefault(m * (heads + 1) // len(passing), []).append(event)
+
+    def hook(point):
+        for event in at_point.get(point, ()):
+            event()
+
+    load.wait()
+    hook(0)
+    flat = packed[...].reshape(tokens, packed.shape[-1])
     lane = lax.broadcasted_iota(jnp.int32, (tokens, 128), 1)
-    kcat[:, NOPE:] = jnp.where(lane < ROPE, packed[:, LATENT:].astype(f32), 0.0).astype(bf)
-    kv[...] = dot_plain(packed[:, :LATENT], we[...]).astype(bf)
+    kcat[:, NOPE:] = jnp.where(lane < ROPE, flat[:, LATENT:].astype(f32), 0.0).astype(bf)
+    loads[2].wait()
+    kv[...] = dot_plain(flat[:, :LATENT], we[...]).astype(bf)
     store = pltpu.make_async_copy(kv, kv_ref, kv_sem)
     store.start()
+    hook(1)
     for h in range(heads):
         kcat[:, :NOPE] = kv[:, h * 256 : h * 256 + NOPE]
         s = dot_rows(q[:, h * 256 : (h + 1) * 256], kcat[...]) * scale + bias[...]
@@ -2137,41 +2105,61 @@
         ctx_ref[:, h * VDIM : (h + 1) * VDIM] = dot_plain(
             p, kv[:, h * 256 + NOPE : (h + 1) * 256]
         ).astype(bf)
+        hook(2 + h)
+    loads[3].wait()
     part[...] = dot_plain(ctx_ref[...], wo[...]).astype(bf).reshape(part.shape)
-    reduce = TensorReduce(grid, part, total, scratch)
+    reduce = TensorReduce(grid, part, total, scratch[10:])
     reduce.start()
     reduce.middle()
     reduce.last()
-    residual = hidden_ref[...].astype(f32) + total[...]
+    residual = hidden_ref[at].astype(f32) + total[...]
     res_ref[...] = residual
-    inverse = lax.rsqrt(jnp.mean(residual * residual, axis=-1, keepdims=True) + epsilon)
-    moe_ref[...] = (residual * inverse * gain_ref[...]).astype(bf)
+    moe_ref[...] = rms(residual, mgain_ref[...]).astype(bf)
     store.wait()
+    for k in range(grid.ny):
+        cots.shared(0, k, 0)
+    cots.own().wait()
+    cots.finish()
     reduce.finish()
 
 
-def attention_call(grid, hidden, gain, q, packed, we, wo, seg, own_seg, collective_id):
-    few, n = hidden.shape
-    rows, tokens, heads = q.shape[0], packed.shape[0], q.shape[1] // 256
+def front_call(
+    grid, hidden, cotangent, attn_gain, latent_gain, moe_gain, gates, routes, cosines, sines, seg, own_seg,
+    latent_weight, query_weight, expand_weight, output_weight, collective_id,
+):
+    rows, n = hidden.shape
+    few = rows // (2 * grid.ny)
+    tokens = grid.size * few
+    heads = query_weight.shape[1] // (NOPE + ROPE)
     bf, f32 = jnp.bfloat16, jnp.float32
     any_space = pl.BlockSpec(memory_space=pl.ANY)
     in_vmem = pl.BlockSpec(memory_space=pltpu.VMEM)
-    return pl.pallas_call(
-        functools.partial(attention_kernel, grid),
+    width = LATENT + 128
+    lay = (grid.na, grid.nb, grid.ny, 2, few)
+    outs = pl.pallas_call(
+        functools.partial(front_kernel, grid),
         out_shape=[
+            jax.ShapeDtypeStruct(lay + (width,), bf),
+            jax.ShapeDtypeStruct(lay + (n,), bf),
             jax.ShapeDtypeStruct((tokens, heads * 256), bf),
+            jax.ShapeDtypeStruct((rows, heads * 256), bf),
+            jax.ShapeDtypeStruct((few, n), bf),
+            jax.ShapeDtypeStruct((few, width), f32),
             jax.ShapeDtypeStruct((heads, rows, 1), f32),
             jax.ShapeDtypeStruct((rows, heads * VDIM), bf),
             jax.ShapeDtypeStruct((few, n), f32),
             jax.ShapeDtypeStruct((few, n), bf),
         ],
-        in_specs=[in_vmem] * 2 + [any_space] * 4 + [in_vmem] * 2,
-        out_specs=[any_space] + [in_vmem] * 4,
+        in_specs=[in_vmem] * 10 + [any_space] * 5,
+        out_specs=[any_space] * 3 + [in_vmem] * 7,
         scratch_shapes=[
-            pltpu.VMEM(q.shape, bf),
-            pltpu.VMEM(packed.shape, bf),
-            pltpu.VMEM(we.shape, bf),
-            pltpu.VMEM(wo.shape, bf),
+            pltpu.VMEM((width, n), bf),
+            pltpu.VMEM(query_weight.shape, bf),
+            pltpu.VMEM(expand_weight.shape, bf),
+            pltpu.VMEM(output_weight.shape, bf),
+            pltpu.VMEM((rows, n), bf),
+            pltpu.VMEM((few, width), bf),
+            pltpu.VMEM(lay + (width,), bf),
             pltpu.VMEM((tokens, heads * 256), bf),
             pltpu.VMEM((tokens, 256), bf),
             pltpu.VMEM((rows, tokens), f32),
@@ -2179,12 +2167,19 @@
             pltpu.VMEM((few, n), f32),
             pltpu.SemaphoreType.DMA((4,)),
             pltpu.SemaphoreType.DMA,
+            pltpu.SemaphoreType.DMA,
         ]
+        + GatherAll.scratch(grid) * 2
         + TensorReduce.scratch(grid, few, n),
+        cost_estimate=microseconds(74),
         compiler_params=pltpu.CompilerParams(
             collective_id=collective_id, has_side_effects=True, vmem_limit_bytes=62 << 20
         ),
-    )(hidden, gain[None], q, packed, we, wo, seg, own_seg)
+    )(
+        hidden, attn_gain[None], latent_gain[None], moe_gain[None], gates, routes, cosines, sines,
+        seg, own_seg, cotangent, latent_weight.T, query_weight, expand_weight, output_weight,
+    )
+    return [outs[0].reshape(tokens, width), outs[1].reshape(tokens, n), *outs[2:]]
 
 
 def rms_scale(values, gain_vec):
@@ -2294,15 +2289,13 @@
     cosines = jnp.concatenate([cosines, cosines, nothing], axis=1)
     sines = jnp.concatenate([sines, -sines, nothing], axis=1)
     hidden_few = quarter(hidden_in)
-    cot_all = lax.all_gather(quarter(cotangent), ALL, axis=0, tiled=True)
-
-    packed_all, queries, normed_few, compressed = first_call(
-        grid, hidden_in, attn_gain, latent_weight, latent_gain, query_weight, gate_values,
-        expert_routes, cosines, sines, 0,
-    )
-    expanded, log_total, merged, residual, moe_in = attention_call(
-        grid, hidden_few, moe_gain, queries, packed_all, expand_weight, output_weight,
-        segments[None, :], own_seg[:, None], 1,
+
+    (
+        packed_all, cot_all, expanded, queries, normed_few, compressed, log_total, merged, residual, moe_in,
+    ) = front_call(
+        grid, hidden_in, cotangent, attn_gain, latent_gain, moe_gain, gate_values, expert_routes,
+        cosines, sines, segments[None, :], own_seg[:, None],
+        latent_weight, query_weight, expand_weight, output_weight, 0,
     )
     hidden_f = hidden_few.astype(jnp.float32)
 
@@ -2313,6 +2306,7 @@
     normed_later, _ = lax.optimization_barrier((normed_few, moe_in[:8]))
     normed_all = lax.all_gather(normed_later, ALL, axis=0, tiled=True)
 
+    grad_moe_in, normed_all = lax.optimization_barrier((grad_moe_in, normed_all))
     _, pull_moe = jax.vjp(rms_scale, residual, moe_gain)
     grad_residual, grad_moe_gain = pull_moe(grad_moe_in)
     grad_residual = grad_residual + quarter(cotangent).astype(jnp.float32)
@@ -2339,6 +2333,9 @@
         grid, out_rows, key_rows, expand_part, normed_rows, grad_q_low, moe_all, cot_all, acts,
         expert_down.shape[1], shared_down.shape[0], 3,
     )
+    output_rows, weight_rows = lax.optimization_barrier((output_rows, weight_rows))
+    output_rows = lax.all_gather(output_rows, "expert", axis=0, tiled=True)
+    weight_rows = lax.all_gather(weight_rows, "expert", axis=0, tiled=True)
     grad_expert_gate, grad_expert_up, grad_expert_down = expert_grads[:3]
     grad_shared_gate, grad_shared_up, grad_shared_down = expert_grads[3:]
     layer_out = low(residual + moe_out)
@@ -2358,11 +2355,9 @@
     gains_low = low(gains - gains_high.astype(jnp.float32))
     spread = gains.shape[1]
     both = jnp.concatenate([layer_out, low(grad_residual + grad_input_norm)], axis=1)
-    last, weight_rows, output_rows, both = last_call(
+    last, both = last_call(
         grid,
         pad_columns(jnp.concatenate([grad_comp_low, gains_high, gains_low], axis=1)),
-        weight_rows,
-        output_rows,
         both,
         8,
     )

time: 535 us -> 512 us (0.957)
  the two profiles are of different devices: /device:TPU:18 before, /device:TPU:0 now
where the time goes in v5:
time: 512 us; the launch traced here: 502 us
  Pallas kernels  393 us (77%)
  other arithmetic  49 us (10%)
  matrix products  22.5 us (4%)
  waiting for transfers between devices  14.8 us (3%)
  between operations  14.4 us (3%)
  local copies, waits for them, and re-layouts  8.48 us (2%)
    pallas_call x1, Pallas kernels, experts_call(): pl.pallas_call(functools.partial(experts_kernel, grid, pieces), out_shape...  142 us
    pallas_call x1, Pallas kernels, gradients_call(): pl.pallas_call(functools.partial(gradients_kernel, grid, pieces, unit, pl...  90.9 us
    pallas_call x1, Pallas kernels, front_call(): pl.pallas_call(functools.partial(front_kernel, grid), out_shape=[jax.Shap...  73.9 us
    pallas_call x1, Pallas kernels, attention_back_call(): pl.pallas_call(functools.partial(attention_back_kernel, grid, pieces), ou...  53.1 us
    pallas_call x1, Pallas kernels, last_call(): pl.pallas_call(functools.partial(last_kernel, grid), out_shape=[jax.Shape...  33.3 us
    dot_general x4, matrix products, dot(): return jnp.dot(left_side, right_side, preferred_element_type=jnp.float32)  22.5 us
    all_gather x1, waiting for transfers between devices, shards(): output_rows = lax.all_gather(output_rows, 'expert', axis=0, tiled=True)  14.7 us
  transfers between devices with their start and end apart: 3, of which 1 were waited for; matrix products, arithmetic and copies ran while one was open for 12% of the time, Pallas kernels for 35%

profile of v5, /device:TPU:0, one launch (start us, length us, event | category | flops | bytes accessed | tf_op | source)
XLA Modules:
  0.0 502.3 jit_solution(13188339088602403255)
XLA Ops:
  7.2 0.0 all-gather.4.cloned.1.call-start
  7.3 0.8 slice_compare_fusion
  8.1 0.8 dynamic_slice.18
  8.9 0.1 add_select_fusion
  8.9 0.3 reduce-window.9
  9.2 0.1 slice.71
  9.3 0.1 slice_reduce_fusion
  9.5 0.8 fusion.27
  10.2 0.1 dynamic-slice_convert_fusion
  10.3 0.8 copy.44.own_seg_ref
  11.1 1.5 copy.42.gate_ref
  12.6 1.5 copy.43.route_ref
  14.1 0.1 pad.29.clone
  14.2 0.5 multiply_sine_fusion
  14.7 0.8 maximum_maximum_fusion.1
  15.6 73.9 %shard_map.289 = (bf16[4,2,2,2,64,640]{5,4,3,2,1,0:T(8,128)(2,1)}, bf16[4,2,2,2,64,2048]{5,4,3,2,1,0:T(8,128)(2,1)}, bf16[2048,1024]{1,0:T(8,128)(2,1)}, bf16[25...) custom-call(bf16[256,2048]{1,0:T(8,128)(2,1)} %hidden_ref.1, ...), custom_call_target="tpu_custom_call" | custom-call | flops 73999998976 | tf_op jit(solution)/shard_map/pallas_call | solution.py:2139
  89.5 0.0 all-gather.4.cloned.1.call-update
  89.5 0.0 all-gather.6.cloned.1.call-start
  89.6 1.1 fusion.5
  90.7 0.6 dynamic-slice_convert_fusion.1
  91.3 1.0 multiply_reduce_fusion.5
  92.3 0.0 copy-start.21
  92.3 1.2 multiply_reduce_fusion.2
  93.5 0.5 fusion.31
  94.0 0.5 fusion.30
  94.6 141.9 %shard_map.290 = (bf16[4,2,2,2,64,2048]{5,4,3,2,1,0:T(8,128)(2,1)}, f32[64,2048]{1,0:T(8,128)}, bf16[4,2,2,2,64,2048]{5,4,3,2,1,0:T(8,128)(2,1)}, bf16[4,2,2,2,64,4608]{5,4,3,2,1,0:T(8,128)(2,1)}) custom-call(bf16[64,2048]{1,0:T(8,128)(2,1)} %get-tuple-element.50.x_ref, bf16[4,2,2,2,64,2048]{5,4,3,2,1,0:T(8,128)(2,1)} %get-tuple-element.51.dz_ref, ...), custom_call_target="tpu_custom_call" | custom-call | flops 130000003072 | tf_op jit(solution)/shard_map/pallas_call | solution.py:1269
  236.5 0.0 all-gather.4.cloned.1.call-done
  236.5 1.3 multiply_reduce_fusion.1
  237.8 2.0 fusion.33.x_ref
  239.9 53.1 %shard_map.291 = (bf16[256,1024]{1,0:T(8,128)(2,1)}, bf16[2048,640]{1,0:T(8,128)(2,1)}, bf16[512,1024]{1,0:T(8,128)(2,1)}, bf16[64,2048]{1,0:T(8,128)(2,1)}) custom-call(bf16[64,2048]{1,0:T(8,128)(2,1)} %fusion.33.x_ref, bf16[512,2048]{1,0:T(8,128)(2,1)} %wo_hbm.3, bf16[256,1024]{1,0:T(8,128)(2,1)} %get-tuple-element.58.q_hbm, ...), custom_call_target="tpu_custom_call" | custom-call | flops 49999998976 | tf_op jit(solution)/shard_map/pallas_call | solution.py:1934
  293.0 1.2 copy.48
  294.2 0.9 copy.47.refs_4_
  295.2 3.9 convolution_convert_fusion
  299.1 0.0 copy-start.15
  299.1 0.0 copy-start.16
  299.1 90.9 %shard_map.292 = (f32[64,2048]{1,0:T(8,128)}, f32[64,640]{1,0:T(8,128)}, bf16[64,1024]{1,0:T(8,128)(2,1)}, f32[64,2048]{1,0:T(8,128)}, bf16[4,2,256,768]{3,2,1,0...) custom-call(bf16[4,2,2,2,64,2048]{5,4,3,2,1,0:T(8,128)(2,1)} %get-tu, ...), custom_call_target="tpu_custom_call" | custom-call | flops 89999998976 | tf_op jit(solution)/shard_map/pallas_call | solution.py:1628
  390.1 0.0 all-gather.6.cloned.1.call-update
  390.1 0.0 all-gather.8.cloned.1.call-start
  390.2 1.2 multiply_reduce_fusion.4
  391.4 1.0 fusion.13
  392.4 1.0 fusion.25
  393.4 0.1 add_convert_fusion.1
  393.5 2.6 fusion.8
  396.2 0.1 reshape.168
  396.3 1.4 add_convert_fusion
  397.7 0.8 pad_maximum_fusion.t_ref
  398.5 0.7 fusion.16.x_ref
  399.2 33.3 %shard_map.293 = (bf16[32,64,768]{2,1,0:T(8,128)(2,1)}, bf16[2,2,64,4096]{3,2,1,0:T(8,128)(2,1)}) custom-call(bf16[64,768]{1,0:T(8,128)(2,1)} %fusion.16.x_ref, bf16[64,4096]{1,0:T(8,128)(2,1)} %pad_maximum_fusion.t_ref), custom_call_target="tpu_custom_call" | custom-call | flops 32000000000 | tf_op jit(solution)/shard_map/pallas_call | solution.py:674
  432.5 1.6 convert_reduce_fusion
  434.1 0.1 slice_add_fusion
  434.2 0.1 reshape.170
  434.3 0.6 slice.80
  434.9 3.3 convert_element_type.74
  438.2 3.3 convert_element_type.75
  441.5 0.6 fusion.34
  442.1 2.0 slice_convert_fusion
  444.1 0.0 all-gather.8.cloned.1.call-update
  444.1 7.9 %convert_bitcast_fusion.2 = (f32[2048,704]{0,1:T(8,128)}, f32[2048,704]{0,1:T(8,128)}) fusion(bf16[704,2048]{1,0:T(8,128)(2,1)} %get-tuple-element.80, bf16[704,2048]{1,0:T(8,128)(2,1)S(1)} %copy-done.6), kind=kLoop, calls=%fused_computation.2 | loop fusion | flops 2883584 | bytes 17301504 | tf_op jit(solution)/shard_map/transpose | solution.py:1663
  452.1 5.9 %convert_bitcast_fusion = (f32[2,2048,352]{1,2,0:T(8,128)}, f32[2,2048,352]{1,2,0:T(8,128)}) fusion(bf16[2,352,2048]{2,1,0:T(8,128)(2,1)S(1)} %copy-done.5, bf16[2,352,2048]{2,1,0:T(8,128)(2,1)S(1)} %copy-done.4), kind=kLoop, calls=%fused_computation | loop fusion | flops 2883584 | bytes 17301504 | tf_op jit(solution)/shard_map/transpose | solution.py:1663
  458.0 7.0 %fusion = f32[2048,576]{0,1:T(8,128)} fusion(bf16[2048,2048]{1,0:T(8,128)(2,1)S(1)} %bitcast.57, bf16[2048,768]{1,0:T(8,128)(2,1)S(1)} %bitcast.49), kind=kOutput, calls=%fused_computation.4 | convolution fusion | flops 4831838208 | bytes 15728640 | tf_op jit(solution)/shard_map/dot_general | solution.py:2234
  465.0 9.0 %fusion.35 = f32[2048,768]{1,0:T(8,128)} fusion(bf16[2048,2048]{1,0:T(8,128)(2,1)S(1)} %bitcast.57, bf16[2048,768]{1,0:T(8,128)(2,1)S(1)} %bitcast.65), kind=kOutput, calls=%fused_computation.83 | convolution fusion | flops 6442450944 | bytes 17825792 | tf_op jit(solution)/shard_map/dot_general | solution.py:2234
  474.0 2.8 convert_element_type.72
  476.8 14.7 %all-gather.8.cloned.1.call-done = bf16[512,2048]{1,0:T(8,128)(2,1)} async-done(((bf16[64,2048]{1,0:T(8,128)(2,1)}), bf16[512,2048]{1,0:T(8,128)(2,1)}) %all-gather.8.cloned.1.call-update) | async-done | bytes 2097168 | tf_op jit(solution)/shard_map/all_gather | solution.py:2337
  491.5 4.1 convert_element_type.73
  (61 shorter events, 0.2 us)
Async XLA Ops:
  7.2 229.3 %all-gather.4.cloned.1.call-start = ((), (), s32[]{:S(2)}) async-start(), calls=%async_computation | async-start | bytes 8650752 | tf_op jit(solution)/shard_map/all_gather | solution.py:2307
  7.2 8.3 %copy-start.14 = (f32[32]{0:T(128)}, f32[32]{0:T(128)S(1)}, u32[]{:S(2)}) copy-start(f32[32]{0:T(128)S(1)} %multiply_power_fusion) | copy-start | bytes 388
  89.5 384.5 %all-gather.6.cloned.1.call-start = ((), (), s32[]{:S(2)}) async-start(), calls=%async_computation.1 | async-start | bytes 1179648 | tf_op jit(solution)/shard_map/all_gather | solution.py:2338
  90.7 3.9 copy-start.18
  92.3 2.3 copy-start.21
  94.6 141.9 %copy-start = (f32[64,2048]{1,0:T(8,128)S(1)}, f32[64,2048]{1,0:T(8,128)}, u32[]{:S(2)}) copy-start(f32[64,2048]{1,0:T(8,128)} %get-tuple-element.57) | copy-start | bytes 1572868
  94.6 141.9 %copy-start.11 = (f32[2048]{0:T(1024)S(1)}, f32[2048]{0:T(1024)}, u32[]{:S(2)}) copy-start(f32[2048]{0:T(1024)} %param.25) | copy-start | bytes 24580
  299.1 91.1 %copy-start.8 = (f32[64,640]{1,0:T(8,128)S(1)}, f32[64,640]{1,0:T(8,128)}, u32[]{:S(2)}) copy-start(f32[64,640]{1,0:T(8,128)} %get-tuple-element.68) | copy-start | bytes 491524
  299.1 91.1 %copy-start.13 = (f32[512]{0:T(512)S(1)}, f32[512]{0:T(512)}, u32[]{:S(2)}) copy-start(f32[512]{0:T(512)} %param.22) | copy-start | bytes 6148
  299.1 91.1 %copy-start.17 = (f32[64]{0:T(128)S(1)}, f32[64]{0:T(128)}, u32[]{:S(2)}) copy-start(f32[64]{0:T(128)} %fusion.30) | copy-start | bytes 772
  299.1 92.3 %copy-start.22 = (f32[64]{0:T(128)S(1)}, f32[64]{0:T(128)}, u32[]{:S(2)}) copy-start(f32[64]{0:T(128)} %copy-done.21) | copy-start | bytes 772
  299.1 93.3 %copy-start.15 = (f32[32]{0:T(128)S(1)}, f32[32]{0:T(128)}, u32[]{:S(2)}) copy-start(f32[32]{0:T(128)} %copy-done.14) | copy-start | bytes 388
  299.1 93.3 %copy-start.20 = (f32[64]{0:T(128)S(1)}, f32[64]{0:T(128)}, u32[]{:S(2)}) copy-start(f32[64]{0:T(128)} %dynamic-slice_convert_fusion.1) | copy-start | bytes 772
  299.1 94.4 %copy-start.12 = (f32[2048]{0:T(1024)S(1)}, f32[2048]{0:T(1024)}, u32[]{:S(2)}) copy-start(f32[2048]{0:T(1024)} %param.19) | copy-start | bytes 24580
  299.1 94.4 %copy-start.16 = (f32[64]{0:T(128)S(1)}, f32[64]{0:T(128)}, u32[]{:S(2)}) copy-start(f32[64]{0:T(128)} %fusion.31) | copy-start | bytes 772
  390.1 6.1 %copy-start.19 = (f32[64]{0:T(128)S(1)}, f32[64]{0:T(128)}, u32[]{:S(2)}) copy-start(f32[64]{0:T(128)} %copy-done.18) | copy-start | bytes 772
  390.1 6.2 %copy-start.1 = (f32[64,2048]{1,0:T(8,128)S(1)}, f32[64,2048]{1,0:T(8,128)}, u32[]{:S(2)}) copy-start(f32[64,2048]{1,0:T(8,128)} %get-tuple-element.56) | copy-start | bytes 1572868
  390.1 6.2 %copy-start.9 = (f32[64,2048]{1,0:T(8,128)S(1)}, f32[64,2048]{1,0:T(8,128)}, u32[]{:S(2)}) copy-start(f32[64,2048]{1,0:T(8,128)} %get-tuple-element.70) | copy-start | bytes 1572868
  390.1 101.4 %all-gather.8.cloned.1.call-start = ((), (), s32[]{:S(2)}) async-start(), calls=%async_computation.2 | async-start | bytes 2359296 | tf_op jit(solution)/shard_map/all_gather | solution.py:2337
  399.2 35.6 %copy-start.3 = (bf16[704,2048]{1,0:T(8,128)(2,1)S(1)}, bf16[704,2048]{1,0:T(8,128)(2,1)}, u32[]{:S(2)}) copy-start(bf16[704,2048]{1,0:T(8,128)(2,1)} %get-tuple-element.81) | copy-start | bytes 8650756
  434.9 3.3 copy-start.2
  438.2 3.9 copy-start.7
  441.5 2.6 copy-start.6
  444.1 7.9 %copy-start.4 = (bf16[2,352,2048]{2,1,0:T(8,128)(2,1)S(1)}, bf16[2,352,2048]{2,1,0:T(8,128)(2,1)}, u32[]{:S(2)}) copy-start(bf16[2,352,2048]{2,1,0:T(8,128)(2,1)} %get-tuple-element.82) | copy-start | bytes 8650756
  444.1 7.9 %copy-start.5 = (bf16[2,352,2048]{2,1,0:T(8,128)(2,1)S(1)}, bf16[2,352,2048]{2,1,0:T(8,128)(2,1)}, u32[]{:S(2)}) copy-start(bf16[2,352,2048]{2,1,0:T(8,128)(2,1)} %get-tuple-element.83) | copy-start | bytes 8650756
  444.1 13.9 %slice-start = ((s8[8388608]{0:T(1024)(128)(4,1)}), s8[4194304]{0:T(1024)(128)(4,1)S(1)}, s32[]{:S(2)}) async-start(s8[8388608]{0:T(1024)(128)(4,1)} %bitcast.56), calls=%async_computation.3 | async-start | bytes 8388608
  452.0 6.0 %slice-start.1 = ((s8[8388608]{0:T(1024)(128)(4,1)}), s8[4194304]{0:T(1024)(128)(4,1)S(1)}, s32[]{:S(2)}) async-start(s8[8388608]{0:T(1024)(128)(4,1)} %bitcast.56), calls=%async_computation.4 | async-start | bytes 8388608
  452.0 6.0 %copy-start.10 = (bf16[32,64,768]{2,1,0:T(8,128)(2,1)S(1)}, bf16[32,64,768]{2,1,0:T(8,128)(2,1)}, u32[]{:S(2)}) copy-start(bf16[32,64,768]{2,1,0:T(8,128)(2,1)} %get-tuple-element.72) | copy-start | bytes 9437188
  458.0 7.0 %copy-start.23 = (bf16[4,2,256,768]{3,2,1,0:T(8,128)(2,1)S(1)}, bf16[4,2,256,768]{3,2,1,0:T(8,128)(2,1)}, u32[]{:S(2)}) copy-start(bf16[4,2,256,768]{3,2,1,0:T(8,128)(2,1)} %get-tuple-element.74) | copy-start | bytes 9437188
Sparse Core Ops, SparseCore 0:
  89.7 90.3 all-gather.3
  390.2 45.9 all-gather.5
  444.2 47.2 all-gather.7

commit v6 on v5

--- a/solution.py
+++ b/solution.py
@@ -663,11 +663,15 @@
                 self.copy_b(i, k).wait_send()
 
 
-def last_kernel(grid, x_ref, t_ref, out_ref, t_out, own_sem, ss, rs, cs, cr, *scratch):
-    gather_kernel(grid, x_ref, out_ref, own_sem, ss, rs, cs, cr, [TensorGather(grid, t_ref, t_out, scratch)])
-
-
-def last_call(grid, x, t, collective_id):
+def last_kernel(grid, x_ref, w_ref, t_ref, out_ref, w_out, t_out, own_sem, ss, rs, cs, cr, *scratch):
+    gathers = [
+        TensorGather(grid, t_ref, t_out, scratch[: TensorGather.count]),
+        PlaneGather(grid, w_ref, w_out, scratch[TensorGather.count :]),
+    ]
+    gather_kernel(grid, x_ref, out_ref, own_sem, ss, rs, cs, cr, gathers)
+
+
+def last_call(grid, x, w, t, collective_id):
     r, n = x.shape
     blocks = grid.na * grid.nb * grid.ny
     any_space = pl.BlockSpec(memory_space=pl.ANY)
@@ -675,10 +679,11 @@
         functools.partial(last_kernel, grid),
         out_shape=[
             jax.ShapeDtypeStruct((grid.size, r, n), x.dtype),
+            jax.ShapeDtypeStruct((grid.na, grid.nb) + w.shape, w.dtype),
             jax.ShapeDtypeStruct((grid.ny, 2) + t.shape, t.dtype),
         ],
-        in_specs=[any_space] * 2,
-        out_specs=[any_space] * 2,
+        in_specs=[any_space] * 3,
+        out_specs=[any_space] * 3,
         scratch_shapes=[
             pltpu.SemaphoreType.DMA,
             pltpu.SemaphoreType.DMA((gather_sends(grid),)),
@@ -686,11 +691,13 @@
             pltpu.SemaphoreType.DMA((2 * blocks,)),
             pltpu.SemaphoreType.DMA((2 * blocks,)),
         ]
-        + TensorGather.scratch(grid),
-        cost_estimate=microseconds(32),
+        + TensorGather.scratch(grid)
+        + PlaneGather.scratch(grid),
+        cost_estimate=microseconds(36),
         compiler_params=pltpu.CompilerParams(collective_id=collective_id, has_side_effects=True),
-    )(x, t)
-    return outs[0], outs[1].reshape(-1, t.shape[-1])
+    )(x, w, t)
+    whole = lambda v: v.reshape(-1, v.shape[-1])
+    return outs[0], whole(outs[1]), whole(outs[2])
 
 
 def dot_rows(left_side, right_side):
@@ -870,7 +877,7 @@
         j, k = pair // ny, pair % ny
         late = [(j, k, i, h, ()) for i in range(na) for h in range(2) if (k if h == 0 else j)]
         for m, event in enumerate(late):
-            hooks.setdefault(("main", pair, m * 3 // len(late)), []).append(event)
+            hooks.setdefault(("main", pair, m * 2 // len(late)), []).append(event)
 
     def hook(stage, step, spot):
         for (when_stage, when, when_spot), events in hooks.items():
@@ -927,7 +934,14 @@
 
     def x_load(step):
         _, _, _, bb, yy, cc = spots(step)
-        return pltpu.make_async_copy(all_ref.at[:, bb, yy, cc], xbuf.at[0], x_sem.at[0])
+        s = lax.rem(step, 2)
+        return pltpu.make_async_copy(all_ref.at[:, bb, yy, cc], xbuf.at[s], x_sem.at[s])
+
+    def await_shared(step):
+        _, _, _, bb, yy, cc = spots(step)
+        for i in range(na):
+            for h in range(2):
+                landed(bb, yy, cc, line(i), h, share_recv)
 
     def stores(step):
         _, _, _, bb, yy, cc = spots(step)
@@ -995,21 +1009,13 @@
         j, k, l, bb, yy, cc = spots(step)
         s = lax.rem(step, 2)
 
-        @pl.when(l == 1)
-        def _():
-            for i in range(na):
-                for h in range(2):
-                    landed(bb, yy, cc, line(i), h, share_recv)
-
-        x_load(step).start()
-
         @pl.when(step >= 2)
         def _():
             for store in stores(step - 2):
                 store.wait()
 
         x_load(step).wait()
-        x = flat(xbuf[0])
+        x = flat(xbuf[s])
         g = dot_rows(x, egu[:ef])
         u = dot_rows(x, egu[ef:])
         gate = flat(gates[:, bb, yy, cc]).astype(f32)
@@ -1035,6 +1041,14 @@
 
         hook("main", step, 1)
 
+        @pl.when((l == 0) & (step + 1 < steps))
+        def _():
+            await_shared(step + 1)
+
+        @pl.when(step + 1 < steps)
+        def _():
+            x_load(step + 1).start()
+
         def column(target):
             for q in range(n // chunk):
                 at = pl.ds(q * chunk, chunk)
@@ -1083,9 +1097,10 @@
                 for p in range(pieces):
                     send_11(p, j, k).start()
 
-        hook("main", step, 2)
         return carry
 
+    await_shared(a * 0)
+    x_load(a * 0).start()
     lax.fori_loop(0, steps, main_body, 0)
     for step in (steps - 2, steps - 1):
         for store in stores(a * 0 + step):
@@ -2335,7 +2350,6 @@
     )
     output_rows, weight_rows = lax.optimization_barrier((output_rows, weight_rows))
     output_rows = lax.all_gather(output_rows, "expert", axis=0, tiled=True)
-    weight_rows = lax.all_gather(weight_rows, "expert", axis=0, tiled=True)
     grad_expert_gate, grad_expert_up, grad_expert_down = expert_grads[:3]
     grad_shared_gate, grad_shared_up, grad_shared_down = expert_grads[3:]
     layer_out = low(residual + moe_out)
@@ -2355,9 +2369,10 @@
     gains_low = low(gains - gains_high.astype(jnp.float32))
     spread = gains.shape[1]
     both = jnp.concatenate([layer_out, low(grad_residual + grad_input_norm)], axis=1)
-    last, both = last_call(
+    last, weight_rows, both = last_call(
         grid,
         pad_columns(jnp.concatenate([grad_comp_low, gains_high, gains_low], axis=1)),
+        weight_rows,
         both,
         8,
     )

time: 512 us -> 504 us (0.984)
  waiting for transfers between devices: 14.8 us -> 6.26 us
    all_gather x1, waiting for transfers between devices: 14.7 us -> 6.2 us  [shards(): output_rows = lax.all_gather(output_rows, 'expert', axis=0, tiled=True)]
    pallas_call x1, Pallas kernels: 33.3 us -> 40 us  [last_call(): pl.pallas_call(functools.partial(last_kernel, grid), out_shape=[jax.Shape...]
    pallas_call x1, Pallas kernels: 142 us -> 135 us  [experts_call(): pl.pallas_call(functools.partial(experts_kernel, grid, pieces), out_shape...]
  transfers between devices with their start and end apart: 3 -> 2, of which waited for: 1 -> 1; matrix products, arithmetic and copies ran while one was open for 12% -> 9% of each run, Pallas kernels for 35% -> 27%
where the time goes in v6:
time: 504 us; the launch traced here: 494 us
  Pallas kernels  392 us (78%)
  other arithmetic  49.2 us (10%)
  matrix products  22.4 us (4%)
  between operations  14.7 us (3%)
  local copies, waits for them, and re-layouts  9.54 us (2%)
  waiting for transfers between devices  6.26 us (1%)
    pallas_call x1, Pallas kernels, experts_call(): pl.pallas_call(functools.partial(experts_kernel, grid, pieces), out_shape...  135 us
    pallas_call x1, Pallas kernels, gradients_call(): pl.pallas_call(functools.partial(gradients_kernel, grid, pieces, unit, pl...  91.6 us
    pallas_call x1, Pallas kernels, front_call(): pl.pallas_call(functools.partial(front_kernel, grid), out_shape=[jax.Shap...  73.9 us
    pallas_call x1, Pallas kernels, attention_back_call(): pl.pallas_call(functools.partial(attention_back_kernel, grid, pieces), ou...  51.1 us
    pallas_call x1, Pallas kernels, last_call(): pl.pallas_call(functools.partial(last_kernel, grid), out_shape=[jax.Shape...  40 us
    dot_general x4, matrix products, dot(): return jnp.dot(left_side, right_side, preferred_element_type=jnp.float32)  22.4 us
  transfers between devices with their start and end apart: 2, of which 1 were waited for; matrix products, arithmetic and copies ran while one was open for 9% of the time, Pallas kernels for 27%

profile of v6, /device:TPU:0, one launch (start us, length us, event | category | flops | bytes accessed | tf_op | source)
XLA Modules:
  0.0 494.3 jit_solution(7865494594257201816)
XLA Ops:
  7.2 0.0 all-gather.3.cloned.1.call-start
  7.2 0.0 copy-start.15
  7.3 0.8 slice_compare_fusion
  8.1 0.8 dynamic_slice.18
  8.9 0.1 add_select_fusion
  8.9 0.3 reduce-window.9
  9.2 0.1 slice.71
  9.3 0.1 slice_reduce_fusion
  9.5 0.8 fusion.27
  10.2 0.1 dynamic-slice_convert_fusion
  10.3 0.8 copy.44.own_seg_ref
  11.1 1.5 copy.42.gate_ref
  12.6 1.5 copy.43.route_ref
  14.1 0.1 pad.29.clone
  14.2 0.5 multiply_sine_fusion
  14.7 0.8 maximum_maximum_fusion.1
  15.6 73.9 %shard_map.289 = (bf16[4,2,2,2,64,640]{5,4,3,2,1,0:T(8,128)(2,1)}, bf16[4,2,2,2,64,2048]{5,4,3,2,1,0:T(8,128)(2,1)}, bf16[2048,1024]{1,0:T(8,128)(2,1)}, bf16[25...) custom-call(bf16[256,2048]{1,0:T(8,128)(2,1)} %hidden_ref.1, ...), custom_call_target="tpu_custom_call" | custom-call | flops 73999998976 | tf_op jit(solution)/shard_map/pallas_call | solution.py:2154
  89.5 0.0 all-gather.3.cloned.1.call-update
  89.5 0.0 all-gather.5.cloned.1.call-start
  89.6 1.1 fusion.5
  90.7 0.6 dynamic-slice_convert_fusion.1
  91.3 1.0 multiply_reduce_fusion.5
  92.3 0.0 copy-start.22
  92.3 1.2 multiply_reduce_fusion.2
  93.5 0.5 fusion.31
  94.0 0.5 fusion.30
  94.6 135.4 %shard_map.290 = (bf16[4,2,2,2,64,2048]{5,4,3,2,1,0:T(8,128)(2,1)}, f32[64,2048]{1,0:T(8,128)}, bf16[4,2,2,2,64,2048]{5,4,3,2,1,0:T(8,128)(2,1)}, bf16[4,2,2,2,64,4608]{5,4,3,2,1,0:T(8,128)(2,1)}) custom-call(bf16[64,2048]{1,0:T(8,128)(2,1)} %get-tuple-element.51.x_ref, bf16[4,2,2,2,64,2048]{5,4,3,2,1,0:T(8,128)(2,1)} %get-tuple-element.52.dz_ref, ...), custom_call_target="tpu_custom_call" | custom-call | flops 130000003072 | tf_op jit(solution)/shard_map/pallas_call | solution.py:1284
  230.0 0.0 all-gather.3.cloned.1.call-done
  230.1 1.3 multiply_reduce_fusion.1
  231.4 2.0 fusion.33.x_ref
  233.4 51.1 %shard_map.291 = (bf16[256,1024]{1,0:T(8,128)(2,1)}, bf16[2048,640]{1,0:T(8,128)(2,1)}, bf16[512,1024]{1,0:T(8,128)(2,1)}, bf16[64,2048]{1,0:T(8,128)(2,1)}) custom-call(bf16[64,2048]{1,0:T(8,128)(2,1)} %fusion.33.x_ref, bf16[512,2048]{1,0:T(8,128)(2,1)} %wo_hbm.3, bf16[256,1024]{1,0:T(8,128)(2,1)} %get-tuple-element.59.q_hbm, ...), custom_call_target="tpu_custom_call" | custom-call | flops 49999998976 | tf_op jit(solution)/shard_map/pallas_call | solution.py:1949
  284.6 1.2 copy.48
  285.8 0.9 copy.47.refs_4_
  286.8 3.9 convolution_convert_fusion
  290.7 0.0 copy-start.13
  290.7 0.0 copy-start.17
  290.7 91.6 %shard_map.292 = (f32[64,2048]{1,0:T(8,128)}, f32[64,640]{1,0:T(8,128)}, bf16[64,1024]{1,0:T(8,128)(2,1)}, f32[64,2048]{1,0:T(8,128)}, bf16[4,2,256,768]{3,2,1,0...) custom-call(bf16[4,2,2,2,64,2048]{5,4,3,2,1,0:T(8,128)(2,1)} %get-tu, ...), custom_call_target="tpu_custom_call" | custom-call | flops 89999998976 | tf_op jit(solution)/shard_map/pallas_call | solution.py:1643
  382.4 1.2 multiply_reduce_fusion.4
  383.6 1.0 fusion.13
  384.6 1.0 fusion.25
  385.7 0.1 add_convert_fusion.1
  385.8 2.6 fusion.8
  388.4 0.1 reshape.171
  388.5 1.4 add_convert_fusion
  389.9 0.8 pad_maximum_fusion.t_ref
  390.7 0.7 fusion.16.x_ref
  391.5 40.0 %shard_map.293 = (bf16[32,64,768]{2,1,0:T(8,128)(2,1)}, bf16[4,2,64,1024]{3,2,1,0:T(8,128)(2,1)}, bf16[2,2,64,4096]{3,2,1,0:T(8,128)(2,1)}) custom-call(bf16[64,768]{1,0:T(8,128)(2,1)} %fusion.16.x_ref, bf16[64,1024]{1,0:T(8,128)(2,1)} %get-tuple-element.73.w_ref, bf16[64,4096]{1,0:T(8,128)(2,1)} %pad_maximum_fusion.t_ref), custom_call_target="tpu_custom_call" | custom-call | flops 35999997952 | tf_op jit(solution)/shard_map/pallas_call | solution.py:678
  431.5 1.7 convert_reduce_fusion
  433.2 0.1 slice_add_fusion
  433.3 0.1 reshape.173
  433.4 0.6 slice.80
  434.0 0.6 fusion.34
  434.6 0.0 all-gather.5.cloned.1.call-update
  434.6 3.7 slice_convert_fusion
  438.3 1.6 bitcast_convert_fusion
  439.9 3.3 convert_element_type.78
  443.2 3.7 convert_element_type.79
  446.9 1.1 copy-done.7
  448.0 6.9 %convert_bitcast_fusion.2 = (f32[2048,704]{0,1:T(8,128)}, f32[2048,704]{0,1:T(8,128)}) fusion(bf16[704,2048]{1,0:T(8,128)(2,1)S(1)} %copy-done.7, bf16[704,2048]{1,0:T(8,128)(2,1)S(1)} %copy-done.6), kind=kLoop, calls=%fused_computation.2 | loop fusion | flops 2883584 | bytes 17301504 | tf_op jit(solution)/shard_map/transpose | solution.py:1678
  454.9 6.1 %convert_bitcast_fusion = (f32[2,2048,352]{1,2,0:T(8,128)}, f32[2,2048,352]{1,2,0:T(8,128)}) fusion(bf16[2,352,2048]{2,1,0:T(8,128)(2,1)S(1)} %copy-done.5, bf16[2,352,2048]{2,1,0:T(8,128)(2,1)S(1)} %copy-done.4), kind=kLoop, calls=%fused_computation | loop fusion | flops 2883584 | bytes 17301504 | tf_op jit(solution)/shard_map/transpose | solution.py:1678
  461.0 7.0 %fusion = f32[2048,576]{0,1:T(8,128)} fusion(bf16[2048,2048]{1,0:T(8,128)(2,1)S(1)} %bitcast.60, bf16[2048,768]{1,0:T(8,128)(2,1)S(1)} %bitcast.52), kind=kOutput, calls=%fused_computation.4 | convolution fusion | flops 4831838208 | bytes 15728640 | tf_op jit(solution)/shard_map/dot_general | solution.py:2249
  468.0 9.0 %fusion.35 = f32[2048,768]{1,0:T(8,128)} fusion(bf16[2048,2048]{1,0:T(8,128)(2,1)S(1)} %bitcast.60, bf16[2048,768]{1,0:T(8,128)(2,1)S(1)} %bitcast.68), kind=kOutput, calls=%fused_computation.84 | convolution fusion | flops 6442450944 | bytes 17825792 | tf_op jit(solution)/shard_map/dot_general | solution.py:2249
  477.0 6.2 %all-gather.5.cloned.1.call-done = bf16[512,2048]{1,0:T(8,128)(2,1)} async-done(((bf16[64,2048]{1,0:T(8,128)(2,1)}), bf16[512,2048]{1,0:T(8,128)(2,1)}) %all-gather.5.cloned.1.call-update) | async-done | bytes 2097168 | tf_op jit(solution)/shard_map/all_gather | solution.py:2352
  483.2 4.1 convert_element_type.77
  (60 shorter events, 0.2 us)
Async XLA Ops:
  7.2 222.9 %all-gather.3.cloned.1.call-start = ((), (), s32[]{:S(2)}) async-start(), calls=%async_computation | async-start | bytes 8650752 | tf_op jit(solution)/shard_map/all_gather | solution.py:2322
  7.2 8.3 %copy-start.15 = (f32[32]{0:T(128)}, f32[32]{0:T(128)S(1)}, u32[]{:S(2)}) copy-start(f32[32]{0:T(128)S(1)} %multiply_power_fusion) | copy-start | bytes 388
  89.5 393.7 %all-gather.5.cloned.1.call-start = ((), (), s32[]{:S(2)}) async-start(), calls=%async_computation.1 | async-start | bytes 2359296 | tf_op jit(solution)/shard_map/all_gather | solution.py:2352
  90.7 3.9 copy-start.19
  92.3 2.3 copy-start.22
  94.6 135.5 %copy-start = (f32[64,2048]{1,0:T(8,128)S(1)}, f32[64,2048]{1,0:T(8,128)}, u32[]{:S(2)}) copy-start(f32[64,2048]{1,0:T(8,128)} %get-tuple-element.58) | copy-start | bytes 1572868
  94.6 135.5 %copy-start.12 = (f32[2048]{0:T(1024)S(1)}, f32[2048]{0:T(1024)}, u32[]{:S(2)}) copy-start(f32[2048]{0:T(1024)} %param.25) | copy-start | bytes 24580
  290.7 91.7 %copy-start.9 = (f32[64,640]{1,0:T(8,128)S(1)}, f32[64,640]{1,0:T(8,128)}, u32[]{:S(2)}) copy-start(f32[64,640]{1,0:T(8,128)} %get-tuple-element.69) | copy-start | bytes 491524
  290.7 91.7 %copy-start.14 = (f32[512]{0:T(512)S(1)}, f32[512]{0:T(512)}, u32[]{:S(2)}) copy-start(f32[512]{0:T(512)} %param.22) | copy-start | bytes 6148
  290.7 91.7 %copy-start.18 = (f32[64]{0:T(128)S(1)}, f32[64]{0:T(128)}, u32[]{:S(2)}) copy-start(f32[64]{0:T(128)} %fusion.30) | copy-start | bytes 772
  290.7 92.9 %copy-start.23 = (f32[64]{0:T(128)S(1)}, f32[64]{0:T(128)}, u32[]{:S(2)}) copy-start(f32[64]{0:T(128)} %copy-done.22) | copy-start | bytes 772
  290.7 94.0 %copy-start.16 = (f32[32]{0:T(128)S(1)}, f32[32]{0:T(128)}, u32[]{:S(2)}) copy-start(f32[32]{0:T(128)} %copy-done.15) | copy-start | bytes 388
  290.7 94.0 %copy-start.21 = (f32[64]{0:T(128)S(1)}, f32[64]{0:T(128)}, u32[]{:S(2)}) copy-start(f32[64]{0:T(128)} %dynamic-slice_convert_fusion.1) | copy-start | bytes 772
  290.7 95.1 %copy-start.13 = (f32[2048]{0:T(1024)S(1)}, f32[2048]{0:T(1024)}, u32[]{:S(2)}) copy-start(f32[2048]{0:T(1024)} %param.19) | copy-start | bytes 24580
  290.7 95.1 %copy-start.17 = (f32[64]{0:T(128)S(1)}, f32[64]{0:T(128)}, u32[]{:S(2)}) copy-start(f32[64]{0:T(128)} %fusion.31) | copy-start | bytes 772
  382.4 6.0 %copy-start.20 = (f32[64]{0:T(128)S(1)}, f32[64]{0:T(128)}, u32[]{:S(2)}) copy-start(f32[64]{0:T(128)} %copy-done.19) | copy-start | bytes 772
  382.4 6.1 %copy-start.1 = (f32[64,2048]{1,0:T(8,128)S(1)}, f32[64,2048]{1,0:T(8,128)}, u32[]{:S(2)}) copy-start(f32[64,2048]{1,0:T(8,128)} %get-tuple-element.57) | copy-start | bytes 1572868
  382.4 6.1 %copy-start.10 = (f32[64,2048]{1,0:T(8,128)S(1)}, f32[64,2048]{1,0:T(8,128)}, u32[]{:S(2)}) copy-start(f32[64,2048]{1,0:T(8,128)} %get-tuple-element.74) | copy-start | bytes 1572868
  431.5 6.8 %copy-start.8 = (bf16[4,2,64,1024]{3,2,1,0:T(8,128)(2,1)S(1)}, bf16[4,2,64,1024]{3,2,1,0:T(8,128)(2,1)}, u32[]{:S(2)}) copy-start(bf16[4,2,64,1024]{3,2,1,0:T(8,128)(2,1)} %get-tuple-element.79) | copy-start | bytes 3145732
  434.6 5.3 %copy-start.3 = (bf16[704,2048]{1,0:T(8,128)(2,1)S(1)}, bf16[704,2048]{1,0:T(8,128)(2,1)}, u32[]{:S(2)}) copy-start(bf16[704,2048]{1,0:T(8,128)(2,1)} %get-tuple-element.83) | copy-start | bytes 8650756
  439.9 3.3 copy-start.2
  443.2 3.7 copy-start.6
  443.2 4.8 copy-start.7
  448.0 6.9 %copy-start.4 = (bf16[2,352,2048]{2,1,0:T(8,128)(2,1)S(1)}, bf16[2,352,2048]{2,1,0:T(8,128)(2,1)}, u32[]{:S(2)}) copy-start(bf16[2,352,2048]{2,1,0:T(8,128)(2,1)} %get-tuple-element.84) | copy-start | bytes 8650756
  448.0 6.9 %copy-start.5 = (bf16[2,352,2048]{2,1,0:T(8,128)(2,1)S(1)}, bf16[2,352,2048]{2,1,0:T(8,128)(2,1)}, u32[]{:S(2)}) copy-start(bf16[2,352,2048]{2,1,0:T(8,128)(2,1)} %get-tuple-element.85) | copy-start | bytes 8650756
  448.0 13.0 %slice-start = ((s8[8388608]{0:T(1024)(128)(4,1)}), s8[4194304]{0:T(1024)(128)(4,1)S(1)}, s32[]{:S(2)}) async-start(s8[8388608]{0:T(1024)(128)(4,1)} %bitcast.59), calls=%async_computation.2 | async-start | bytes 8388608
  454.9 6.1 %slice-start.1 = ((s8[8388608]{0:T(1024)(128)(4,1)}), s8[4194304]{0:T(1024)(128)(4,1)S(1)}, s32[]{:S(2)}) async-start(s8[8388608]{0:T(1024)(128)(4,1)} %bitcast.59), calls=%async_computation.3 | async-start | bytes 8388608
  454.9 6.1 %copy-start.11 = (bf16[32,64,768]{2,1,0:T(8,128)(2,1)S(1)}, bf16[32,64,768]{2,1,0:T(8,128)(2,1)}, u32[]{:S(2)}) copy-start(bf16[32,64,768]{2,1,0:T(8,128)(2,1)} %get-tuple-element.76) | copy-start | bytes 9437188
  461.0 7.0 %copy-start.24 = (bf16[4,2,256,768]{3,2,1,0:T(8,128)(2,1)S(1)}, bf16[4,2,256,768]{3,2,1,0:T(8,128)(2,1)}, u32[]{:S(2)}) copy-start(bf16[4,2,256,768]{3,2,1,0:T(8,128)(2,1)} %get-tuple-element.78) | copy-start | bytes 9437188
Sparse Core Ops, SparseCore 0:
  89.6 90.3 all-gather.2
  434.7 48.4 all-gather.4

commit v7 on v6

--- a/solution.py
+++ b/solution.py
@@ -1541,7 +1541,7 @@
     ]
     big_loads[0].start()
     greet(grid)
-    for one in sums + flat_sums + [q_gather]:
+    for one in [q_gather] + flat_sums + sums:
         one.start()
     left_load(grid.here()[0] * 0).start()
     if slots > 1:
@@ -1552,7 +1552,7 @@
     for p, one in enumerate(flat_sums):
         work.insert(min(len(work), 3 + 3 * p), one.middle)
     for i in range(1, grid.na):
-        work.insert(min(len(work), 3 + 3 * i), functools.partial(q_gather.middle, i))
+        work.insert(min(len(work), 2 + 2 * i), functools.partial(q_gather.middle, i))
     turns = {}
     for n, item in enumerate(work):
         turns.setdefault(n * tiles // len(work), []).append(item)

time: 504 us -> 502 us (level)
  no operation moved by 1% of the time
where the time goes in v7:
time: 502 us; the launch traced here: 493 us
  Pallas kernels  391 us (78%)
  other arithmetic  49.2 us (10%)
  matrix products  22.4 us (4%)
  between operations  14.7 us (3%)
  local copies, waits for them, and re-layouts  9.54 us (2%)
  waiting for transfers between devices  5.97 us (1%)
    pallas_call x1, Pallas kernels, experts_call(): pl.pallas_call(functools.partial(experts_kernel, grid, pieces), out_shape...  135 us
    pallas_call x1, Pallas kernels, gradients_call(): pl.pallas_call(functools.partial(gradients_kernel, grid, pieces, unit, pl...  93.2 us
    pallas_call x1, Pallas kernels, front_call(): pl.pallas_call(functools.partial(front_kernel, grid), out_shape=[jax.Shap...  73.9 us
    pallas_call x1, Pallas kernels, attention_back_call(): pl.pallas_call(functools.partial(attention_back_kernel, grid, pieces), ou...  51.1 us
    pallas_call x1, Pallas kernels, last_call(): pl.pallas_call(functools.partial(last_kernel, grid), out_shape=[jax.Shape...  37.1 us
    dot_general x4, matrix products, dot(): return jnp.dot(left_side, right_side, preferred_element_type=jnp.float32)  22.4 us
  transfers between devices with their start and end apart: 2, of which 1 were waited for; matrix products, arithmetic and copies ran while one was open for 9% of the time, Pallas kernels for 27%

profile of v7, /device:TPU:0, one launch (start us, length us, event | category | flops | bytes accessed | tf_op | source)
XLA Modules:
  0.0 492.7 jit_solution(6775908848104552921)
XLA Ops:
  7.2 0.0 all-gather.3.cloned.1.call-start
  7.3 0.8 slice_compare_fusion
  8.1 0.8 dynamic_slice.18
  8.9 0.1 add_select_fusion
  8.9 0.3 reduce-window.9
  9.2 0.1 slice.71
  9.3 0.1 slice_reduce_fusion
  9.5 0.8 fusion.27
  10.2 0.1 dynamic-slice_convert_fusion
  10.3 0.8 copy.44.own_seg_ref
  11.1 1.5 copy.42.gate_ref
  12.6 1.5 copy.43.route_ref
  14.1 0.1 pad.29.clone
  14.2 0.5 multiply_sine_fusion
  14.7 0.8 maximum_maximum_fusion.1
  15.6 73.9 %shard_map.289 = (bf16[4,2,2,2,64,640]{5,4,3,2,1,0:T(8,128)(2,1)}, bf16[4,2,2,2,64,2048]{5,4,3,2,1,0:T(8,128)(2,1)}, bf16[2048,1024]{1,0:T(8,128)(2,1)}, bf16[25...) custom-call(bf16[256,2048]{1,0:T(8,128)(2,1)} %hidden_ref.1, ...), custom_call_target="tpu_custom_call" | custom-call | flops 73999998976 | tf_op jit(solution)/shard_map/pallas_call | solution.py:2154
  89.5 0.0 all-gather.3.cloned.1.call-update
  89.5 0.0 all-gather.5.cloned.1.call-start
  89.6 1.1 fusion.5
  90.7 0.0 copy-start.19
  90.7 0.6 dynamic-slice_convert_fusion.1
  91.3 1.0 multiply_reduce_fusion.5
  92.3 1.2 multiply_reduce_fusion.2
  93.5 0.5 fusion.31
  94.0 0.5 fusion.30
  94.6 0.0 copy-start.12
  94.6 135.4 %shard_map.290 = (bf16[4,2,2,2,64,2048]{5,4,3,2,1,0:T(8,128)(2,1)}, f32[64,2048]{1,0:T(8,128)}, bf16[4,2,2,2,64,2048]{5,4,3,2,1,0:T(8,128)(2,1)}, bf16[4,2,2,2,64,4608]{5,4,3,2,1,0:T(8,128)(2,1)}) custom-call(bf16[64,2048]{1,0:T(8,128)(2,1)} %get-tuple-element.51.x_ref, bf16[4,2,2,2,64,2048]{5,4,3,2,1,0:T(8,128)(2,1)} %get-tuple-element.52.dz_ref, ...), custom_call_target="tpu_custom_call" | custom-call | flops 130000003072 | tf_op jit(solution)/shard_map/pallas_call | solution.py:1284
  230.0 0.0 all-gather.3.cloned.1.call-done
  230.1 1.3 multiply_reduce_fusion.1
  231.4 2.0 fusion.33.x_ref
  233.4 51.1 %shard_map.291 = (bf16[256,1024]{1,0:T(8,128)(2,1)}, bf16[2048,640]{1,0:T(8,128)(2,1)}, bf16[512,1024]{1,0:T(8,128)(2,1)}, bf16[64,2048]{1,0:T(8,128)(2,1)}) custom-call(bf16[64,2048]{1,0:T(8,128)(2,1)} %fusion.33.x_ref, bf16[512,2048]{1,0:T(8,128)(2,1)} %wo_hbm.3, bf16[256,1024]{1,0:T(8,128)(2,1)} %get-tuple-element.59.q_hbm, ...), custom_call_target="tpu_custom_call" | custom-call | flops 49999998976 | tf_op jit(solution)/shard_map/pallas_call | solution.py:1949
  284.6 1.2 copy.48
  285.8 0.9 copy.47.refs_4_
  286.8 3.9 convolution_convert_fusion
  290.7 0.0 copy-start.21
  290.7 0.0 copy-start.13
  290.7 93.2 %shard_map.292 = (f32[64,2048]{1,0:T(8,128)}, f32[64,640]{1,0:T(8,128)}, bf16[64,1024]{1,0:T(8,128)(2,1)}, f32[64,2048]{1,0:T(8,128)}, bf16[4,2,256,768]{3,2,1,0...) custom-call(bf16[4,2,2,2,64,2048]{5,4,3,2,1,0:T(8,128)(2,1)} %get-tu, ...), custom_call_target="tpu_custom_call" | custom-call | flops 89999998976 | tf_op jit(solution)/shard_map/pallas_call | solution.py:1643
  384.0 1.2 multiply_reduce_fusion.4
  385.2 1.0 fusion.13
  386.2 1.0 fusion.25
  387.2 0.1 add_convert_fusion.1
  387.3 2.6 fusion.8
  389.9 0.1 reshape.171
  390.1 1.4 add_convert_fusion
  391.5 0.8 pad_maximum_fusion.t_ref
  392.3 0.7 fusion.16.x_ref
  393.0 37.1 %shard_map.293 = (bf16[32,64,768]{2,1,0:T(8,128)(2,1)}, bf16[4,2,64,1024]{3,2,1,0:T(8,128)(2,1)}, bf16[2,2,64,4096]{3,2,1,0:T(8,128)(2,1)}) custom-call(bf16[64,768]{1,0:T(8,128)(2,1)} %fusion.16.x_ref, bf16[64,1024]{1,0:T(8,128)(2,1)} %get-tuple-element.73.w_ref, bf16[64,4096]{1,0:T(8,128)(2,1)} %pad_maximum_fusion.t_ref), custom_call_target="tpu_custom_call" | custom-call | flops 35999997952 | tf_op jit(solution)/shard_map/pallas_call | solution.py:678
  430.1 1.7 convert_reduce_fusion
  431.8 0.1 slice_add_fusion
  431.9 0.1 reshape.173
  432.0 0.6 slice.80
  432.6 0.6 fusion.34
  433.2 0.0 all-gather.5.cloned.1.call-update
  433.2 3.7 slice_convert_fusion
  436.9 1.6 bitcast_convert_fusion
  438.5 3.3 convert_element_type.78
  441.8 3.7 convert_element_type.79
  445.5 1.1 copy-done.7
  446.6 6.8 %convert_bitcast_fusion.2 = (f32[2048,704]{0,1:T(8,128)}, f32[2048,704]{0,1:T(8,128)}) fusion(bf16[704,2048]{1,0:T(8,128)(2,1)S(1)} %copy-done.7, bf16[704,2048]{1,0:T(8,128)(2,1)S(1)} %copy-done.6), kind=kLoop, calls=%fused_computation.2 | loop fusion | flops 2883584 | bytes 17301504 | tf_op jit(solution)/shard_map/transpose | solution.py:1678
  453.5 6.1 %convert_bitcast_fusion = (f32[2,2048,352]{1,2,0:T(8,128)}, f32[2,2048,352]{1,2,0:T(8,128)}) fusion(bf16[2,352,2048]{2,1,0:T(8,128)(2,1)S(1)} %copy-done.5, bf16[2,352,2048]{2,1,0:T(8,128)(2,1)S(1)} %copy-done.4), kind=kLoop, calls=%fused_computation | loop fusion | flops 2883584 | bytes 17301504 | tf_op jit(solution)/shard_map/transpose | solution.py:1678
  459.6 7.0 %fusion = f32[2048,576]{0,1:T(8,128)} fusion(bf16[2048,2048]{1,0:T(8,128)(2,1)S(1)} %bitcast.60, bf16[2048,768]{1,0:T(8,128)(2,1)S(1)} %bitcast.52), kind=kOutput, calls=%fused_computation.4 | convolution fusion | flops 4831838208 | bytes 15728640 | tf_op jit(solution)/shard_map/dot_general | solution.py:2249
  466.6 9.0 %fusion.35 = f32[2048,768]{1,0:T(8,128)} fusion(bf16[2048,2048]{1,0:T(8,128)(2,1)S(1)} %bitcast.60, bf16[2048,768]{1,0:T(8,128)(2,1)S(1)} %bitcast.68), kind=kOutput, calls=%fused_computation.84 | convolution fusion | flops 6442450944 | bytes 17825792 | tf_op jit(solution)/shard_map/dot_general | solution.py:2249
  475.6 5.9 %all-gather.5.cloned.1.call-done = bf16[512,2048]{1,0:T(8,128)(2,1)} async-done(((bf16[64,2048]{1,0:T(8,128)(2,1)}), bf16[512,2048]{1,0:T(8,128)(2,1)}) %all-gather.5.cloned.1.call-update) | async-done | bytes 2097168 | tf_op jit(solution)/shard_map/all_gather | solution.py:2352
  481.5 4.1 convert_element_type.77
  (60 shorter events, 0.2 us)
Async XLA Ops:
  7.2 222.9 %all-gather.3.cloned.1.call-start = ((), (), s32[]{:S(2)}) async-start(), calls=%async_computation | async-start | bytes 8650752 | tf_op jit(solution)/shard_map/all_gather | solution.py:2322
  7.2 8.3 %copy-start.15 = (f32[32]{0:T(128)}, f32[32]{0:T(128)S(1)}, u32[]{:S(2)}) copy-start(f32[32]{0:T(128)S(1)} %multiply_power_fusion) | copy-start | bytes 388
  89.5 392.0 %all-gather.5.cloned.1.call-start = ((), (), s32[]{:S(2)}) async-start(), calls=%async_computation.1 | async-start | bytes 2359296 | tf_op jit(solution)/shard_map/all_gather | solution.py:2352
  90.7 3.9 copy-start.19
  92.3 2.3 copy-start.22
  94.6 135.5 %copy-start = (f32[64,2048]{1,0:T(8,128)S(1)}, f32[64,2048]{1,0:T(8,128)}, u32[]{:S(2)}) copy-start(f32[64,2048]{1,0:T(8,128)} %get-tuple-element.58) | copy-start | bytes 1572868
  94.6 135.5 %copy-start.12 = (f32[2048]{0:T(1024)S(1)}, f32[2048]{0:T(1024)}, u32[]{:S(2)}) copy-start(f32[2048]{0:T(1024)} %param.25) | copy-start | bytes 24580
  290.7 93.3 %copy-start.9 = (f32[64,640]{1,0:T(8,128)S(1)}, f32[64,640]{1,0:T(8,128)}, u32[]{:S(2)}) copy-start(f32[64,640]{1,0:T(8,128)} %get-tuple-element.69) | copy-start | bytes 491524
  290.7 93.3 %copy-start.14 = (f32[512]{0:T(512)S(1)}, f32[512]{0:T(512)}, u32[]{:S(2)}) copy-start(f32[512]{0:T(512)} %param.22) | copy-start | bytes 6148
  290.7 93.3 %copy-start.18 = (f32[64]{0:T(128)S(1)}, f32[64]{0:T(128)}, u32[]{:S(2)}) copy-start(f32[64]{0:T(128)} %fusion.30) | copy-start | bytes 772
  290.7 94.5 %copy-start.23 = (f32[64]{0:T(128)S(1)}, f32[64]{0:T(128)}, u32[]{:S(2)}) copy-start(f32[64]{0:T(128)} %copy-done.22) | copy-start | bytes 772
  290.7 95.5 %copy-start.16 = (f32[32]{0:T(128)S(1)}, f32[32]{0:T(128)}, u32[]{:S(2)}) copy-start(f32[32]{0:T(128)} %copy-done.15) | copy-start | bytes 388
  290.7 95.5 %copy-start.21 = (f32[64]{0:T(128)S(1)}, f32[64]{0:T(128)}, u32[]{:S(2)}) copy-start(f32[64]{0:T(128)} %dynamic-slice_convert_fusion.1) | copy-start | bytes 772
  290.7 96.6 %copy-start.13 = (f32[2048]{0:T(1024)S(1)}, f32[2048]{0:T(1024)}, u32[]{:S(2)}) copy-start(f32[2048]{0:T(1024)} %param.19) | copy-start | bytes 24580
  290.7 96.6 %copy-start.17 = (f32[64]{0:T(128)S(1)}, f32[64]{0:T(128)}, u32[]{:S(2)}) copy-start(f32[64]{0:T(128)} %fusion.31) | copy-start | bytes 772
  383.9 6.0 %copy-start.20 = (f32[64]{0:T(128)S(1)}, f32[64]{0:T(128)}, u32[]{:S(2)}) copy-start(f32[64]{0:T(128)} %copy-done.19) | copy-start | bytes 772
  383.9 6.1 %copy-start.1 = (f32[64,2048]{1,0:T(8,128)S(1)}, f32[64,2048]{1,0:T(8,128)}, u32[]{:S(2)}) copy-start(f32[64,2048]{1,0:T(8,128)} %get-tuple-element.57) | copy-start | bytes 1572868
  383.9 6.1 %copy-start.10 = (f32[64,2048]{1,0:T(8,128)S(1)}, f32[64,2048]{1,0:T(8,128)}, u32[]{:S(2)}) copy-start(f32[64,2048]{1,0:T(8,128)} %get-tuple-element.74) | copy-start | bytes 1572868
  430.1 6.8 %copy-start.8 = (bf16[4,2,64,1024]{3,2,1,0:T(8,128)(2,1)S(1)}, bf16[4,2,64,1024]{3,2,1,0:T(8,128)(2,1)}, u32[]{:S(2)}) copy-start(bf16[4,2,64,1024]{3,2,1,0:T(8,128)(2,1)} %get-tuple-element.79) | copy-start | bytes 3145732
  433.2 5.3 %copy-start.3 = (bf16[704,2048]{1,0:T(8,128)(2,1)S(1)}, bf16[704,2048]{1,0:T(8,128)(2,1)}, u32[]{:S(2)}) copy-start(bf16[704,2048]{1,0:T(8,128)(2,1)} %get-tuple-element.83) | copy-start | bytes 8650756
  438.5 3.3 copy-start.2
  441.8 3.7 copy-start.6
  441.8 4.8 copy-start.7
  446.6 6.9 %copy-start.4 = (bf16[2,352,2048]{2,1,0:T(8,128)(2,1)S(1)}, bf16[2,352,2048]{2,1,0:T(8,128)(2,1)}, u32[]{:S(2)}) copy-start(bf16[2,352,2048]{2,1,0:T(8,128)(2,1)} %get-tuple-element.84) | copy-start | bytes 8650756
  446.6 6.9 %copy-start.5 = (bf16[2,352,2048]{2,1,0:T(8,128)(2,1)S(1)}, bf16[2,352,2048]{2,1,0:T(8,128)(2,1)}, u32[]{:S(2)}) copy-start(bf16[2,352,2048]{2,1,0:T(8,128)(2,1)} %get-tuple-element.85) | copy-start | bytes 8650756
  446.6 13.0 %slice-start = ((s8[8388608]{0:T(1024)(128)(4,1)}), s8[4194304]{0:T(1024)(128)(4,1)S(1)}, s32[]{:S(2)}) async-start(s8[8388608]{0:T(1024)(128)(4,1)} %bitcast.59), calls=%async_computation.2 | async-start | bytes 8388608
  453.5 6.1 %slice-start.1 = ((s8[8388608]{0:T(1024)(128)(4,1)}), s8[4194304]{0:T(1024)(128)(4,1)S(1)}, s32[]{:S(2)}) async-start(s8[8388608]{0:T(1024)(128)(4,1)} %bitcast.59), calls=%async_computation.3 | async-start | bytes 8388608
  453.5 6.1 %copy-start.11 = (bf16[32,64,768]{2,1,0:T(8,128)(2,1)S(1)}, bf16[32,64,768]{2,1,0:T(8,128)(2,1)}, u32[]{:S(2)}) copy-start(bf16[32,64,768]{2,1,0:T(8,128)(2,1)} %get-tuple-element.76) | copy-start | bytes 9437188
  459.6 7.0 %copy-start.24 = (bf16[4,2,256,768]{3,2,1,0:T(8,128)(2,1)S(1)}, bf16[4,2,256,768]{3,2,1,0:T(8,128)(2,1)}, u32[]{:S(2)}) copy-start(bf16[4,2,256,768]{3,2,1,0:T(8,128)(2,1)} %get-tuple-element.78) | copy-start | bytes 9437188
Sparse Core Ops, SparseCore 0:
  89.6 90.3 all-gather.2
  433.3 48.1 all-gather.4
